TPU v7x, 128 devices: a whole 4x4x4 slice. The times are simulated.
128 devices in a mesh: dp: 32 (over y, x_hi, z), mp: 4 (over x_lo, core).
Axes of the slice: x: 4 (x_hi: 2, x_lo: 2; x = x_hi * 2 + x_lo), y: 4, z: 4, core: 2. Of those that a mesh axis runs over, the one named last changes fastest.
Arguments:
- lag_sequences: bfloat16 [98304, 336], P(('dp', 'mp')), may hold values from -6 to 6
- sample_cluster_label: int32 [98304], P(('dp', 'mp')), may hold values from 0 to 3
- entry_dense_matrix: bfloat16 [2, 560, 512], P(None, None, 'mp'), may hold values from -0.5 to 0.5
- dense_matrix_middle: bfloat16 [2, 512, 512], P(None, 'mp'), may hold values from -0.25 to 0.25
- dense_matrix_later: bfloat16 [2, 512, 512], P(None, None, 'mp'), may hold values from -0.25 to 0.25
- dense_matrix_last: bfloat16 [2, 512, 512], P(None, 'mp'), may hold values from -0.25 to 0.25
- past_coefficient_matrix: bfloat16 [2, 512, 512], P(None, None, 'mp'), may hold values from -0.25 to 0.25
- future_coefficient_matrix: bfloat16 [2, 512, 512], P(None, None, 'mp'), may hold values from -0.25 to 0.25
- generic_expansion_matrix: bfloat16 [2, 512, 640], P(None, 'mp'), may hold values from -0.25 to 0.25
- prediction_adjoint: bfloat16 [98304, 48], P(('dp', 'mp')), may hold values from -6 to 6
- leftover_cotan: bfloat16 [98304, 336], P(('dp', 'mp')), may hold values from -6 to 6
Outputs:
- outlook_aggregate: float32 [98304, 48], P(('dp', 'mp'))
- residual: float32 [98304, 336], P(('dp', 'mp'))
- sequence_slope: float32 [98304, 336], P(('dp', 'mp'))
- grad_input: float32 [2, 560, 512], P(None, None, 'mp')
- grad_second: float32 [2, 512, 512], P(None, 'mp')
- grad_third: float32 [2, 512, 512], P(None, None, 'mp')
- grad_fourth: float32 [2, 512, 512], P(None, 'mp')
- grad_back: float32 [2, 512, 512], P(None, None, 'mp')
- grad_fore: float32 [2, 512, 512], P(None, None, 'mp')
- grad_basis: float32 [2, 512, 640], P(None, 'mp')
Inputs may be any that keep to these rules, and one draw needn't show every extreme that they name: `sample_cluster_label`: each window's frequency group: 0 yearly, 1 quarterly, 2 monthly, 3 hourly.
All inputs are finite; a program needn't handle non-finite values.
Results may differ from a plain program's by a relative error of at most 0.015.
Values may be sent and summed in bfloat16 or wider, within the bound.
No kernel may reach another device: no remote copies, remote signals or barrier semaphores. Data moves between devices by JAX's collectives and lax.ppermute only.
A program may use at most 192 MiB of HBM per device.

v0:
```python
import functools
import math

import jax
import jax.numpy as jnp
from jax import lax
from jax.experimental import pallas as pl
from jax.experimental.pallas import tpu as pltpu
from jax.sharding import PartitionSpec as P

BF = jnp.bfloat16
F32 = jnp.float32
ROWS = 768
ENTRY, SECOND, THIRD, FOURTH, BACK, FORE, BASIS, USED = 0, 560, 1072, 1584, 2096, 2608, 3120, 3760
PACK = 3840
CHUNK, PIECE = PACK // 4, PACK // 16


def place(y, x, z, c):
    y, x, z, c = y % 4, x % 4, z % 4, c % 2
    return ((((y * 2 + x // 2) * 4 + z) * 2) + x % 2) * 2 + c


def pairs(move):
    out = []
    for y in range(4):
        for x in range(4):
            for z in range(4):
                for c in range(2):
                    out.append((place(y, x, z, c), place(*move(y, x, z, c))))
    return tuple(out)


def to_core():
    return pairs(lambda y, x, z, c: (y, x, z, 1 - c))


def to_x(step):
    return pairs(lambda y, x, z, c: (y, x + step, z, c))


def to_x_by_core():
    return pairs(lambda y, x, z, c: (y, x + 1 - 2 * c, z, c))


def to_first(step):
    return pairs(lambda y, x, z, c: (y + step, x, z, c) if c == 0 else (y, x, z + step, c))


def to_second(step):
    return pairs(lambda y, x, z, c: (y, x, z + step, c) if c == 0 else (y + step, x, z, c))


def send(values, where):
    return lax.ppermute(values, ("dp", "mp"), where)


def row_of(count, begin=0):
    return lax.broadcasted_iota(jnp.int32, (count, ROWS), 0) + begin


def turn(values, shift):
    return pltpu.roll(values, shift % values.shape[0], 0)


def widen_look(v, label):
    zero = jnp.float32(0)
    e = [label == g for g in range(4)]
    near = turn(v[:56], 2)
    far = turn(v[:128], 2)
    top = row_of(56) < 2
    tip = row_of(8) < 2
    mid = jnp.where(
        top, jnp.where(e[0], v[40:96], zero), jnp.where(e[1], near, zero)
    )
    joint = jnp.where(
        tip, jnp.where(e[1], near[:8], zero), jnp.where(e[2], far[:8], zero)
    )
    return jnp.concatenate(
        [
            jnp.where(e[0], v[:40], zero),
            mid,
            joint,
            jnp.where(e[2], far[8:], zero),
            jnp.where(e[3], v, zero),
        ],
        axis=0,
    )


def pick_look(u, label):
    zero = jnp.float32(0)
    e = [label == g for g in range(4)]
    last = jnp.where(e[3], u[224:560], zero)
    near = turn(u[40:104], -2)
    far = turn(u[96:224], -2)
    row = row_of(56)
    begin = jnp.where(
        e[2],
        far[:56],
        jnp.where(e[1], near[:56], jnp.where(e[0] & (row < 42), u[:56], last[:56])),
    )
    middle = jnp.where(e[2] & (row_of(72, 56) < 126), far[56:], last[56:128])
    return jnp.concatenate([begin, middle, last[128:]], axis=0)


def widen_reach(a, label):
    zero = jnp.float32(0)
    e = [label == g for g in range(4)]
    one = turn(a[:16], 6)
    two = turn(a[:24], 6)
    row = row_of(8)
    return jnp.concatenate(
        [
            jnp.where(row < 6, jnp.where(e[0], a[:8], zero), jnp.where(e[1], one[:8], zero)),
            jnp.where(row < 6, jnp.where(e[1], one[8:], zero), jnp.where(e[2], two[:8], zero)),
            jnp.where(e[2], two[8:], zero),
            jnp.where(e[3], a, zero),
        ],
        axis=0,
    )


def pick_reach(u, label):
    zero = jnp.float32(0)
    e = [label == g for g in range(4)]
    last = jnp.where(e[3], u[32:], zero)
    one = turn(u[:16], -6)
    two = turn(u[8:32], -6)
    row = row_of(8)
    return jnp.concatenate(
        [
            jnp.where(
                e[2],
                two[:8],
                jnp.where(e[1], one[:8], jnp.where(e[0] & (row < 6), u[:8], last[:8])),
            ),
            jnp.where(e[2] & (row_of(16, 8) < 18), two[8:], last[8:24]),
            last[24:],
        ],
        axis=0,
    )


def look_mask(label):
    reach = jnp.where(label == 0, 42, jnp.where(label == 1, 56, jnp.where(label == 2, 126, 336)))
    return row_of(336) < reach


def by_columns(slots, begin, count):
    return jnp.concatenate([slot[begin : begin + count, :] for slot in slots], axis=1)


def by_rows(slots, begin, count):
    return jnp.concatenate(
        [
            jnp.concatenate(
                [slot[begin + 128 * i : begin + 128 * (i + 1), :] for i in range(count)], axis=1
            )
            for slot in slots
        ],
        axis=0,
    )


def dot(a, b):
    return jnp.dot(a, b, preferred_element_type=F32)


def dot_t(a, b):
    return lax.dot_general(a, b, (((1,), (1,)), ((), ())), preferred_element_type=F32)


def t_dot(a, b):
    return lax.dot_general(a, b, (((0,), (0,)), ((), ())), preferred_element_type=F32)


def silu_both(pre):
    s = 0.5 * jnp.tanh(0.5 * pre) + 0.5
    act = pre * s
    return act.astype(BF), (s + act * (1.0 - s)).astype(BF)


TABLES = {
    "entry": (ENTRY, 560),
    "second": (SECOND, 512),
    "third": (THIRD, 512),
    "fourth": (FOURTH, 512),
    "back": (BACK, 512),
    "fore": (FORE, 512),
    "basis": (BASIS, 640),
}


class Weights:
    def __init__(self, slots):
        self.slots = slots

    def get(self, name):
        begin, count = TABLES[name]
        if name in ("second", "fourth"):
            return by_rows(self.slots, begin, 4)
        return by_columns(self.slots, begin, count)


def run_forward(state, label, weights, e_ref, act_ref, slope_ref, theta_ref):
    e_ref[...] = widen_look(state, label).astype(BF)
    act, slope = silu_both(t_dot(weights.get("entry"), e_ref[...]))
    act_ref[0], slope_ref[0] = act, slope
    for i, name in enumerate(("second", "third", "fourth")):
        act, slope = silu_both(t_dot(weights.get(name), act_ref[i]))
        act_ref[i + 1], slope_ref[i + 1] = act, slope
    theta_ref[0] = t_dot(weights.get("back"), act_ref[3]).astype(BF)
    theta_ref[1] = t_dot(weights.get("fore"), act_ref[3]).astype(BF)
    basis = weights.get("basis")
    return dot(basis[:560], theta_ref[0]), dot(basis[560:], theta_ref[1])


class Grads:
    def __init__(self, outs, base=0):
        self.outs, self.base = outs, base

    def put(self, name, grad):
        begin, count = TABLES[name]
        at = begin - self.base
        for slot in range(4):
            out = self.outs[slot % 2]
            if name in ("second", "fourth"):
                for i in range(4):
                    out[slot // 2, at + 128 * i : at + 128 * (i + 1), :] = grad[
                        128 * slot : 128 * (slot + 1), 128 * i : 128 * (i + 1)
                    ].astype(BF)
            else:
                out[slot // 2, at : at + count, :] = grad[:, 128 * slot : 128 * (slot + 1)].astype(BF)
        if name == "basis":
            for out in self.outs:
                out[:, USED - self.base : PACK - self.base, :] = jnp.zeros((2, PACK - USED, 128), BF)


def backward_heads(g, fore_wide, label, weights, act_ref, slope_ref, theta_ref, grads):
    d_back = -widen_look(g, label).astype(BF)
    d_fore = fore_wide.astype(BF)
    basis = weights.get("basis")
    d_theta_b = t_dot(basis[:560], d_back).astype(BF)
    d_theta_f = t_dot(basis[560:], d_fore).astype(BF)
    grads.put(
        "basis",
        jnp.concatenate([dot_t(d_back, theta_ref[0]), dot_t(d_fore, theta_ref[1])], axis=0),
    )
    d_act = dot(weights.get("back"), d_theta_b) + dot(weights.get("fore"), d_theta_f)
    grads.put("back", dot_t(act_ref[3], d_theta_b))
    grads.put("fore", dot_t(act_ref[3], d_theta_f))
    d_pre = (d_act * slope_ref[3].astype(F32)).astype(BF)
    grads.put("fourth", dot_t(act_ref[2], d_pre))
    return d_pre


def backward_layers(g, d_pre, label, weights, e_ref, act_ref, slope_ref, grads):
    d_act = dot(weights.get("fourth"), d_pre)
    d_pre = (d_act * slope_ref[2].astype(F32)).astype(BF)
    grads.put("third", dot_t(act_ref[1], d_pre))
    d_act = dot(weights.get("third"), d_pre)
    d_pre = (d_act * slope_ref[1].astype(F32)).astype(BF)
    grads.put("second", dot_t(act_ref[0], d_pre))
    d_act = dot(weights.get("second"), d_pre)
    d_pre = (d_act * slope_ref[0].astype(F32)).astype(BF)
    grads.put("entry", dot_t(e_ref[...], d_pre))
    return g + pick_look(dot(weights.get("entry"), d_pre), label)


def places():
    dp, core = lax.axis_index("dp"), lax.rem(lax.axis_index("mp"), 2)
    y, z = lax.div(dp, 8), lax.rem(dp, 4)
    return jnp.where(core == 0, y, z), jnp.where(core == 0, z, y)


def pack_kernel(k, *refs):
    ins, out, quarter = refs[:7], refs[7], refs[8:]
    entry, second, third, fourth, back, fore, basis = (ref.at[k] for ref in ins)
    out[ENTRY:SECOND, :] = entry[...]
    out[THIRD:FOURTH, :] = third[...]
    out[BACK:FORE, :] = back[...]
    out[FORE:BASIS, :] = fore[...]
    for i in range(4):
        out[SECOND + 128 * i : SECOND + 128 * (i + 1), :] = second[:, 128 * i : 128 * (i + 1)]
        out[FOURTH + 128 * i : FOURTH + 128 * (i + 1), :] = fourth[:, 128 * i : 128 * (i + 1)]
    for i in range(5):
        out[BASIS + 128 * i : BASIS + 128 * (i + 1), :] = basis[:, 128 * i : 128 * (i + 1)].T
    out[USED:PACK, :] = jnp.zeros((PACK - USED, 128), BF)
    if quarter:
        i1, _ = places()
        quarter[0][...] = out[pl.ds(pl.multiple_of(i1 * CHUNK, CHUNK), CHUNK), :]


def join_kernel(q0, q1, q2, q3, out):
    i1, _ = places()
    for a, quarter in zip((0, 3, 1, 2), (q0, q1, q2, q3)):
        begin = pl.multiple_of(lax.rem(i1 + a, 4) * CHUNK, CHUNK)
        out[pl.ds(begin, CHUNK), :] = quarter[...]


def first_kernel(label, lag, s0, s1, s2, s3, state_out, look_out, e, act, slope, theta):
    weights = Weights((s0, s1, s2, s3))
    labels = label[...]
    state = jnp.where(look_mask(labels), lag[...].astype(F32), 0.0)
    heads, fore = run_forward(state, labels, weights, e, act, slope, theta)
    state_out[...] = state - pick_look(heads, labels)
    look_out[...] = pick_reach(fore, labels)


def second_kernel(
    label, state_in, look_in, left, adjoint, s0, s1, s2, s3, rest, look, g_out, mine, theirs, e, act, slope, theta
):
    weights = Weights((s0, s1, s2, s3))
    labels = label[...]
    heads, fore = run_forward(state_in[...], labels, weights, e, act, slope, theta)
    rest[...] = state_in[...] - pick_look(heads, labels)
    look[...] = look_in[...] + pick_reach(fore, labels)
    grads = Grads((mine, theirs))
    g = left[...].astype(F32)
    fore_wide = widen_reach(adjoint[...].astype(F32), labels)
    d_pre = backward_heads(g, fore_wide, labels, weights, act, slope, theta, grads)
    g_out[...] = backward_layers(g, d_pre, labels, weights, e, act, slope, grads)


def third_kernel(label, g_in, adjoint, s0, s1, s2, s3, act, slope, theta, d_out, mine, theirs):
    grads = Grads((mine, theirs), FOURTH)
    labels = label[...]
    fore_wide = widen_reach(adjoint[...].astype(F32), labels)
    d_out[...] = backward_heads(
        g_in[...], fore_wide, labels, Weights((s0, s1, s2, s3)), act, slope, theta, grads
    )


def fourth_kernel(label, g_in, d_in, s0, s1, s2, s3, e, act, slope, steep, mine, theirs):
    grads = Grads((mine, theirs))
    labels = label[...]
    g = backward_layers(g_in[...], d_in[...], labels, Weights((s0, s1, s2, s3)), e, act, slope, grads)
    steep[...] = jnp.where(look_mask(labels), g, 0.0)


def cut_kernel(count, *refs):
    parts, outs, whole = refs[: 2 * count], refs[2 * count : -1], refs[-1]
    i1, _ = places()
    at = 0
    for mine, got in zip(parts[:count], parts[count:]):
        rows = mine.shape[1]
        whole[:, at : at + rows, :] = (
            mine[...].astype(F32) + got[...].astype(F32)
        ).astype(BF)
        at += rows
    for a, out in zip((1, 3, 2, 0), outs):
        begin = pl.multiple_of(lax.rem(i1 + a, 4) * CHUNK, CHUNK)
        out[...] = whole[:, pl.ds(begin, CHUNK), :]


def piece_kernel(*refs):
    chunks, outs, whole = refs[:8], refs[8:12], refs[12]
    _, i2 = places()
    for k in range(2):
        own, a, b, c = (ref[...].astype(F32) for ref in chunks[4 * k : 4 * k + 4])
        whole[:, k] = ((own + a) + (b + c)).astype(BF)
    for a, out in zip((1, 3, 2, 0), outs):
        begin = pl.multiple_of(lax.rem(i2 + a, 4) * PIECE, PIECE)
        out[...] = whole[:, :, pl.ds(begin, PIECE), :]


def unpack_kernel(s0, s1, s2, s3, entry, second, third, fourth, back, fore, basis, whole, sem):
    i1, i2 = places()
    copies = []
    for a, stack in zip((0, 3, 1, 2), (s0, s1, s2, s3)):
        chunk = lax.rem(i1 + a, 4)
        for slot, b in enumerate((0, 3, 1, 2)):
            piece = lax.rem(i2 + b, 4)
            at = pl.multiple_of(chunk * CHUNK + piece * PIECE, PIECE)
            copy = pltpu.make_async_copy(
                stack.at[slot], whole.at[:, pl.ds(at, PIECE), :], sem.at[len(copies)]
            )
            copy.start()
            copies.append(copy)
    for copy in copies:
        copy.wait()
    scale = 1.0 / math.sqrt(98304)

    def part(k, begin, count):
        return whole[k, begin : begin + count, :].astype(F32) * scale

    for k in range(2):
        entry[k] = part(k, ENTRY, 560)
        third[k] = part(k, THIRD, 512)
        back[k] = part(k, BACK, 512)
        fore[k] = part(k, FORE, 512)
        for i in range(4):
            second[k, :, 128 * i : 128 * (i + 1)] = part(k, SECOND + 128 * i, 128)
            fourth[k, :, 128 * i : 128 * (i + 1)] = part(k, FOURTH + 128 * i, 128)
        for i in range(5):
            basis[k, :, 128 * i : 128 * (i + 1)] = part(k, BASIS + 128 * i, 128).T


def shape(*dims, kind=F32):
    return jax.ShapeDtypeStruct(dims, kind)


def vmem(*dims, kind=BF):
    return pltpu.VMEM(dims, kind)


M1, M2, M3, M4, M5 = 12, 20, 12, 12, 8
DMA = pltpu.SemaphoreType.DMA
IN_VMEM = pl.BlockSpec(memory_space=pltpu.VMEM)
ANYWHERE = pl.BlockSpec(memory_space=pl.ANY)


def call(kernel, name, ins, outs, scratch, mib, us):
    return pl.pallas_call(
        kernel,
        out_shape=[o[0] for o in outs],
        in_specs=ins,
        out_specs=[o[1] for o in outs],
        scratch_shapes=scratch,
        compiler_params=pltpu.CompilerParams(vmem_limit_bytes=mib * 1024 * 1024),
        cost_estimate=pl.CostEstimate(
            flops=int(us * 8e8), bytes_accessed=int(us * 1e6), transcendentals=0
        ),
        name=name,
    )


ACTS = (4, 512, ROWS)
KEPT = [(560, ROWS), ACTS, ACTS, (2, 512, ROWS)]
TOP, LOW = PACK - FOURTH, FOURTH


def plus(*parts):
    return sum(part.astype(F32) for part in parts).astype(BF)


def shards(lag, label, entry, second, third, fourth, back, fore, basis, adjoint, left):
    label = label[None, :]
    lag, adjoint, left = lag.T, adjoint.T, left.T
    whole, part = shape(PACK, 128, kind=BF), shape(CHUNK, 128, kind=BF)
    tables = (entry, second, third, fourth, back, fore, basis)
    two, quarter = call(
        functools.partial(pack_kernel, 1), "pack_two", [IN_VMEM] * 7, [(whole, IN_VMEM), (part, IN_VMEM)], [], 60, 2
    )(*tables)
    quarter, *tables = lax.optimization_barrier((quarter, *tables))
    one = call(functools.partial(pack_kernel, 0), "pack_one", [IN_VMEM] * 7, [(whole, IN_VMEM)], [], 60, 2)(*tables)[0]
    quarter = send(quarter, to_x_by_core())
    quarters = [quarter]
    one, quarters[0] = lax.optimization_barrier((one, quarters[0]))
    across = send(one, to_x_by_core())
    quarters += [send(quarters[0], to_first(a)) for a in (1, 3, 2)]
    across, *quarters = lax.optimization_barrier((across, *quarters))
    slots1 = (one, send(one, to_core()), across, send(across, to_core()))
    across = call(join_kernel, "join", [IN_VMEM] * 4, [(whole, IN_VMEM)], [], M5, 1)(*quarters)[0]
    slots2 = (two, send(two, to_core()), across, send(across, to_core()))
    state1, look1, e1, act1, slope1, theta1 = call(
        first_kernel,
        "forward_one",
        [IN_VMEM] * 6,
        [(shape(336, ROWS), IN_VMEM), (shape(48, ROWS), IN_VMEM)]
        + [(shape(*k, kind=BF), IN_VMEM) for k in KEPT],
        [],
        M1,
        6,
    )(label, lag, *slots1)
    rest, look, g1, mine2, theirs2 = call(
        second_kernel,
        "block_two",
        [IN_VMEM] * 9,
        [(shape(336, ROWS), IN_VMEM), (shape(48, ROWS), IN_VMEM), (shape(336, ROWS), IN_VMEM)]
        + [(shape(2, PACK, 128, kind=BF), IN_VMEM)] * 2,
        [vmem(*k) for k in KEPT],
        M2,
        14,
    )(label, state1, look1, left, adjoint, *slots2)
    got2 = send(theirs2, to_core())
    d_pre, mine1a, theirs1a = call(
        third_kernel,
        "backward_one_heads",
        [IN_VMEM] * 10,
        [(shape(512, ROWS, kind=BF), IN_VMEM)] + [(shape(2, TOP, 128, kind=BF), IN_VMEM)] * 2,
        [],
        M3,
        6,
    )(label, g1, adjoint, *slots1, act1, slope1, theta1)
    got1a = send(theirs1a, to_core())

    def cut(mine, got, name):
        return call(
            functools.partial(cut_kernel, len(mine)),
            name,
            [IN_VMEM] * (2 * len(mine)),
            [(shape(2, CHUNK, 128, kind=BF), IN_VMEM)] * 4,
            [vmem(2, PACK, 128)],
            M5,
            2,
        )(*mine, *got)

    *out2, own2 = cut([mine2], [got2], "cut_two")
    got2 = [send(part, to_first(a)) for part, a in zip(out2, (1, 3, 2))]
    d_pre, *out2 = lax.optimization_barrier((d_pre, *out2))
    steep, mine1b, theirs1b = call(
        fourth_kernel,
        "backward_one_layers",
        [IN_VMEM] * 10,
        [(shape(336, ROWS), IN_VMEM)] + [(shape(2, LOW, 128, kind=BF), IN_VMEM)] * 2,
        [],
        M4,
        6,
    )(label, g1, d_pre, *slots1, e1, act1, slope1)
    got1b = send(theirs1b, to_core())
    *out1, own1 = cut([mine1b, mine1a], [got1b, got1a], "cut_one")
    got1 = [send(part, to_first(a)) for part, a in zip(out1, (1, 3, 2))]
    *out, own = call(
        piece_kernel,
        "pieces",
        [IN_VMEM] * 8,
        [(shape(2, 2, PIECE, 128, kind=BF), IN_VMEM)] * 4,
        [vmem(2, 2, CHUNK, 128)],
        M5,
        2,
    )(own1, *got1, own2, *got2)
    got = [send(part, to_second(b)) for part, b in zip(out, (1, 3, 2))]
    done = plus(own, *got)
    got = [send(done[1], to_x(1)), send(done[1], to_x(3)), send(done[0], to_x(2))]
    done = plus(done[0], *got)
    stack = jnp.stack([done] + [send(done, to_second(b)) for b in (1, 3, 2)])
    stacks = [stack] + [send(stack, to_first(a)) for a in (1, 3, 2)]
    grads = call(
        unpack_kernel,
        "unpack",
        [ANYWHERE] * 4,
        [
            (shape(*dims), IN_VMEM)
            for dims in (
                (2, 560, 128), (2, 128, 512), (2, 512, 128), (2, 128, 512), (2, 512, 128), (2, 512, 128), (2, 128, 640),
            )
        ],
        [vmem(2, PACK, 128), DMA((16,))],
        32,
        3,
    )(*stacks)
    return (look.T, rest.T, steep.T, *grads)


def solution(mesh):
    windows = P(("dp", "mp"), None)
    columns, rows = P(None, None, "mp"), P(None, "mp", None)
    tables = (columns, rows, columns, rows, columns, columns, rows)
    return jax.shard_map(
        shards,
        mesh=mesh,
        in_specs=(windows, P(("dp", "mp")), *tables, windows, windows),
        out_specs=(windows, windows, windows, *tables),
        check_vma=False,
    )
```

profile of v0, /device:TPU:0, one launch (start us, length us, event | category | flops | bytes accessed | tf_op | source)
XLA Modules:
  0.0 137.8 jit_solution(11792071423432068719)
XLA Ops:
  0.6 2.6 %pack_two.1 = (bf16[3840,128]{1,0:T(8,128)(2,1)}, bf16[960,128]{1,0:T(8,128)(2,1)}) custom-call(bf16[2,560,128]{2,1,0:T(8,128)(2,1)} %refs_0_.2, bf16[2,128,512]{2,1,0:T(8,128)(2,1)} %refs_1_.2, bf16[2,512,128]{2,1,0:T(8,128)(2,1)} %refs_2_.2, bf16[2,128,512]{2,1,0:T(8,128)(2,1)} %refs_3_.2, bf16[2,512,128]{2,1,0:T(8,128)(2,1)} %refs_4_.2, ...), custom_call_target="tpu_custom_call" | custom-call | flops 1600000000 | bytes 2000000 | tf_op jit(solution)/shard_map/pack_two/pallas_call | solution.py:443
  3.2 1.6 %collective-permute-start = (bf16[960,128]{1,0:T(8,128)(2,1)}, bf16[960,128]{1,0:T(8,128)(2,1)S(1)}, u32[]{:S(2)}, u32[]{:S(2)}) collective-permute-start(bf16[960,128]{1,0:T(8,128)(2,1)} %get-tuple-element.72), channel_id=1, source_target_pairs={{0,2},{1,19},{4,6},{5,23},{8,10},{9,27},{12,14},{13,31},{2,16},{3,... | collective-permute-start | bytes 737288 | tf_op jit(solution)/shard_map/ppermute | solution.py:55
  4.8 2.5 %pack_one.1.s0 = bf16[3840,128]{1,0:T(8,128)(2,1)} custom-call(bf16[2,560,128]{2,1,0:T(8,128)(2,1)} %refs_0_.2, bf16[2,128,512]{2,1,0:T(8,128)(2,1)} %refs_1_.2, bf16[2,512,128]{2,1,0:T(8,128)(2,1)} %refs_2_.2, bf16[2,128,512]{2,1,0:T(8,128)(2,1)} %refs_3_.2, bf16[2,512,128]{2,1,0:T(8,128)(2,1)} %refs_4_.2, bf16[2,512,128]{2,1,0:T(8,128)(2,1)} %refs_5_.2, ...), custom_call_target="tpu_custom_call" | custom-call | flops 1600000000 | bytes 2000000 | tf_op jit(solution)/shard_map/pack_one/pallas_call | solution.py:447
  7.3 3.5 %collective-permute-done.q0 = bf16[960,128]{1,0:T(8,128)(2,1)S(1)} collective-permute-done((bf16[960,128]{1,0:T(8,128)(2,1)}, bf16[960,128]{1,0:T(8,128)(2,1)S(1)}, u32[]{:S(2)}, u32[]{:S(2)}) %collective-permute-start) | collective-permute-done | bytes 245792 | tf_op jit(solution)/shard_map/ppermute | solution.py:55
  10.8 0.4 collective-permute-start.2
  11.2 3.2 %collective-permute-start.5 = (bf16[960,128]{1,0:T(8,128)(2,1)S(1)}, bf16[960,128]{1,0:T(8,128)(2,1)S(1)}, u32[]{:S(2)}, u32[]{:S(2)}) collective-permute-start(bf16[960,128]{1,0:T(8,128)(2,1)S(1)} %collective-permute-done.q0), channel_id=1, source_target_pairs={{0,64},{1,9},{4,68},{5,13},{8,72},{9,1},{12,76},{13,5},{2,66},{3,1... | collective-permute-start | bytes 737288 | tf_op jit(solution)/shard_map/ppermute | solution.py:55
  14.4 1.1 collective-permute-start.4
  15.5 1.0 collective-permute-start.3
  16.4 0.7 collective-permute-start.1
  17.2 1.8 %collective-permute-done.5.q3 = bf16[960,128]{1,0:T(8,128)(2,1)S(1)} collective-permute-done((bf16[960,128]{1,0:T(8,128)(2,1)S(1)}, bf16[960,128]{1,0:T(8,128)(2,1)S(1)}, u32[]{:S(2)}, u32[]{:S(2)}) %collective-permute-start.5) | collective-permute-done | bytes 245792 | tf_op jit(solution)/shard_map/ppermute | solution.py:55
  18.9 3.0 %collective-permute-done.4.q2 = bf16[960,128]{1,0:T(8,128)(2,1)S(1)} collective-permute-done((bf16[960,128]{1,0:T(8,128)(2,1)S(1)}, bf16[960,128]{1,0:T(8,128)(2,1)S(1)}, u32[]{:S(2)}, u32[]{:S(2)}) %collective-permute-start.4) | collective-permute-done | bytes 245792 | tf_op jit(solution)/shard_map/ppermute | solution.py:55
  21.9 1.0 collective-permute-done.3.q1
  22.9 3.5 %collective-permute-done.2.s2 = bf16[3840,128]{1,0:T(8,128)(2,1)S(1)} collective-permute-done((bf16[3840,128]{1,0:T(8,128)(2,1)}, bf16[3840,128]{1,0:T(8,128)(2,1)S(1)}, u32[]{:S(2)}, u32[]{:S(2)}) %collective-permute-start.2) | collective-permute-done | bytes 983072 | tf_op jit(solution)/shard_map/ppermute | solution.py:55
  26.4 0.5 collective-permute-start.7
  26.9 0.1 join.1.s2
  27.0 0.3 collective-permute-start.8
  27.3 0.0 collective-permute-done.1.s1
  27.3 1.7 %collective-permute-done.6.s3 = bf16[3840,128]{1,0:T(8,128)(2,1)S(1)} collective-permute-done((bf16[3840,128]{1,0:T(8,128)(2,1)S(1)}, bf16[3840,128]{1,0:T(8,128)(2,1)S(1)}, u32[]{:S(2)}, u32[]{:S(2)}) %collective-permute-start.6) | collective-permute-done | bytes 983072 | tf_op jit(solution)/shard_map/ppermute | solution.py:55
  28.9 4.2 %forward_one.1 = (f32[336,768]{1,0:T(8,128)S(1)}, f32[48,768]{1,0:T(8,128)S(1)}, bf16[560,768]{1,0:T(8,128)(2,1)S(1)}, bf16[4,512,768]{2,1,0:T(8,128)(2,1)S(1)},...) custom-call(s32[1,768]{1,0:T(1,128)S(1)} %broadcast_in_dim.3.label, bf16[336,768]{1,0:T(8,128)(2,1)S(1)} %bitcast.16, ...), custom_call_target="tpu_custom_call" | custom-call | flops 4800000000 | bytes 6000000 | tf_op jit(solution)/shard_map/forward_one/pallas_call | solution.py:457
  33.1 0.0 collective-permute-done.8.s3
  33.2 10.5 %block_two.1 = (f32[336,768]{1,0:T(8,128)}, f32[48,768]{1,0:T(8,128)}, f32[336,768]{1,0:T(8,128)S(1)}, bf16[2,3840,128]{2,1,0:T(8,128)(2,1)S(1)}, bf16[2,3840,128]{2,1,0:T(8,128)(2,1)S(1)}) custom-call(s32[1,768]{1,0:T(1,128)S(1)} %broadcast_in_dim.3.label, f32[336,768]{1,0:T(8,128)S(1)} %get-tuple-element.76.state_in, ...), custom_call_target="tpu_custom_call" | custom-call | flops 11200000000 | bytes 14000000 | tf_op jit(solution)/shard_map/block_two/pallas_call | solution.py:467
  43.7 0.2 collective-permute-start.9
  43.9 3.8 %backward_one_heads.1 = (bf16[512,768]{1,0:T(8,128)(2,1)S(1)}, bf16[2,2256,128]{2,1,0:T(8,128)(2,1)S(1)}, bf16[2,2256,128]{2,1,0:T(8,128)(2,1)S(1)}) custom-call(s32[1,768]{1,0:T(1,128)S(1)} %broadcast_in_dim.3.label, f32[336,768]{1,0:T(8,128)S(1)} %get-tuple-element.85.g_in, bf16[48,768]{1,0:T(8,128)(2,1)S(1)} %bitcast.19, bf16[3840,128]{1,0:T(8,128)(2,1)S(1)} %copy-done, ...), custom_call_target="tpu_custom_call" | custom-call | flops 4800000000 | bytes 6000000 | tf_op jit(solution)/shard_map/backward_one_heads/pallas_call | solution.py:478
  47.7 0.5 collective-permute-start.11
  48.1 0.0 collective-permute-done.9.refs_1_
  48.1 1.2 cut_two.1
  49.4 4.2 %backward_one_layers.1 = (f32[336,768]{1,0:T(8,128)}, bf16[2,1584,128]{2,1,0:T(8,128)(2,1)S(1)}, bf16[2,1584,128]{2,1,0:T(8,128)(2,1)S(1)}) custom-call(s32[1,768]{1,0:T(1,128)S(1)} %broadcast_in_dim.3.label, f32[336,768]{1,0:T(8,128)S(1)} %get-tuple-element.85.g_in, bf16[512,768]{1,0:T(8,128)(2,1)S(1)} %get-tuple-element.95.d_in, ...), custom_call_target="tpu_custom_call" | custom-call | flops 4800000000 | bytes 6000000 | tf_op jit(solution)/shard_map/backward_one_layers/pallas_call | solution.py:503
  53.5 0.1 collective-permute-start.10
  53.7 1.7 %collective-permute-start.15 = (bf16[2,960,128]{2,1,0:T(8,128)(2,1)S(1)}, bf16[2,960,128]{2,1,0:T(8,128)(2,1)S(1)}, u32[]{:S(2)}, u32[]{:S(2)}) collective-permute-start(bf16[2,960,128]{2,1,0:T(8,128)(2,1)S(1)} %get-tuple-element.92), channel_id=1, source_target_pairs={{0,32},{1,5},{4,36},{5,9},{8,40},{9,13},{12,44},{13,1},{2,34},{3,7... | collective-permute-start | bytes 1474568 | tf_op jit(solution)/shard_map/ppermute | solution.py:55
  55.3 1.6 %collective-permute-start.16 = (bf16[2,960,128]{2,1,0:T(8,128)(2,1)S(1)}, bf16[2,960,128]{2,1,0:T(8,128)(2,1)S(1)}, u32[]{:S(2)}, u32[]{:S(2)}) collective-permute-start(bf16[2,960,128]{2,1,0:T(8,128)(2,1)S(1)} %get-tuple-element.93), channel_id=1, source_target_pairs={{0,96},{1,13},{4,100},{5,1},{8,104},{9,5},{12,108},{13,9},{2,98},{... | collective-permute-start | bytes 1474568 | tf_op jit(solution)/shard_map/ppermute | solution.py:55
  56.9 2.1 %collective-permute-start.17 = (bf16[2,960,128]{2,1,0:T(8,128)(2,1)S(1)}, bf16[2,960,128]{2,1,0:T(8,128)(2,1)S(1)}, u32[]{:S(2)}, u32[]{:S(2)}) collective-permute-start(bf16[2,960,128]{2,1,0:T(8,128)(2,1)S(1)} %get-tuple-element.94), channel_id=1, source_target_pairs={{0,64},{1,9},{4,68},{5,13},{8,72},{9,1},{12,76},{13,5},{2,66},{3,1... | collective-permute-start | bytes 1474568 | tf_op jit(solution)/shard_map/ppermute | solution.py:55
  59.0 1.2 cut_one.1
  60.1 0.7 collective-permute-start.12
  60.9 2.6 %collective-permute-start.13 = (bf16[2,960,128]{2,1,0:T(8,128)(2,1)S(1)}, bf16[2,960,128]{2,1,0:T(8,128)(2,1)S(1)}, u32[]{:S(2)}, u32[]{:S(2)}) collective-permute-start(bf16[2,960,128]{2,1,0:T(8,128)(2,1)S(1)} %get-tuple-element.104), channel_id=1, source_target_pairs={{0,96},{1,13},{4,100},{5,1},{8,104},{9,5},{12,108},{13,9},{2,98},{... | collective-permute-start | bytes 1474568 | tf_op jit(solution)/shard_map/ppermute | solution.py:55
  63.5 0.3 collective-permute-done.15.refs_5_
  63.7 7.3 %collective-permute-start.14 = (bf16[2,960,128]{2,1,0:T(8,128)(2,1)S(1)}, bf16[2,960,128]{2,1,0:T(8,128)(2,1)S(1)}, u32[]{:S(2)}, u32[]{:S(2)}) collective-permute-start(bf16[2,960,128]{2,1,0:T(8,128)(2,1)S(1)} %get-tuple-element.105), channel_id=1, source_target_pairs={{0,64},{1,9},{4,68},{5,13},{8,72},{9,1},{12,76},{13,5},{2,66},{3,1... | collective-permute-start | bytes 1474568 | tf_op jit(solution)/shard_map/ppermute | solution.py:55
  71.0 4.5 %collective-permute-done.12.refs_1_ = bf16[2,960,128]{2,1,0:T(8,128)(2,1)S(1)} collective-permute-done((bf16[2,960,128]{2,1,0:T(8,128)(2,1)S(1)}, bf16[2,960,128]{2,1,0:T(8,128)(2,1)S(1)}, u32[]{:S(2)}, u32[]{:S(2)}) %collective-permute-start.12) | collective-permute-done | bytes 491552 | tf_op jit(solution)/shard_map/ppermute | solution.py:55
  75.5 5.3 %collective-permute-done.14.refs_3_ = bf16[2,960,128]{2,1,0:T(8,128)(2,1)S(1)} collective-permute-done((bf16[2,960,128]{2,1,0:T(8,128)(2,1)S(1)}, bf16[2,960,128]{2,1,0:T(8,128)(2,1)S(1)}, u32[]{:S(2)}, u32[]{:S(2)}) %collective-permute-start.14) | collective-permute-done | bytes 491552 | tf_op jit(solution)/shard_map/ppermute | solution.py:55
  80.9 1.1 pieces.1
  82.0 2.0 %collective-permute-start.18 = (bf16[2,2,240,128]{3,2,1,0:T(8,128)(2,1)S(1)}, bf16[2,2,240,128]{3,2,1,0:T(8,128)(2,1)S(1)}, u32[]{:S(2)}, u32[]{:S(2)}) collective-permute-start(bf16[2,2,240,128]{3,2,1,0:T(8,128)(2,1)S(1)} %get-tuple-element.108), channel_id=1, source_target_pairs={{0,4},{1,33},{4,8},{5,37},{8,12},{9,41},{12,0},{13,45},{2,6},{3,35... | collective-permute-start | bytes 737288 | tf_op jit(solution)/shard_map/ppermute | solution.py:55
  84.0 2.2 %collective-permute-start.19 = (bf16[2,2,240,128]{3,2,1,0:T(8,128)(2,1)S(1)}, bf16[2,2,240,128]{3,2,1,0:T(8,128)(2,1)S(1)}, u32[]{:S(2)}, u32[]{:S(2)}) collective-permute-start(bf16[2,2,240,128]{3,2,1,0:T(8,128)(2,1)S(1)} %get-tuple-element.109), channel_id=1, source_target_pairs={{0,12},{1,97},{4,0},{5,101},{8,4},{9,105},{12,8},{13,109},{2,14},{... | collective-permute-start | bytes 737288 | tf_op jit(solution)/shard_map/ppermute | solution.py:55
  86.2 1.8 %collective-permute-start.20 = (bf16[2,2,240,128]{3,2,1,0:T(8,128)(2,1)S(1)}, bf16[2,2,240,128]{3,2,1,0:T(8,128)(2,1)S(1)}, u32[]{:S(2)}, u32[]{:S(2)}) collective-permute-start(bf16[2,2,240,128]{3,2,1,0:T(8,128)(2,1)S(1)} %get-tuple-element.110), channel_id=1, source_target_pairs={{0,8},{1,65},{4,12},{5,69},{8,0},{9,73},{12,4},{13,77},{2,10},{3,6... | collective-permute-start | bytes 737288 | tf_op jit(solution)/shard_map/ppermute | solution.py:55
  88.0 2.3 %collective-permute-done.18 = bf16[2,2,240,128]{3,2,1,0:T(8,128)(2,1)S(1)} collective-permute-done((bf16[2,2,240,128]{3,2,1,0:T(8,128)(2,1)S(1)}, bf16[2,2,240,128]{3,2,1,0:T(8,128)(2,1)S(1)}, u32[]{:S(2)}, u32[]{:S(2)}) %collective-permute-start.18) | collective-permute-done | bytes 245792 | tf_op jit(solution)/shard_map/ppermute | solution.py:55
  90.3 2.3 %collective-permute-done.19 = bf16[2,2,240,128]{3,2,1,0:T(8,128)(2,1)S(1)} collective-permute-done((bf16[2,2,240,128]{3,2,1,0:T(8,128)(2,1)S(1)}, bf16[2,2,240,128]{3,2,1,0:T(8,128)(2,1)S(1)}, u32[]{:S(2)}, u32[]{:S(2)}) %collective-permute-start.19) | collective-permute-done | bytes 245792 | tf_op jit(solution)/shard_map/ppermute | solution.py:55
  92.6 1.8 %collective-permute-done.20 = bf16[2,2,240,128]{3,2,1,0:T(8,128)(2,1)S(1)} collective-permute-done((bf16[2,2,240,128]{3,2,1,0:T(8,128)(2,1)S(1)}, bf16[2,2,240,128]{3,2,1,0:T(8,128)(2,1)S(1)}, u32[]{:S(2)}, u32[]{:S(2)}) %collective-permute-start.20) | collective-permute-done | bytes 245792 | tf_op jit(solution)/shard_map/ppermute | solution.py:55
  94.4 0.1 add_convert_fusion
  94.5 0.7 collective-permute-start.23
  95.2 1.1 collective-permute-start.22
  96.4 0.9 collective-permute-start.21
  97.2 3.9 %collective-permute-done.23 = bf16[2,240,128]{2,1,0:T(8,128)(2,1)S(1)} collective-permute-done((bf16[2,240,128]{2,1,0:T(8,128)(2,1)S(1)}, bf16[2,240,128]{2,1,0:T(8,128)(2,1)S(1)}, u32[]{:S(2)}, u32[]{:S(2)}) %collective-permute-start.23) | collective-permute-done | bytes 122912 | tf_op jit(solution)/shard_map/ppermute | solution.py:55
  101.2 1.3 collective-permute-done.21
  102.5 0.1 add_convert_fusion.1
  102.6 1.3 collective-permute-start.26
  103.9 2.8 %collective-permute-start.25 = (bf16[2,240,128]{2,1,0:T(8,128)(2,1)S(1)}, bf16[2,240,128]{2,1,0:T(8,128)(2,1)S(1)}, u32[]{:S(2)}, u32[]{:S(2)}) collective-permute-start(bf16[2,240,128]{2,1,0:T(8,128)(2,1)S(1)} %add_convert_fusion.1), channel_id=1, source_target_pairs={{0,12},{1,97},{4,0},{5,101},{8,4},{9,105},{12,8},{13,109},{2,14},{... | collective-permute-start | bytes 368648 | tf_op jit(solution)/shard_map/ppermute | solution.py:55
  106.7 2.3 %collective-permute-done.26 = bf16[2,240,128]{2,1,0:T(8,128)(2,1)S(1)} collective-permute-done((bf16[2,240,128]{2,1,0:T(8,128)(2,1)S(1)}, bf16[2,240,128]{2,1,0:T(8,128)(2,1)S(1)}, u32[]{:S(2)}, u32[]{:S(2)}) %collective-permute-start.26) | collective-permute-done | bytes 122912 | tf_op jit(solution)/shard_map/ppermute | solution.py:55
  109.0 0.7 collective-permute-done.25
  109.7 8.5 %collective-permute-done.24 = bf16[2,240,128]{2,1,0:T(8,128)(2,1)S(1)} collective-permute-done((bf16[2,240,128]{2,1,0:T(8,128)(2,1)S(1)}, bf16[2,240,128]{2,1,0:T(8,128)(2,1)S(1)}, u32[]{:S(2)}, u32[]{:S(2)}) %collective-permute-start.24) | collective-permute-done | bytes 122912 | tf_op jit(solution)/shard_map/ppermute | solution.py:55
  118.2 0.1 pad_maximum_fusion.s0
  118.3 1.9 %collective-permute-start.29 = (bf16[4,2,240,128]{3,2,1,0:T(8,128)(2,1)S(1)}, bf16[4,2,240,128]{3,2,1,0:T(8,128)(2,1)S(1)}, u32[]{:S(2)}, u32[]{:S(2)}) collective-permute-start(bf16[4,2,240,128]{3,2,1,0:T(8,128)(2,1)S(1)} %pad_maximum_fusion.s0), channel_id=1, source_target_pairs={{0,64},{1,9},{4,68},{5,13},{8,72},{9,1},{12,76},{13,5},{2,66},{3,1... | collective-permute-start | bytes 1474568 | tf_op jit(solution)/shard_map/ppermute | solution.py:55
  120.3 2.2 %collective-permute-start.28 = (bf16[4,2,240,128]{3,2,1,0:T(8,128)(2,1)S(1)}, bf16[4,2,240,128]{3,2,1,0:T(8,128)(2,1)S(1)}, u32[]{:S(2)}, u32[]{:S(2)}) collective-permute-start(bf16[4,2,240,128]{3,2,1,0:T(8,128)(2,1)S(1)} %pad_maximum_fusion.s0), channel_id=1, source_target_pairs={{0,96},{1,13},{4,100},{5,1},{8,104},{9,5},{12,108},{13,9},{2,98},{... | collective-permute-start | bytes 1474568 | tf_op jit(solution)/shard_map/ppermute | solution.py:55
  122.4 6.4 %collective-permute-done.29.s3 = bf16[4,2,240,128]{3,2,1,0:T(8,128)(2,1)S(1)} collective-permute-done((bf16[4,2,240,128]{3,2,1,0:T(8,128)(2,1)S(1)}, bf16[4,2,240,128]{3,2,1,0:T(8,128)(2,1)S(1)}, u32[]{:S(2)}, u32[]{:S(2)}) %collective-permute-start.29) | collective-permute-done | bytes 491552 | tf_op jit(solution)/shard_map/ppermute | solution.py:55
  128.8 4.9 %collective-permute-done.28.s2 = bf16[4,2,240,128]{3,2,1,0:T(8,128)(2,1)S(1)} collective-permute-done((bf16[4,2,240,128]{3,2,1,0:T(8,128)(2,1)S(1)}, bf16[4,2,240,128]{3,2,1,0:T(8,128)(2,1)S(1)}, u32[]{:S(2)}, u32[]{:S(2)}) %collective-permute-start.28) | collective-permute-done | bytes 491552 | tf_op jit(solution)/shard_map/ppermute | solution.py:55
  133.7 0.3 collective-permute-done.27.s1
  134.0 3.6 %unpack.1 = (f32[2,560,128]{2,1,0:T(8,128)}, f32[2,128,512]{2,1,0:T(8,128)}, f32[2,512,128]{2,1,0:T(8,128)}, f32[2,128,512]{2,1,0:T(8,128)}, f32[2,512,128]{2,1,...) custom-call(bf16[4,2,240,128]{3,2,1,0:T(8,128)(2,1)S(1)} %pad_maximum_fusion.s0, ...), custom_call_target="tpu_custom_call" | custom-call | flops 2400000000 | bytes 3000000 | tf_op jit(solution)/shard_map/unpack/pallas_call | solution.py:530
  (24 shorter events, 0.1 us)
Async XLA Ops:
  3.2 23.1 %copy-start.1 = (bf16[3840,128]{1,0:T(8,128)(2,1)S(1)}, bf16[3840,128]{1,0:T(8,128)(2,1)}, u32[]{:S(2)}) copy-start(bf16[3840,128]{1,0:T(8,128)(2,1)} %get-tuple-element.78.s0) | copy-start | bytes 2949124
  3.2 7.6 %collective-permute-start = (bf16[960,128]{1,0:T(8,128)(2,1)}, bf16[960,128]{1,0:T(8,128)(2,1)S(1)}, u32[]{:S(2)}, u32[]{:S(2)}) collective-permute-start(bf16[960,128]{1,0:T(8,128)(2,1)} %get-tuple-element.72), channel_id=1, source_target_pairs={{0,2},{1,19},{4,6},{5,23},{8,10},{9,27},{12,14},{13,31},{2,16},{3,... | collective-permute-start | bytes 737288 | tf_op jit(solution)/shard_map/ppermute | solution.py:55
  7.3 19.9 %copy-start.5 = (s32[768]{0:T(1024)S(1)}, s32[768]{0:T(1024)}, u32[]{:S(2)}) copy-start(s32[768]{0:T(1024)} %param.12) | copy-start | bytes 9220
  7.3 21.6 %copy-start = (bf16[3840,128]{1,0:T(8,128)(2,1)S(1)}, bf16[3840,128]{1,0:T(8,128)(2,1)}, u32[]{:S(2)}) copy-start(bf16[3840,128]{1,0:T(8,128)(2,1)} %pack_one.1.s0) | copy-start | bytes 2949124
  7.3 21.6 %copy-start.2 = (bf16[768,336]{0,1:T(8,128)(2,1)S(1)}, bf16[768,336]{0,1:T(8,128)(2,1)}, u32[]{:S(2)}) copy-start(bf16[768,336]{0,1:T(8,128)(2,1)} %param.11) | copy-start | bytes 1548292
  10.8 15.5 %collective-permute-start.2 = (bf16[3840,128]{1,0:T(8,128)(2,1)}, bf16[3840,128]{1,0:T(8,128)(2,1)S(1)}, u32[]{:S(2)}, u32[]{:S(2)}) collective-permute-start(bf16[3840,128]{1,0:T(8,128)(2,1)} %pack_one.1.s0), channel_id=1, source_target_pairs={{0,2},{1,19},{4,6},{5,23},{8,10},{9,27},{12,14},{13,31},{2,16},{3,... | collective-permute-start | bytes 2949128 | tf_op jit(solution)/shard_map/ppermute | solution.py:55
  11.2 7.7 %collective-permute-start.5 = (bf16[960,128]{1,0:T(8,128)(2,1)S(1)}, bf16[960,128]{1,0:T(8,128)(2,1)S(1)}, u32[]{:S(2)}, u32[]{:S(2)}) collective-permute-start(bf16[960,128]{1,0:T(8,128)(2,1)S(1)} %collective-permute-done.q0), channel_id=1, source_target_pairs={{0,64},{1,9},{4,68},{5,13},{8,72},{9,1},{12,76},{13,5},{2,66},{3,1... | collective-permute-start | bytes 737288 | tf_op jit(solution)/shard_map/ppermute | solution.py:55
  14.4 7.5 %collective-permute-start.4 = (bf16[960,128]{1,0:T(8,128)(2,1)S(1)}, bf16[960,128]{1,0:T(8,128)(2,1)S(1)}, u32[]{:S(2)}, u32[]{:S(2)}) collective-permute-start(bf16[960,128]{1,0:T(8,128)(2,1)S(1)} %collective-permute-done.q0), channel_id=1, source_target_pairs={{0,96},{1,13},{4,100},{5,1},{8,104},{9,5},{12,108},{13,9},{2,98},{... | collective-permute-start | bytes 737288 | tf_op jit(solution)/shard_map/ppermute | solution.py:55
  15.5 7.4 %collective-permute-start.3 = (bf16[960,128]{1,0:T(8,128)(2,1)S(1)}, bf16[960,128]{1,0:T(8,128)(2,1)S(1)}, u32[]{:S(2)}, u32[]{:S(2)}) collective-permute-start(bf16[960,128]{1,0:T(8,128)(2,1)S(1)} %collective-permute-done.q0), channel_id=1, source_target_pairs={{0,32},{1,5},{4,36},{5,9},{8,40},{9,13},{12,44},{13,1},{2,34},{3,7... | collective-permute-start | bytes 737288 | tf_op jit(solution)/shard_map/ppermute | solution.py:55
  16.4 10.8 %collective-permute-start.1 = (bf16[3840,128]{1,0:T(8,128)(2,1)}, bf16[3840,128]{1,0:T(8,128)(2,1)S(1)}, u32[]{:S(2)}, u32[]{:S(2)}) collective-permute-start(bf16[3840,128]{1,0:T(8,128)(2,1)} %pack_one.1.s0), channel_id=1, source_target_pairs={{0,1},{1,0},{4,5},{5,4},{8,9},{9,8},{12,13},{13,12},{2,3},{3,2},{6... | collective-permute-start | bytes 2949128 | tf_op jit(solution)/shard_map/ppermute | solution.py:55
  26.4 2.6 %collective-permute-start.6 = (bf16[3840,128]{1,0:T(8,128)(2,1)S(1)}, bf16[3840,128]{1,0:T(8,128)(2,1)S(1)}, u32[]{:S(2)}, u32[]{:S(2)}) collective-permute-start(bf16[3840,128]{1,0:T(8,128)(2,1)S(1)} %collective-permute-done.2.s2), channel_id=1, source_target_pairs={{0,1},{1,0},{4,5},{5,4},{8,9},{9,8},{12,13},{13,12},{2,3},{3,2},{6... | collective-permute-start | bytes 2949128 | tf_op jit(solution)/shard_map/ppermute | solution.py:55
  26.4 6.8 %collective-permute-start.7 = (bf16[3840,128]{1,0:T(8,128)(2,1)S(1)}, bf16[3840,128]{1,0:T(8,128)(2,1)S(1)}, u32[]{:S(2)}, u32[]{:S(2)}) collective-permute-start(bf16[3840,128]{1,0:T(8,128)(2,1)S(1)} %copy-done.1), channel_id=1, source_target_pairs={{0,1},{1,0},{4,5},{5,4},{8,9},{9,8},{12,13},{13,12},{2,3},{3,2},{6... | collective-permute-start | bytes 2949128 | tf_op jit(solution)/shard_map/ppermute | solution.py:55
  27.0 6.2 %collective-permute-start.8 = (bf16[3840,128]{1,0:T(8,128)(2,1)S(1)}, bf16[3840,128]{1,0:T(8,128)(2,1)S(1)}, u32[]{:S(2)}, u32[]{:S(2)}) collective-permute-start(bf16[3840,128]{1,0:T(8,128)(2,1)S(1)} %join.1.s2), channel_id=1, source_target_pairs={{0,1},{1,0},{4,5},{5,4},{8,9},{9,8},{12,13},{13,12},{2,3},{3,2},{6... | collective-permute-start | bytes 2949128 | tf_op jit(solution)/shard_map/ppermute | solution.py:55
  28.9 4.2 %copy-start.3 = (bf16[768,336]{0,1:T(8,128)(2,1)S(1)}, bf16[768,336]{0,1:T(8,128)(2,1)}, u32[]{:S(2)}) copy-start(bf16[768,336]{0,1:T(8,128)(2,1)} %param.21) | copy-start | bytes 1548292
  28.9 4.2 %copy-start.4 = (bf16[768,48]{0,1:T(8,128)(2,1)S(1)}, bf16[768,48]{0,1:T(8,128)(2,1)}, u32[]{:S(2)}) copy-start(bf16[768,48]{0,1:T(8,128)(2,1)} %param.20) | copy-start | bytes 221188
  43.7 4.4 %collective-permute-start.9 = (bf16[2,3840,128]{2,1,0:T(8,128)(2,1)S(1)}, bf16[2,3840,128]{2,1,0:T(8,128)(2,1)S(1)}, u32[]{:S(2)}, u32[]{:S(2)}) collective-permute-start(bf16[2,3840,128]{2,1,0:T(8,128)(2,1)S(1)} %get-tuple-element.91), channel_id=1, source_target_pairs={{0,1},{1,0},{4,5},{5,4},{8,9},{9,8},{12,13},{13,12},{2,3},{3,2},{6... | collective-permute-start | bytes 5898248 | tf_op jit(solution)/shard_map/ppermute | solution.py:55
  47.7 11.3 %collective-permute-start.11 = (bf16[2,2256,128]{2,1,0:T(8,128)(2,1)S(1)}, bf16[2,2256,128]{2,1,0:T(8,128)(2,1)S(1)}, u32[]{:S(2)}, u32[]{:S(2)}) collective-permute-start(bf16[2,2256,128]{2,1,0:T(8,128)(2,1)S(1)} %get-tuple-element.101), channel_id=1, source_target_pairs={{0,1},{1,0},{4,5},{5,4},{8,9},{9,8},{12,13},{13,12},{2,3},{3,2},{6... | collective-permute-start | bytes 3465224 | tf_op jit(solution)/shard_map/ppermute | solution.py:55
  53.5 5.4 %collective-permute-start.10 = (bf16[2,1584,128]{2,1,0:T(8,128)(2,1)S(1)}, bf16[2,1584,128]{2,1,0:T(8,128)(2,1)S(1)}, u32[]{:S(2)}, u32[]{:S(2)}) collective-permute-start(bf16[2,1584,128]{2,1,0:T(8,128)(2,1)S(1)} %get-tuple-element.100), channel_id=1, source_target_pairs={{0,1},{1,0},{4,5},{5,4},{8,9},{9,8},{12,13},{13,12},{2,3},{3,2},{6... | collective-permute-start | bytes 2433032 | tf_op jit(solution)/shard_map/ppermute | solution.py:55
  53.7 10.0 %collective-permute-start.15 = (bf16[2,960,128]{2,1,0:T(8,128)(2,1)S(1)}, bf16[2,960,128]{2,1,0:T(8,128)(2,1)S(1)}, u32[]{:S(2)}, u32[]{:S(2)}) collective-permute-start(bf16[2,960,128]{2,1,0:T(8,128)(2,1)S(1)} %get-tuple-element.92), channel_id=1, source_target_pairs={{0,32},{1,5},{4,36},{5,9},{8,40},{9,13},{12,44},{13,1},{2,34},{3,7... | collective-permute-start | bytes 1474568 | tf_op jit(solution)/shard_map/ppermute | solution.py:55
  55.3 15.7 %collective-permute-start.16 = (bf16[2,960,128]{2,1,0:T(8,128)(2,1)S(1)}, bf16[2,960,128]{2,1,0:T(8,128)(2,1)S(1)}, u32[]{:S(2)}, u32[]{:S(2)}) collective-permute-start(bf16[2,960,128]{2,1,0:T(8,128)(2,1)S(1)} %get-tuple-element.93), channel_id=1, source_target_pairs={{0,96},{1,13},{4,100},{5,1},{8,104},{9,5},{12,108},{13,9},{2,98},{... | collective-permute-start | bytes 1474568 | tf_op jit(solution)/shard_map/ppermute | solution.py:55
  56.9 14.1 %collective-permute-start.17 = (bf16[2,960,128]{2,1,0:T(8,128)(2,1)S(1)}, bf16[2,960,128]{2,1,0:T(8,128)(2,1)S(1)}, u32[]{:S(2)}, u32[]{:S(2)}) collective-permute-start(bf16[2,960,128]{2,1,0:T(8,128)(2,1)S(1)} %get-tuple-element.94), channel_id=1, source_target_pairs={{0,64},{1,9},{4,68},{5,13},{8,72},{9,1},{12,76},{13,5},{2,66},{3,1... | collective-permute-start | bytes 1474568 | tf_op jit(solution)/shard_map/ppermute | solution.py:55
  60.1 15.4 %collective-permute-start.12 = (bf16[2,960,128]{2,1,0:T(8,128)(2,1)S(1)}, bf16[2,960,128]{2,1,0:T(8,128)(2,1)S(1)}, u32[]{:S(2)}, u32[]{:S(2)}) collective-permute-start(bf16[2,960,128]{2,1,0:T(8,128)(2,1)S(1)} %get-tuple-element.103), channel_id=1, source_target_pairs={{0,32},{1,5},{4,36},{5,9},{8,40},{9,13},{12,44},{13,1},{2,34},{3,7... | collective-permute-start | bytes 1474568 | tf_op jit(solution)/shard_map/ppermute | solution.py:55
  60.9 14.6 %collective-permute-start.13 = (bf16[2,960,128]{2,1,0:T(8,128)(2,1)S(1)}, bf16[2,960,128]{2,1,0:T(8,128)(2,1)S(1)}, u32[]{:S(2)}, u32[]{:S(2)}) collective-permute-start(bf16[2,960,128]{2,1,0:T(8,128)(2,1)S(1)} %get-tuple-element.104), channel_id=1, source_target_pairs={{0,96},{1,13},{4,100},{5,1},{8,104},{9,5},{12,108},{13,9},{2,98},{... | collective-permute-start | bytes 1474568 | tf_op jit(solution)/shard_map/ppermute | solution.py:55
  63.7 17.2 %collective-permute-start.14 = (bf16[2,960,128]{2,1,0:T(8,128)(2,1)S(1)}, bf16[2,960,128]{2,1,0:T(8,128)(2,1)S(1)}, u32[]{:S(2)}, u32[]{:S(2)}) collective-permute-start(bf16[2,960,128]{2,1,0:T(8,128)(2,1)S(1)} %get-tuple-element.105), channel_id=1, source_target_pairs={{0,64},{1,9},{4,68},{5,13},{8,72},{9,1},{12,76},{13,5},{2,66},{3,1... | collective-permute-start | bytes 1474568 | tf_op jit(solution)/shard_map/ppermute | solution.py:55
  82.0 8.3 %collective-permute-start.18 = (bf16[2,2,240,128]{3,2,1,0:T(8,128)(2,1)S(1)}, bf16[2,2,240,128]{3,2,1,0:T(8,128)(2,1)S(1)}, u32[]{:S(2)}, u32[]{:S(2)}) collective-permute-start(bf16[2,2,240,128]{3,2,1,0:T(8,128)(2,1)S(1)} %get-tuple-element.108), channel_id=1, source_target_pairs={{0,4},{1,33},{4,8},{5,37},{8,12},{9,41},{12,0},{13,45},{2,6},{3,35... | collective-permute-start | bytes 737288 | tf_op jit(solution)/shard_map/ppermute | solution.py:55
  84.0 8.6 %collective-permute-start.19 = (bf16[2,2,240,128]{3,2,1,0:T(8,128)(2,1)S(1)}, bf16[2,2,240,128]{3,2,1,0:T(8,128)(2,1)S(1)}, u32[]{:S(2)}, u32[]{:S(2)}) collective-permute-start(bf16[2,2,240,128]{3,2,1,0:T(8,128)(2,1)S(1)} %get-tuple-element.109), channel_id=1, source_target_pairs={{0,12},{1,97},{4,0},{5,101},{8,4},{9,105},{12,8},{13,109},{2,14},{... | collective-permute-start | bytes 737288 | tf_op jit(solution)/shard_map/ppermute | solution.py:55
  86.2 8.2 %collective-permute-start.20 = (bf16[2,2,240,128]{3,2,1,0:T(8,128)(2,1)S(1)}, bf16[2,2,240,128]{3,2,1,0:T(8,128)(2,1)S(1)}, u32[]{:S(2)}, u32[]{:S(2)}) collective-permute-start(bf16[2,2,240,128]{3,2,1,0:T(8,128)(2,1)S(1)} %get-tuple-element.110), channel_id=1, source_target_pairs={{0,8},{1,65},{4,12},{5,69},{8,0},{9,73},{12,4},{13,77},{2,10},{3,6... | collective-permute-start | bytes 737288 | tf_op jit(solution)/shard_map/ppermute | solution.py:55
  94.5 6.6 %collective-permute-start.23 = (bf16[2,240,128]{2,1,0:T(8,128)(2,1)S(1)}, bf16[2,240,128]{2,1,0:T(8,128)(2,1)S(1)}, u32[]{:S(2)}, u32[]{:S(2)}) collective-permute-start(bf16[2,240,128]{2,1,0:T(8,128)(2,1)S(1)} %get-tuple-element.119), channel_id=1, source_target_pairs={{0,16},{1,17},{4,20},{5,21},{8,24},{9,25},{12,28},{13,29},{2,18},{... | collective-permute-start | bytes 368648 | tf_op jit(solution)/shard_map/ppermute | solution.py:55
  95.2 6.0 %collective-permute-start.22 = (bf16[2,240,128]{2,1,0:T(8,128)(2,1)S(1)}, bf16[2,240,128]{2,1,0:T(8,128)(2,1)S(1)}, u32[]{:S(2)}, u32[]{:S(2)}) collective-permute-start(bf16[2,240,128]{2,1,0:T(8,128)(2,1)S(1)} %get-tuple-element.118), channel_id=1, source_target_pairs={{0,18},{1,19},{4,22},{5,23},{8,26},{9,27},{12,30},{13,31},{2,0},{3... | collective-permute-start | bytes 368648 | tf_op jit(solution)/shard_map/ppermute | solution.py:55
  96.4 6.1 %collective-permute-start.21 = (bf16[2,240,128]{2,1,0:T(8,128)(2,1)S(1)}, bf16[2,240,128]{2,1,0:T(8,128)(2,1)S(1)}, u32[]{:S(2)}, u32[]{:S(2)}) collective-permute-start(bf16[2,240,128]{2,1,0:T(8,128)(2,1)S(1)} %get-tuple-element.118), channel_id=1, source_target_pairs={{0,2},{1,3},{4,6},{5,7},{8,10},{9,11},{12,14},{13,15},{2,16},{3,17... | collective-permute-start | bytes 368648 | tf_op jit(solution)/shard_map/ppermute | solution.py:55
  102.6 6.5 %collective-permute-start.26 = (bf16[2,240,128]{2,1,0:T(8,128)(2,1)S(1)}, bf16[2,240,128]{2,1,0:T(8,128)(2,1)S(1)}, u32[]{:S(2)}, u32[]{:S(2)}) collective-permute-start(bf16[2,240,128]{2,1,0:T(8,128)(2,1)S(1)} %add_convert_fusion.1), channel_id=1, source_target_pairs={{0,8},{1,65},{4,12},{5,69},{8,0},{9,73},{12,4},{13,77},{2,10},{3,6... | collective-permute-start | bytes 368648 | tf_op jit(solution)/shard_map/ppermute | solution.py:55
  103.9 5.8 %collective-permute-start.25 = (bf16[2,240,128]{2,1,0:T(8,128)(2,1)S(1)}, bf16[2,240,128]{2,1,0:T(8,128)(2,1)S(1)}, u32[]{:S(2)}, u32[]{:S(2)}) collective-permute-start(bf16[2,240,128]{2,1,0:T(8,128)(2,1)S(1)} %add_convert_fusion.1), channel_id=1, source_target_pairs={{0,12},{1,97},{4,0},{5,101},{8,4},{9,105},{12,8},{13,109},{2,14},{... | collective-permute-start | bytes 368648 | tf_op jit(solution)/shard_map/ppermute | solution.py:55
  106.7 11.6 %collective-permute-start.24 = (bf16[2,240,128]{2,1,0:T(8,128)(2,1)S(1)}, bf16[2,240,128]{2,1,0:T(8,128)(2,1)S(1)}, u32[]{:S(2)}, u32[]{:S(2)}) collective-permute-start(bf16[2,240,128]{2,1,0:T(8,128)(2,1)S(1)} %add_convert_fusion.1), channel_id=1, source_target_pairs={{0,4},{1,33},{4,8},{5,37},{8,12},{9,41},{12,0},{13,45},{2,6},{3,35... | collective-permute-start | bytes 368648 | tf_op jit(solution)/shard_map/ppermute | solution.py:55
  118.3 10.5 %collective-permute-start.29 = (bf16[4,2,240,128]{3,2,1,0:T(8,128)(2,1)S(1)}, bf16[4,2,240,128]{3,2,1,0:T(8,128)(2,1)S(1)}, u32[]{:S(2)}, u32[]{:S(2)}) collective-permute-start(bf16[4,2,240,128]{3,2,1,0:T(8,128)(2,1)S(1)} %pad_maximum_fusion.s0), channel_id=1, source_target_pairs={{0,64},{1,9},{4,68},{5,13},{8,72},{9,1},{12,76},{13,5},{2,66},{3,1... | collective-permute-start | bytes 1474568 | tf_op jit(solution)/shard_map/ppermute | solution.py:55
  120.3 13.5 %collective-permute-start.28 = (bf16[4,2,240,128]{3,2,1,0:T(8,128)(2,1)S(1)}, bf16[4,2,240,128]{3,2,1,0:T(8,128)(2,1)S(1)}, u32[]{:S(2)}, u32[]{:S(2)}) collective-permute-start(bf16[4,2,240,128]{3,2,1,0:T(8,128)(2,1)S(1)} %pad_maximum_fusion.s0), channel_id=1, source_target_pairs={{0,96},{1,13},{4,100},{5,1},{8,104},{9,5},{12,108},{13,9},{2,98},{... | collective-permute-start | bytes 1474568 | tf_op jit(solution)/shard_map/ppermute | solution.py:55
  122.4 11.6 %collective-permute-start.27 = (bf16[4,2,240,128]{3,2,1,0:T(8,128)(2,1)S(1)}, bf16[4,2,240,128]{3,2,1,0:T(8,128)(2,1)S(1)}, u32[]{:S(2)}, u32[]{:S(2)}) collective-permute-start(bf16[4,2,240,128]{3,2,1,0:T(8,128)(2,1)S(1)} %pad_maximum_fusion.s0), channel_id=1, source_target_pairs={{0,32},{1,5},{4,36},{5,9},{8,40},{9,13},{12,44},{13,1},{2,34},{3,7... | collective-permute-start | bytes 1474568 | tf_op jit(solution)/shard_map/ppermute | solution.py:55
where the time goes:
time: 138 us
  waiting for transfers between devices  59.3 us (43%)
  starting transfers between devices  42.3 us (31%)
  Pallas kernels  34.9 us (25%)
    ppermute x30, waiting for transfers between devices, send(): return lax.ppermute(values, ('dp', 'mp'), where)  59.3 us
    ppermute x30, starting transfers between devices, send(): return lax.ppermute(values, ('dp', 'mp'), where)  42.3 us
    pallas_call x1, Pallas kernels, shards(): call(second_kernel, 'block_two', [IN_VMEM] * 9, [(shape(336, ROWS), IN_VM...  10.5 us
    pallas_call x1, Pallas kernels, shards(): call(first_kernel, 'forward_one', [IN_VMEM] * 6, [(shape(336, ROWS), IN_V...  4.18 us
    pallas_call x1, Pallas kernels, shards(): call(fourth_kernel, 'backward_one_layers', [IN_VMEM] * 10, [(shape(336, R...  4.17 us
    pallas_call x1, Pallas kernels, shards(): call(third_kernel, 'backward_one_heads', [IN_VMEM] * 10, [(shape(512, ROW...  3.75 us
    pallas_call x1, Pallas kernels, shards(): call(unpack_kernel, 'unpack', [ANYWHERE] * 4, [(shape(*dims), IN_VMEM) fo...  3.57 us
  transfers between devices with their start and end apart: 30, of which 20 were waited for; matrix products, arithmetic and copies ran while one was open for 0% of the time, Pallas kernels for 12%

commit v1 on v0

--- a/solution.py
+++ b/solution.py
@@ -13,6 +13,7 @@
 ROWS = 768
 ENTRY, SECOND, THIRD, FOURTH, BACK, FORE, BASIS, USED = 0, 560, 1072, 1584, 2096, 2608, 3120, 3760
 PACK = 3840
+PEERS = (1, 3, 2)
 CHUNK, PIECE = PACK // 4, PACK // 16
 
 
@@ -35,20 +36,20 @@
     return pairs(lambda y, x, z, c: (y, x, z, 1 - c))
 
 
-def to_x(step):
-    return pairs(lambda y, x, z, c: (y, x + step, z, c))
+def to_x(bits):
+    return pairs(lambda y, x, z, c: (y, x ^ bits, z, c))
 
 
 def to_x_by_core():
-    return pairs(lambda y, x, z, c: (y, x + 1 - 2 * c, z, c))
-
-
-def to_first(step):
-    return pairs(lambda y, x, z, c: (y + step, x, z, c) if c == 0 else (y, x, z + step, c))
-
-
-def to_second(step):
-    return pairs(lambda y, x, z, c: (y, x, z + step, c) if c == 0 else (y + step, x, z, c))
+    return pairs(lambda y, x, z, c: (y, x ^ (1 if c == 0 else 3), z, c))
+
+
+def to_first(bits):
+    return pairs(lambda y, x, z, c: (y ^ bits, x, z, c) if c == 0 else (y, x, z ^ bits, c))
+
+
+def to_second(bits):
+    return pairs(lambda y, x, z, c: (y, x, z ^ bits, c) if c == 0 else (y ^ bits, x, z, c))
 
 
 def send(values, where):
@@ -294,8 +295,8 @@
 
 def join_kernel(q0, q1, q2, q3, out):
     i1, _ = places()
-    for a, quarter in zip((0, 3, 1, 2), (q0, q1, q2, q3)):
-        begin = pl.multiple_of(lax.rem(i1 + a, 4) * CHUNK, CHUNK)
+    for bits, quarter in zip((0, *PEERS), (q0, q1, q2, q3)):
+        begin = pl.multiple_of((i1 ^ bits) * CHUNK, CHUNK)
         out[pl.ds(begin, CHUNK), :] = quarter[...]
 
 
@@ -349,8 +350,8 @@
             mine[...].astype(F32) + got[...].astype(F32)
         ).astype(BF)
         at += rows
-    for a, out in zip((1, 3, 2, 0), outs):
-        begin = pl.multiple_of(lax.rem(i1 + a, 4) * CHUNK, CHUNK)
+    for bits, out in zip((*PEERS, 0), outs):
+        begin = pl.multiple_of((i1 ^ bits) * CHUNK, CHUNK)
         out[...] = whole[:, pl.ds(begin, CHUNK), :]
 
 
@@ -360,41 +361,32 @@
     for k in range(2):
         own, a, b, c = (ref[...].astype(F32) for ref in chunks[4 * k : 4 * k + 4])
         whole[:, k] = ((own + a) + (b + c)).astype(BF)
-    for a, out in zip((1, 3, 2, 0), outs):
-        begin = pl.multiple_of(lax.rem(i2 + a, 4) * PIECE, PIECE)
+    for bits, out in zip((*PEERS, 0), outs):
+        begin = pl.multiple_of((i2 ^ bits) * PIECE, PIECE)
         out[...] = whole[:, :, pl.ds(begin, PIECE), :]
 
 
-def unpack_kernel(s0, s1, s2, s3, entry, second, third, fourth, back, fore, basis, whole, sem):
+def unpack_kernel(s0, s1, s2, s3, *refs):
+    outs, whole, bufs, sem = refs[:7], refs[7], refs[8:15], refs[15]
     i1, i2 = places()
+    for a, stack in zip((0, *PEERS), (s0, s1, s2, s3)):
+        for slot, b in enumerate((0, *PEERS)):
+            at = pl.multiple_of((i1 ^ a) * CHUNK + (i2 ^ b) * PIECE, PIECE)
+            whole[:, pl.ds(at, PIECE), :] = stack[slot]
+    scale = 1.0 / math.sqrt(98304)
     copies = []
-    for a, stack in zip((0, 3, 1, 2), (s0, s1, s2, s3)):
-        chunk = lax.rem(i1 + a, 4)
-        for slot, b in enumerate((0, 3, 1, 2)):
-            piece = lax.rem(i2 + b, 4)
-            at = pl.multiple_of(chunk * CHUNK + piece * PIECE, PIECE)
-            copy = pltpu.make_async_copy(
-                stack.at[slot], whole.at[:, pl.ds(at, PIECE), :], sem.at[len(copies)]
-            )
-            copy.start()
-            copies.append(copy)
+    for (name, (begin, count)), out, buf in zip(TABLES.items(), outs, bufs):
+        for k in range(2):
+            if buf.shape[2] == 128:
+                buf[k] = whole[k, begin : begin + count, :].astype(F32) * scale
+            else:
+                for i in range(count // 128):
+                    part = whole[k, begin + 128 * i : begin + 128 * (i + 1), :].astype(F32) * scale
+                    buf[k, :, 128 * i : 128 * (i + 1)] = part.T if name == "basis" else part
+        copies.append(pltpu.make_async_copy(buf, out, sem.at[len(copies)]))
+        copies[-1].start()
     for copy in copies:
         copy.wait()
-    scale = 1.0 / math.sqrt(98304)
-
-    def part(k, begin, count):
-        return whole[k, begin : begin + count, :].astype(F32) * scale
-
-    for k in range(2):
-        entry[k] = part(k, ENTRY, 560)
-        third[k] = part(k, THIRD, 512)
-        back[k] = part(k, BACK, 512)
-        fore[k] = part(k, FORE, 512)
-        for i in range(4):
-            second[k, :, 128 * i : 128 * (i + 1)] = part(k, SECOND + 128 * i, 128)
-            fourth[k, :, 128 * i : 128 * (i + 1)] = part(k, FOURTH + 128 * i, 128)
-        for i in range(5):
-            basis[k, :, 128 * i : 128 * (i + 1)] = part(k, BASIS + 128 * i, 128).T
 
 
 def shape(*dims, kind=F32):
@@ -449,7 +441,7 @@
     quarters = [quarter]
     one, quarters[0] = lax.optimization_barrier((one, quarters[0]))
     across = send(one, to_x_by_core())
-    quarters += [send(quarters[0], to_first(a)) for a in (1, 3, 2)]
+    quarters += [send(quarters[0], to_first(a)) for a in PEERS]
     across, *quarters = lax.optimization_barrier((across, *quarters))
     slots1 = (one, send(one, to_core()), across, send(across, to_core()))
     across = call(join_kernel, "join", [IN_VMEM] * 4, [(whole, IN_VMEM)], [], M5, 1)(*quarters)[0]
@@ -498,7 +490,7 @@
         )(*mine, *got)
 
     *out2, own2 = cut([mine2], [got2], "cut_two")
-    got2 = [send(part, to_first(a)) for part, a in zip(out2, (1, 3, 2))]
+    got2 = [send(part, to_first(a)) for part, a in zip(out2, PEERS)]
     d_pre, *out2 = lax.optimization_barrier((d_pre, *out2))
     steep, mine1b, theirs1b = call(
         fourth_kernel,
@@ -511,7 +503,7 @@
     )(label, g1, d_pre, *slots1, e1, act1, slope1)
     got1b = send(theirs1b, to_core())
     *out1, own1 = cut([mine1b, mine1a], [got1b, got1a], "cut_one")
-    got1 = [send(part, to_first(a)) for part, a in zip(out1, (1, 3, 2))]
+    got1 = [send(part, to_first(a)) for part, a in zip(out1, PEERS)]
     *out, own = call(
         piece_kernel,
         "pieces",
@@ -521,24 +513,22 @@
         M5,
         2,
     )(own1, *got1, own2, *got2)
-    got = [send(part, to_second(b)) for part, b in zip(out, (1, 3, 2))]
+    got = [send(part, to_second(b)) for part, b in zip(out, PEERS)]
     done = plus(own, *got)
     got = [send(done[1], to_x(1)), send(done[1], to_x(3)), send(done[0], to_x(2))]
     done = plus(done[0], *got)
-    stack = jnp.stack([done] + [send(done, to_second(b)) for b in (1, 3, 2)])
-    stacks = [stack] + [send(stack, to_first(a)) for a in (1, 3, 2)]
+    stack = jnp.stack([done] + [send(done, to_second(b)) for b in PEERS])
+    stacks = [stack] + [send(stack, to_first(a)) for a in PEERS]
+    outs = (
+        (2, 560, 128), (2, 128, 512), (2, 512, 128), (2, 128, 512), (2, 512, 128), (2, 512, 128), (2, 128, 640),
+    )
     grads = call(
         unpack_kernel,
         "unpack",
-        [ANYWHERE] * 4,
-        [
-            (shape(*dims), IN_VMEM)
-            for dims in (
-                (2, 560, 128), (2, 128, 512), (2, 512, 128), (2, 128, 512), (2, 512, 128), (2, 512, 128), (2, 128, 640),
-            )
-        ],
-        [vmem(2, PACK, 128), DMA((16,))],
-        32,
+        [IN_VMEM] * 4,
+        [(shape(*dims), ANYWHERE) for dims in outs],
+        [vmem(2, PACK, 128)] + [vmem(*dims, kind=F32) for dims in outs] + [DMA((7,))],
+        16,
         3,
     )(*stacks)
     return (look.T, rest.T, steep.T, *grads)

time: 138 us -> 129 us (0.935)
  starting transfers between devices: 42.3 us -> 37.9 us
  waiting for transfers between devices: 59.3 us -> 55.7 us
    ppermute x30, starting transfers between devices: 42.3 us -> 37.9 us  [send(): return lax.ppermute(values, ('dp', 'mp'), where)]
    ppermute x30, waiting for transfers between devices: 59.3 us -> 55.7 us  [send(): return lax.ppermute(values, ('dp', 'mp'), where)]
  transfers between devices with their start and end apart: 30 -> 30, of which waited for: 20 -> 19; matrix products, arithmetic and copies ran while one was open for 0% -> 0% of each run, Pallas kernels for 12% -> 13%
where the time goes in v1:
time: 129 us; the launch traced here: 128 us
  waiting for transfers between devices  55.7 us (43%)
  starting transfers between devices  37.9 us (29%)
  Pallas kernels  33.6 us (26%)
    ppermute x30, waiting for transfers between devices, send(): return lax.ppermute(values, ('dp', 'mp'), where)  55.7 us
    ppermute x30, starting transfers between devices, send(): return lax.ppermute(values, ('dp', 'mp'), where)  37.9 us
    pallas_call x1, Pallas kernels, shards(): call(second_kernel, 'block_two', [IN_VMEM] * 9, [(shape(336, ROWS), IN_VM...  10.5 us
    pallas_call x1, Pallas kernels, shards(): call(first_kernel, 'forward_one', [IN_VMEM] * 6, [(shape(336, ROWS), IN_V...  4.18 us
    pallas_call x1, Pallas kernels, shards(): call(fourth_kernel, 'backward_one_layers', [IN_VMEM] * 10, [(shape(336, R...  4.17 us
    pallas_call x1, Pallas kernels, shards(): call(third_kernel, 'backward_one_heads', [IN_VMEM] * 10, [(shape(512, ROW...  3.75 us
    pallas_call x1, Pallas kernels, shards(): call(functools.partial(pack_kernel, 1), 'pack_two', [IN_VMEM] * 7, [(whol...  2.58 us
  transfers between devices with their start and end apart: 30, of which 19 were waited for; matrix products, arithmetic and copies ran while one was open for 0% of the time, Pallas kernels for 13%

profile of v1, /device:TPU:0, one launch (start us, length us, event | category | flops | bytes accessed | tf_op | source)
XLA Modules:
  0.0 128.5 jit_solution(4694899621660295085)
XLA Ops:
  0.6 2.6 %pack_two.1 = (bf16[3840,128]{1,0:T(8,128)(2,1)}, bf16[960,128]{1,0:T(8,128)(2,1)}) custom-call(bf16[2,560,128]{2,1,0:T(8,128)(2,1)} %refs_0_.2, bf16[2,128,512]{2,1,0:T(8,128)(2,1)} %refs_1_.2, bf16[2,512,128]{2,1,0:T(8,128)(2,1)} %refs_2_.2, bf16[2,128,512]{2,1,0:T(8,128)(2,1)} %refs_3_.2, bf16[2,512,128]{2,1,0:T(8,128)(2,1)} %refs_4_.2, ...), custom_call_target="tpu_custom_call" | custom-call | flops 1600000000 | bytes 2000000 | tf_op jit(solution)/shard_map/pack_two/pallas_call | solution.py:435
  3.2 1.6 %collective-permute-start = (bf16[960,128]{1,0:T(8,128)(2,1)}, bf16[960,128]{1,0:T(8,128)(2,1)S(1)}, u32[]{:S(2)}, u32[]{:S(2)}) collective-permute-start(bf16[960,128]{1,0:T(8,128)(2,1)} %get-tuple-element.72), channel_id=1, source_target_pairs={{0,2},{1,19},{4,6},{5,23},{8,10},{9,27},{12,14},{13,31},{2,0},{3,1... | collective-permute-start | bytes 737288 | tf_op jit(solution)/shard_map/ppermute | solution.py:56
  4.8 2.5 %pack_one.1.s0 = bf16[3840,128]{1,0:T(8,128)(2,1)} custom-call(bf16[2,560,128]{2,1,0:T(8,128)(2,1)} %refs_0_.2, bf16[2,128,512]{2,1,0:T(8,128)(2,1)} %refs_1_.2, bf16[2,512,128]{2,1,0:T(8,128)(2,1)} %refs_2_.2, bf16[2,128,512]{2,1,0:T(8,128)(2,1)} %refs_3_.2, bf16[2,512,128]{2,1,0:T(8,128)(2,1)} %refs_4_.2, bf16[2,512,128]{2,1,0:T(8,128)(2,1)} %refs_5_.2, ...), custom_call_target="tpu_custom_call" | custom-call | flops 1600000000 | bytes 2000000 | tf_op jit(solution)/shard_map/pack_one/pallas_call | solution.py:439
  7.3 2.3 %collective-permute-done.q0 = bf16[960,128]{1,0:T(8,128)(2,1)S(1)} collective-permute-done((bf16[960,128]{1,0:T(8,128)(2,1)}, bf16[960,128]{1,0:T(8,128)(2,1)S(1)}, u32[]{:S(2)}, u32[]{:S(2)}) %collective-permute-start) | collective-permute-done | bytes 245792 | tf_op jit(solution)/shard_map/ppermute | solution.py:56
  9.6 1.6 %collective-permute-start.2 = (bf16[3840,128]{1,0:T(8,128)(2,1)}, bf16[3840,128]{1,0:T(8,128)(2,1)S(1)}, u32[]{:S(2)}, u32[]{:S(2)}) collective-permute-start(bf16[3840,128]{1,0:T(8,128)(2,1)} %pack_one.1.s0), channel_id=1, source_target_pairs={{0,2},{1,19},{4,6},{5,23},{8,10},{9,27},{12,14},{13,31},{2,0},{3,1... | collective-permute-start | bytes 2949128 | tf_op jit(solution)/shard_map/ppermute | solution.py:56
  11.2 3.2 %collective-permute-start.5 = (bf16[960,128]{1,0:T(8,128)(2,1)S(1)}, bf16[960,128]{1,0:T(8,128)(2,1)S(1)}, u32[]{:S(2)}, u32[]{:S(2)}) collective-permute-start(bf16[960,128]{1,0:T(8,128)(2,1)S(1)} %collective-permute-done.q0), channel_id=1, source_target_pairs={{0,64},{1,9},{4,68},{5,13},{8,72},{9,1},{12,76},{13,5},{2,66},{3,1... | collective-permute-start | bytes 737288 | tf_op jit(solution)/shard_map/ppermute | solution.py:56
  14.4 1.1 collective-permute-start.4
  15.5 1.0 collective-permute-start.1
  16.4 2.5 %collective-permute-done.5.q3 = bf16[960,128]{1,0:T(8,128)(2,1)S(1)} collective-permute-done((bf16[960,128]{1,0:T(8,128)(2,1)S(1)}, bf16[960,128]{1,0:T(8,128)(2,1)S(1)}, u32[]{:S(2)}, u32[]{:S(2)}) %collective-permute-start.5) | collective-permute-done | bytes 245792 | tf_op jit(solution)/shard_map/ppermute | solution.py:56
  18.9 2.9 %collective-permute-done.4.q2 = bf16[960,128]{1,0:T(8,128)(2,1)S(1)} collective-permute-done((bf16[960,128]{1,0:T(8,128)(2,1)S(1)}, bf16[960,128]{1,0:T(8,128)(2,1)S(1)}, u32[]{:S(2)}, u32[]{:S(2)}) %collective-permute-start.4) | collective-permute-done | bytes 245792 | tf_op jit(solution)/shard_map/ppermute | solution.py:56
  21.8 0.1 collective-permute-done.3.q1
  21.9 2.0 %collective-permute-done.2.s2 = bf16[3840,128]{1,0:T(8,128)(2,1)S(1)} collective-permute-done((bf16[3840,128]{1,0:T(8,128)(2,1)}, bf16[3840,128]{1,0:T(8,128)(2,1)S(1)}, u32[]{:S(2)}, u32[]{:S(2)}) %collective-permute-start.2) | collective-permute-done | bytes 983072 | tf_op jit(solution)/shard_map/ppermute | solution.py:56
  23.9 0.0 collective-permute-start.6
  23.9 0.5 collective-permute-start.7
  24.5 0.1 join.1.s2
  24.5 0.3 collective-permute-start.8
  24.8 0.0 collective-permute-done.1.s1
  24.9 1.7 %collective-permute-done.6.s3 = bf16[3840,128]{1,0:T(8,128)(2,1)S(1)} collective-permute-done((bf16[3840,128]{1,0:T(8,128)(2,1)S(1)}, bf16[3840,128]{1,0:T(8,128)(2,1)S(1)}, u32[]{:S(2)}, u32[]{:S(2)}) %collective-permute-start.6) | collective-permute-done | bytes 983072 | tf_op jit(solution)/shard_map/ppermute | solution.py:56
  26.5 4.2 %forward_one.1 = (f32[336,768]{1,0:T(8,128)S(1)}, f32[48,768]{1,0:T(8,128)S(1)}, bf16[560,768]{1,0:T(8,128)(2,1)S(1)}, bf16[4,512,768]{2,1,0:T(8,128)(2,1)S(1)},...) custom-call(s32[1,768]{1,0:T(1,128)S(1)} %broadcast_in_dim.3.label, bf16[336,768]{1,0:T(8,128)(2,1)S(1)} %bitcast.16, ...), custom_call_target="tpu_custom_call" | custom-call | flops 4800000000 | bytes 6000000 | tf_op jit(solution)/shard_map/forward_one/pallas_call | solution.py:449
  30.7 10.5 %block_two.1 = (f32[336,768]{1,0:T(8,128)}, f32[48,768]{1,0:T(8,128)}, f32[336,768]{1,0:T(8,128)S(1)}, bf16[2,3840,128]{2,1,0:T(8,128)(2,1)S(1)}, bf16[2,3840,128]{2,1,0:T(8,128)(2,1)S(1)}) custom-call(s32[1,768]{1,0:T(1,128)S(1)} %broadcast_in_dim.3.label, f32[336,768]{1,0:T(8,128)S(1)} %get-tuple-element.76.state_in, ...), custom_call_target="tpu_custom_call" | custom-call | flops 11200000000 | bytes 14000000 | tf_op jit(solution)/shard_map/block_two/pallas_call | solution.py:459
  41.3 0.2 collective-permute-start.9
  41.5 3.7 %backward_one_heads.1 = (bf16[512,768]{1,0:T(8,128)(2,1)S(1)}, bf16[2,2256,128]{2,1,0:T(8,128)(2,1)S(1)}, bf16[2,2256,128]{2,1,0:T(8,128)(2,1)S(1)}) custom-call(s32[1,768]{1,0:T(1,128)S(1)} %broadcast_in_dim.3.label, f32[336,768]{1,0:T(8,128)S(1)} %get-tuple-element.85.g_in, bf16[48,768]{1,0:T(8,128)(2,1)S(1)} %bitcast.19, bf16[3840,128]{1,0:T(8,128)(2,1)S(1)} %copy-done, ...), custom_call_target="tpu_custom_call" | custom-call | flops 4800000000 | bytes 6000000 | tf_op jit(solution)/shard_map/backward_one_heads/pallas_call | solution.py:470
  45.2 0.5 collective-permute-start.11
  45.7 0.0 collective-permute-done.9.refs_1_
  45.7 1.2 cut_two.1
  46.9 4.2 %backward_one_layers.1 = (f32[336,768]{1,0:T(8,128)}, bf16[2,1584,128]{2,1,0:T(8,128)(2,1)S(1)}, bf16[2,1584,128]{2,1,0:T(8,128)(2,1)S(1)}) custom-call(s32[1,768]{1,0:T(1,128)S(1)} %broadcast_in_dim.3.label, f32[336,768]{1,0:T(8,128)S(1)} %get-tuple-element.85.g_in, bf16[512,768]{1,0:T(8,128)(2,1)S(1)} %get-tuple-element.95.d_in, ...), custom_call_target="tpu_custom_call" | custom-call | flops 4800000000 | bytes 6000000 | tf_op jit(solution)/shard_map/backward_one_layers/pallas_call | solution.py:495
  51.1 0.1 collective-permute-start.10
  51.2 1.7 %collective-permute-start.15 = (bf16[2,960,128]{2,1,0:T(8,128)(2,1)S(1)}, bf16[2,960,128]{2,1,0:T(8,128)(2,1)S(1)}, u32[]{:S(2)}, u32[]{:S(2)}) collective-permute-start(bf16[2,960,128]{2,1,0:T(8,128)(2,1)S(1)} %get-tuple-element.92), channel_id=1, source_target_pairs={{0,32},{1,5},{4,36},{5,1},{8,40},{9,13},{12,44},{13,9},{2,34},{3,7... | collective-permute-start | bytes 1474568 | tf_op jit(solution)/shard_map/ppermute | solution.py:56
  52.8 2.2 %collective-permute-start.16 = (bf16[2,960,128]{2,1,0:T(8,128)(2,1)S(1)}, bf16[2,960,128]{2,1,0:T(8,128)(2,1)S(1)}, u32[]{:S(2)}, u32[]{:S(2)}) collective-permute-start(bf16[2,960,128]{2,1,0:T(8,128)(2,1)S(1)} %get-tuple-element.93), channel_id=1, source_target_pairs={{0,96},{1,13},{4,100},{5,9},{8,104},{9,5},{12,108},{13,1},{2,98},{... | collective-permute-start | bytes 1474568 | tf_op jit(solution)/shard_map/ppermute | solution.py:56
  55.0 0.7 collective-permute-start.17
  55.8 1.1 cut_one.1
  56.9 1.3 collective-permute-start.12
  58.2 2.2 %collective-permute-start.13 = (bf16[2,960,128]{2,1,0:T(8,128)(2,1)S(1)}, bf16[2,960,128]{2,1,0:T(8,128)(2,1)S(1)}, u32[]{:S(2)}, u32[]{:S(2)}) collective-permute-start(bf16[2,960,128]{2,1,0:T(8,128)(2,1)S(1)} %get-tuple-element.104), channel_id=1, source_target_pairs={{0,96},{1,13},{4,100},{5,9},{8,104},{9,5},{12,108},{13,1},{2,98},{... | collective-permute-start | bytes 1474568 | tf_op jit(solution)/shard_map/ppermute | solution.py:56
  60.4 0.0 collective-permute-done.15.refs_5_
  60.4 2.9 %collective-permute-start.14 = (bf16[2,960,128]{2,1,0:T(8,128)(2,1)S(1)}, bf16[2,960,128]{2,1,0:T(8,128)(2,1)S(1)}, u32[]{:S(2)}, u32[]{:S(2)}) collective-permute-start(bf16[2,960,128]{2,1,0:T(8,128)(2,1)S(1)} %get-tuple-element.105), channel_id=1, source_target_pairs={{0,64},{1,9},{4,68},{5,13},{8,72},{9,1},{12,76},{13,5},{2,66},{3,1... | collective-permute-start | bytes 1474568 | tf_op jit(solution)/shard_map/ppermute | solution.py:56
  63.3 4.9 %collective-permute-done.16.refs_6_ = bf16[2,960,128]{2,1,0:T(8,128)(2,1)S(1)} collective-permute-done((bf16[2,960,128]{2,1,0:T(8,128)(2,1)S(1)}, bf16[2,960,128]{2,1,0:T(8,128)(2,1)S(1)}, u32[]{:S(2)}, u32[]{:S(2)}) %collective-permute-start.16) | collective-permute-done | bytes 491552 | tf_op jit(solution)/shard_map/ppermute | solution.py:56
  68.2 0.0 collective-permute-done.17.refs_7_
  68.2 2.4 %collective-permute-done.12.refs_1_ = bf16[2,960,128]{2,1,0:T(8,128)(2,1)S(1)} collective-permute-done((bf16[2,960,128]{2,1,0:T(8,128)(2,1)S(1)}, bf16[2,960,128]{2,1,0:T(8,128)(2,1)S(1)}, u32[]{:S(2)}, u32[]{:S(2)}) %collective-permute-start.12) | collective-permute-done | bytes 491552 | tf_op jit(solution)/shard_map/ppermute | solution.py:56
  70.6 8.1 %collective-permute-done.13.refs_2_ = bf16[2,960,128]{2,1,0:T(8,128)(2,1)S(1)} collective-permute-done((bf16[2,960,128]{2,1,0:T(8,128)(2,1)S(1)}, bf16[2,960,128]{2,1,0:T(8,128)(2,1)S(1)}, u32[]{:S(2)}, u32[]{:S(2)}) %collective-permute-start.13) | collective-permute-done | bytes 491552 | tf_op jit(solution)/shard_map/ppermute | solution.py:56
  78.7 1.1 pieces.1
  79.8 2.0 %collective-permute-start.18 = (bf16[2,2,240,128]{3,2,1,0:T(8,128)(2,1)S(1)}, bf16[2,2,240,128]{3,2,1,0:T(8,128)(2,1)S(1)}, u32[]{:S(2)}, u32[]{:S(2)}) collective-permute-start(bf16[2,2,240,128]{3,2,1,0:T(8,128)(2,1)S(1)} %get-tuple-element.108), channel_id=1, source_target_pairs={{0,4},{1,33},{4,0},{5,37},{8,12},{9,41},{12,8},{13,45},{2,6},{3,35... | collective-permute-start | bytes 737288 | tf_op jit(solution)/shard_map/ppermute | solution.py:56
  81.8 2.5 %collective-permute-start.19 = (bf16[2,2,240,128]{3,2,1,0:T(8,128)(2,1)S(1)}, bf16[2,2,240,128]{3,2,1,0:T(8,128)(2,1)S(1)}, u32[]{:S(2)}, u32[]{:S(2)}) collective-permute-start(bf16[2,2,240,128]{3,2,1,0:T(8,128)(2,1)S(1)} %get-tuple-element.109), channel_id=1, source_target_pairs={{0,12},{1,97},{4,8},{5,101},{8,4},{9,105},{12,0},{13,109},{2,14},{... | collective-permute-start | bytes 737288 | tf_op jit(solution)/shard_map/ppermute | solution.py:56
  84.4 1.1 collective-permute-start.20
  85.4 0.7 collective-permute-done.18
  86.1 4.6 %collective-permute-done.19 = bf16[2,2,240,128]{3,2,1,0:T(8,128)(2,1)S(1)} collective-permute-done((bf16[2,2,240,128]{3,2,1,0:T(8,128)(2,1)S(1)}, bf16[2,2,240,128]{3,2,1,0:T(8,128)(2,1)S(1)}, u32[]{:S(2)}, u32[]{:S(2)}) %collective-permute-start.19) | collective-permute-done | bytes 245792 | tf_op jit(solution)/shard_map/ppermute | solution.py:56
  90.7 1.5 %collective-permute-done.20 = bf16[2,2,240,128]{3,2,1,0:T(8,128)(2,1)S(1)} collective-permute-done((bf16[2,2,240,128]{3,2,1,0:T(8,128)(2,1)S(1)}, bf16[2,2,240,128]{3,2,1,0:T(8,128)(2,1)S(1)}, u32[]{:S(2)}, u32[]{:S(2)}) %collective-permute-start.20) | collective-permute-done | bytes 245792 | tf_op jit(solution)/shard_map/ppermute | solution.py:56
  92.2 0.1 add_convert_fusion
  92.4 3.1 %collective-permute-start.23 = (bf16[2,240,128]{2,1,0:T(8,128)(2,1)S(1)}, bf16[2,240,128]{2,1,0:T(8,128)(2,1)S(1)}, u32[]{:S(2)}, u32[]{:S(2)}) collective-permute-start(bf16[2,240,128]{2,1,0:T(8,128)(2,1)S(1)} %get-tuple-element.119), channel_id=1, source_target_pairs={{0,16},{1,17},{4,20},{5,21},{8,24},{9,25},{12,28},{13,29},{2,18},{... | collective-permute-start | bytes 368648 | tf_op jit(solution)/shard_map/ppermute | solution.py:56
  95.5 1.1 collective-permute-start.22
  96.6 2.8 %collective-permute-done.23 = bf16[2,240,128]{2,1,0:T(8,128)(2,1)S(1)} collective-permute-done((bf16[2,240,128]{2,1,0:T(8,128)(2,1)S(1)}, bf16[2,240,128]{2,1,0:T(8,128)(2,1)S(1)}, u32[]{:S(2)}, u32[]{:S(2)}) %collective-permute-start.23) | collective-permute-done | bytes 122912 | tf_op jit(solution)/shard_map/ppermute | solution.py:56
  99.5 2.1 %collective-permute-done.22 = bf16[2,240,128]{2,1,0:T(8,128)(2,1)S(1)} collective-permute-done((bf16[2,240,128]{2,1,0:T(8,128)(2,1)S(1)}, bf16[2,240,128]{2,1,0:T(8,128)(2,1)S(1)}, u32[]{:S(2)}, u32[]{:S(2)}) %collective-permute-start.22) | collective-permute-done | bytes 122912 | tf_op jit(solution)/shard_map/ppermute | solution.py:56
  101.6 0.1 add_convert_fusion.1
  101.7 2.1 %collective-permute-start.26 = (bf16[2,240,128]{2,1,0:T(8,128)(2,1)S(1)}, bf16[2,240,128]{2,1,0:T(8,128)(2,1)S(1)}, u32[]{:S(2)}, u32[]{:S(2)}) collective-permute-start(bf16[2,240,128]{2,1,0:T(8,128)(2,1)S(1)} %add_convert_fusion.1), channel_id=1, source_target_pairs={{0,8},{1,65},{4,12},{5,69},{8,0},{9,73},{12,4},{13,77},{2,10},{3,6... | collective-permute-start | bytes 368648 | tf_op jit(solution)/shard_map/ppermute | solution.py:56
  103.8 1.5 %collective-permute-start.25 = (bf16[2,240,128]{2,1,0:T(8,128)(2,1)S(1)}, bf16[2,240,128]{2,1,0:T(8,128)(2,1)S(1)}, u32[]{:S(2)}, u32[]{:S(2)}) collective-permute-start(bf16[2,240,128]{2,1,0:T(8,128)(2,1)S(1)} %add_convert_fusion.1), channel_id=1, source_target_pairs={{0,12},{1,97},{4,8},{5,101},{8,4},{9,105},{12,0},{13,109},{2,14},{... | collective-permute-start | bytes 368648 | tf_op jit(solution)/shard_map/ppermute | solution.py:56
  105.3 2.9 %collective-permute-done.26 = bf16[2,240,128]{2,1,0:T(8,128)(2,1)S(1)} collective-permute-done((bf16[2,240,128]{2,1,0:T(8,128)(2,1)S(1)}, bf16[2,240,128]{2,1,0:T(8,128)(2,1)S(1)}, u32[]{:S(2)}, u32[]{:S(2)}) %collective-permute-start.26) | collective-permute-done | bytes 122912 | tf_op jit(solution)/shard_map/ppermute | solution.py:56
  108.1 1.7 %collective-permute-done.25 = bf16[2,240,128]{2,1,0:T(8,128)(2,1)S(1)} collective-permute-done((bf16[2,240,128]{2,1,0:T(8,128)(2,1)S(1)}, bf16[2,240,128]{2,1,0:T(8,128)(2,1)S(1)}, u32[]{:S(2)}, u32[]{:S(2)}) %collective-permute-start.25) | collective-permute-done | bytes 122912 | tf_op jit(solution)/shard_map/ppermute | solution.py:56
  109.9 0.3 collective-permute-done.24
  110.2 0.1 pad_maximum_fusion.s0
  110.3 1.8 %collective-permute-start.29 = (bf16[4,2,240,128]{3,2,1,0:T(8,128)(2,1)S(1)}, bf16[4,2,240,128]{3,2,1,0:T(8,128)(2,1)S(1)}, u32[]{:S(2)}, u32[]{:S(2)}) collective-permute-start(bf16[4,2,240,128]{3,2,1,0:T(8,128)(2,1)S(1)} %pad_maximum_fusion.s0), channel_id=1, source_target_pairs={{0,64},{1,9},{4,68},{5,13},{8,72},{9,1},{12,76},{13,5},{2,66},{3,1... | collective-permute-start | bytes 1474568 | tf_op jit(solution)/shard_map/ppermute | solution.py:56
  112.1 0.9 collective-permute-start.28
  113.0 0.8 collective-permute-start.27
  113.8 6.9 %collective-permute-done.29.s3 = bf16[4,2,240,128]{3,2,1,0:T(8,128)(2,1)S(1)} collective-permute-done((bf16[4,2,240,128]{3,2,1,0:T(8,128)(2,1)S(1)}, bf16[4,2,240,128]{3,2,1,0:T(8,128)(2,1)S(1)}, u32[]{:S(2)}, u32[]{:S(2)}) %collective-permute-start.29) | collective-permute-done | bytes 491552 | tf_op jit(solution)/shard_map/ppermute | solution.py:56
  120.8 5.2 %collective-permute-done.28.s2 = bf16[4,2,240,128]{3,2,1,0:T(8,128)(2,1)S(1)} collective-permute-done((bf16[4,2,240,128]{3,2,1,0:T(8,128)(2,1)S(1)}, bf16[4,2,240,128]{3,2,1,0:T(8,128)(2,1)S(1)}, u32[]{:S(2)}, u32[]{:S(2)}) %collective-permute-start.28) | collective-permute-done | bytes 491552 | tf_op jit(solution)/shard_map/ppermute | solution.py:56
  125.9 2.3 %unpack.1 = (f32[2,560,128]{2,1,0:T(8,128)}, f32[2,128,512]{2,1,0:T(8,128)}, f32[2,512,128]{2,1,0:T(8,128)}, f32[2,128,512]{2,1,0:T(8,128)}, f32[2,512,128]{2,1,...) custom-call(bf16[4,2,240,128]{3,2,1,0:T(8,128)(2,1)S(1)} %pad_maximum_fusion.s0, ...), custom_call_target="tpu_custom_call" | custom-call | flops 2400000000 | bytes 3000000 | tf_op jit(solution)/shard_map/unpack/pallas_call | solution.py:525
  (24 shorter events, 0.1 us)
Async XLA Ops:
  3.2 20.7 %copy-start.1 = (bf16[3840,128]{1,0:T(8,128)(2,1)S(1)}, bf16[3840,128]{1,0:T(8,128)(2,1)}, u32[]{:S(2)}) copy-start(bf16[3840,128]{1,0:T(8,128)(2,1)} %get-tuple-element.78.s0) | copy-start | bytes 2949124
  3.2 6.4 %collective-permute-start = (bf16[960,128]{1,0:T(8,128)(2,1)}, bf16[960,128]{1,0:T(8,128)(2,1)S(1)}, u32[]{:S(2)}, u32[]{:S(2)}) collective-permute-start(bf16[960,128]{1,0:T(8,128)(2,1)} %get-tuple-element.72), channel_id=1, source_target_pairs={{0,2},{1,19},{4,6},{5,23},{8,10},{9,27},{12,14},{13,31},{2,0},{3,1... | collective-permute-start | bytes 737288 | tf_op jit(solution)/shard_map/ppermute | solution.py:56
  7.3 17.5 %copy-start.5 = (s32[768]{0:T(1024)S(1)}, s32[768]{0:T(1024)}, u32[]{:S(2)}) copy-start(s32[768]{0:T(1024)} %param.12) | copy-start | bytes 9220
  7.3 19.2 %copy-start = (bf16[3840,128]{1,0:T(8,128)(2,1)S(1)}, bf16[3840,128]{1,0:T(8,128)(2,1)}, u32[]{:S(2)}) copy-start(bf16[3840,128]{1,0:T(8,128)(2,1)} %pack_one.1.s0) | copy-start | bytes 2949124
  7.3 19.2 %copy-start.2 = (bf16[768,336]{0,1:T(8,128)(2,1)S(1)}, bf16[768,336]{0,1:T(8,128)(2,1)}, u32[]{:S(2)}) copy-start(bf16[768,336]{0,1:T(8,128)(2,1)} %param.11) | copy-start | bytes 1548292
  9.6 14.3 %collective-permute-start.2 = (bf16[3840,128]{1,0:T(8,128)(2,1)}, bf16[3840,128]{1,0:T(8,128)(2,1)S(1)}, u32[]{:S(2)}, u32[]{:S(2)}) collective-permute-start(bf16[3840,128]{1,0:T(8,128)(2,1)} %pack_one.1.s0), channel_id=1, source_target_pairs={{0,2},{1,19},{4,6},{5,23},{8,10},{9,27},{12,14},{13,31},{2,0},{3,1... | collective-permute-start | bytes 2949128 | tf_op jit(solution)/shard_map/ppermute | solution.py:56
  11.2 7.7 %collective-permute-start.5 = (bf16[960,128]{1,0:T(8,128)(2,1)S(1)}, bf16[960,128]{1,0:T(8,128)(2,1)S(1)}, u32[]{:S(2)}, u32[]{:S(2)}) collective-permute-start(bf16[960,128]{1,0:T(8,128)(2,1)S(1)} %collective-permute-done.q0), channel_id=1, source_target_pairs={{0,64},{1,9},{4,68},{5,13},{8,72},{9,1},{12,76},{13,5},{2,66},{3,1... | collective-permute-start | bytes 737288 | tf_op jit(solution)/shard_map/ppermute | solution.py:56
  14.4 7.4 %collective-permute-start.4 = (bf16[960,128]{1,0:T(8,128)(2,1)S(1)}, bf16[960,128]{1,0:T(8,128)(2,1)S(1)}, u32[]{:S(2)}, u32[]{:S(2)}) collective-permute-start(bf16[960,128]{1,0:T(8,128)(2,1)S(1)} %collective-permute-done.q0), channel_id=1, source_target_pairs={{0,96},{1,13},{4,100},{5,9},{8,104},{9,5},{12,108},{13,1},{2,98},{... | collective-permute-start | bytes 737288 | tf_op jit(solution)/shard_map/ppermute | solution.py:56
  15.5 6.4 %collective-permute-start.3 = (bf16[960,128]{1,0:T(8,128)(2,1)S(1)}, bf16[960,128]{1,0:T(8,128)(2,1)S(1)}, u32[]{:S(2)}, u32[]{:S(2)}) collective-permute-start(bf16[960,128]{1,0:T(8,128)(2,1)S(1)} %collective-permute-done.q0), channel_id=1, source_target_pairs={{0,32},{1,5},{4,36},{5,1},{8,40},{9,13},{12,44},{13,9},{2,34},{3,7... | collective-permute-start | bytes 737288 | tf_op jit(solution)/shard_map/ppermute | solution.py:56
  15.5 9.4 %collective-permute-start.1 = (bf16[3840,128]{1,0:T(8,128)(2,1)}, bf16[3840,128]{1,0:T(8,128)(2,1)S(1)}, u32[]{:S(2)}, u32[]{:S(2)}) collective-permute-start(bf16[3840,128]{1,0:T(8,128)(2,1)} %pack_one.1.s0), channel_id=1, source_target_pairs={{0,1},{1,0},{4,5},{5,4},{8,9},{9,8},{12,13},{13,12},{2,3},{3,2},{6... | collective-permute-start | bytes 2949128 | tf_op jit(solution)/shard_map/ppermute | solution.py:56
  23.9 2.6 %collective-permute-start.6 = (bf16[3840,128]{1,0:T(8,128)(2,1)S(1)}, bf16[3840,128]{1,0:T(8,128)(2,1)S(1)}, u32[]{:S(2)}, u32[]{:S(2)}) collective-permute-start(bf16[3840,128]{1,0:T(8,128)(2,1)S(1)} %collective-permute-done.2.s2), channel_id=1, source_target_pairs={{0,1},{1,0},{4,5},{5,4},{8,9},{9,8},{12,13},{13,12},{2,3},{3,2},{6... | collective-permute-start | bytes 2949128 | tf_op jit(solution)/shard_map/ppermute | solution.py:56
  23.9 6.8 %collective-permute-start.7 = (bf16[3840,128]{1,0:T(8,128)(2,1)S(1)}, bf16[3840,128]{1,0:T(8,128)(2,1)S(1)}, u32[]{:S(2)}, u32[]{:S(2)}) collective-permute-start(bf16[3840,128]{1,0:T(8,128)(2,1)S(1)} %copy-done.1), channel_id=1, source_target_pairs={{0,1},{1,0},{4,5},{5,4},{8,9},{9,8},{12,13},{13,12},{2,3},{3,2},{6... | collective-permute-start | bytes 2949128 | tf_op jit(solution)/shard_map/ppermute | solution.py:56
  24.5 6.2 %collective-permute-start.8 = (bf16[3840,128]{1,0:T(8,128)(2,1)S(1)}, bf16[3840,128]{1,0:T(8,128)(2,1)S(1)}, u32[]{:S(2)}, u32[]{:S(2)}) collective-permute-start(bf16[3840,128]{1,0:T(8,128)(2,1)S(1)} %join.1.s2), channel_id=1, source_target_pairs={{0,1},{1,0},{4,5},{5,4},{8,9},{9,8},{12,13},{13,12},{2,3},{3,2},{6... | collective-permute-start | bytes 2949128 | tf_op jit(solution)/shard_map/ppermute | solution.py:56
  26.5 4.2 %copy-start.3 = (bf16[768,336]{0,1:T(8,128)(2,1)S(1)}, bf16[768,336]{0,1:T(8,128)(2,1)}, u32[]{:S(2)}) copy-start(bf16[768,336]{0,1:T(8,128)(2,1)} %param.21) | copy-start | bytes 1548292
  26.5 4.2 %copy-start.4 = (bf16[768,48]{0,1:T(8,128)(2,1)S(1)}, bf16[768,48]{0,1:T(8,128)(2,1)}, u32[]{:S(2)}) copy-start(bf16[768,48]{0,1:T(8,128)(2,1)} %param.20) | copy-start | bytes 221188
  41.3 4.4 %collective-permute-start.9 = (bf16[2,3840,128]{2,1,0:T(8,128)(2,1)S(1)}, bf16[2,3840,128]{2,1,0:T(8,128)(2,1)S(1)}, u32[]{:S(2)}, u32[]{:S(2)}) collective-permute-start(bf16[2,3840,128]{2,1,0:T(8,128)(2,1)S(1)} %get-tuple-element.91), channel_id=1, source_target_pairs={{0,1},{1,0},{4,5},{5,4},{8,9},{9,8},{12,13},{13,12},{2,3},{3,2},{6... | collective-permute-start | bytes 5898248 | tf_op jit(solution)/shard_map/ppermute | solution.py:56
  45.2 10.5 %collective-permute-start.11 = (bf16[2,2256,128]{2,1,0:T(8,128)(2,1)S(1)}, bf16[2,2256,128]{2,1,0:T(8,128)(2,1)S(1)}, u32[]{:S(2)}, u32[]{:S(2)}) collective-permute-start(bf16[2,2256,128]{2,1,0:T(8,128)(2,1)S(1)} %get-tuple-element.101), channel_id=1, source_target_pairs={{0,1},{1,0},{4,5},{5,4},{8,9},{9,8},{12,13},{13,12},{2,3},{3,2},{6... | collective-permute-start | bytes 3465224 | tf_op jit(solution)/shard_map/ppermute | solution.py:56
  51.1 4.7 %collective-permute-start.10 = (bf16[2,1584,128]{2,1,0:T(8,128)(2,1)S(1)}, bf16[2,1584,128]{2,1,0:T(8,128)(2,1)S(1)}, u32[]{:S(2)}, u32[]{:S(2)}) collective-permute-start(bf16[2,1584,128]{2,1,0:T(8,128)(2,1)S(1)} %get-tuple-element.100), channel_id=1, source_target_pairs={{0,1},{1,0},{4,5},{5,4},{8,9},{9,8},{12,13},{13,12},{2,3},{3,2},{6... | collective-permute-start | bytes 2433032 | tf_op jit(solution)/shard_map/ppermute | solution.py:56
  51.2 9.2 %collective-permute-start.15 = (bf16[2,960,128]{2,1,0:T(8,128)(2,1)S(1)}, bf16[2,960,128]{2,1,0:T(8,128)(2,1)S(1)}, u32[]{:S(2)}, u32[]{:S(2)}) collective-permute-start(bf16[2,960,128]{2,1,0:T(8,128)(2,1)S(1)} %get-tuple-element.92), channel_id=1, source_target_pairs={{0,32},{1,5},{4,36},{5,1},{8,40},{9,13},{12,44},{13,9},{2,34},{3,7... | collective-permute-start | bytes 1474568 | tf_op jit(solution)/shard_map/ppermute | solution.py:56
  52.8 15.3 %collective-permute-start.16 = (bf16[2,960,128]{2,1,0:T(8,128)(2,1)S(1)}, bf16[2,960,128]{2,1,0:T(8,128)(2,1)S(1)}, u32[]{:S(2)}, u32[]{:S(2)}) collective-permute-start(bf16[2,960,128]{2,1,0:T(8,128)(2,1)S(1)} %get-tuple-element.93), channel_id=1, source_target_pairs={{0,96},{1,13},{4,100},{5,9},{8,104},{9,5},{12,108},{13,1},{2,98},{... | collective-permute-start | bytes 1474568 | tf_op jit(solution)/shard_map/ppermute | solution.py:56
  55.0 13.1 %collective-permute-start.17 = (bf16[2,960,128]{2,1,0:T(8,128)(2,1)S(1)}, bf16[2,960,128]{2,1,0:T(8,128)(2,1)S(1)}, u32[]{:S(2)}, u32[]{:S(2)}) collective-permute-start(bf16[2,960,128]{2,1,0:T(8,128)(2,1)S(1)} %get-tuple-element.94), channel_id=1, source_target_pairs={{0,64},{1,9},{4,68},{5,13},{8,72},{9,1},{12,76},{13,5},{2,66},{3,1... | collective-permute-start | bytes 1474568 | tf_op jit(solution)/shard_map/ppermute | solution.py:56
  56.9 13.7 %collective-permute-start.12 = (bf16[2,960,128]{2,1,0:T(8,128)(2,1)S(1)}, bf16[2,960,128]{2,1,0:T(8,128)(2,1)S(1)}, u32[]{:S(2)}, u32[]{:S(2)}) collective-permute-start(bf16[2,960,128]{2,1,0:T(8,128)(2,1)S(1)} %get-tuple-element.103), channel_id=1, source_target_pairs={{0,32},{1,5},{4,36},{5,1},{8,40},{9,13},{12,44},{13,9},{2,34},{3,7... | collective-permute-start | bytes 1474568 | tf_op jit(solution)/shard_map/ppermute | solution.py:56
  58.2 20.5 %collective-permute-start.13 = (bf16[2,960,128]{2,1,0:T(8,128)(2,1)S(1)}, bf16[2,960,128]{2,1,0:T(8,128)(2,1)S(1)}, u32[]{:S(2)}, u32[]{:S(2)}) collective-permute-start(bf16[2,960,128]{2,1,0:T(8,128)(2,1)S(1)} %get-tuple-element.104), channel_id=1, source_target_pairs={{0,96},{1,13},{4,100},{5,9},{8,104},{9,5},{12,108},{13,1},{2,98},{... | collective-permute-start | bytes 1474568 | tf_op jit(solution)/shard_map/ppermute | solution.py:56
  60.4 18.3 %collective-permute-start.14 = (bf16[2,960,128]{2,1,0:T(8,128)(2,1)S(1)}, bf16[2,960,128]{2,1,0:T(8,128)(2,1)S(1)}, u32[]{:S(2)}, u32[]{:S(2)}) collective-permute-start(bf16[2,960,128]{2,1,0:T(8,128)(2,1)S(1)} %get-tuple-element.105), channel_id=1, source_target_pairs={{0,64},{1,9},{4,68},{5,13},{8,72},{9,1},{12,76},{13,5},{2,66},{3,1... | collective-permute-start | bytes 1474568 | tf_op jit(solution)/shard_map/ppermute | solution.py:56
  79.8 6.3 %collective-permute-start.18 = (bf16[2,2,240,128]{3,2,1,0:T(8,128)(2,1)S(1)}, bf16[2,2,240,128]{3,2,1,0:T(8,128)(2,1)S(1)}, u32[]{:S(2)}, u32[]{:S(2)}) collective-permute-start(bf16[2,2,240,128]{3,2,1,0:T(8,128)(2,1)S(1)} %get-tuple-element.108), channel_id=1, source_target_pairs={{0,4},{1,33},{4,0},{5,37},{8,12},{9,41},{12,8},{13,45},{2,6},{3,35... | collective-permute-start | bytes 737288 | tf_op jit(solution)/shard_map/ppermute | solution.py:56
  81.8 8.9 %collective-permute-start.19 = (bf16[2,2,240,128]{3,2,1,0:T(8,128)(2,1)S(1)}, bf16[2,2,240,128]{3,2,1,0:T(8,128)(2,1)S(1)}, u32[]{:S(2)}, u32[]{:S(2)}) collective-permute-start(bf16[2,2,240,128]{3,2,1,0:T(8,128)(2,1)S(1)} %get-tuple-element.109), channel_id=1, source_target_pairs={{0,12},{1,97},{4,8},{5,101},{8,4},{9,105},{12,0},{13,109},{2,14},{... | collective-permute-start | bytes 737288 | tf_op jit(solution)/shard_map/ppermute | solution.py:56
  84.4 7.9 %collective-permute-start.20 = (bf16[2,2,240,128]{3,2,1,0:T(8,128)(2,1)S(1)}, bf16[2,2,240,128]{3,2,1,0:T(8,128)(2,1)S(1)}, u32[]{:S(2)}, u32[]{:S(2)}) collective-permute-start(bf16[2,2,240,128]{3,2,1,0:T(8,128)(2,1)S(1)} %get-tuple-element.110), channel_id=1, source_target_pairs={{0,8},{1,65},{4,12},{5,69},{8,0},{9,73},{12,4},{13,77},{2,10},{3,6... | collective-permute-start | bytes 737288 | tf_op jit(solution)/shard_map/ppermute | solution.py:56
  92.4 7.1 %collective-permute-start.23 = (bf16[2,240,128]{2,1,0:T(8,128)(2,1)S(1)}, bf16[2,240,128]{2,1,0:T(8,128)(2,1)S(1)}, u32[]{:S(2)}, u32[]{:S(2)}) collective-permute-start(bf16[2,240,128]{2,1,0:T(8,128)(2,1)S(1)} %get-tuple-element.119), channel_id=1, source_target_pairs={{0,16},{1,17},{4,20},{5,21},{8,24},{9,25},{12,28},{13,29},{2,18},{... | collective-permute-start | bytes 368648 | tf_op jit(solution)/shard_map/ppermute | solution.py:56
  95.5 6.1 %collective-permute-start.22 = (bf16[2,240,128]{2,1,0:T(8,128)(2,1)S(1)}, bf16[2,240,128]{2,1,0:T(8,128)(2,1)S(1)}, u32[]{:S(2)}, u32[]{:S(2)}) collective-permute-start(bf16[2,240,128]{2,1,0:T(8,128)(2,1)S(1)} %get-tuple-element.118), channel_id=1, source_target_pairs={{0,18},{1,19},{4,22},{5,23},{8,26},{9,27},{12,30},{13,31},{2,16},{... | collective-permute-start | bytes 368648 | tf_op jit(solution)/shard_map/ppermute | solution.py:56
  96.6 5.0 %collective-permute-start.21 = (bf16[2,240,128]{2,1,0:T(8,128)(2,1)S(1)}, bf16[2,240,128]{2,1,0:T(8,128)(2,1)S(1)}, u32[]{:S(2)}, u32[]{:S(2)}) collective-permute-start(bf16[2,240,128]{2,1,0:T(8,128)(2,1)S(1)} %get-tuple-element.118), channel_id=1, source_target_pairs={{0,2},{1,3},{4,6},{5,7},{8,10},{9,11},{12,14},{13,15},{2,0},{3,1},... | collective-permute-start | bytes 368648 | tf_op jit(solution)/shard_map/ppermute | solution.py:56
  101.7 6.5 %collective-permute-start.26 = (bf16[2,240,128]{2,1,0:T(8,128)(2,1)S(1)}, bf16[2,240,128]{2,1,0:T(8,128)(2,1)S(1)}, u32[]{:S(2)}, u32[]{:S(2)}) collective-permute-start(bf16[2,240,128]{2,1,0:T(8,128)(2,1)S(1)} %add_convert_fusion.1), channel_id=1, source_target_pairs={{0,8},{1,65},{4,12},{5,69},{8,0},{9,73},{12,4},{13,77},{2,10},{3,6... | collective-permute-start | bytes 368648 | tf_op jit(solution)/shard_map/ppermute | solution.py:56
  103.8 6.1 %collective-permute-start.25 = (bf16[2,240,128]{2,1,0:T(8,128)(2,1)S(1)}, bf16[2,240,128]{2,1,0:T(8,128)(2,1)S(1)}, u32[]{:S(2)}, u32[]{:S(2)}) collective-permute-start(bf16[2,240,128]{2,1,0:T(8,128)(2,1)S(1)} %add_convert_fusion.1), channel_id=1, source_target_pairs={{0,12},{1,97},{4,8},{5,101},{8,4},{9,105},{12,0},{13,109},{2,14},{... | collective-permute-start | bytes 368648 | tf_op jit(solution)/shard_map/ppermute | solution.py:56
  105.3 4.9 %collective-permute-start.24 = (bf16[2,240,128]{2,1,0:T(8,128)(2,1)S(1)}, bf16[2,240,128]{2,1,0:T(8,128)(2,1)S(1)}, u32[]{:S(2)}, u32[]{:S(2)}) collective-permute-start(bf16[2,240,128]{2,1,0:T(8,128)(2,1)S(1)} %add_convert_fusion.1), channel_id=1, source_target_pairs={{0,4},{1,33},{4,0},{5,37},{8,12},{9,41},{12,8},{13,45},{2,6},{3,35... | collective-permute-start | bytes 368648 | tf_op jit(solution)/shard_map/ppermute | solution.py:56
  110.3 10.5 %collective-permute-start.29 = (bf16[4,2,240,128]{3,2,1,0:T(8,128)(2,1)S(1)}, bf16[4,2,240,128]{3,2,1,0:T(8,128)(2,1)S(1)}, u32[]{:S(2)}, u32[]{:S(2)}) collective-permute-start(bf16[4,2,240,128]{3,2,1,0:T(8,128)(2,1)S(1)} %pad_maximum_fusion.s0), channel_id=1, source_target_pairs={{0,64},{1,9},{4,68},{5,13},{8,72},{9,1},{12,76},{13,5},{2,66},{3,1... | collective-permute-start | bytes 1474568 | tf_op jit(solution)/shard_map/ppermute | solution.py:56
  112.1 13.9 %collective-permute-start.28 = (bf16[4,2,240,128]{3,2,1,0:T(8,128)(2,1)S(1)}, bf16[4,2,240,128]{3,2,1,0:T(8,128)(2,1)S(1)}, u32[]{:S(2)}, u32[]{:S(2)}) collective-permute-start(bf16[4,2,240,128]{3,2,1,0:T(8,128)(2,1)S(1)} %pad_maximum_fusion.s0), channel_id=1, source_target_pairs={{0,96},{1,13},{4,100},{5,9},{8,104},{9,5},{12,108},{13,1},{2,98},{... | collective-permute-start | bytes 1474568 | tf_op jit(solution)/shard_map/ppermute | solution.py:56
  113.0 12.9 %collective-permute-start.27 = (bf16[4,2,240,128]{3,2,1,0:T(8,128)(2,1)S(1)}, bf16[4,2,240,128]{3,2,1,0:T(8,128)(2,1)S(1)}, u32[]{:S(2)}, u32[]{:S(2)}) collective-permute-start(bf16[4,2,240,128]{3,2,1,0:T(8,128)(2,1)S(1)} %pad_maximum_fusion.s0), channel_id=1, source_target_pairs={{0,32},{1,5},{4,36},{5,1},{8,40},{9,13},{12,44},{13,9},{2,34},{3,7... | collective-permute-start | bytes 1474568 | tf_op jit(solution)/shard_map/ppermute | solution.py:56

commit v2 on v1

--- a/solution.py
+++ b/solution.py
@@ -226,13 +226,14 @@
         at = begin - self.base
         for slot in range(4):
             out = self.outs[slot % 2]
+            out = out[slot // 2] if isinstance(out, tuple) else out.at[slot // 2]
             if name in ("second", "fourth"):
                 for i in range(4):
-                    out[slot // 2, at + 128 * i : at + 128 * (i + 1), :] = grad[
+                    out[at + 128 * i : at + 128 * (i + 1), :] = grad[
                         128 * slot : 128 * (slot + 1), 128 * i : 128 * (i + 1)
                     ].astype(BF)
             else:
-                out[slot // 2, at : at + count, :] = grad[:, 128 * slot : 128 * (slot + 1)].astype(BF)
+                out[at : at + count, :] = grad[:, 128 * slot : 128 * (slot + 1)].astype(BF)
         if name == "basis":
             for out in self.outs:
                 out[:, USED - self.base : PACK - self.base, :] = jnp.zeros((2, PACK - USED, 128), BF)
@@ -333,23 +334,27 @@
     )
 
 
-def fourth_kernel(label, g_in, d_in, s0, s1, s2, s3, e, act, slope, steep, mine, theirs):
-    grads = Grads((mine, theirs))
+def fourth_kernel(label, g_in, d_in, s0, s1, s2, s3, e, act, slope, steep, mine, near, far):
+    grads = Grads((mine, (near, far)))
     labels = label[...]
     g = backward_layers(g_in[...], d_in[...], labels, Weights((s0, s1, s2, s3)), e, act, slope, grads)
     steep[...] = jnp.where(look_mask(labels), g, 0.0)
 
 
-def cut_kernel(count, *refs):
-    parts, outs, whole = refs[: 2 * count], refs[2 * count : -1], refs[-1]
+def cut_kernel(rows, *refs):
+    refs = list(refs)
+    mine = [refs.pop(0) for _ in rows]
+    got = [(refs.pop(0), refs.pop(0)) if count < 0 else refs.pop(0) for count in rows]
+    outs, whole = refs[:4], refs[4]
     i1, _ = places()
     at = 0
-    for mine, got in zip(parts[:count], parts[count:]):
-        rows = mine.shape[1]
-        whole[:, at : at + rows, :] = (
-            mine[...].astype(F32) + got[...].astype(F32)
-        ).astype(BF)
-        at += rows
+    for count, kept, came in zip(rows, mine, got):
+        for half in range(2):
+            part = came[half] if count < 0 else came.at[half]
+            whole[half, at : at + abs(count), :] = (
+                kept[half].astype(F32) + part[...].astype(F32)
+            ).astype(BF)
+        at += abs(count)
     for bits, out in zip((*PEERS, 0), outs):
         begin = pl.multiple_of((i1 ^ bits) * CHUNK, CHUNK)
         out[...] = whole[:, pl.ds(begin, CHUNK), :]
@@ -366,7 +371,7 @@
         out[...] = whole[:, :, pl.ds(begin, PIECE), :]
 
 
-def unpack_kernel(s0, s1, s2, s3, *refs):
+def unpack_kernel(here, s0, s1, s2, s3, *refs):
     outs, whole, bufs, sem = refs[:7], refs[7], refs[8:15], refs[15]
     i1, i2 = places()
     for a, stack in zip((0, *PEERS), (s0, s1, s2, s3)):
@@ -478,31 +483,33 @@
     )(label, g1, adjoint, *slots1, act1, slope1, theta1)
     got1a = send(theirs1a, to_core())
 
-    def cut(mine, got, name):
+    def cut(rows, mine, got, name):
         return call(
-            functools.partial(cut_kernel, len(mine)),
+            functools.partial(cut_kernel, rows),
             name,
-            [IN_VMEM] * (2 * len(mine)),
+            [IN_VMEM] * (len(mine) + len(got)),
             [(shape(2, CHUNK, 128, kind=BF), IN_VMEM)] * 4,
             [vmem(2, PACK, 128)],
             M5,
             2,
         )(*mine, *got)
 
-    *out2, own2 = cut([mine2], [got2], "cut_two")
+    *out2, own2 = cut((PACK,), [mine2], [got2], "cut_two")
     got2 = [send(part, to_first(a)) for part, a in zip(out2, PEERS)]
-    d_pre, *out2 = lax.optimization_barrier((d_pre, *out2))
-    steep, mine1b, theirs1b = call(
+    d_pre, got1a, *out2 = lax.optimization_barrier((d_pre, got1a, *out2))
+    steep, mine1b, *theirs1b = call(
         fourth_kernel,
         "backward_one_layers",
         [IN_VMEM] * 10,
-        [(shape(336, ROWS), IN_VMEM)] + [(shape(2, LOW, 128, kind=BF), IN_VMEM)] * 2,
+        [(shape(336, ROWS), IN_VMEM), (shape(2, LOW, 128, kind=BF), IN_VMEM)]
+        + [(shape(LOW, 128, kind=BF), IN_VMEM)] * 2,
         [],
         M4,
         6,
     )(label, g1, d_pre, *slots1, e1, act1, slope1)
-    got1b = send(theirs1b, to_core())
-    *out1, own1 = cut([mine1b, mine1a], [got1b, got1a], "cut_one")
+    got1b = [send(part, to_core()) for part in theirs1b]
+    mine1b, got2[2] = lax.optimization_barrier((mine1b, got2[2]))
+    *out1, own1 = cut((-LOW, TOP), [mine1b, mine1a], [*got1b, got1a], "cut_one")
     got1 = [send(part, to_first(a)) for part, a in zip(out1, PEERS)]
     *out, own = call(
         piece_kernel,
@@ -518,6 +525,7 @@
     got = [send(done[1], to_x(1)), send(done[1], to_x(3)), send(done[0], to_x(2))]
     done = plus(done[0], *got)
     stack = jnp.stack([done] + [send(done, to_second(b)) for b in PEERS])
+    stack, here = lax.optimization_barrier((stack, send(stack[:, 0, :8], to_core())))
     stacks = [stack] + [send(stack, to_first(a)) for a in PEERS]
     outs = (
         (2, 560, 128), (2, 128, 512), (2, 512, 128), (2, 128, 512), (2, 512, 128), (2, 512, 128), (2, 128, 640),
@@ -525,12 +533,12 @@
     grads = call(
         unpack_kernel,
         "unpack",
-        [IN_VMEM] * 4,
+        [ANYWHERE] + [IN_VMEM] * 4,
         [(shape(*dims), ANYWHERE) for dims in outs],
         [vmem(2, PACK, 128)] + [vmem(*dims, kind=F32) for dims in outs] + [DMA((7,))],
         16,
         3,
-    )(*stacks)
+    )(here, *stacks)
     return (look.T, rest.T, steep.T, *grads)
 
 

time: 129 us -> 127 us (0.984)
    ppermute x30 -> x32, waiting for transfers between devices: 55.7 us -> 54.5 us  [send(): return lax.ppermute(values, ('dp', 'mp'), where)]
    ppermute x30 -> x32, starting transfers between devices: 37.9 us -> 37.7 us  [send(): return lax.ppermute(values, ('dp', 'mp'), where)]
  transfers between devices with their start and end apart: 30 -> 32, of which waited for: 19 -> 20; matrix products, arithmetic and copies ran while one was open for 0% -> 0% of each run, Pallas kernels for 13% -> 13%
where the time goes in v2:
time: 127 us
  waiting for transfers between devices  54.5 us (43%)
  starting transfers between devices  37.7 us (30%)
  Pallas kernels  33.5 us (26%)
    ppermute x32, waiting for transfers between devices, send(): return lax.ppermute(values, ('dp', 'mp'), where)  54.5 us
    ppermute x32, starting transfers between devices, send(): return lax.ppermute(values, ('dp', 'mp'), where)  37.7 us
    pallas_call x1, Pallas kernels, shards(): call(second_kernel, 'block_two', [IN_VMEM] * 9, [(shape(336, ROWS), IN_VM...  10.5 us
    pallas_call x1, Pallas kernels, shards(): call(first_kernel, 'forward_one', [IN_VMEM] * 6, [(shape(336, ROWS), IN_V...  4.18 us
    pallas_call x1, Pallas kernels, shards(): call(fourth_kernel, 'backward_one_layers', [IN_VMEM] * 10, [(shape(336, R...  4.16 us
    pallas_call x1, Pallas kernels, shards(): call(third_kernel, 'backward_one_heads', [IN_VMEM] * 10, [(shape(512, ROW...  3.75 us
    pallas_call x1, Pallas kernels, shards(): call(functools.partial(pack_kernel, 1), 'pack_two', [IN_VMEM] * 7, [(whol...  2.58 us
  transfers between devices with their start and end apart: 32, of which 20 were waited for; matrix products, arithmetic and copies ran while one was open for 0% of the time, Pallas kernels for 13%

profile of v2, /device:TPU:0, one launch (start us, length us, event | category | flops | bytes accessed | tf_op | source)
XLA Modules:
  0.0 127.1 jit_solution(2604808259076677029)
XLA Ops:
  0.6 2.6 %pack_two.1 = (bf16[3840,128]{1,0:T(8,128)(2,1)}, bf16[960,128]{1,0:T(8,128)(2,1)}) custom-call(bf16[2,560,128]{2,1,0:T(8,128)(2,1)} %refs_0_.2, bf16[2,128,512]{2,1,0:T(8,128)(2,1)} %refs_1_.2, bf16[2,512,128]{2,1,0:T(8,128)(2,1)} %refs_2_.2, bf16[2,128,512]{2,1,0:T(8,128)(2,1)} %refs_3_.2, bf16[2,512,128]{2,1,0:T(8,128)(2,1)} %refs_4_.2, ...), custom_call_target="tpu_custom_call" | custom-call | flops 1600000000 | bytes 2000000 | tf_op jit(solution)/shard_map/pack_two/pallas_call | solution.py:440
  3.2 1.6 %collective-permute-start = (bf16[960,128]{1,0:T(8,128)(2,1)}, bf16[960,128]{1,0:T(8,128)(2,1)S(1)}, u32[]{:S(2)}, u32[]{:S(2)}) collective-permute-start(bf16[960,128]{1,0:T(8,128)(2,1)} %get-tuple-element.78), channel_id=1, source_target_pairs={{0,2},{1,19},{4,6},{5,23},{8,10},{9,27},{12,14},{13,31},{2,0},{3,1... | collective-permute-start | bytes 737288 | tf_op jit(solution)/shard_map/ppermute | solution.py:56
  4.8 2.5 %pack_one.1.s0 = bf16[3840,128]{1,0:T(8,128)(2,1)} custom-call(bf16[2,560,128]{2,1,0:T(8,128)(2,1)} %refs_0_.2, bf16[2,128,512]{2,1,0:T(8,128)(2,1)} %refs_1_.2, bf16[2,512,128]{2,1,0:T(8,128)(2,1)} %refs_2_.2, bf16[2,128,512]{2,1,0:T(8,128)(2,1)} %refs_3_.2, bf16[2,512,128]{2,1,0:T(8,128)(2,1)} %refs_4_.2, bf16[2,512,128]{2,1,0:T(8,128)(2,1)} %refs_5_.2, ...), custom_call_target="tpu_custom_call" | custom-call | flops 1600000000 | bytes 2000000 | tf_op jit(solution)/shard_map/pack_one/pallas_call | solution.py:444
  7.3 2.3 %collective-permute-done.q0 = bf16[960,128]{1,0:T(8,128)(2,1)S(1)} collective-permute-done((bf16[960,128]{1,0:T(8,128)(2,1)}, bf16[960,128]{1,0:T(8,128)(2,1)S(1)}, u32[]{:S(2)}, u32[]{:S(2)}) %collective-permute-start) | collective-permute-done | bytes 245792 | tf_op jit(solution)/shard_map/ppermute | solution.py:56
  9.6 1.6 %collective-permute-start.2 = (bf16[3840,128]{1,0:T(8,128)(2,1)}, bf16[3840,128]{1,0:T(8,128)(2,1)S(1)}, u32[]{:S(2)}, u32[]{:S(2)}) collective-permute-start(bf16[3840,128]{1,0:T(8,128)(2,1)} %pack_one.1.s0), channel_id=1, source_target_pairs={{0,2},{1,19},{4,6},{5,23},{8,10},{9,27},{12,14},{13,31},{2,0},{3,1... | collective-permute-start | bytes 2949128 | tf_op jit(solution)/shard_map/ppermute | solution.py:56
  11.2 3.2 %collective-permute-start.5 = (bf16[960,128]{1,0:T(8,128)(2,1)S(1)}, bf16[960,128]{1,0:T(8,128)(2,1)S(1)}, u32[]{:S(2)}, u32[]{:S(2)}) collective-permute-start(bf16[960,128]{1,0:T(8,128)(2,1)S(1)} %collective-permute-done.q0), channel_id=1, source_target_pairs={{0,64},{1,9},{4,68},{5,13},{8,72},{9,1},{12,76},{13,5},{2,66},{3,1... | collective-permute-start | bytes 737288 | tf_op jit(solution)/shard_map/ppermute | solution.py:56
  14.4 1.1 collective-permute-start.4
  15.5 0.0 collective-permute-start.3
  15.5 1.0 collective-permute-start.1
  16.4 2.5 %collective-permute-done.5.q3 = bf16[960,128]{1,0:T(8,128)(2,1)S(1)} collective-permute-done((bf16[960,128]{1,0:T(8,128)(2,1)S(1)}, bf16[960,128]{1,0:T(8,128)(2,1)S(1)}, u32[]{:S(2)}, u32[]{:S(2)}) %collective-permute-start.5) | collective-permute-done | bytes 245792 | tf_op jit(solution)/shard_map/ppermute | solution.py:56
  18.9 2.9 %collective-permute-done.4.q2 = bf16[960,128]{1,0:T(8,128)(2,1)S(1)} collective-permute-done((bf16[960,128]{1,0:T(8,128)(2,1)S(1)}, bf16[960,128]{1,0:T(8,128)(2,1)S(1)}, u32[]{:S(2)}, u32[]{:S(2)}) %collective-permute-start.4) | collective-permute-done | bytes 245792 | tf_op jit(solution)/shard_map/ppermute | solution.py:56
  21.8 0.1 collective-permute-done.3.q1
  21.9 2.0 %collective-permute-done.2.s2 = bf16[3840,128]{1,0:T(8,128)(2,1)S(1)} collective-permute-done((bf16[3840,128]{1,0:T(8,128)(2,1)}, bf16[3840,128]{1,0:T(8,128)(2,1)S(1)}, u32[]{:S(2)}, u32[]{:S(2)}) %collective-permute-start.2) | collective-permute-done | bytes 983072 | tf_op jit(solution)/shard_map/ppermute | solution.py:56
  23.9 0.0 collective-permute-start.6
  23.9 0.5 collective-permute-start.7
  24.5 0.1 join.1.s2
  24.5 0.3 collective-permute-start.8
  24.8 0.0 collective-permute-done.1.s1
  24.9 1.7 %collective-permute-done.6.s3 = bf16[3840,128]{1,0:T(8,128)(2,1)S(1)} collective-permute-done((bf16[3840,128]{1,0:T(8,128)(2,1)S(1)}, bf16[3840,128]{1,0:T(8,128)(2,1)S(1)}, u32[]{:S(2)}, u32[]{:S(2)}) %collective-permute-start.6) | collective-permute-done | bytes 983072 | tf_op jit(solution)/shard_map/ppermute | solution.py:56
  26.5 4.2 %forward_one.1 = (f32[336,768]{1,0:T(8,128)S(1)}, f32[48,768]{1,0:T(8,128)S(1)}, bf16[560,768]{1,0:T(8,128)(2,1)S(1)}, bf16[4,512,768]{2,1,0:T(8,128)(2,1)S(1)},...) custom-call(s32[1,768]{1,0:T(1,128)S(1)} %broadcast_in_dim.3.label, bf16[336,768]{1,0:T(8,128)(2,1)S(1)} %bitcast.18, ...), custom_call_target="tpu_custom_call" | custom-call | flops 4800000000 | bytes 6000000 | tf_op jit(solution)/shard_map/forward_one/pallas_call | solution.py:454
  30.7 10.5 %block_two.1 = (f32[336,768]{1,0:T(8,128)}, f32[48,768]{1,0:T(8,128)}, f32[336,768]{1,0:T(8,128)S(1)}, bf16[2,3840,128]{2,1,0:T(8,128)(2,1)S(1)}, bf16[2,3840,128]{2,1,0:T(8,128)(2,1)S(1)}) custom-call(s32[1,768]{1,0:T(1,128)S(1)} %broadcast_in_dim.3.label, f32[336,768]{1,0:T(8,128)S(1)} %get-tuple-element.82.state_in, ...), custom_call_target="tpu_custom_call" | custom-call | flops 11200000000 | bytes 14000000 | tf_op jit(solution)/shard_map/block_two/pallas_call | solution.py:464
  41.3 0.2 collective-permute-start.10
  41.5 3.7 %backward_one_heads.1 = (bf16[512,768]{1,0:T(8,128)(2,1)S(1)}, bf16[2,2256,128]{2,1,0:T(8,128)(2,1)S(1)}, bf16[2,2256,128]{2,1,0:T(8,128)(2,1)S(1)}) custom-call(s32[1,768]{1,0:T(1,128)S(1)} %broadcast_in_dim.3.label, f32[336,768]{1,0:T(8,128)S(1)} %get-tuple-element.91.g_in, bf16[48,768]{1,0:T(8,128)(2,1)S(1)} %bitcast.21, bf16[3840,128]{1,0:T(8,128)(2,1)S(1)} %copy-done, ...), custom_call_target="tpu_custom_call" | custom-call | flops 4800000000 | bytes 6000000 | tf_op jit(solution)/shard_map/backward_one_heads/pallas_call | solution.py:475
  45.2 0.5 collective-permute-start.9
  45.7 1.1 cut_two.1
  46.9 3.4 %collective-permute-start.11 = (bf16[2,960,128]{2,1,0:T(8,128)(2,1)S(1)}, bf16[2,960,128]{2,1,0:T(8,128)(2,1)S(1)}, u32[]{:S(2)}, u32[]{:S(2)}) collective-permute-start(bf16[2,960,128]{2,1,0:T(8,128)(2,1)S(1)} %get-tuple-element.101), channel_id=1, source_target_pairs={{0,64},{1,9},{4,68},{5,13},{8,72},{9,1},{12,76},{13,5},{2,66},{3,1... | collective-permute-start | bytes 1474568 | tf_op jit(solution)/shard_map/ppermute | solution.py:56
  50.2 4.2 %backward_one_layers.1 = (f32[336,768]{1,0:T(8,128)}, bf16[2,1584,128]{2,1,0:T(8,128)(2,1)S(1)}, bf16[1584,128]{1,0:T(8,128)(2,1)S(1)}, bf16[1584,128]{1,0:T(8,128)(2,1)S(1)}) custom-call(s32[1,768]{1,0:T(1,128)S(1)} %broadcast_in_dim.3.label, f32[336,768]{1,0:T(8,128)S(1)} %get-tuple-element.91.g_in, bf16[512,768]{1,0:T(8,128)(2,1)S(1)} %get-tuple-element.102.d_in, ...), custom_call_target="tpu_custom_call" | custom-call | flops 4800000000 | bytes 6000000 | tf_op jit(solution)/shard_map/backward_one_layers/pallas_call | solution.py:500
  54.4 0.5 collective-permute-start.12
  54.9 1.6 %collective-permute-start.17 = (bf16[2,960,128]{2,1,0:T(8,128)(2,1)S(1)}, bf16[2,960,128]{2,1,0:T(8,128)(2,1)S(1)}, u32[]{:S(2)}, u32[]{:S(2)}) collective-permute-start(bf16[2,960,128]{2,1,0:T(8,128)(2,1)S(1)} %get-tuple-element.99), channel_id=1, source_target_pairs={{0,32},{1,5},{4,36},{5,1},{8,40},{9,13},{12,44},{13,9},{2,34},{3,7... | collective-permute-start | bytes 1474568 | tf_op jit(solution)/shard_map/ppermute | solution.py:56
  56.5 2.2 %collective-permute-start.18 = (bf16[2,960,128]{2,1,0:T(8,128)(2,1)S(1)}, bf16[2,960,128]{2,1,0:T(8,128)(2,1)S(1)}, u32[]{:S(2)}, u32[]{:S(2)}) collective-permute-start(bf16[2,960,128]{2,1,0:T(8,128)(2,1)S(1)} %get-tuple-element.100), channel_id=1, source_target_pairs={{0,96},{1,13},{4,100},{5,9},{8,104},{9,5},{12,108},{13,1},{2,98},{... | collective-permute-start | bytes 1474568 | tf_op jit(solution)/shard_map/ppermute | solution.py:56
  58.7 1.1 cut_one.1
  59.8 0.8 collective-permute-start.14
  60.5 1.7 %collective-permute-start.15 = (bf16[2,960,128]{2,1,0:T(8,128)(2,1)S(1)}, bf16[2,960,128]{2,1,0:T(8,128)(2,1)S(1)}, u32[]{:S(2)}, u32[]{:S(2)}) collective-permute-start(bf16[2,960,128]{2,1,0:T(8,128)(2,1)S(1)} %get-tuple-element.113), channel_id=1, source_target_pairs={{0,96},{1,13},{4,100},{5,9},{8,104},{9,5},{12,108},{13,1},{2,98},{... | collective-permute-start | bytes 1474568 | tf_op jit(solution)/shard_map/ppermute | solution.py:56
  62.3 1.7 %collective-permute-start.16 = (bf16[2,960,128]{2,1,0:T(8,128)(2,1)S(1)}, bf16[2,960,128]{2,1,0:T(8,128)(2,1)S(1)}, u32[]{:S(2)}, u32[]{:S(2)}) collective-permute-start(bf16[2,960,128]{2,1,0:T(8,128)(2,1)S(1)} %get-tuple-element.114), channel_id=1, source_target_pairs={{0,64},{1,9},{4,68},{5,13},{8,72},{9,1},{12,76},{13,5},{2,66},{3,1... | collective-permute-start | bytes 1474568 | tf_op jit(solution)/shard_map/ppermute | solution.py:56
  64.0 2.6 %collective-permute-done.18.refs_6_ = bf16[2,960,128]{2,1,0:T(8,128)(2,1)S(1)} collective-permute-done((bf16[2,960,128]{2,1,0:T(8,128)(2,1)S(1)}, bf16[2,960,128]{2,1,0:T(8,128)(2,1)S(1)}, u32[]{:S(2)}, u32[]{:S(2)}) %collective-permute-start.18) | collective-permute-done | bytes 491552 | tf_op jit(solution)/shard_map/ppermute | solution.py:56
  66.5 2.5 %collective-permute-done.14.refs_1_ = bf16[2,960,128]{2,1,0:T(8,128)(2,1)S(1)} collective-permute-done((bf16[2,960,128]{2,1,0:T(8,128)(2,1)S(1)}, bf16[2,960,128]{2,1,0:T(8,128)(2,1)S(1)}, u32[]{:S(2)}, u32[]{:S(2)}) %collective-permute-start.14) | collective-permute-done | bytes 491552 | tf_op jit(solution)/shard_map/ppermute | solution.py:56
  69.0 8.1 %collective-permute-done.15.refs_2_ = bf16[2,960,128]{2,1,0:T(8,128)(2,1)S(1)} collective-permute-done((bf16[2,960,128]{2,1,0:T(8,128)(2,1)S(1)}, bf16[2,960,128]{2,1,0:T(8,128)(2,1)S(1)}, u32[]{:S(2)}, u32[]{:S(2)}) %collective-permute-start.15) | collective-permute-done | bytes 491552 | tf_op jit(solution)/shard_map/ppermute | solution.py:56
  77.1 1.1 pieces.1
  78.2 1.1 collective-permute-start.19
  79.3 2.5 %collective-permute-start.20 = (bf16[2,2,240,128]{3,2,1,0:T(8,128)(2,1)S(1)}, bf16[2,2,240,128]{3,2,1,0:T(8,128)(2,1)S(1)}, u32[]{:S(2)}, u32[]{:S(2)}) collective-permute-start(bf16[2,2,240,128]{3,2,1,0:T(8,128)(2,1)S(1)} %get-tuple-element.119), channel_id=1, source_target_pairs={{0,12},{1,97},{4,8},{5,101},{8,4},{9,105},{12,0},{13,109},{2,14},{... | collective-permute-start | bytes 737288 | tf_op jit(solution)/shard_map/ppermute | solution.py:56
  81.8 1.1 collective-permute-start.21
  82.9 1.6 %collective-permute-done.19 = bf16[2,2,240,128]{3,2,1,0:T(8,128)(2,1)S(1)} collective-permute-done((bf16[2,2,240,128]{3,2,1,0:T(8,128)(2,1)S(1)}, bf16[2,2,240,128]{3,2,1,0:T(8,128)(2,1)S(1)}, u32[]{:S(2)}, u32[]{:S(2)}) %collective-permute-start.19) | collective-permute-done | bytes 245792 | tf_op jit(solution)/shard_map/ppermute | solution.py:56
  84.5 3.7 %collective-permute-done.20 = bf16[2,2,240,128]{3,2,1,0:T(8,128)(2,1)S(1)} collective-permute-done((bf16[2,2,240,128]{3,2,1,0:T(8,128)(2,1)S(1)}, bf16[2,2,240,128]{3,2,1,0:T(8,128)(2,1)S(1)}, u32[]{:S(2)}, u32[]{:S(2)}) %collective-permute-start.20) | collective-permute-done | bytes 245792 | tf_op jit(solution)/shard_map/ppermute | solution.py:56
  88.2 1.5 %collective-permute-done.21 = bf16[2,2,240,128]{3,2,1,0:T(8,128)(2,1)S(1)} collective-permute-done((bf16[2,2,240,128]{3,2,1,0:T(8,128)(2,1)S(1)}, bf16[2,2,240,128]{3,2,1,0:T(8,128)(2,1)S(1)}, u32[]{:S(2)}, u32[]{:S(2)}) %collective-permute-start.21) | collective-permute-done | bytes 245792 | tf_op jit(solution)/shard_map/ppermute | solution.py:56
  89.7 0.1 add_convert_fusion
  89.8 3.1 %collective-permute-start.24 = (bf16[2,240,128]{2,1,0:T(8,128)(2,1)S(1)}, bf16[2,240,128]{2,1,0:T(8,128)(2,1)S(1)}, u32[]{:S(2)}, u32[]{:S(2)}) collective-permute-start(bf16[2,240,128]{2,1,0:T(8,128)(2,1)S(1)} %get-tuple-element.131), channel_id=1, source_target_pairs={{0,16},{1,17},{4,20},{5,21},{8,24},{9,25},{12,28},{13,29},{2,18},{... | collective-permute-start | bytes 368648 | tf_op jit(solution)/shard_map/ppermute | solution.py:56
  92.9 1.1 collective-permute-start.23
  94.1 3.1 %collective-permute-done.24 = bf16[2,240,128]{2,1,0:T(8,128)(2,1)S(1)} collective-permute-done((bf16[2,240,128]{2,1,0:T(8,128)(2,1)S(1)}, bf16[2,240,128]{2,1,0:T(8,128)(2,1)S(1)}, u32[]{:S(2)}, u32[]{:S(2)}) %collective-permute-start.24) | collective-permute-done | bytes 122912 | tf_op jit(solution)/shard_map/ppermute | solution.py:56
  97.2 1.9 %collective-permute-done.23 = bf16[2,240,128]{2,1,0:T(8,128)(2,1)S(1)} collective-permute-done((bf16[2,240,128]{2,1,0:T(8,128)(2,1)S(1)}, bf16[2,240,128]{2,1,0:T(8,128)(2,1)S(1)}, u32[]{:S(2)}, u32[]{:S(2)}) %collective-permute-start.23) | collective-permute-done | bytes 122912 | tf_op jit(solution)/shard_map/ppermute | solution.py:56
  99.0 0.1 add_convert_fusion.1
  99.1 2.1 %collective-permute-start.27 = (bf16[2,240,128]{2,1,0:T(8,128)(2,1)S(1)}, bf16[2,240,128]{2,1,0:T(8,128)(2,1)S(1)}, u32[]{:S(2)}, u32[]{:S(2)}) collective-permute-start(bf16[2,240,128]{2,1,0:T(8,128)(2,1)S(1)} %add_convert_fusion.1), channel_id=1, source_target_pairs={{0,8},{1,65},{4,12},{5,69},{8,0},{9,73},{12,4},{13,77},{2,10},{3,6... | collective-permute-start | bytes 368648 | tf_op jit(solution)/shard_map/ppermute | solution.py:56
  101.2 1.5 %collective-permute-start.26 = (bf16[2,240,128]{2,1,0:T(8,128)(2,1)S(1)}, bf16[2,240,128]{2,1,0:T(8,128)(2,1)S(1)}, u32[]{:S(2)}, u32[]{:S(2)}) collective-permute-start(bf16[2,240,128]{2,1,0:T(8,128)(2,1)S(1)} %add_convert_fusion.1), channel_id=1, source_target_pairs={{0,12},{1,97},{4,8},{5,101},{8,4},{9,105},{12,0},{13,109},{2,14},{... | collective-permute-start | bytes 368648 | tf_op jit(solution)/shard_map/ppermute | solution.py:56
  102.7 2.9 %collective-permute-done.27 = bf16[2,240,128]{2,1,0:T(8,128)(2,1)S(1)} collective-permute-done((bf16[2,240,128]{2,1,0:T(8,128)(2,1)S(1)}, bf16[2,240,128]{2,1,0:T(8,128)(2,1)S(1)}, u32[]{:S(2)}, u32[]{:S(2)}) %collective-permute-start.27) | collective-permute-done | bytes 122912 | tf_op jit(solution)/shard_map/ppermute | solution.py:56
  105.6 1.7 %collective-permute-done.26 = bf16[2,240,128]{2,1,0:T(8,128)(2,1)S(1)} collective-permute-done((bf16[2,240,128]{2,1,0:T(8,128)(2,1)S(1)}, bf16[2,240,128]{2,1,0:T(8,128)(2,1)S(1)}, u32[]{:S(2)}, u32[]{:S(2)}) %collective-permute-start.26) | collective-permute-done | bytes 122912 | tf_op jit(solution)/shard_map/ppermute | solution.py:56
  107.3 0.3 collective-permute-done.25
  107.6 0.1 pad_maximum_fusion.s0
  107.7 0.1 collective-permute-start.28
  107.8 1.2 collective-permute-done.28.here
  108.9 1.0 collective-permute-start.31
  109.9 1.9 %collective-permute-start.30 = (bf16[4,2,240,128]{3,2,1,0:T(8,128)(2,1)S(1)}, bf16[4,2,240,128]{3,2,1,0:T(8,128)(2,1)S(1)}, u32[]{:S(2)}, u32[]{:S(2)}) collective-permute-start(bf16[4,2,240,128]{3,2,1,0:T(8,128)(2,1)S(1)} %pad_maximum_fusion.s0), channel_id=1, source_target_pairs={{0,96},{1,13},{4,100},{5,9},{8,104},{9,5},{12,108},{13,1},{2,98},{... | collective-permute-start | bytes 1474568 | tf_op jit(solution)/shard_map/ppermute | solution.py:56
  111.7 0.7 collective-permute-start.29
  112.4 6.9 %collective-permute-done.31.s3 = bf16[4,2,240,128]{3,2,1,0:T(8,128)(2,1)S(1)} collective-permute-done((bf16[4,2,240,128]{3,2,1,0:T(8,128)(2,1)S(1)}, bf16[4,2,240,128]{3,2,1,0:T(8,128)(2,1)S(1)}, u32[]{:S(2)}, u32[]{:S(2)}) %collective-permute-start.31) | collective-permute-done | bytes 491552 | tf_op jit(solution)/shard_map/ppermute | solution.py:56
  119.4 5.2 %collective-permute-done.30.s2 = bf16[4,2,240,128]{3,2,1,0:T(8,128)(2,1)S(1)} collective-permute-done((bf16[4,2,240,128]{3,2,1,0:T(8,128)(2,1)S(1)}, bf16[4,2,240,128]{3,2,1,0:T(8,128)(2,1)S(1)}, u32[]{:S(2)}, u32[]{:S(2)}) %collective-permute-start.30) | collective-permute-done | bytes 491552 | tf_op jit(solution)/shard_map/ppermute | solution.py:56
  124.5 2.3 %unpack.1 = (f32[2,560,128]{2,1,0:T(8,128)}, f32[2,128,512]{2,1,0:T(8,128)}, f32[2,512,128]{2,1,0:T(8,128)}, f32[2,128,512]{2,1,0:T(8,128)}, f32[2,512,128]{2,1,...) custom-call(bf16[4,8,128]{2,1,0:T(8,128)(2,1)S(1)} %collective-permute-done.28.here, ...), custom_call_target="tpu_custom_call" | custom-call | flops 2400000000 | bytes 3000000 | tf_op jit(solution)/shard_map/unpack/pallas_call | solution.py:533
  (29 shorter events, 0.1 us)
Async XLA Ops:
  3.2 20.7 %copy-start.1 = (bf16[3840,128]{1,0:T(8,128)(2,1)S(1)}, bf16[3840,128]{1,0:T(8,128)(2,1)}, u32[]{:S(2)}) copy-start(bf16[3840,128]{1,0:T(8,128)(2,1)} %get-tuple-element.84.s0) | copy-start | bytes 2949124
  3.2 6.4 %collective-permute-start = (bf16[960,128]{1,0:T(8,128)(2,1)}, bf16[960,128]{1,0:T(8,128)(2,1)S(1)}, u32[]{:S(2)}, u32[]{:S(2)}) collective-permute-start(bf16[960,128]{1,0:T(8,128)(2,1)} %get-tuple-element.78), channel_id=1, source_target_pairs={{0,2},{1,19},{4,6},{5,23},{8,10},{9,27},{12,14},{13,31},{2,0},{3,1... | collective-permute-start | bytes 737288 | tf_op jit(solution)/shard_map/ppermute | solution.py:56
  7.3 17.5 %copy-start.5 = (s32[768]{0:T(1024)S(1)}, s32[768]{0:T(1024)}, u32[]{:S(2)}) copy-start(s32[768]{0:T(1024)} %param.12) | copy-start | bytes 9220
  7.3 19.2 %copy-start = (bf16[3840,128]{1,0:T(8,128)(2,1)S(1)}, bf16[3840,128]{1,0:T(8,128)(2,1)}, u32[]{:S(2)}) copy-start(bf16[3840,128]{1,0:T(8,128)(2,1)} %pack_one.1.s0) | copy-start | bytes 2949124
  7.3 19.2 %copy-start.2 = (bf16[768,336]{0,1:T(8,128)(2,1)S(1)}, bf16[768,336]{0,1:T(8,128)(2,1)}, u32[]{:S(2)}) copy-start(bf16[768,336]{0,1:T(8,128)(2,1)} %param.11) | copy-start | bytes 1548292
  9.6 14.3 %collective-permute-start.2 = (bf16[3840,128]{1,0:T(8,128)(2,1)}, bf16[3840,128]{1,0:T(8,128)(2,1)S(1)}, u32[]{:S(2)}, u32[]{:S(2)}) collective-permute-start(bf16[3840,128]{1,0:T(8,128)(2,1)} %pack_one.1.s0), channel_id=1, source_target_pairs={{0,2},{1,19},{4,6},{5,23},{8,10},{9,27},{12,14},{13,31},{2,0},{3,1... | collective-permute-start | bytes 2949128 | tf_op jit(solution)/shard_map/ppermute | solution.py:56
  11.2 7.7 %collective-permute-start.5 = (bf16[960,128]{1,0:T(8,128)(2,1)S(1)}, bf16[960,128]{1,0:T(8,128)(2,1)S(1)}, u32[]{:S(2)}, u32[]{:S(2)}) collective-permute-start(bf16[960,128]{1,0:T(8,128)(2,1)S(1)} %collective-permute-done.q0), channel_id=1, source_target_pairs={{0,64},{1,9},{4,68},{5,13},{8,72},{9,1},{12,76},{13,5},{2,66},{3,1... | collective-permute-start | bytes 737288 | tf_op jit(solution)/shard_map/ppermute | solution.py:56
  14.4 7.4 %collective-permute-start.4 = (bf16[960,128]{1,0:T(8,128)(2,1)S(1)}, bf16[960,128]{1,0:T(8,128)(2,1)S(1)}, u32[]{:S(2)}, u32[]{:S(2)}) collective-permute-start(bf16[960,128]{1,0:T(8,128)(2,1)S(1)} %collective-permute-done.q0), channel_id=1, source_target_pairs={{0,96},{1,13},{4,100},{5,9},{8,104},{9,5},{12,108},{13,1},{2,98},{... | collective-permute-start | bytes 737288 | tf_op jit(solution)/shard_map/ppermute | solution.py:56
  15.5 6.4 %collective-permute-start.3 = (bf16[960,128]{1,0:T(8,128)(2,1)S(1)}, bf16[960,128]{1,0:T(8,128)(2,1)S(1)}, u32[]{:S(2)}, u32[]{:S(2)}) collective-permute-start(bf16[960,128]{1,0:T(8,128)(2,1)S(1)} %collective-permute-done.q0), channel_id=1, source_target_pairs={{0,32},{1,5},{4,36},{5,1},{8,40},{9,13},{12,44},{13,9},{2,34},{3,7... | collective-permute-start | bytes 737288 | tf_op jit(solution)/shard_map/ppermute | solution.py:56
  15.5 9.4 %collective-permute-start.1 = (bf16[3840,128]{1,0:T(8,128)(2,1)}, bf16[3840,128]{1,0:T(8,128)(2,1)S(1)}, u32[]{:S(2)}, u32[]{:S(2)}) collective-permute-start(bf16[3840,128]{1,0:T(8,128)(2,1)} %pack_one.1.s0), channel_id=1, source_target_pairs={{0,1},{1,0},{4,5},{5,4},{8,9},{9,8},{12,13},{13,12},{2,3},{3,2},{6... | collective-permute-start | bytes 2949128 | tf_op jit(solution)/shard_map/ppermute | solution.py:56
  23.9 2.6 %collective-permute-start.6 = (bf16[3840,128]{1,0:T(8,128)(2,1)S(1)}, bf16[3840,128]{1,0:T(8,128)(2,1)S(1)}, u32[]{:S(2)}, u32[]{:S(2)}) collective-permute-start(bf16[3840,128]{1,0:T(8,128)(2,1)S(1)} %collective-permute-done.2.s2), channel_id=1, source_target_pairs={{0,1},{1,0},{4,5},{5,4},{8,9},{9,8},{12,13},{13,12},{2,3},{3,2},{6... | collective-permute-start | bytes 2949128 | tf_op jit(solution)/shard_map/ppermute | solution.py:56
  23.9 6.8 %collective-permute-start.7 = (bf16[3840,128]{1,0:T(8,128)(2,1)S(1)}, bf16[3840,128]{1,0:T(8,128)(2,1)S(1)}, u32[]{:S(2)}, u32[]{:S(2)}) collective-permute-start(bf16[3840,128]{1,0:T(8,128)(2,1)S(1)} %copy-done.1), channel_id=1, source_target_pairs={{0,1},{1,0},{4,5},{5,4},{8,9},{9,8},{12,13},{13,12},{2,3},{3,2},{6... | collective-permute-start | bytes 2949128 | tf_op jit(solution)/shard_map/ppermute | solution.py:56
  24.5 6.2 %collective-permute-start.8 = (bf16[3840,128]{1,0:T(8,128)(2,1)S(1)}, bf16[3840,128]{1,0:T(8,128)(2,1)S(1)}, u32[]{:S(2)}, u32[]{:S(2)}) collective-permute-start(bf16[3840,128]{1,0:T(8,128)(2,1)S(1)} %join.1.s2), channel_id=1, source_target_pairs={{0,1},{1,0},{4,5},{5,4},{8,9},{9,8},{12,13},{13,12},{2,3},{3,2},{6... | collective-permute-start | bytes 2949128 | tf_op jit(solution)/shard_map/ppermute | solution.py:56
  26.5 4.2 %copy-start.3 = (bf16[768,336]{0,1:T(8,128)(2,1)S(1)}, bf16[768,336]{0,1:T(8,128)(2,1)}, u32[]{:S(2)}) copy-start(bf16[768,336]{0,1:T(8,128)(2,1)} %param.21) | copy-start | bytes 1548292
  26.5 4.2 %copy-start.4 = (bf16[768,48]{0,1:T(8,128)(2,1)S(1)}, bf16[768,48]{0,1:T(8,128)(2,1)}, u32[]{:S(2)}) copy-start(bf16[768,48]{0,1:T(8,128)(2,1)} %param.20) | copy-start | bytes 221188
  41.3 4.4 %collective-permute-start.10 = (bf16[2,3840,128]{2,1,0:T(8,128)(2,1)S(1)}, bf16[2,3840,128]{2,1,0:T(8,128)(2,1)S(1)}, u32[]{:S(2)}, u32[]{:S(2)}) collective-permute-start(bf16[2,3840,128]{2,1,0:T(8,128)(2,1)S(1)} %get-tuple-element.98), channel_id=1, source_target_pairs={{0,1},{1,0},{4,5},{5,4},{8,9},{9,8},{12,13},{13,12},{2,3},{3,2},{6... | collective-permute-start | bytes 5898248 | tf_op jit(solution)/shard_map/ppermute | solution.py:56
  45.2 5.0 %collective-permute-start.9 = (bf16[2,2256,128]{2,1,0:T(8,128)(2,1)S(1)}, bf16[2,2256,128]{2,1,0:T(8,128)(2,1)S(1)}, u32[]{:S(2)}, u32[]{:S(2)}) collective-permute-start(bf16[2,2256,128]{2,1,0:T(8,128)(2,1)S(1)} %get-tuple-element.96), channel_id=1, source_target_pairs={{0,1},{1,0},{4,5},{5,4},{8,9},{9,8},{12,13},{13,12},{2,3},{3,2},{6... | collective-permute-start | bytes 3465224 | tf_op jit(solution)/shard_map/ppermute | solution.py:56
  46.9 11.8 %collective-permute-start.11 = (bf16[2,960,128]{2,1,0:T(8,128)(2,1)S(1)}, bf16[2,960,128]{2,1,0:T(8,128)(2,1)S(1)}, u32[]{:S(2)}, u32[]{:S(2)}) collective-permute-start(bf16[2,960,128]{2,1,0:T(8,128)(2,1)S(1)} %get-tuple-element.101), channel_id=1, source_target_pairs={{0,64},{1,9},{4,68},{5,13},{8,72},{9,1},{12,76},{13,5},{2,66},{3,1... | collective-permute-start | bytes 1474568 | tf_op jit(solution)/shard_map/ppermute | solution.py:56
  54.4 4.3 %collective-permute-start.12 = (bf16[1584,128]{1,0:T(8,128)(2,1)S(1)}, bf16[1584,128]{1,0:T(8,128)(2,1)S(1)}, u32[]{:S(2)}, u32[]{:S(2)}) collective-permute-start(bf16[1584,128]{1,0:T(8,128)(2,1)S(1)} %get-tuple-element.108), channel_id=1, source_target_pairs={{0,1},{1,0},{4,5},{5,4},{8,9},{9,8},{12,13},{13,12},{2,3},{3,2},{6... | collective-permute-start | bytes 1216520 | tf_op jit(solution)/shard_map/ppermute | solution.py:56
  54.9 3.8 %collective-permute-start.13 = (bf16[1584,128]{1,0:T(8,128)(2,1)S(1)}, bf16[1584,128]{1,0:T(8,128)(2,1)S(1)}, u32[]{:S(2)}, u32[]{:S(2)}) collective-permute-start(bf16[1584,128]{1,0:T(8,128)(2,1)S(1)} %get-tuple-element.109), channel_id=1, source_target_pairs={{0,1},{1,0},{4,5},{5,4},{8,9},{9,8},{12,13},{13,12},{2,3},{3,2},{6... | collective-permute-start | bytes 1216520 | tf_op jit(solution)/shard_map/ppermute | solution.py:56
  54.9 9.0 %collective-permute-start.17 = (bf16[2,960,128]{2,1,0:T(8,128)(2,1)S(1)}, bf16[2,960,128]{2,1,0:T(8,128)(2,1)S(1)}, u32[]{:S(2)}, u32[]{:S(2)}) collective-permute-start(bf16[2,960,128]{2,1,0:T(8,128)(2,1)S(1)} %get-tuple-element.99), channel_id=1, source_target_pairs={{0,32},{1,5},{4,36},{5,1},{8,40},{9,13},{12,44},{13,9},{2,34},{3,7... | collective-permute-start | bytes 1474568 | tf_op jit(solution)/shard_map/ppermute | solution.py:56
  56.5 10.0 %collective-permute-start.18 = (bf16[2,960,128]{2,1,0:T(8,128)(2,1)S(1)}, bf16[2,960,128]{2,1,0:T(8,128)(2,1)S(1)}, u32[]{:S(2)}, u32[]{:S(2)}) collective-permute-start(bf16[2,960,128]{2,1,0:T(8,128)(2,1)S(1)} %get-tuple-element.100), channel_id=1, source_target_pairs={{0,96},{1,13},{4,100},{5,9},{8,104},{9,5},{12,108},{13,1},{2,98},{... | collective-permute-start | bytes 1474568 | tf_op jit(solution)/shard_map/ppermute | solution.py:56
  59.8 9.2 %collective-permute-start.14 = (bf16[2,960,128]{2,1,0:T(8,128)(2,1)S(1)}, bf16[2,960,128]{2,1,0:T(8,128)(2,1)S(1)}, u32[]{:S(2)}, u32[]{:S(2)}) collective-permute-start(bf16[2,960,128]{2,1,0:T(8,128)(2,1)S(1)} %get-tuple-element.112), channel_id=1, source_target_pairs={{0,32},{1,5},{4,36},{5,1},{8,40},{9,13},{12,44},{13,9},{2,34},{3,7... | collective-permute-start | bytes 1474568 | tf_op jit(solution)/shard_map/ppermute | solution.py:56
  60.5 16.5 %collective-permute-start.15 = (bf16[2,960,128]{2,1,0:T(8,128)(2,1)S(1)}, bf16[2,960,128]{2,1,0:T(8,128)(2,1)S(1)}, u32[]{:S(2)}, u32[]{:S(2)}) collective-permute-start(bf16[2,960,128]{2,1,0:T(8,128)(2,1)S(1)} %get-tuple-element.113), channel_id=1, source_target_pairs={{0,96},{1,13},{4,100},{5,9},{8,104},{9,5},{12,108},{13,1},{2,98},{... | collective-permute-start | bytes 1474568 | tf_op jit(solution)/shard_map/ppermute | solution.py:56
  62.3 14.8 %collective-permute-start.16 = (bf16[2,960,128]{2,1,0:T(8,128)(2,1)S(1)}, bf16[2,960,128]{2,1,0:T(8,128)(2,1)S(1)}, u32[]{:S(2)}, u32[]{:S(2)}) collective-permute-start(bf16[2,960,128]{2,1,0:T(8,128)(2,1)S(1)} %get-tuple-element.114), channel_id=1, source_target_pairs={{0,64},{1,9},{4,68},{5,13},{8,72},{9,1},{12,76},{13,5},{2,66},{3,1... | collective-permute-start | bytes 1474568 | tf_op jit(solution)/shard_map/ppermute | solution.py:56
  78.2 6.3 %collective-permute-start.19 = (bf16[2,2,240,128]{3,2,1,0:T(8,128)(2,1)S(1)}, bf16[2,2,240,128]{3,2,1,0:T(8,128)(2,1)S(1)}, u32[]{:S(2)}, u32[]{:S(2)}) collective-permute-start(bf16[2,2,240,128]{3,2,1,0:T(8,128)(2,1)S(1)} %get-tuple-element.118), channel_id=1, source_target_pairs={{0,4},{1,33},{4,0},{5,37},{8,12},{9,41},{12,8},{13,45},{2,6},{3,35... | collective-permute-start | bytes 737288 | tf_op jit(solution)/shard_map/ppermute | solution.py:56
  79.3 8.8 %collective-permute-start.20 = (bf16[2,2,240,128]{3,2,1,0:T(8,128)(2,1)S(1)}, bf16[2,2,240,128]{3,2,1,0:T(8,128)(2,1)S(1)}, u32[]{:S(2)}, u32[]{:S(2)}) collective-permute-start(bf16[2,2,240,128]{3,2,1,0:T(8,128)(2,1)S(1)} %get-tuple-element.119), channel_id=1, source_target_pairs={{0,12},{1,97},{4,8},{5,101},{8,4},{9,105},{12,0},{13,109},{2,14},{... | collective-permute-start | bytes 737288 | tf_op jit(solution)/shard_map/ppermute | solution.py:56
  81.8 7.9 %collective-permute-start.21 = (bf16[2,2,240,128]{3,2,1,0:T(8,128)(2,1)S(1)}, bf16[2,2,240,128]{3,2,1,0:T(8,128)(2,1)S(1)}, u32[]{:S(2)}, u32[]{:S(2)}) collective-permute-start(bf16[2,2,240,128]{3,2,1,0:T(8,128)(2,1)S(1)} %get-tuple-element.120), channel_id=1, source_target_pairs={{0,8},{1,65},{4,12},{5,69},{8,0},{9,73},{12,4},{13,77},{2,10},{3,6... | collective-permute-start | bytes 737288 | tf_op jit(solution)/shard_map/ppermute | solution.py:56
  89.8 7.3 %collective-permute-start.24 = (bf16[2,240,128]{2,1,0:T(8,128)(2,1)S(1)}, bf16[2,240,128]{2,1,0:T(8,128)(2,1)S(1)}, u32[]{:S(2)}, u32[]{:S(2)}) collective-permute-start(bf16[2,240,128]{2,1,0:T(8,128)(2,1)S(1)} %get-tuple-element.131), channel_id=1, source_target_pairs={{0,16},{1,17},{4,20},{5,21},{8,24},{9,25},{12,28},{13,29},{2,18},{... | collective-permute-start | bytes 368648 | tf_op jit(solution)/shard_map/ppermute | solution.py:56
  92.9 6.1 %collective-permute-start.23 = (bf16[2,240,128]{2,1,0:T(8,128)(2,1)S(1)}, bf16[2,240,128]{2,1,0:T(8,128)(2,1)S(1)}, u32[]{:S(2)}, u32[]{:S(2)}) collective-permute-start(bf16[2,240,128]{2,1,0:T(8,128)(2,1)S(1)} %get-tuple-element.130), channel_id=1, source_target_pairs={{0,18},{1,19},{4,22},{5,23},{8,26},{9,27},{12,30},{13,31},{2,16},{... | collective-permute-start | bytes 368648 | tf_op jit(solution)/shard_map/ppermute | solution.py:56
  94.1 5.0 %collective-permute-start.22 = (bf16[2,240,128]{2,1,0:T(8,128)(2,1)S(1)}, bf16[2,240,128]{2,1,0:T(8,128)(2,1)S(1)}, u32[]{:S(2)}, u32[]{:S(2)}) collective-permute-start(bf16[2,240,128]{2,1,0:T(8,128)(2,1)S(1)} %get-tuple-element.130), channel_id=1, source_target_pairs={{0,2},{1,3},{4,6},{5,7},{8,10},{9,11},{12,14},{13,15},{2,0},{3,1},... | collective-permute-start | bytes 368648 | tf_op jit(solution)/shard_map/ppermute | solution.py:56
  99.1 6.5 %collective-permute-start.27 = (bf16[2,240,128]{2,1,0:T(8,128)(2,1)S(1)}, bf16[2,240,128]{2,1,0:T(8,128)(2,1)S(1)}, u32[]{:S(2)}, u32[]{:S(2)}) collective-permute-start(bf16[2,240,128]{2,1,0:T(8,128)(2,1)S(1)} %add_convert_fusion.1), channel_id=1, source_target_pairs={{0,8},{1,65},{4,12},{5,69},{8,0},{9,73},{12,4},{13,77},{2,10},{3,6... | collective-permute-start | bytes 368648 | tf_op jit(solution)/shard_map/ppermute | solution.py:56
  101.2 6.1 %collective-permute-start.26 = (bf16[2,240,128]{2,1,0:T(8,128)(2,1)S(1)}, bf16[2,240,128]{2,1,0:T(8,128)(2,1)S(1)}, u32[]{:S(2)}, u32[]{:S(2)}) collective-permute-start(bf16[2,240,128]{2,1,0:T(8,128)(2,1)S(1)} %add_convert_fusion.1), channel_id=1, source_target_pairs={{0,12},{1,97},{4,8},{5,101},{8,4},{9,105},{12,0},{13,109},{2,14},{... | collective-permute-start | bytes 368648 | tf_op jit(solution)/shard_map/ppermute | solution.py:56
  102.7 4.9 %collective-permute-start.25 = (bf16[2,240,128]{2,1,0:T(8,128)(2,1)S(1)}, bf16[2,240,128]{2,1,0:T(8,128)(2,1)S(1)}, u32[]{:S(2)}, u32[]{:S(2)}) collective-permute-start(bf16[2,240,128]{2,1,0:T(8,128)(2,1)S(1)} %add_convert_fusion.1), channel_id=1, source_target_pairs={{0,4},{1,33},{4,0},{5,37},{8,12},{9,41},{12,8},{13,45},{2,6},{3,35... | collective-permute-start | bytes 368648 | tf_op jit(solution)/shard_map/ppermute | solution.py:56
  107.7 1.3 collective-permute-start.28
  108.9 10.4 %collective-permute-start.31 = (bf16[4,2,240,128]{3,2,1,0:T(8,128)(2,1)S(1)}, bf16[4,2,240,128]{3,2,1,0:T(8,128)(2,1)S(1)}, u32[]{:S(2)}, u32[]{:S(2)}) collective-permute-start(bf16[4,2,240,128]{3,2,1,0:T(8,128)(2,1)S(1)} %pad_maximum_fusion.s0), channel_id=1, source_target_pairs={{0,64},{1,9},{4,68},{5,13},{8,72},{9,1},{12,76},{13,5},{2,66},{3,1... | collective-permute-start | bytes 1474568 | tf_op jit(solution)/shard_map/ppermute | solution.py:56
  109.9 14.6 %collective-permute-start.30 = (bf16[4,2,240,128]{3,2,1,0:T(8,128)(2,1)S(1)}, bf16[4,2,240,128]{3,2,1,0:T(8,128)(2,1)S(1)}, u32[]{:S(2)}, u32[]{:S(2)}) collective-permute-start(bf16[4,2,240,128]{3,2,1,0:T(8,128)(2,1)S(1)} %pad_maximum_fusion.s0), channel_id=1, source_target_pairs={{0,96},{1,13},{4,100},{5,9},{8,104},{9,5},{12,108},{13,1},{2,98},{... | collective-permute-start | bytes 1474568 | tf_op jit(solution)/shard_map/ppermute | solution.py:56
  111.7 12.8 %collective-permute-start.29 = (bf16[4,2,240,128]{3,2,1,0:T(8,128)(2,1)S(1)}, bf16[4,2,240,128]{3,2,1,0:T(8,128)(2,1)S(1)}, u32[]{:S(2)}, u32[]{:S(2)}) collective-permute-start(bf16[4,2,240,128]{3,2,1,0:T(8,128)(2,1)S(1)} %pad_maximum_fusion.s0), channel_id=1, source_target_pairs={{0,32},{1,5},{4,36},{5,1},{8,40},{9,13},{12,44},{13,9},{2,34},{3,7... | collective-permute-start | bytes 1474568 | tf_op jit(solution)/shard_map/ppermute | solution.py:56

commit v3 on v2

--- a/solution.py
+++ b/solution.py
@@ -360,35 +360,37 @@
         out[...] = whole[:, pl.ds(begin, CHUNK), :]
 
 
-def piece_kernel(*refs):
-    chunks, outs, whole = refs[:8], refs[8:12], refs[12]
+def piece_kernel(own, a, b, c, *refs):
+    before, outs, whole = refs[:-5], refs[-5:-1], refs[-1]
     _, i2 = places()
-    for k in range(2):
-        own, a, b, c = (ref[...].astype(F32) for ref in chunks[4 * k : 4 * k + 4])
-        whole[:, k] = ((own + a) + (b + c)).astype(BF)
-    for bits, out in zip((*PEERS, 0), outs):
+    own, a, b, c = (ref[...].astype(F32) for ref in (own, a, b, c))
+    whole[...] = ((own + a) + (b + c)).astype(BF)
+    for n, (bits, out) in enumerate(zip((*PEERS, 0), outs)):
         begin = pl.multiple_of((i2 ^ bits) * PIECE, PIECE)
-        out[...] = whole[:, :, pl.ds(begin, PIECE), :]
-
-
-def unpack_kernel(here, s0, s1, s2, s3, *refs):
-    outs, whole, bufs, sem = refs[:7], refs[7], refs[8:15], refs[15]
+        if before:
+            out[:, 0] = whole[:, pl.ds(begin, PIECE), :]
+            out[:, 1] = before[n][...]
+        else:
+            out[...] = whole[:, pl.ds(begin, PIECE), :]
+
+
+def unpack_kernel(k, *refs):
+    stacks, outs, whole, bufs, sem = refs[:4], refs[-16:-9], refs[-9], refs[-8:-1], refs[-1]
     i1, i2 = places()
-    for a, stack in zip((0, *PEERS), (s0, s1, s2, s3)):
+    for a, stack in zip((0, *PEERS), stacks):
         for slot, b in enumerate((0, *PEERS)):
             at = pl.multiple_of((i1 ^ a) * CHUNK + (i2 ^ b) * PIECE, PIECE)
-            whole[:, pl.ds(at, PIECE), :] = stack[slot]
+            whole[pl.ds(at, PIECE), :] = stack[slot]
     scale = 1.0 / math.sqrt(98304)
     copies = []
     for (name, (begin, count)), out, buf in zip(TABLES.items(), outs, bufs):
-        for k in range(2):
-            if buf.shape[2] == 128:
-                buf[k] = whole[k, begin : begin + count, :].astype(F32) * scale
-            else:
-                for i in range(count // 128):
-                    part = whole[k, begin + 128 * i : begin + 128 * (i + 1), :].astype(F32) * scale
-                    buf[k, :, 128 * i : 128 * (i + 1)] = part.T if name == "basis" else part
-        copies.append(pltpu.make_async_copy(buf, out, sem.at[len(copies)]))
+        if buf.shape[1] == 128:
+            buf[...] = whole[begin : begin + count, :].astype(F32) * scale
+        else:
+            for i in range(count // 128):
+                part = whole[begin + 128 * i : begin + 128 * (i + 1), :].astype(F32) * scale
+                buf[:, 128 * i : 128 * (i + 1)] = part.T if name == "basis" else part
+        copies.append(pltpu.make_async_copy(buf, out.at[k], sem.at[len(copies)]))
         copies[-1].start()
     for copy in copies:
         copy.wait()
@@ -408,7 +410,7 @@
 ANYWHERE = pl.BlockSpec(memory_space=pl.ANY)
 
 
-def call(kernel, name, ins, outs, scratch, mib, us):
+def call(kernel, name, ins, outs, scratch, mib, us, aliases={}):
     return pl.pallas_call(
         kernel,
         out_shape=[o[0] for o in outs],
@@ -420,6 +422,7 @@
             flops=int(us * 8e8), bytes_accessed=int(us * 1e6), transcendentals=0
         ),
         name=name,
+        input_output_aliases=aliases,
     )
 
 
@@ -511,34 +514,40 @@
     mine1b, got2[2] = lax.optimization_barrier((mine1b, got2[2]))
     *out1, own1 = cut((-LOW, TOP), [mine1b, mine1a], [*got1b, got1a], "cut_one")
     got1 = [send(part, to_first(a)) for part, a in zip(out1, PEERS)]
-    *out, own = call(
-        piece_kernel,
-        "pieces",
-        [IN_VMEM] * 8,
-        [(shape(2, 2, PIECE, 128, kind=BF), IN_VMEM)] * 4,
-        [vmem(2, 2, CHUNK, 128)],
-        M5,
-        2,
-    )(own1, *got1, own2, *got2)
+
+    def pieces(own, got, before, dims):
+        return call(
+            piece_kernel,
+            "pieces",
+            [IN_VMEM] * (4 + len(before)),
+            [(shape(2, *dims, PIECE, 128, kind=BF), IN_VMEM)] * 4,
+            [vmem(2, CHUNK, 128)],
+            M5,
+            1,
+        )(own, *got, *before)
+
+    *out, own = pieces(own1, got1, pieces(own2, got2, (), ()), (2,))
     got = [send(part, to_second(b)) for part, b in zip(out, PEERS)]
     done = plus(own, *got)
     got = [send(done[1], to_x(1)), send(done[1], to_x(3)), send(done[0], to_x(2))]
     done = plus(done[0], *got)
-    stack = jnp.stack([done] + [send(done, to_second(b)) for b in PEERS])
-    stack, here = lax.optimization_barrier((stack, send(stack[:, 0, :8], to_core())))
-    stacks = [stack] + [send(stack, to_first(a)) for a in PEERS]
-    outs = (
-        (2, 560, 128), (2, 128, 512), (2, 512, 128), (2, 128, 512), (2, 512, 128), (2, 512, 128), (2, 128, 640),
-    )
-    grads = call(
-        unpack_kernel,
-        "unpack",
-        [ANYWHERE] + [IN_VMEM] * 4,
-        [(shape(*dims), ANYWHERE) for dims in outs],
-        [vmem(2, PACK, 128)] + [vmem(*dims, kind=F32) for dims in outs] + [DMA((7,))],
-        16,
-        3,
-    )(here, *stacks)
+    stack = jnp.stack([done] + [send(done, to_second(b)) for b in PEERS], axis=1)
+    grads = ()
+    for k in (1, 0):
+        stacks = [stack[k]] + [send(stack[k], to_first(a)) for a in PEERS]
+        outs = (
+            (560, 128), (128, 512), (512, 128), (128, 512), (512, 128), (512, 128), (128, 640),
+        )
+        grads = call(
+            functools.partial(unpack_kernel, k),
+            "unpack",
+            [IN_VMEM] * 4 + [ANYWHERE] * (len(grads)),
+            [(shape(2, *dims), ANYWHERE) for dims in outs],
+            [vmem(PACK, 128)] + [vmem(*dims, kind=F32) for dims in outs] + [DMA((7,))],
+            16,
+            2,
+            {4 + n: n for n in range(len(grads))},
+        )(*stacks, *grads)
     return (look.T, rest.T, steep.T, *grads)
 
 

time: 127 us -> 126 us (level)
  waiting for transfers between devices: 54.5 us -> 48.5 us
  starting transfers between devices: 37.7 us -> 41.4 us
    ppermute x32 -> x34, waiting for transfers between devices: 54.5 us -> 48.5 us  [send(): return lax.ppermute(values, ('dp', 'mp'), where)]
    ppermute x32 -> x34, starting transfers between devices: 37.7 us -> 41.4 us  [send(): return lax.ppermute(values, ('dp', 'mp'), where)]
    pallas_call x2 -> x4, Pallas kernels: 3.46 us -> 4.2 us  [the longest x2 3.04 us: shards(): call(functools.partial(unpack_kernel, k), 'unpack', [IN_VMEM] * 4 + [ANYW...]
  transfers between devices with their start and end apart: 32 -> 34, of which waited for: 20 -> 21; matrix products, arithmetic and copies ran while one was open for 0% -> 0% of each run, Pallas kernels for 13% -> 15%
where the time goes in v3:
time: 126 us
  waiting for transfers between devices  48.5 us (38%)
  starting transfers between devices  41.4 us (33%)
  Pallas kernels  34.2 us (27%)
    ppermute x34, waiting for transfers between devices, send(): return lax.ppermute(values, ('dp', 'mp'), where)  48.5 us
    ppermute x34, starting transfers between devices, send(): return lax.ppermute(values, ('dp', 'mp'), where)  41.4 us
    pallas_call x1, Pallas kernels, shards(): call(second_kernel, 'block_two', [IN_VMEM] * 9, [(shape(336, ROWS), IN_VM...  10.5 us
    pallas_call x1, Pallas kernels, shards(): call(first_kernel, 'forward_one', [IN_VMEM] * 6, [(shape(336, ROWS), IN_V...  4.18 us
    pallas_call x1, Pallas kernels, shards(): call(fourth_kernel, 'backward_one_layers', [IN_VMEM] * 10, [(shape(336, R...  4.16 us
    pallas_call x1, Pallas kernels, shards(): call(third_kernel, 'backward_one_heads', [IN_VMEM] * 10, [(shape(512, ROW...  3.75 us
    pallas_call x2, Pallas kernels, shards(): call(functools.partial(unpack_kernel, k), 'unpack', [IN_VMEM] * 4 + [ANYW...  3.04 us
    pallas_call x1, Pallas kernels, shards(): call(functools.partial(pack_kernel, 1), 'pack_two', [IN_VMEM] * 7, [(whol...  2.58 us
  transfers between devices with their start and end apart: 34, of which 21 were waited for; matrix products, arithmetic and copies ran while one was open for 0% of the time, Pallas kernels for 15%

profile of v3, /device:TPU:0, one launch (start us, length us, event | category | flops | bytes accessed | tf_op | source)
XLA Modules:
  0.0 125.5 jit_solution(11040078969117299589)
XLA Ops:
  0.6 2.6 %pack_two.1 = (bf16[3840,128]{1,0:T(8,128)(2,1)}, bf16[960,128]{1,0:T(8,128)(2,1)}) custom-call(bf16[2,560,128]{2,1,0:T(8,128)(2,1)} %refs_0_.2, bf16[2,128,512]{2,1,0:T(8,128)(2,1)} %refs_1_.2, bf16[2,512,128]{2,1,0:T(8,128)(2,1)} %refs_2_.2, bf16[2,128,512]{2,1,0:T(8,128)(2,1)} %refs_3_.2, bf16[2,512,128]{2,1,0:T(8,128)(2,1)} %refs_4_.2, ...), custom_call_target="tpu_custom_call" | custom-call | flops 1600000000 | bytes 2000000 | tf_op jit(solution)/shard_map/pack_two/pallas_call | solution.py:443
  3.2 1.6 %collective-permute-start = (bf16[960,128]{1,0:T(8,128)(2,1)}, bf16[960,128]{1,0:T(8,128)(2,1)S(1)}, u32[]{:S(2)}, u32[]{:S(2)}) collective-permute-start(bf16[960,128]{1,0:T(8,128)(2,1)} %get-tuple-element.87), channel_id=1, source_target_pairs={{0,2},{1,19},{4,6},{5,23},{8,10},{9,27},{12,14},{13,31},{2,0},{3,1... | collective-permute-start | bytes 737288 | tf_op jit(solution)/shard_map/ppermute | solution.py:56
  4.8 2.5 %pack_one.1.s0 = bf16[3840,128]{1,0:T(8,128)(2,1)} custom-call(bf16[2,560,128]{2,1,0:T(8,128)(2,1)} %refs_0_.2, bf16[2,128,512]{2,1,0:T(8,128)(2,1)} %refs_1_.2, bf16[2,512,128]{2,1,0:T(8,128)(2,1)} %refs_2_.2, bf16[2,128,512]{2,1,0:T(8,128)(2,1)} %refs_3_.2, bf16[2,512,128]{2,1,0:T(8,128)(2,1)} %refs_4_.2, bf16[2,512,128]{2,1,0:T(8,128)(2,1)} %refs_5_.2, ...), custom_call_target="tpu_custom_call" | custom-call | flops 1600000000 | bytes 2000000 | tf_op jit(solution)/shard_map/pack_one/pallas_call | solution.py:447
  7.3 2.3 %collective-permute-done.q0 = bf16[960,128]{1,0:T(8,128)(2,1)S(1)} collective-permute-done((bf16[960,128]{1,0:T(8,128)(2,1)}, bf16[960,128]{1,0:T(8,128)(2,1)S(1)}, u32[]{:S(2)}, u32[]{:S(2)}) %collective-permute-start) | collective-permute-done | bytes 245792 | tf_op jit(solution)/shard_map/ppermute | solution.py:56
  9.6 1.6 %collective-permute-start.2 = (bf16[3840,128]{1,0:T(8,128)(2,1)}, bf16[3840,128]{1,0:T(8,128)(2,1)S(1)}, u32[]{:S(2)}, u32[]{:S(2)}) collective-permute-start(bf16[3840,128]{1,0:T(8,128)(2,1)} %pack_one.1.s0), channel_id=1, source_target_pairs={{0,2},{1,19},{4,6},{5,23},{8,10},{9,27},{12,14},{13,31},{2,0},{3,1... | collective-permute-start | bytes 2949128 | tf_op jit(solution)/shard_map/ppermute | solution.py:56
  11.2 3.2 %collective-permute-start.5 = (bf16[960,128]{1,0:T(8,128)(2,1)S(1)}, bf16[960,128]{1,0:T(8,128)(2,1)S(1)}, u32[]{:S(2)}, u32[]{:S(2)}) collective-permute-start(bf16[960,128]{1,0:T(8,128)(2,1)S(1)} %collective-permute-done.q0), channel_id=1, source_target_pairs={{0,64},{1,9},{4,68},{5,13},{8,72},{9,1},{12,76},{13,5},{2,66},{3,1... | collective-permute-start | bytes 737288 | tf_op jit(solution)/shard_map/ppermute | solution.py:56
  14.4 1.1 collective-permute-start.4
  15.5 1.0 collective-permute-start.1
  16.4 2.5 %collective-permute-done.5.q3 = bf16[960,128]{1,0:T(8,128)(2,1)S(1)} collective-permute-done((bf16[960,128]{1,0:T(8,128)(2,1)S(1)}, bf16[960,128]{1,0:T(8,128)(2,1)S(1)}, u32[]{:S(2)}, u32[]{:S(2)}) %collective-permute-start.5) | collective-permute-done | bytes 245792 | tf_op jit(solution)/shard_map/ppermute | solution.py:56
  18.9 2.9 %collective-permute-done.4.q2 = bf16[960,128]{1,0:T(8,128)(2,1)S(1)} collective-permute-done((bf16[960,128]{1,0:T(8,128)(2,1)S(1)}, bf16[960,128]{1,0:T(8,128)(2,1)S(1)}, u32[]{:S(2)}, u32[]{:S(2)}) %collective-permute-start.4) | collective-permute-done | bytes 245792 | tf_op jit(solution)/shard_map/ppermute | solution.py:56
  21.8 0.1 collective-permute-done.3.q1
  21.9 2.0 %collective-permute-done.2.s2 = bf16[3840,128]{1,0:T(8,128)(2,1)S(1)} collective-permute-done((bf16[3840,128]{1,0:T(8,128)(2,1)}, bf16[3840,128]{1,0:T(8,128)(2,1)S(1)}, u32[]{:S(2)}, u32[]{:S(2)}) %collective-permute-start.2) | collective-permute-done | bytes 983072 | tf_op jit(solution)/shard_map/ppermute | solution.py:56
  23.9 0.5 collective-permute-start.7
  24.5 0.1 join.1.s2
  24.5 0.3 collective-permute-start.8
  24.9 1.7 %collective-permute-done.6.s3 = bf16[3840,128]{1,0:T(8,128)(2,1)S(1)} collective-permute-done((bf16[3840,128]{1,0:T(8,128)(2,1)S(1)}, bf16[3840,128]{1,0:T(8,128)(2,1)S(1)}, u32[]{:S(2)}, u32[]{:S(2)}) %collective-permute-start.6) | collective-permute-done | bytes 983072 | tf_op jit(solution)/shard_map/ppermute | solution.py:56
  26.5 4.2 %forward_one.1 = (f32[336,768]{1,0:T(8,128)S(1)}, f32[48,768]{1,0:T(8,128)S(1)}, bf16[560,768]{1,0:T(8,128)(2,1)S(1)}, bf16[4,512,768]{2,1,0:T(8,128)(2,1)S(1)},...) custom-call(s32[1,768]{1,0:T(1,128)S(1)} %broadcast_in_dim.3.label, bf16[336,768]{1,0:T(8,128)(2,1)S(1)} %bitcast.26, ...), custom_call_target="tpu_custom_call" | custom-call | flops 4800000000 | bytes 6000000 | tf_op jit(solution)/shard_map/forward_one/pallas_call | solution.py:457
  30.7 10.5 %block_two.1 = (f32[336,768]{1,0:T(8,128)}, f32[48,768]{1,0:T(8,128)}, f32[336,768]{1,0:T(8,128)S(1)}, bf16[2,3840,128]{2,1,0:T(8,128)(2,1)S(1)}, bf16[2,3840,128]{2,1,0:T(8,128)(2,1)S(1)}) custom-call(s32[1,768]{1,0:T(1,128)S(1)} %broadcast_in_dim.3.label, f32[336,768]{1,0:T(8,128)S(1)} %get-tuple-element.91.state_in, ...), custom_call_target="tpu_custom_call" | custom-call | flops 11200000000 | bytes 14000000 | tf_op jit(solution)/shard_map/block_two/pallas_call | solution.py:467
  41.3 0.2 collective-permute-start.10
  41.5 3.7 %backward_one_heads.1 = (bf16[512,768]{1,0:T(8,128)(2,1)S(1)}, bf16[2,2256,128]{2,1,0:T(8,128)(2,1)S(1)}, bf16[2,2256,128]{2,1,0:T(8,128)(2,1)S(1)}) custom-call(s32[1,768]{1,0:T(1,128)S(1)} %broadcast_in_dim.3.label, f32[336,768]{1,0:T(8,128)S(1)} %get-tuple-element.100.g_in, bf16[48,768]{1,0:T(8,128)(2,1)S(1)} %bitcast.29, bf16[3840,128]{1,0:T(8,128)(2,1)S(1)} %copy-done, ...), custom_call_target="tpu_custom_call" | custom-call | flops 4800000000 | bytes 6000000 | tf_op jit(solution)/shard_map/backward_one_heads/pallas_call | solution.py:478
  45.2 0.5 collective-permute-start.9
  45.7 1.1 cut_two.1
  46.9 3.4 %collective-permute-start.11 = (bf16[2,960,128]{2,1,0:T(8,128)(2,1)S(1)}, bf16[2,960,128]{2,1,0:T(8,128)(2,1)S(1)}, u32[]{:S(2)}, u32[]{:S(2)}) collective-permute-start(bf16[2,960,128]{2,1,0:T(8,128)(2,1)S(1)} %get-tuple-element.110), channel_id=1, source_target_pairs={{0,64},{1,9},{4,68},{5,13},{8,72},{9,1},{12,76},{13,5},{2,66},{3,1... | collective-permute-start | bytes 1474568 | tf_op jit(solution)/shard_map/ppermute | solution.py:56
  50.2 4.2 %backward_one_layers.1 = (f32[336,768]{1,0:T(8,128)}, bf16[2,1584,128]{2,1,0:T(8,128)(2,1)S(1)}, bf16[1584,128]{1,0:T(8,128)(2,1)S(1)}, bf16[1584,128]{1,0:T(8,128)(2,1)S(1)}) custom-call(s32[1,768]{1,0:T(1,128)S(1)} %broadcast_in_dim.3.label, f32[336,768]{1,0:T(8,128)S(1)} %get-tuple-element.100.g_in, bf16[512,768]{1,0:T(8,128)(2,1)S(1)} %get-tuple-element.111.d_in, ...), custom_call_target="tpu_custom_call" | custom-call | flops 4800000000 | bytes 6000000 | tf_op jit(solution)/shard_map/backward_one_layers/pallas_call | solution.py:503
  54.4 0.5 collective-permute-start.12
  54.9 1.6 %collective-permute-start.17 = (bf16[2,960,128]{2,1,0:T(8,128)(2,1)S(1)}, bf16[2,960,128]{2,1,0:T(8,128)(2,1)S(1)}, u32[]{:S(2)}, u32[]{:S(2)}) collective-permute-start(bf16[2,960,128]{2,1,0:T(8,128)(2,1)S(1)} %get-tuple-element.108), channel_id=1, source_target_pairs={{0,32},{1,5},{4,36},{5,1},{8,40},{9,13},{12,44},{13,9},{2,34},{3,7... | collective-permute-start | bytes 1474568 | tf_op jit(solution)/shard_map/ppermute | solution.py:56
  56.5 2.2 %collective-permute-start.18 = (bf16[2,960,128]{2,1,0:T(8,128)(2,1)S(1)}, bf16[2,960,128]{2,1,0:T(8,128)(2,1)S(1)}, u32[]{:S(2)}, u32[]{:S(2)}) collective-permute-start(bf16[2,960,128]{2,1,0:T(8,128)(2,1)S(1)} %get-tuple-element.109), channel_id=1, source_target_pairs={{0,96},{1,13},{4,100},{5,9},{8,104},{9,5},{12,108},{13,1},{2,98},{... | collective-permute-start | bytes 1474568 | tf_op jit(solution)/shard_map/ppermute | solution.py:56
  58.7 1.1 cut_one.1
  59.8 0.8 collective-permute-start.14
  60.5 1.7 %collective-permute-start.15 = (bf16[2,960,128]{2,1,0:T(8,128)(2,1)S(1)}, bf16[2,960,128]{2,1,0:T(8,128)(2,1)S(1)}, u32[]{:S(2)}, u32[]{:S(2)}) collective-permute-start(bf16[2,960,128]{2,1,0:T(8,128)(2,1)S(1)} %get-tuple-element.122), channel_id=1, source_target_pairs={{0,96},{1,13},{4,100},{5,9},{8,104},{9,5},{12,108},{13,1},{2,98},{... | collective-permute-start | bytes 1474568 | tf_op jit(solution)/shard_map/ppermute | solution.py:56
  62.3 1.7 %collective-permute-start.16 = (bf16[2,960,128]{2,1,0:T(8,128)(2,1)S(1)}, bf16[2,960,128]{2,1,0:T(8,128)(2,1)S(1)}, u32[]{:S(2)}, u32[]{:S(2)}) collective-permute-start(bf16[2,960,128]{2,1,0:T(8,128)(2,1)S(1)} %get-tuple-element.123), channel_id=1, source_target_pairs={{0,64},{1,9},{4,68},{5,13},{8,72},{9,1},{12,76},{13,5},{2,66},{3,1... | collective-permute-start | bytes 1474568 | tf_op jit(solution)/shard_map/ppermute | solution.py:56
  64.0 2.6 %collective-permute-done.18.b = bf16[2,960,128]{2,1,0:T(8,128)(2,1)S(1)} collective-permute-done((bf16[2,960,128]{2,1,0:T(8,128)(2,1)S(1)}, bf16[2,960,128]{2,1,0:T(8,128)(2,1)S(1)}, u32[]{:S(2)}, u32[]{:S(2)}) %collective-permute-start.18) | collective-permute-done | bytes 491552 | tf_op jit(solution)/shard_map/ppermute | solution.py:56
  66.5 0.6 pieces.2
  67.1 1.9 %collective-permute-done.14.a = bf16[2,960,128]{2,1,0:T(8,128)(2,1)S(1)} collective-permute-done((bf16[2,960,128]{2,1,0:T(8,128)(2,1)S(1)}, bf16[2,960,128]{2,1,0:T(8,128)(2,1)S(1)}, u32[]{:S(2)}, u32[]{:S(2)}) %collective-permute-start.14) | collective-permute-done | bytes 491552 | tf_op jit(solution)/shard_map/ppermute | solution.py:56
  69.0 8.1 %collective-permute-done.15.b = bf16[2,960,128]{2,1,0:T(8,128)(2,1)S(1)} collective-permute-done((bf16[2,960,128]{2,1,0:T(8,128)(2,1)S(1)}, bf16[2,960,128]{2,1,0:T(8,128)(2,1)S(1)}, u32[]{:S(2)}, u32[]{:S(2)}) %collective-permute-start.15) | collective-permute-done | bytes 491552 | tf_op jit(solution)/shard_map/ppermute | solution.py:56
  77.1 0.6 pieces.3
  77.7 1.1 collective-permute-start.19
  78.8 2.5 %collective-permute-start.20 = (bf16[2,2,240,128]{3,2,1,0:T(8,128)(2,1)S(1)}, bf16[2,2,240,128]{3,2,1,0:T(8,128)(2,1)S(1)}, u32[]{:S(2)}, u32[]{:S(2)}) collective-permute-start(bf16[2,2,240,128]{3,2,1,0:T(8,128)(2,1)S(1)} %get-tuple-element.132), channel_id=1, source_target_pairs={{0,12},{1,97},{4,8},{5,101},{8,4},{9,105},{12,0},{13,109},{2,14},{... | collective-permute-start | bytes 737288 | tf_op jit(solution)/shard_map/ppermute | solution.py:56
  81.3 1.1 collective-permute-start.21
  82.3 1.6 %collective-permute-done.19 = bf16[2,2,240,128]{3,2,1,0:T(8,128)(2,1)S(1)} collective-permute-done((bf16[2,2,240,128]{3,2,1,0:T(8,128)(2,1)S(1)}, bf16[2,2,240,128]{3,2,1,0:T(8,128)(2,1)S(1)}, u32[]{:S(2)}, u32[]{:S(2)}) %collective-permute-start.19) | collective-permute-done | bytes 245792 | tf_op jit(solution)/shard_map/ppermute | solution.py:56
  84.0 3.7 %collective-permute-done.20 = bf16[2,2,240,128]{3,2,1,0:T(8,128)(2,1)S(1)} collective-permute-done((bf16[2,2,240,128]{3,2,1,0:T(8,128)(2,1)S(1)}, bf16[2,2,240,128]{3,2,1,0:T(8,128)(2,1)S(1)}, u32[]{:S(2)}, u32[]{:S(2)}) %collective-permute-start.20) | collective-permute-done | bytes 245792 | tf_op jit(solution)/shard_map/ppermute | solution.py:56
  87.6 1.5 %collective-permute-done.21 = bf16[2,2,240,128]{3,2,1,0:T(8,128)(2,1)S(1)} collective-permute-done((bf16[2,2,240,128]{3,2,1,0:T(8,128)(2,1)S(1)}, bf16[2,2,240,128]{3,2,1,0:T(8,128)(2,1)S(1)}, u32[]{:S(2)}, u32[]{:S(2)}) %collective-permute-start.21) | collective-permute-done | bytes 245792 | tf_op jit(solution)/shard_map/ppermute | solution.py:56
  89.1 0.1 add_convert_fusion
  89.3 3.1 %collective-permute-start.24 = (bf16[2,240,128]{2,1,0:T(8,128)(2,1)S(1)}, bf16[2,240,128]{2,1,0:T(8,128)(2,1)S(1)}, u32[]{:S(2)}, u32[]{:S(2)}) collective-permute-start(bf16[2,240,128]{2,1,0:T(8,128)(2,1)S(1)} %get-tuple-element.151), channel_id=1, source_target_pairs={{0,16},{1,17},{4,20},{5,21},{8,24},{9,25},{12,28},{13,29},{2,18},{... | collective-permute-start | bytes 368648 | tf_op jit(solution)/shard_map/ppermute | solution.py:56
  92.4 1.1 collective-permute-start.23
  93.5 3.1 %collective-permute-done.24 = bf16[2,240,128]{2,1,0:T(8,128)(2,1)S(1)} collective-permute-done((bf16[2,240,128]{2,1,0:T(8,128)(2,1)S(1)}, bf16[2,240,128]{2,1,0:T(8,128)(2,1)S(1)}, u32[]{:S(2)}, u32[]{:S(2)}) %collective-permute-start.24) | collective-permute-done | bytes 122912 | tf_op jit(solution)/shard_map/ppermute | solution.py:56
  96.6 1.9 %collective-permute-done.23 = bf16[2,240,128]{2,1,0:T(8,128)(2,1)S(1)} collective-permute-done((bf16[2,240,128]{2,1,0:T(8,128)(2,1)S(1)}, bf16[2,240,128]{2,1,0:T(8,128)(2,1)S(1)}, u32[]{:S(2)}, u32[]{:S(2)}) %collective-permute-start.23) | collective-permute-done | bytes 122912 | tf_op jit(solution)/shard_map/ppermute | solution.py:56
  98.5 0.1 add_convert_fusion.1
  98.6 2.1 %collective-permute-start.27 = (bf16[2,240,128]{2,1,0:T(8,128)(2,1)S(1)}, bf16[2,240,128]{2,1,0:T(8,128)(2,1)S(1)}, u32[]{:S(2)}, u32[]{:S(2)}) collective-permute-start(bf16[2,240,128]{2,1,0:T(8,128)(2,1)S(1)} %add_convert_fusion.1), channel_id=1, source_target_pairs={{0,8},{1,65},{4,12},{5,69},{8,0},{9,73},{12,4},{13,77},{2,10},{3,6... | collective-permute-start | bytes 368648 | tf_op jit(solution)/shard_map/ppermute | solution.py:56
  100.7 1.5 %collective-permute-start.26 = (bf16[2,240,128]{2,1,0:T(8,128)(2,1)S(1)}, bf16[2,240,128]{2,1,0:T(8,128)(2,1)S(1)}, u32[]{:S(2)}, u32[]{:S(2)}) collective-permute-start(bf16[2,240,128]{2,1,0:T(8,128)(2,1)S(1)} %add_convert_fusion.1), channel_id=1, source_target_pairs={{0,12},{1,97},{4,8},{5,101},{8,4},{9,105},{12,0},{13,109},{2,14},{... | collective-permute-start | bytes 368648 | tf_op jit(solution)/shard_map/ppermute | solution.py:56
  102.2 2.9 %collective-permute-done.27 = bf16[2,240,128]{2,1,0:T(8,128)(2,1)S(1)} collective-permute-done((bf16[2,240,128]{2,1,0:T(8,128)(2,1)S(1)}, bf16[2,240,128]{2,1,0:T(8,128)(2,1)S(1)}, u32[]{:S(2)}, u32[]{:S(2)}) %collective-permute-start.27) | collective-permute-done | bytes 122912 | tf_op jit(solution)/shard_map/ppermute | solution.py:56
  105.0 1.7 %collective-permute-done.26 = bf16[2,240,128]{2,1,0:T(8,128)(2,1)S(1)} collective-permute-done((bf16[2,240,128]{2,1,0:T(8,128)(2,1)S(1)}, bf16[2,240,128]{2,1,0:T(8,128)(2,1)S(1)}, u32[]{:S(2)}, u32[]{:S(2)}) %collective-permute-start.26) | collective-permute-done | bytes 122912 | tf_op jit(solution)/shard_map/ppermute | solution.py:56
  106.8 1.3 %collective-permute-done.25 = bf16[2,240,128]{2,1,0:T(8,128)(2,1)S(1)} collective-permute-done((bf16[2,240,128]{2,1,0:T(8,128)(2,1)S(1)}, bf16[2,240,128]{2,1,0:T(8,128)(2,1)S(1)}, u32[]{:S(2)}, u32[]{:S(2)}) %collective-permute-start.25) | collective-permute-done | bytes 122912 | tf_op jit(solution)/shard_map/ppermute | solution.py:56
  108.1 0.7 collective-permute-start.33
  108.8 1.9 %collective-permute-start.32 = (bf16[4,240,128]{2,1,0:T(8,128)(2,1)S(1)}, bf16[4,240,128]{2,1,0:T(8,128)(2,1)S(1)}, u32[]{:S(2)}, u32[]{:S(2)}) collective-permute-start(bf16[4,240,128]{2,1,0:T(8,128)(2,1)S(1)} %get-tuple-element.148.refs_0_), channel_id=1, source_target_pairs={{0,96},{1,13},{4,100},{5,9},{8,104},{9,5},{12,108},{13,1},{2,98},{... | collective-permute-start | bytes 737288 | tf_op jit(solution)/shard_map/ppermute | solution.py:56
  110.7 1.0 collective-permute-start.31
  111.7 1.8 %collective-permute-start.30 = (bf16[4,240,128]{2,1,0:T(8,128)(2,1)S(1)}, bf16[4,240,128]{2,1,0:T(8,128)(2,1)S(1)}, u32[]{:S(2)}, u32[]{:S(2)}) collective-permute-start(bf16[4,240,128]{2,1,0:T(8,128)(2,1)S(1)} %get-tuple-element.149.refs_0_), channel_id=1, source_target_pairs={{0,64},{1,9},{4,68},{5,13},{8,72},{9,1},{12,76},{13,5},{2,66},{3,1... | collective-permute-start | bytes 737288 | tf_op jit(solution)/shard_map/ppermute | solution.py:56
  113.5 1.9 %collective-permute-start.29 = (bf16[4,240,128]{2,1,0:T(8,128)(2,1)S(1)}, bf16[4,240,128]{2,1,0:T(8,128)(2,1)S(1)}, u32[]{:S(2)}, u32[]{:S(2)}) collective-permute-start(bf16[4,240,128]{2,1,0:T(8,128)(2,1)S(1)} %get-tuple-element.149.refs_0_), channel_id=1, source_target_pairs={{0,96},{1,13},{4,100},{5,9},{8,104},{9,5},{12,108},{13,1},{2,98},{... | collective-permute-start | bytes 737288 | tf_op jit(solution)/shard_map/ppermute | solution.py:56
  115.4 0.6 collective-permute-done.33.refs_3_
  116.0 2.5 %collective-permute-done.32.refs_2_ = bf16[4,240,128]{2,1,0:T(8,128)(2,1)S(1)} collective-permute-done((bf16[4,240,128]{2,1,0:T(8,128)(2,1)S(1)}, bf16[4,240,128]{2,1,0:T(8,128)(2,1)S(1)}, u32[]{:S(2)}, u32[]{:S(2)}) %collective-permute-start.32) | collective-permute-done | bytes 245792 | tf_op jit(solution)/shard_map/ppermute | solution.py:56
  118.5 1.5 %unpack.2 = (f32[2,560,128]{2,1,0:T(8,128)}, f32[2,128,512]{2,1,0:T(8,128)}, f32[2,512,128]{2,1,0:T(8,128)}, f32[2,128,512]{2,1,0:T(8,128)}, f32[2,512,128]{2,1,...) custom-call(bf16[4,240,128]{2,1,0:T(8,128)(2,1)S(1)} %get-tuple-element.148.refs_0_, ...), custom_call_target="tpu_custom_call" | custom-call | flops 1600000000 | bytes 2000000 | tf_op jit(solution)/shard_map/unpack/pallas_call | solution.py:541
  120.1 1.3 collective-permute-done.30.refs_3_
  121.3 2.5 %collective-permute-done.29.refs_2_ = bf16[4,240,128]{2,1,0:T(8,128)(2,1)S(1)} collective-permute-done((bf16[4,240,128]{2,1,0:T(8,128)(2,1)S(1)}, bf16[4,240,128]{2,1,0:T(8,128)(2,1)S(1)}, u32[]{:S(2)}, u32[]{:S(2)}) %collective-permute-start.29) | collective-permute-done | bytes 245792 | tf_op jit(solution)/shard_map/ppermute | solution.py:56
  123.8 1.5 %unpack.3 = (f32[2,560,128]{2,1,0:T(8,128)}, f32[2,128,512]{2,1,0:T(8,128)}, f32[2,512,128]{2,1,0:T(8,128)}, f32[2,128,512]{2,1,0:T(8,128)}, f32[2,512,128]{2,1,...) custom-call(bf16[4,240,128]{2,1,0:T(8,128)(2,1)S(1)} %get-tuple-elem, ...), custom_call_target="tpu_custom_call", output_to_operand_aliasing={{0}: (4, {}), {1}: (5, {}), {2}: (6, {}), {3}: (7, {}), {4}... | custom-call | flops 1600000000 | bytes 2000000 | tf_op jit(solution)/shard_map/unpack/pallas_call | solution.py:541
  (35 shorter events, 0.2 us)
Async XLA Ops:
  3.2 20.7 %copy-start.1 = (bf16[3840,128]{1,0:T(8,128)(2,1)S(1)}, bf16[3840,128]{1,0:T(8,128)(2,1)}, u32[]{:S(2)}) copy-start(bf16[3840,128]{1,0:T(8,128)(2,1)} %get-tuple-element.93.s0) | copy-start | bytes 2949124
  3.2 6.4 %collective-permute-start = (bf16[960,128]{1,0:T(8,128)(2,1)}, bf16[960,128]{1,0:T(8,128)(2,1)S(1)}, u32[]{:S(2)}, u32[]{:S(2)}) collective-permute-start(bf16[960,128]{1,0:T(8,128)(2,1)} %get-tuple-element.87), channel_id=1, source_target_pairs={{0,2},{1,19},{4,6},{5,23},{8,10},{9,27},{12,14},{13,31},{2,0},{3,1... | collective-permute-start | bytes 737288 | tf_op jit(solution)/shard_map/ppermute | solution.py:56
  7.3 17.5 %copy-start.5 = (s32[768]{0:T(1024)S(1)}, s32[768]{0:T(1024)}, u32[]{:S(2)}) copy-start(s32[768]{0:T(1024)} %param.12) | copy-start | bytes 9220
  7.3 19.2 %copy-start = (bf16[3840,128]{1,0:T(8,128)(2,1)S(1)}, bf16[3840,128]{1,0:T(8,128)(2,1)}, u32[]{:S(2)}) copy-start(bf16[3840,128]{1,0:T(8,128)(2,1)} %pack_one.1.s0) | copy-start | bytes 2949124
  7.3 19.2 %copy-start.2 = (bf16[768,336]{0,1:T(8,128)(2,1)S(1)}, bf16[768,336]{0,1:T(8,128)(2,1)}, u32[]{:S(2)}) copy-start(bf16[768,336]{0,1:T(8,128)(2,1)} %param.11) | copy-start | bytes 1548292
  9.6 14.3 %collective-permute-start.2 = (bf16[3840,128]{1,0:T(8,128)(2,1)}, bf16[3840,128]{1,0:T(8,128)(2,1)S(1)}, u32[]{:S(2)}, u32[]{:S(2)}) collective-permute-start(bf16[3840,128]{1,0:T(8,128)(2,1)} %pack_one.1.s0), channel_id=1, source_target_pairs={{0,2},{1,19},{4,6},{5,23},{8,10},{9,27},{12,14},{13,31},{2,0},{3,1... | collective-permute-start | bytes 2949128 | tf_op jit(solution)/shard_map/ppermute | solution.py:56
  11.2 7.7 %collective-permute-start.5 = (bf16[960,128]{1,0:T(8,128)(2,1)S(1)}, bf16[960,128]{1,0:T(8,128)(2,1)S(1)}, u32[]{:S(2)}, u32[]{:S(2)}) collective-permute-start(bf16[960,128]{1,0:T(8,128)(2,1)S(1)} %collective-permute-done.q0), channel_id=1, source_target_pairs={{0,64},{1,9},{4,68},{5,13},{8,72},{9,1},{12,76},{13,5},{2,66},{3,1... | collective-permute-start | bytes 737288 | tf_op jit(solution)/shard_map/ppermute | solution.py:56
  14.4 7.4 %collective-permute-start.4 = (bf16[960,128]{1,0:T(8,128)(2,1)S(1)}, bf16[960,128]{1,0:T(8,128)(2,1)S(1)}, u32[]{:S(2)}, u32[]{:S(2)}) collective-permute-start(bf16[960,128]{1,0:T(8,128)(2,1)S(1)} %collective-permute-done.q0), channel_id=1, source_target_pairs={{0,96},{1,13},{4,100},{5,9},{8,104},{9,5},{12,108},{13,1},{2,98},{... | collective-permute-start | bytes 737288 | tf_op jit(solution)/shard_map/ppermute | solution.py:56
  15.5 6.4 %collective-permute-start.3 = (bf16[960,128]{1,0:T(8,128)(2,1)S(1)}, bf16[960,128]{1,0:T(8,128)(2,1)S(1)}, u32[]{:S(2)}, u32[]{:S(2)}) collective-permute-start(bf16[960,128]{1,0:T(8,128)(2,1)S(1)} %collective-permute-done.q0), channel_id=1, source_target_pairs={{0,32},{1,5},{4,36},{5,1},{8,40},{9,13},{12,44},{13,9},{2,34},{3,7... | collective-permute-start | bytes 737288 | tf_op jit(solution)/shard_map/ppermute | solution.py:56
  15.5 9.4 %collective-permute-start.1 = (bf16[3840,128]{1,0:T(8,128)(2,1)}, bf16[3840,128]{1,0:T(8,128)(2,1)S(1)}, u32[]{:S(2)}, u32[]{:S(2)}) collective-permute-start(bf16[3840,128]{1,0:T(8,128)(2,1)} %pack_one.1.s0), channel_id=1, source_target_pairs={{0,1},{1,0},{4,5},{5,4},{8,9},{9,8},{12,13},{13,12},{2,3},{3,2},{6... | collective-permute-start | bytes 2949128 | tf_op jit(solution)/shard_map/ppermute | solution.py:56
  23.9 2.6 %collective-permute-start.6 = (bf16[3840,128]{1,0:T(8,128)(2,1)S(1)}, bf16[3840,128]{1,0:T(8,128)(2,1)S(1)}, u32[]{:S(2)}, u32[]{:S(2)}) collective-permute-start(bf16[3840,128]{1,0:T(8,128)(2,1)S(1)} %collective-permute-done.2.s2), channel_id=1, source_target_pairs={{0,1},{1,0},{4,5},{5,4},{8,9},{9,8},{12,13},{13,12},{2,3},{3,2},{6... | collective-permute-start | bytes 2949128 | tf_op jit(solution)/shard_map/ppermute | solution.py:56
  23.9 6.8 %collective-permute-start.7 = (bf16[3840,128]{1,0:T(8,128)(2,1)S(1)}, bf16[3840,128]{1,0:T(8,128)(2,1)S(1)}, u32[]{:S(2)}, u32[]{:S(2)}) collective-permute-start(bf16[3840,128]{1,0:T(8,128)(2,1)S(1)} %copy-done.1), channel_id=1, source_target_pairs={{0,1},{1,0},{4,5},{5,4},{8,9},{9,8},{12,13},{13,12},{2,3},{3,2},{6... | collective-permute-start | bytes 2949128 | tf_op jit(solution)/shard_map/ppermute | solution.py:56
  24.5 6.2 %collective-permute-start.8 = (bf16[3840,128]{1,0:T(8,128)(2,1)S(1)}, bf16[3840,128]{1,0:T(8,128)(2,1)S(1)}, u32[]{:S(2)}, u32[]{:S(2)}) collective-permute-start(bf16[3840,128]{1,0:T(8,128)(2,1)S(1)} %join.1.s2), channel_id=1, source_target_pairs={{0,1},{1,0},{4,5},{5,4},{8,9},{9,8},{12,13},{13,12},{2,3},{3,2},{6... | collective-permute-start | bytes 2949128 | tf_op jit(solution)/shard_map/ppermute | solution.py:56
  26.5 4.2 %copy-start.3 = (bf16[768,336]{0,1:T(8,128)(2,1)S(1)}, bf16[768,336]{0,1:T(8,128)(2,1)}, u32[]{:S(2)}) copy-start(bf16[768,336]{0,1:T(8,128)(2,1)} %param.21) | copy-start | bytes 1548292
  26.5 4.2 %copy-start.4 = (bf16[768,48]{0,1:T(8,128)(2,1)S(1)}, bf16[768,48]{0,1:T(8,128)(2,1)}, u32[]{:S(2)}) copy-start(bf16[768,48]{0,1:T(8,128)(2,1)} %param.20) | copy-start | bytes 221188
  41.3 4.4 %collective-permute-start.10 = (bf16[2,3840,128]{2,1,0:T(8,128)(2,1)S(1)}, bf16[2,3840,128]{2,1,0:T(8,128)(2,1)S(1)}, u32[]{:S(2)}, u32[]{:S(2)}) collective-permute-start(bf16[2,3840,128]{2,1,0:T(8,128)(2,1)S(1)} %get-tuple-element.107), channel_id=1, source_target_pairs={{0,1},{1,0},{4,5},{5,4},{8,9},{9,8},{12,13},{13,12},{2,3},{3,2},{6... | collective-permute-start | bytes 5898248 | tf_op jit(solution)/shard_map/ppermute | solution.py:56
  45.2 5.0 %collective-permute-start.9 = (bf16[2,2256,128]{2,1,0:T(8,128)(2,1)S(1)}, bf16[2,2256,128]{2,1,0:T(8,128)(2,1)S(1)}, u32[]{:S(2)}, u32[]{:S(2)}) collective-permute-start(bf16[2,2256,128]{2,1,0:T(8,128)(2,1)S(1)} %get-tuple-element.105), channel_id=1, source_target_pairs={{0,1},{1,0},{4,5},{5,4},{8,9},{9,8},{12,13},{13,12},{2,3},{3,2},{6... | collective-permute-start | bytes 3465224 | tf_op jit(solution)/shard_map/ppermute | solution.py:56
  46.9 11.8 %collective-permute-start.11 = (bf16[2,960,128]{2,1,0:T(8,128)(2,1)S(1)}, bf16[2,960,128]{2,1,0:T(8,128)(2,1)S(1)}, u32[]{:S(2)}, u32[]{:S(2)}) collective-permute-start(bf16[2,960,128]{2,1,0:T(8,128)(2,1)S(1)} %get-tuple-element.110), channel_id=1, source_target_pairs={{0,64},{1,9},{4,68},{5,13},{8,72},{9,1},{12,76},{13,5},{2,66},{3,1... | collective-permute-start | bytes 1474568 | tf_op jit(solution)/shard_map/ppermute | solution.py:56
  54.4 4.3 %collective-permute-start.12 = (bf16[1584,128]{1,0:T(8,128)(2,1)S(1)}, bf16[1584,128]{1,0:T(8,128)(2,1)S(1)}, u32[]{:S(2)}, u32[]{:S(2)}) collective-permute-start(bf16[1584,128]{1,0:T(8,128)(2,1)S(1)} %get-tuple-element.117), channel_id=1, source_target_pairs={{0,1},{1,0},{4,5},{5,4},{8,9},{9,8},{12,13},{13,12},{2,3},{3,2},{6... | collective-permute-start | bytes 1216520 | tf_op jit(solution)/shard_map/ppermute | solution.py:56
  54.9 3.8 %collective-permute-start.13 = (bf16[1584,128]{1,0:T(8,128)(2,1)S(1)}, bf16[1584,128]{1,0:T(8,128)(2,1)S(1)}, u32[]{:S(2)}, u32[]{:S(2)}) collective-permute-start(bf16[1584,128]{1,0:T(8,128)(2,1)S(1)} %get-tuple-element.118), channel_id=1, source_target_pairs={{0,1},{1,0},{4,5},{5,4},{8,9},{9,8},{12,13},{13,12},{2,3},{3,2},{6... | collective-permute-start | bytes 1216520 | tf_op jit(solution)/shard_map/ppermute | solution.py:56
  54.9 9.0 %collective-permute-start.17 = (bf16[2,960,128]{2,1,0:T(8,128)(2,1)S(1)}, bf16[2,960,128]{2,1,0:T(8,128)(2,1)S(1)}, u32[]{:S(2)}, u32[]{:S(2)}) collective-permute-start(bf16[2,960,128]{2,1,0:T(8,128)(2,1)S(1)} %get-tuple-element.108), channel_id=1, source_target_pairs={{0,32},{1,5},{4,36},{5,1},{8,40},{9,13},{12,44},{13,9},{2,34},{3,7... | collective-permute-start | bytes 1474568 | tf_op jit(solution)/shard_map/ppermute | solution.py:56
  56.5 10.0 %collective-permute-start.18 = (bf16[2,960,128]{2,1,0:T(8,128)(2,1)S(1)}, bf16[2,960,128]{2,1,0:T(8,128)(2,1)S(1)}, u32[]{:S(2)}, u32[]{:S(2)}) collective-permute-start(bf16[2,960,128]{2,1,0:T(8,128)(2,1)S(1)} %get-tuple-element.109), channel_id=1, source_target_pairs={{0,96},{1,13},{4,100},{5,9},{8,104},{9,5},{12,108},{13,1},{2,98},{... | collective-permute-start | bytes 1474568 | tf_op jit(solution)/shard_map/ppermute | solution.py:56
  59.8 9.2 %collective-permute-start.14 = (bf16[2,960,128]{2,1,0:T(8,128)(2,1)S(1)}, bf16[2,960,128]{2,1,0:T(8,128)(2,1)S(1)}, u32[]{:S(2)}, u32[]{:S(2)}) collective-permute-start(bf16[2,960,128]{2,1,0:T(8,128)(2,1)S(1)} %get-tuple-element.121), channel_id=1, source_target_pairs={{0,32},{1,5},{4,36},{5,1},{8,40},{9,13},{12,44},{13,9},{2,34},{3,7... | collective-permute-start | bytes 1474568 | tf_op jit(solution)/shard_map/ppermute | solution.py:56
  60.5 16.5 %collective-permute-start.15 = (bf16[2,960,128]{2,1,0:T(8,128)(2,1)S(1)}, bf16[2,960,128]{2,1,0:T(8,128)(2,1)S(1)}, u32[]{:S(2)}, u32[]{:S(2)}) collective-permute-start(bf16[2,960,128]{2,1,0:T(8,128)(2,1)S(1)} %get-tuple-element.122), channel_id=1, source_target_pairs={{0,96},{1,13},{4,100},{5,9},{8,104},{9,5},{12,108},{13,1},{2,98},{... | collective-permute-start | bytes 1474568 | tf_op jit(solution)/shard_map/ppermute | solution.py:56
  62.3 14.8 %collective-permute-start.16 = (bf16[2,960,128]{2,1,0:T(8,128)(2,1)S(1)}, bf16[2,960,128]{2,1,0:T(8,128)(2,1)S(1)}, u32[]{:S(2)}, u32[]{:S(2)}) collective-permute-start(bf16[2,960,128]{2,1,0:T(8,128)(2,1)S(1)} %get-tuple-element.123), channel_id=1, source_target_pairs={{0,64},{1,9},{4,68},{5,13},{8,72},{9,1},{12,76},{13,5},{2,66},{3,1... | collective-permute-start | bytes 1474568 | tf_op jit(solution)/shard_map/ppermute | solution.py:56
  77.7 6.3 %collective-permute-start.19 = (bf16[2,2,240,128]{3,2,1,0:T(8,128)(2,1)S(1)}, bf16[2,2,240,128]{3,2,1,0:T(8,128)(2,1)S(1)}, u32[]{:S(2)}, u32[]{:S(2)}) collective-permute-start(bf16[2,2,240,128]{3,2,1,0:T(8,128)(2,1)S(1)} %get-tuple-element.131), channel_id=1, source_target_pairs={{0,4},{1,33},{4,0},{5,37},{8,12},{9,41},{12,8},{13,45},{2,6},{3,35... | collective-permute-start | bytes 737288 | tf_op jit(solution)/shard_map/ppermute | solution.py:56
  78.8 8.8 %collective-permute-start.20 = (bf16[2,2,240,128]{3,2,1,0:T(8,128)(2,1)S(1)}, bf16[2,2,240,128]{3,2,1,0:T(8,128)(2,1)S(1)}, u32[]{:S(2)}, u32[]{:S(2)}) collective-permute-start(bf16[2,2,240,128]{3,2,1,0:T(8,128)(2,1)S(1)} %get-tuple-element.132), channel_id=1, source_target_pairs={{0,12},{1,97},{4,8},{5,101},{8,4},{9,105},{12,0},{13,109},{2,14},{... | collective-permute-start | bytes 737288 | tf_op jit(solution)/shard_map/ppermute | solution.py:56
  81.3 7.9 %collective-permute-start.21 = (bf16[2,2,240,128]{3,2,1,0:T(8,128)(2,1)S(1)}, bf16[2,2,240,128]{3,2,1,0:T(8,128)(2,1)S(1)}, u32[]{:S(2)}, u32[]{:S(2)}) collective-permute-start(bf16[2,2,240,128]{3,2,1,0:T(8,128)(2,1)S(1)} %get-tuple-element.133), channel_id=1, source_target_pairs={{0,8},{1,65},{4,12},{5,69},{8,0},{9,73},{12,4},{13,77},{2,10},{3,6... | collective-permute-start | bytes 737288 | tf_op jit(solution)/shard_map/ppermute | solution.py:56
  89.3 7.3 %collective-permute-start.24 = (bf16[2,240,128]{2,1,0:T(8,128)(2,1)S(1)}, bf16[2,240,128]{2,1,0:T(8,128)(2,1)S(1)}, u32[]{:S(2)}, u32[]{:S(2)}) collective-permute-start(bf16[2,240,128]{2,1,0:T(8,128)(2,1)S(1)} %get-tuple-element.151), channel_id=1, source_target_pairs={{0,16},{1,17},{4,20},{5,21},{8,24},{9,25},{12,28},{13,29},{2,18},{... | collective-permute-start | bytes 368648 | tf_op jit(solution)/shard_map/ppermute | solution.py:56
  92.4 6.1 %collective-permute-start.23 = (bf16[2,240,128]{2,1,0:T(8,128)(2,1)S(1)}, bf16[2,240,128]{2,1,0:T(8,128)(2,1)S(1)}, u32[]{:S(2)}, u32[]{:S(2)}) collective-permute-start(bf16[2,240,128]{2,1,0:T(8,128)(2,1)S(1)} %get-tuple-element.150), channel_id=1, source_target_pairs={{0,18},{1,19},{4,22},{5,23},{8,26},{9,27},{12,30},{13,31},{2,16},{... | collective-permute-start | bytes 368648 | tf_op jit(solution)/shard_map/ppermute | solution.py:56
  93.5 5.0 %collective-permute-start.22 = (bf16[2,240,128]{2,1,0:T(8,128)(2,1)S(1)}, bf16[2,240,128]{2,1,0:T(8,128)(2,1)S(1)}, u32[]{:S(2)}, u32[]{:S(2)}) collective-permute-start(bf16[2,240,128]{2,1,0:T(8,128)(2,1)S(1)} %get-tuple-element.150), channel_id=1, source_target_pairs={{0,2},{1,3},{4,6},{5,7},{8,10},{9,11},{12,14},{13,15},{2,0},{3,1},... | collective-permute-start | bytes 368648 | tf_op jit(solution)/shard_map/ppermute | solution.py:56
  98.6 6.5 %collective-permute-start.27 = (bf16[2,240,128]{2,1,0:T(8,128)(2,1)S(1)}, bf16[2,240,128]{2,1,0:T(8,128)(2,1)S(1)}, u32[]{:S(2)}, u32[]{:S(2)}) collective-permute-start(bf16[2,240,128]{2,1,0:T(8,128)(2,1)S(1)} %add_convert_fusion.1), channel_id=1, source_target_pairs={{0,8},{1,65},{4,12},{5,69},{8,0},{9,73},{12,4},{13,77},{2,10},{3,6... | collective-permute-start | bytes 368648 | tf_op jit(solution)/shard_map/ppermute | solution.py:56
  100.7 6.1 %collective-permute-start.26 = (bf16[2,240,128]{2,1,0:T(8,128)(2,1)S(1)}, bf16[2,240,128]{2,1,0:T(8,128)(2,1)S(1)}, u32[]{:S(2)}, u32[]{:S(2)}) collective-permute-start(bf16[2,240,128]{2,1,0:T(8,128)(2,1)S(1)} %add_convert_fusion.1), channel_id=1, source_target_pairs={{0,12},{1,97},{4,8},{5,101},{8,4},{9,105},{12,0},{13,109},{2,14},{... | collective-permute-start | bytes 368648 | tf_op jit(solution)/shard_map/ppermute | solution.py:56
  102.2 5.9 %collective-permute-start.25 = (bf16[2,240,128]{2,1,0:T(8,128)(2,1)S(1)}, bf16[2,240,128]{2,1,0:T(8,128)(2,1)S(1)}, u32[]{:S(2)}, u32[]{:S(2)}) collective-permute-start(bf16[2,240,128]{2,1,0:T(8,128)(2,1)S(1)} %add_convert_fusion.1), channel_id=1, source_target_pairs={{0,4},{1,33},{4,0},{5,37},{8,12},{9,41},{12,8},{13,45},{2,6},{3,35... | collective-permute-start | bytes 368648 | tf_op jit(solution)/shard_map/ppermute | solution.py:56
  108.1 7.9 %collective-permute-start.33 = (bf16[4,240,128]{2,1,0:T(8,128)(2,1)S(1)}, bf16[4,240,128]{2,1,0:T(8,128)(2,1)S(1)}, u32[]{:S(2)}, u32[]{:S(2)}) collective-permute-start(bf16[4,240,128]{2,1,0:T(8,128)(2,1)S(1)} %get-tuple-element.148.refs_0_), channel_id=1, source_target_pairs={{0,64},{1,9},{4,68},{5,13},{8,72},{9,1},{12,76},{13,5},{2,66},{3,1... | collective-permute-start | bytes 737288 | tf_op jit(solution)/shard_map/ppermute | solution.py:56
  108.8 9.7 %collective-permute-start.32 = (bf16[4,240,128]{2,1,0:T(8,128)(2,1)S(1)}, bf16[4,240,128]{2,1,0:T(8,128)(2,1)S(1)}, u32[]{:S(2)}, u32[]{:S(2)}) collective-permute-start(bf16[4,240,128]{2,1,0:T(8,128)(2,1)S(1)} %get-tuple-element.148.refs_0_), channel_id=1, source_target_pairs={{0,96},{1,13},{4,100},{5,9},{8,104},{9,5},{12,108},{13,1},{2,98},{... | collective-permute-start | bytes 737288 | tf_op jit(solution)/shard_map/ppermute | solution.py:56
  110.7 7.8 %collective-permute-start.31 = (bf16[4,240,128]{2,1,0:T(8,128)(2,1)S(1)}, bf16[4,240,128]{2,1,0:T(8,128)(2,1)S(1)}, u32[]{:S(2)}, u32[]{:S(2)}) collective-permute-start(bf16[4,240,128]{2,1,0:T(8,128)(2,1)S(1)} %get-tuple-element.148.refs_0_), channel_id=1, source_target_pairs={{0,32},{1,5},{4,36},{5,1},{8,40},{9,13},{12,44},{13,9},{2,34},{3,7... | collective-permute-start | bytes 737288 | tf_op jit(solution)/shard_map/ppermute | solution.py:56
  111.7 9.6 %collective-permute-start.30 = (bf16[4,240,128]{2,1,0:T(8,128)(2,1)S(1)}, bf16[4,240,128]{2,1,0:T(8,128)(2,1)S(1)}, u32[]{:S(2)}, u32[]{:S(2)}) collective-permute-start(bf16[4,240,128]{2,1,0:T(8,128)(2,1)S(1)} %get-tuple-element.149.refs_0_), channel_id=1, source_target_pairs={{0,64},{1,9},{4,68},{5,13},{8,72},{9,1},{12,76},{13,5},{2,66},{3,1... | collective-permute-start | bytes 737288 | tf_op jit(solution)/shard_map/ppermute | solution.py:56
  113.5 10.3 %collective-permute-start.29 = (bf16[4,240,128]{2,1,0:T(8,128)(2,1)S(1)}, bf16[4,240,128]{2,1,0:T(8,128)(2,1)S(1)}, u32[]{:S(2)}, u32[]{:S(2)}) collective-permute-start(bf16[4,240,128]{2,1,0:T(8,128)(2,1)S(1)} %get-tuple-element.149.refs_0_), channel_id=1, source_target_pairs={{0,96},{1,13},{4,100},{5,9},{8,104},{9,5},{12,108},{13,1},{2,98},{... | collective-permute-start | bytes 737288 | tf_op jit(solution)/shard_map/ppermute | solution.py:56
  116.0 7.8 %collective-permute-start.28 = (bf16[4,240,128]{2,1,0:T(8,128)(2,1)S(1)}, bf16[4,240,128]{2,1,0:T(8,128)(2,1)S(1)}, u32[]{:S(2)}, u32[]{:S(2)}) collective-permute-start(bf16[4,240,128]{2,1,0:T(8,128)(2,1)S(1)} %get-tuple-element.149.refs_0_), channel_id=1, source_target_pairs={{0,32},{1,5},{4,36},{5,1},{8,40},{9,13},{12,44},{13,9},{2,34},{3,7... | collective-permute-start | bytes 737288 | tf_op jit(solution)/shard_map/ppermute | solution.py:56

commit v4 on v3

--- a/solution.py
+++ b/solution.py
@@ -14,6 +14,7 @@
 ENTRY, SECOND, THIRD, FOURTH, BACK, FORE, BASIS, USED = 0, 560, 1072, 1584, 2096, 2608, 3120, 3760
 PACK = 3840
 PEERS = (1, 3, 2)
+FAR_FIRST = (2, 3, 1)
 CHUNK, PIECE = PACK // 4, PACK // 16
 
 
@@ -276,22 +277,53 @@
     return jnp.where(core == 0, y, z), jnp.where(core == 0, z, y)
 
 
-def pack_kernel(k, *refs):
-    ins, out, quarter = refs[:7], refs[7], refs[8:]
-    entry, second, third, fourth, back, fore, basis = (ref.at[k] for ref in ins)
-    out[ENTRY:SECOND, :] = entry[...]
-    out[THIRD:FOURTH, :] = third[...]
-    out[BACK:FORE, :] = back[...]
-    out[FORE:BASIS, :] = fore[...]
-    for i in range(4):
-        out[SECOND + 128 * i : SECOND + 128 * (i + 1), :] = second[:, 128 * i : 128 * (i + 1)]
-        out[FOURTH + 128 * i : FOURTH + 128 * (i + 1), :] = fourth[:, 128 * i : 128 * (i + 1)]
-    for i in range(5):
-        out[BASIS + 128 * i : BASIS + 128 * (i + 1), :] = basis[:, 128 * i : 128 * (i + 1)].T
-    out[USED:PACK, :] = jnp.zeros((PACK - USED, 128), BF)
-    if quarter:
-        i1, _ = places()
-        quarter[0][...] = out[pl.ds(pl.multiple_of(i1 * CHUNK, CHUNK), CHUNK), :]
+def pack_kernel(*refs):
+    tables, both, one = refs[:7], refs[7], refs[8]
+    for k in range(2):
+        for (name, (begin, count)), table in zip(TABLES.items(), tables):
+            if table.shape[2] == 128:
+                both[k, begin : begin + count, :] = table[k]
+                continue
+            for i in range(count // 128):
+                block = table[k, :, 128 * i : 128 * (i + 1)]
+                both[k, begin + 128 * i : begin + 128 * (i + 1), :] = block.T if name == "basis" else block
+        both[k, USED:PACK, :] = jnp.zeros((PACK - USED, 128), BF)
+    one[...] = both[0]
+
+
+def quarter_kernel(*refs):
+    tables, out, turned, sem = refs[:7], refs[7], refs[8], refs[9]
+    i1, _ = places()
+    for n in range(4):
+
+        @pl.when(i1 == n)
+        def _():
+            copies = []
+
+            def copy(source, target):
+                copies.append(pltpu.make_async_copy(source, target, sem.at[len(copies)]))
+                copies[-1].start()
+
+            for (name, (begin, count)), table in zip(TABLES.items(), tables):
+                step = 128 if table.shape[2] > 128 else count
+                for at in range(begin, begin + count, step):
+                    low, high = max(at, n * CHUNK), min(at + step, (n + 1) * CHUNK)
+                    if low >= high or name == "basis":
+                        continue
+                    columns = at - begin if step == 128 else 0
+                    copy(
+                        table.at[1, pl.ds(low - at, high - low), pl.ds(columns, 128)],
+                        out.at[pl.ds(low - n * CHUNK, high - low)],
+                    )
+            if n == 3:
+                copy(tables[6].at[1], turned)
+                out[USED - n * CHUNK :, :] = jnp.zeros((PACK - USED, 128), BF)
+            for c in copies:
+                c.wait()
+            if n == 3:
+                for i in range(5):
+                    at = BASIS - n * CHUNK + 128 * i
+                    out[at : at + 128, :] = turned[:, 128 * i : 128 * (i + 1)].T
 
 
 def join_kernel(q0, q1, q2, q3, out):
@@ -302,7 +334,7 @@
 
 
 def first_kernel(label, lag, s0, s1, s2, s3, state_out, look_out, e, act, slope, theta):
-    weights = Weights((s0, s1, s2, s3))
+    weights = Weights((s0.at[0], s1.at[0], s2, s3))
     labels = label[...]
     state = jnp.where(look_mask(labels), lag[...].astype(F32), 0.0)
     heads, fore = run_forward(state, labels, weights, e, act, slope, theta)
@@ -313,7 +345,7 @@
 def second_kernel(
     label, state_in, look_in, left, adjoint, s0, s1, s2, s3, rest, look, g_out, mine, theirs, e, act, slope, theta
 ):
-    weights = Weights((s0, s1, s2, s3))
+    weights = Weights((s0.at[1], s1.at[1], s2, s3))
     labels = label[...]
     heads, fore = run_forward(state_in[...], labels, weights, e, act, slope, theta)
     rest[...] = state_in[...] - pick_look(heads, labels)
@@ -330,14 +362,14 @@
     labels = label[...]
     fore_wide = widen_reach(adjoint[...].astype(F32), labels)
     d_out[...] = backward_heads(
-        g_in[...], fore_wide, labels, Weights((s0, s1, s2, s3)), act, slope, theta, grads
+        g_in[...], fore_wide, labels, Weights((s0.at[0], s1.at[0], s2, s3)), act, slope, theta, grads
     )
 
 
 def fourth_kernel(label, g_in, d_in, s0, s1, s2, s3, e, act, slope, steep, mine, near, far):
     grads = Grads((mine, (near, far)))
     labels = label[...]
-    g = backward_layers(g_in[...], d_in[...], labels, Weights((s0, s1, s2, s3)), e, act, slope, grads)
+    g = backward_layers(g_in[...], d_in[...], labels, Weights((s0.at[0], s1.at[0], s2, s3)), e, act, slope, grads)
     steep[...] = jnp.where(look_mask(labels), g, 0.0)
 
 
@@ -360,25 +392,48 @@
         out[...] = whole[:, pl.ds(begin, CHUNK), :]
 
 
-def piece_kernel(own, a, b, c, *refs):
-    before, outs, whole = refs[:-5], refs[-5:-1], refs[-1]
+def total(refs):
+    a, b, c, d = (ref[...].astype(F32) for ref in refs)
+    return ((a + b) + (c + d)).astype(BF)
+
+
+def fold_kernel(own, a, b, c, near, far):
+    near[...], far[...] = total((own, a, b, c))
+
+
+def piece_kernel(own, a, b, c, near, came, *refs):
+    outs, whole = refs[:4], refs[4]
     _, i2 = places()
-    own, a, b, c = (ref[...].astype(F32) for ref in (own, a, b, c))
-    whole[...] = ((own + a) + (b + c)).astype(BF)
-    for n, (bits, out) in enumerate(zip((*PEERS, 0), outs)):
+    whole[0], whole[2] = total((own, a, b, c))
+    whole[1] = (near[...].astype(F32) + came[...].astype(F32)).astype(BF)
+    for bits, out in zip((*PEERS, 0), outs):
         begin = pl.multiple_of((i2 ^ bits) * PIECE, PIECE)
-        if before:
-            out[:, 0] = whole[:, pl.ds(begin, PIECE), :]
-            out[:, 1] = before[n][...]
-        else:
-            out[...] = whole[:, pl.ds(begin, PIECE), :]
+        out[...] = whole[:, pl.ds(begin, PIECE), :]
+
+
+def sum_kernel(own, a, b, c, near, far):
+    sums = total((own, a, b, c))
+    near[...] = sums[:2]
+    far[...] = sums[2]
+
+
+def across_kernel(near, a, b, c, out):
+    both = near[...].astype(F32) + a[...].astype(F32)
+    out[0] = (both[0] + (b[...].astype(F32) + c[...].astype(F32))).astype(BF)
+    out[1] = both[1].astype(BF)
+
+
+def stack_kernel(*refs):
+    for k in range(2):
+        for n in range(4):
+            refs[4 + k][n] = refs[n][k]
 
 
 def unpack_kernel(k, *refs):
     stacks, outs, whole, bufs, sem = refs[:4], refs[-16:-9], refs[-9], refs[-8:-1], refs[-1]
     i1, i2 = places()
-    for a, stack in zip((0, *PEERS), stacks):
-        for slot, b in enumerate((0, *PEERS)):
+    for a, stack in zip((0, *FAR_FIRST), stacks):
+        for slot, b in enumerate((0, *FAR_FIRST)):
             at = pl.multiple_of((i1 ^ a) * CHUNK + (i2 ^ b) * PIECE, PIECE)
             whole[pl.ds(at, PIECE), :] = stack[slot]
     scale = 1.0 / math.sqrt(98304)
@@ -440,20 +495,34 @@
     lag, adjoint, left = lag.T, adjoint.T, left.T
     whole, part = shape(PACK, 128, kind=BF), shape(CHUNK, 128, kind=BF)
     tables = (entry, second, third, fourth, back, fore, basis)
-    two, quarter = call(
-        functools.partial(pack_kernel, 1), "pack_two", [IN_VMEM] * 7, [(whole, IN_VMEM), (part, IN_VMEM)], [], 60, 2
+    quarter = call(
+        quarter_kernel,
+        "pack_quarter",
+        [ANYWHERE] * 7,
+        [(part, IN_VMEM)],
+        [vmem(128, 640), DMA((8,))],
+        60,
+        1,
+    )(*tables)[0]
+    quarter, *tables = lax.optimization_barrier((quarter, *tables))
+    both, one = call(
+        pack_kernel,
+        "pack",
+        [IN_VMEM] * 7,
+        [(shape(2, PACK, 128, kind=BF), IN_VMEM), (whole, IN_VMEM)],
+        [],
+        60,
+        3,
     )(*tables)
-    quarter, *tables = lax.optimization_barrier((quarter, *tables))
-    one = call(functools.partial(pack_kernel, 0), "pack_one", [IN_VMEM] * 7, [(whole, IN_VMEM)], [], 60, 2)(*tables)[0]
     quarter = send(quarter, to_x_by_core())
-    quarters = [quarter]
-    one, quarters[0] = lax.optimization_barrier((one, quarters[0]))
+    one, quarter = lax.optimization_barrier((one, quarter))
     across = send(one, to_x_by_core())
-    quarters += [send(quarters[0], to_first(a)) for a in PEERS]
+    quarters = [quarter] + [send(quarter, to_first(a)) for a in PEERS]
+    other = send(both, to_core())
     across, *quarters = lax.optimization_barrier((across, *quarters))
-    slots1 = (one, send(one, to_core()), across, send(across, to_core()))
+    slots1 = (both, other, across, send(across, to_core()))
     across = call(join_kernel, "join", [IN_VMEM] * 4, [(whole, IN_VMEM)], [], M5, 1)(*quarters)[0]
-    slots2 = (two, send(two, to_core()), across, send(across, to_core()))
+    slots2 = (both, other, across, send(across, to_core()))
     state1, look1, e1, act1, slope1, theta1 = call(
         first_kernel,
         "forward_one",
@@ -515,26 +584,37 @@
     *out1, own1 = cut((-LOW, TOP), [mine1b, mine1a], [*got1b, got1a], "cut_one")
     got1 = [send(part, to_first(a)) for part, a in zip(out1, PEERS)]
 
-    def pieces(own, got, before, dims):
+    def small(kernel, name, outs, *args, scratch=()):
         return call(
-            piece_kernel,
-            "pieces",
-            [IN_VMEM] * (4 + len(before)),
-            [(shape(2, *dims, PIECE, 128, kind=BF), IN_VMEM)] * 4,
-            [vmem(2, CHUNK, 128)],
+            kernel,
+            name,
+            [IN_VMEM] * len(args),
+            [(shape(*dims, 128, kind=BF), IN_VMEM) for dims in outs],
+            scratch,
             M5,
             1,
-        )(own, *got, *before)
-
-    *out, own = pieces(own1, got1, pieces(own2, got2, (), ()), (2,))
+        )(*args)
+
+    near2, far2 = small(fold_kernel, "fold", [(CHUNK,)] * 2, own2, *got2)
+    *out, own = small(
+        piece_kernel,
+        "pieces",
+        [(3, PIECE)] * 4,
+        own1,
+        *got1,
+        near2,
+        send(far2, to_x_by_core()),
+        scratch=[vmem(3, CHUNK, 128)],
+    )
     got = [send(part, to_second(b)) for part, b in zip(out, PEERS)]
-    done = plus(own, *got)
-    got = [send(done[1], to_x(1)), send(done[1], to_x(3)), send(done[0], to_x(2))]
-    done = plus(done[0], *got)
-    stack = jnp.stack([done] + [send(done, to_second(b)) for b in PEERS], axis=1)
+    near, far = small(sum_kernel, "sums", [(2, PIECE), (PIECE,)], own, *got)
+    got = [send(near, to_x(2)), send(far, to_x(3)), send(far, to_x(1))]
+    done = small(across_kernel, "across", [(2, PIECE)], near, *got)[0]
+    got = [send(done, to_second(b)) for b in FAR_FIRST]
+    stack = small(stack_kernel, "stack", [(4, PIECE)] * 2, done, *got)
     grads = ()
     for k in (1, 0):
-        stacks = [stack[k]] + [send(stack[k], to_first(a)) for a in PEERS]
+        stacks = [stack[k]] + [send(stack[k], to_first(a)) for a in FAR_FIRST]
         outs = (
             (560, 128), (128, 512), (512, 128), (128, 512), (512, 128), (512, 128), (128, 640),
         )

time: 126 us -> 124 us (0.984)
  waiting for transfers between devices: 48.5 us -> 44.9 us
  starting transfers between devices: 41.4 us -> 43.8 us
    ppermute x34, waiting for transfers between devices: 48.5 us -> 44.9 us  [send(): return lax.ppermute(values, ('dp', 'mp'), where)]
    ppermute x34, starting transfers between devices: 41.4 us -> 43.8 us  [send(): return lax.ppermute(values, ('dp', 'mp'), where)]
    pallas_call x4 -> x7, Pallas kernels: 6.25 us -> 6.13 us  [the longest x1 3.33 us: shards(): call(pack_kernel, 'pack', [IN_VMEM] * 7, [(shape(2, PACK, 128, kind=BF),...]
  transfers between devices with their start and end apart: 34 -> 34, of which waited for: 21 -> 19; matrix products, arithmetic and copies ran while one was open for 0% -> 0% of each run, Pallas kernels for 15% -> 16%
where the time goes in v4:
time: 124 us
  waiting for transfers between devices  44.9 us (36%)
  starting transfers between devices  43.8 us (35%)
  Pallas kernels  34 us (27%)
    ppermute x34, waiting for transfers between devices, send(): return lax.ppermute(values, ('dp', 'mp'), where)  44.9 us
    ppermute x34, starting transfers between devices, send(): return lax.ppermute(values, ('dp', 'mp'), where)  43.8 us
    pallas_call x1, Pallas kernels, shards(): call(second_kernel, 'block_two', [IN_VMEM] * 9, [(shape(336, ROWS), IN_VM...  10.5 us
    pallas_call x1, Pallas kernels, shards(): call(fourth_kernel, 'backward_one_layers', [IN_VMEM] * 10, [(shape(336, R...  4.16 us
    pallas_call x1, Pallas kernels, shards(): call(first_kernel, 'forward_one', [IN_VMEM] * 6, [(shape(336, ROWS), IN_V...  4.13 us
    pallas_call x1, Pallas kernels, shards(): call(third_kernel, 'backward_one_heads', [IN_VMEM] * 10, [(shape(512, ROW...  3.76 us
    pallas_call x1, Pallas kernels, shards(): call(pack_kernel, 'pack', [IN_VMEM] * 7, [(shape(2, PACK, 128, kind=BF),...  3.33 us
    pallas_call x2, Pallas kernels, shards(): call(functools.partial(unpack_kernel, k), 'unpack', [IN_VMEM] * 4 + [ANYW...  3.04 us
  transfers between devices with their start and end apart: 34, of which 19 were waited for; matrix products, arithmetic and copies ran while one was open for 0% of the time, Pallas kernels for 16%

profile of v4, /device:TPU:0, one launch (start us, length us, event | category | flops | bytes accessed | tf_op | source)
XLA Modules:
  0.0 123.8 jit_solution(6748187889380712248)
XLA Ops:
  0.6 1.7 %pack_quarter.1 = bf16[960,128]{1,0:T(8,128)(2,1)} custom-call(bf16[2,560,128]{2,1,0:T(8,128)(2,1)} %refs_0_.2, bf16[2,128,512]{2,1,0:T(8,128)(2,1)} %refs_1_.2, bf16[2,512,128]{2,1,0:T(8,128)(2,1)} %refs_2_.2, bf16[2,128,512]{2,1,0:T(8,128)(2,1)} %refs_3_.2, bf16[2,512,128]{2,1,0:T(8,128)(2,1)} %refs_4_.2, bf16[2,512,128]{2,1,0:T(8,128)(2,1)} %refs_5_.2, ...), custom_call_target="tpu_custom_call" | custom-call | flops 800000000 | bytes 1000000 | tf_op jit(solution)/shard_map/pack_quarter/pallas_call | solution.py:498
  2.3 1.7 %collective-permute-start.1 = (bf16[960,128]{1,0:T(8,128)(2,1)}, bf16[960,128]{1,0:T(8,128)(2,1)S(1)}, u32[]{:S(2)}, u32[]{:S(2)}) collective-permute-start(bf16[960,128]{1,0:T(8,128)(2,1)} %pack_quarter.1), channel_id=1, source_target_pairs={{0,2},{1,19},{4,6},{5,23},{8,10},{9,27},{12,14},{13,31},{2,0},{3,1... | collective-permute-start | bytes 737288 | tf_op jit(solution)/shard_map/ppermute | solution.py:57
  4.0 3.3 %pack.1 = (bf16[2,3840,128]{2,1,0:T(8,128)(2,1)}, bf16[3840,128]{1,0:T(8,128)(2,1)}) custom-call(bf16[2,560,128]{2,1,0:T(8,128)(2,1)} %refs_0_.2, bf16[2,128,512]{2,1,0:T(8,128)(2,1)} %refs_1_.2, bf16[2,512,128]{2,1,0:T(8,128)(2,1)} %refs_2_.2, bf16[2,128,512]{2,1,0:T(8,128)(2,1)} %refs_3_.2, bf16[2,512,128]{2,1,0:T(8,128)(2,1)} %refs_4_.2, ...), custom_call_target="tpu_custom_call" | custom-call | flops 2400000000 | bytes 3000000 | tf_op jit(solution)/shard_map/pack/pallas_call | solution.py:508
  7.3 1.5 %collective-permute-done.1.q0 = bf16[960,128]{1,0:T(8,128)(2,1)S(1)} collective-permute-done((bf16[960,128]{1,0:T(8,128)(2,1)}, bf16[960,128]{1,0:T(8,128)(2,1)S(1)}, u32[]{:S(2)}, u32[]{:S(2)}) %collective-permute-start.1) | collective-permute-done | bytes 245792 | tf_op jit(solution)/shard_map/ppermute | solution.py:57
  8.8 1.6 %collective-permute-start.2 = (bf16[3840,128]{1,0:T(8,128)(2,1)}, bf16[3840,128]{1,0:T(8,128)(2,1)S(1)}, u32[]{:S(2)}, u32[]{:S(2)}) collective-permute-start(bf16[3840,128]{1,0:T(8,128)(2,1)} %get-tuple-element.91), channel_id=1, source_target_pairs={{0,2},{1,19},{4,6},{5,23},{8,10},{9,27},{12,14},{13,31},{2,0},{3,1... | collective-permute-start | bytes 2949128 | tf_op jit(solution)/shard_map/ppermute | solution.py:57
  10.4 0.9 collective-permute-start
  11.3 1.6 %collective-permute-start.3 = (bf16[960,128]{1,0:T(8,128)(2,1)S(1)}, bf16[960,128]{1,0:T(8,128)(2,1)S(1)}, u32[]{:S(2)}, u32[]{:S(2)}) collective-permute-start(bf16[960,128]{1,0:T(8,128)(2,1)S(1)} %collective-permute-done.1.q0), channel_id=1, source_target_pairs={{0,32},{1,5},{4,36},{5,1},{8,40},{9,13},{12,44},{13,9},{2,34},{3,7... | collective-permute-start | bytes 737288 | tf_op jit(solution)/shard_map/ppermute | solution.py:57
  12.9 2.2 %collective-permute-start.4 = (bf16[960,128]{1,0:T(8,128)(2,1)S(1)}, bf16[960,128]{1,0:T(8,128)(2,1)S(1)}, u32[]{:S(2)}, u32[]{:S(2)}) collective-permute-start(bf16[960,128]{1,0:T(8,128)(2,1)S(1)} %collective-permute-done.1.q0), channel_id=1, source_target_pairs={{0,96},{1,13},{4,100},{5,9},{8,104},{9,5},{12,108},{13,1},{2,98},{... | collective-permute-start | bytes 737288 | tf_op jit(solution)/shard_map/ppermute | solution.py:57
  15.0 0.7 collective-permute-start.5
  15.8 1.7 %collective-permute-done.3.q1 = bf16[960,128]{1,0:T(8,128)(2,1)S(1)} collective-permute-done((bf16[960,128]{1,0:T(8,128)(2,1)S(1)}, bf16[960,128]{1,0:T(8,128)(2,1)S(1)}, u32[]{:S(2)}, u32[]{:S(2)}) %collective-permute-start.3) | collective-permute-done | bytes 245792 | tf_op jit(solution)/shard_map/ppermute | solution.py:57
  17.5 5.4 %collective-permute-done.4.q2 = bf16[960,128]{1,0:T(8,128)(2,1)S(1)} collective-permute-done((bf16[960,128]{1,0:T(8,128)(2,1)S(1)}, bf16[960,128]{1,0:T(8,128)(2,1)S(1)}, u32[]{:S(2)}, u32[]{:S(2)}) %collective-permute-start.4) | collective-permute-done | bytes 245792 | tf_op jit(solution)/shard_map/ppermute | solution.py:57
  22.9 0.2 collective-permute-done.2.s2
  23.1 0.1 join.1.s2
  23.2 0.8 collective-permute-start.7
  24.0 1.7 %collective-permute-done.6.s3 = bf16[3840,128]{1,0:T(8,128)(2,1)S(1)} collective-permute-done((bf16[3840,128]{1,0:T(8,128)(2,1)S(1)}, bf16[3840,128]{1,0:T(8,128)(2,1)S(1)}, u32[]{:S(2)}, u32[]{:S(2)}) %collective-permute-start.6) | collective-permute-done | bytes 983072 | tf_op jit(solution)/shard_map/ppermute | solution.py:57
  25.7 4.1 %forward_one.1 = (f32[336,768]{1,0:T(8,128)S(1)}, f32[48,768]{1,0:T(8,128)S(1)}, bf16[560,768]{1,0:T(8,128)(2,1)S(1)}, bf16[4,512,768]{2,1,0:T(8,128)(2,1)S(1)},...) custom-call(s32[1,768]{1,0:T(1,128)S(1)} %broadcast_in_dim.3.label, bf16[336,768]{1,0:T(8,128)(2,1)S(1)} %bitcast.6, ...), custom_call_target="tpu_custom_call" | custom-call | flops 4800000000 | bytes 6000000 | tf_op jit(solution)/shard_map/forward_one/pallas_call | solution.py:526
  29.9 10.5 %block_two.1 = (f32[336,768]{1,0:T(8,128)}, f32[48,768]{1,0:T(8,128)}, f32[336,768]{1,0:T(8,128)S(1)}, bf16[2,3840,128]{2,1,0:T(8,128)(2,1)S(1)}, bf16[2,3840,128]{2,1,0:T(8,128)(2,1)S(1)}) custom-call(s32[1,768]{1,0:T(1,128)S(1)} %broadcast_in_dim.3.label, f32[336,768]{1,0:T(8,128)S(1)} %get-tuple-element.94.state_in, ...), custom_call_target="tpu_custom_call" | custom-call | flops 11200000000 | bytes 14000000 | tf_op jit(solution)/shard_map/block_two/pallas_call | solution.py:536
  40.4 0.2 collective-permute-start.9
  40.6 3.8 %backward_one_heads.1 = (bf16[512,768]{1,0:T(8,128)(2,1)S(1)}, bf16[2,2256,128]{2,1,0:T(8,128)(2,1)S(1)}, bf16[2,2256,128]{2,1,0:T(8,128)(2,1)S(1)}) custom-call(s32[1,768]{1,0:T(1,128)S(1)} %broadcast_in_dim.3.label, f32[336,768]{1,0:T(8,128)S(1)} %get-tuple-element.102.g_in, bf16[48,768]{1,0:T(8,128)(2,1)S(1)} %bitcast.9, ...), custom_call_target="tpu_custom_call" | custom-call | flops 4800000000 | bytes 6000000 | tf_op jit(solution)/shard_map/backward_one_heads/pallas_call | solution.py:547
  44.4 0.5 collective-permute-start.8
  44.8 1.1 cut_two.1
  46.0 3.5 %collective-permute-start.10 = (bf16[2,960,128]{2,1,0:T(8,128)(2,1)S(1)}, bf16[2,960,128]{2,1,0:T(8,128)(2,1)S(1)}, u32[]{:S(2)}, u32[]{:S(2)}) collective-permute-start(bf16[2,960,128]{2,1,0:T(8,128)(2,1)S(1)} %get-tuple-element.112), channel_id=1, source_target_pairs={{0,64},{1,9},{4,68},{5,13},{8,72},{9,1},{12,76},{13,5},{2,66},{3,1... | collective-permute-start | bytes 1474568 | tf_op jit(solution)/shard_map/ppermute | solution.py:57
  49.5 4.2 %backward_one_layers.1 = (f32[336,768]{1,0:T(8,128)}, bf16[2,1584,128]{2,1,0:T(8,128)(2,1)S(1)}, bf16[1584,128]{1,0:T(8,128)(2,1)S(1)}, bf16[1584,128]{1,0:T(8,128)(2,1)S(1)}) custom-call(s32[1,768]{1,0:T(1,128)S(1)} %broadcast_in_dim.3.label, f32[336,768]{1,0:T(8,128)S(1)} %get-tuple-element.102.g_in, bf16[512,768]{1,0:T(8,128)(2,1)S(1)} %get-tuple-element.113.d_in, ...), custom_call_target="tpu_custom_call" | custom-call | flops 4800000000 | bytes 6000000 | tf_op jit(solution)/shard_map/backward_one_layers/pallas_call | solution.py:572
  53.6 0.4 collective-permute-start.11
  54.1 0.1 collective-permute-start.12
  54.1 1.5 %collective-permute-start.16 = (bf16[2,960,128]{2,1,0:T(8,128)(2,1)S(1)}, bf16[2,960,128]{2,1,0:T(8,128)(2,1)S(1)}, u32[]{:S(2)}, u32[]{:S(2)}) collective-permute-start(bf16[2,960,128]{2,1,0:T(8,128)(2,1)S(1)} %get-tuple-element.110), channel_id=1, source_target_pairs={{0,32},{1,5},{4,36},{5,1},{8,40},{9,13},{12,44},{13,9},{2,34},{3,7... | collective-permute-start | bytes 1474568 | tf_op jit(solution)/shard_map/ppermute | solution.py:57
  55.7 2.2 %collective-permute-start.17 = (bf16[2,960,128]{2,1,0:T(8,128)(2,1)S(1)}, bf16[2,960,128]{2,1,0:T(8,128)(2,1)S(1)}, u32[]{:S(2)}, u32[]{:S(2)}) collective-permute-start(bf16[2,960,128]{2,1,0:T(8,128)(2,1)S(1)} %get-tuple-element.111), channel_id=1, source_target_pairs={{0,96},{1,13},{4,100},{5,9},{8,104},{9,5},{12,108},{13,1},{2,98},{... | collective-permute-start | bytes 1474568 | tf_op jit(solution)/shard_map/ppermute | solution.py:57
  57.9 1.1 cut_one.1
  59.0 0.8 collective-permute-start.13
  59.8 1.7 %collective-permute-start.14 = (bf16[2,960,128]{2,1,0:T(8,128)(2,1)S(1)}, bf16[2,960,128]{2,1,0:T(8,128)(2,1)S(1)}, u32[]{:S(2)}, u32[]{:S(2)}) collective-permute-start(bf16[2,960,128]{2,1,0:T(8,128)(2,1)S(1)} %get-tuple-element.124), channel_id=1, source_target_pairs={{0,96},{1,13},{4,100},{5,9},{8,104},{9,5},{12,108},{13,1},{2,98},{... | collective-permute-start | bytes 1474568 | tf_op jit(solution)/shard_map/ppermute | solution.py:57
  61.5 1.7 %collective-permute-start.15 = (bf16[2,960,128]{2,1,0:T(8,128)(2,1)S(1)}, bf16[2,960,128]{2,1,0:T(8,128)(2,1)S(1)}, u32[]{:S(2)}, u32[]{:S(2)}) collective-permute-start(bf16[2,960,128]{2,1,0:T(8,128)(2,1)S(1)} %get-tuple-element.125), channel_id=1, source_target_pairs={{0,64},{1,9},{4,68},{5,13},{8,72},{9,1},{12,76},{13,5},{2,66},{3,1... | collective-permute-start | bytes 1474568 | tf_op jit(solution)/shard_map/ppermute | solution.py:57
  63.2 2.5 %collective-permute-done.17.b = bf16[2,960,128]{2,1,0:T(8,128)(2,1)S(1)} collective-permute-done((bf16[2,960,128]{2,1,0:T(8,128)(2,1)S(1)}, bf16[2,960,128]{2,1,0:T(8,128)(2,1)S(1)}, u32[]{:S(2)}, u32[]{:S(2)}) %collective-permute-start.17) | collective-permute-done | bytes 491552 | tf_op jit(solution)/shard_map/ppermute | solution.py:57
  65.7 0.2 fold.1
  65.9 1.6 %collective-permute-start.18 = (bf16[960,128]{1,0:T(8,128)(2,1)S(1)}, bf16[960,128]{1,0:T(8,128)(2,1)S(1)}, u32[]{:S(2)}, u32[]{:S(2)}) collective-permute-start(bf16[960,128]{1,0:T(8,128)(2,1)S(1)} %get-tuple-element.129), channel_id=1, source_target_pairs={{0,2},{1,19},{4,6},{5,23},{8,10},{9,27},{12,14},{13,31},{2,0},{3,1... | collective-permute-start | bytes 737288 | tf_op jit(solution)/shard_map/ppermute | solution.py:57
  67.5 4.7 %collective-permute-done.18.came = bf16[960,128]{1,0:T(8,128)(2,1)S(1)} collective-permute-done((bf16[960,128]{1,0:T(8,128)(2,1)S(1)}, bf16[960,128]{1,0:T(8,128)(2,1)S(1)}, u32[]{:S(2)}, u32[]{:S(2)}) %collective-permute-start.18) | collective-permute-done | bytes 245792 | tf_op jit(solution)/shard_map/ppermute | solution.py:57
  72.2 4.0 %collective-permute-done.14.b = bf16[2,960,128]{2,1,0:T(8,128)(2,1)S(1)} collective-permute-done((bf16[2,960,128]{2,1,0:T(8,128)(2,1)S(1)}, bf16[2,960,128]{2,1,0:T(8,128)(2,1)S(1)}, u32[]{:S(2)}, u32[]{:S(2)}) %collective-permute-start.14) | collective-permute-done | bytes 491552 | tf_op jit(solution)/shard_map/ppermute | solution.py:57
  76.2 0.7 pieces.1
  76.9 1.2 collective-permute-start.19
  78.1 2.5 %collective-permute-start.20 = (bf16[3,240,128]{2,1,0:T(8,128)(2,1)S(1)}, bf16[3,240,128]{2,1,0:T(8,128)(2,1)S(1)}, u32[]{:S(2)}, u32[]{:S(2)}) collective-permute-start(bf16[3,240,128]{2,1,0:T(8,128)(2,1)S(1)} %get-tuple-element.132), channel_id=1, source_target_pairs={{0,12},{1,97},{4,8},{5,101},{8,4},{9,105},{12,0},{13,109},{2,14},{... | collective-permute-start | bytes 552968 | tf_op jit(solution)/shard_map/ppermute | solution.py:57
  80.7 1.1 collective-permute-start.21
  81.7 0.8 collective-permute-done.19.a
  82.5 3.2 %collective-permute-done.20.b = bf16[3,240,128]{2,1,0:T(8,128)(2,1)S(1)} collective-permute-done((bf16[3,240,128]{2,1,0:T(8,128)(2,1)S(1)}, bf16[3,240,128]{2,1,0:T(8,128)(2,1)S(1)}, u32[]{:S(2)}, u32[]{:S(2)}) %collective-permute-start.20) | collective-permute-done | bytes 184352 | tf_op jit(solution)/shard_map/ppermute | solution.py:57
  85.7 2.0 %collective-permute-done.21.c = bf16[3,240,128]{2,1,0:T(8,128)(2,1)S(1)} collective-permute-done((bf16[3,240,128]{2,1,0:T(8,128)(2,1)S(1)}, bf16[3,240,128]{2,1,0:T(8,128)(2,1)S(1)}, u32[]{:S(2)}, u32[]{:S(2)}) %collective-permute-start.21) | collective-permute-done | bytes 184352 | tf_op jit(solution)/shard_map/ppermute | solution.py:57
  87.7 0.1 sums.1
  87.8 3.1 %collective-permute-start.22 = (bf16[2,240,128]{2,1,0:T(8,128)(2,1)S(1)}, bf16[2,240,128]{2,1,0:T(8,128)(2,1)S(1)}, u32[]{:S(2)}, u32[]{:S(2)}) collective-permute-start(bf16[2,240,128]{2,1,0:T(8,128)(2,1)S(1)} %get-tuple-element.134.near), channel_id=1, source_target_pairs={{0,16},{1,17},{4,20},{5,21},{8,24},{9,25},{12,28},{13,29},{2,18},{... | collective-permute-start | bytes 368648 | tf_op jit(solution)/shard_map/ppermute | solution.py:57
  90.9 1.1 collective-permute-start.23
  92.1 4.3 %collective-permute-done.23.b = bf16[240,128]{1,0:T(8,128)(2,1)S(1)} collective-permute-done((bf16[240,128]{1,0:T(8,128)(2,1)S(1)}, bf16[240,128]{1,0:T(8,128)(2,1)S(1)}, u32[]{:S(2)}, u32[]{:S(2)}) %collective-permute-start.23) | collective-permute-done | bytes 61472 | tf_op jit(solution)/shard_map/ppermute | solution.py:57
  96.4 1.6 %collective-permute-start.25 = (bf16[2,240,128]{2,1,0:T(8,128)(2,1)S(1)}, bf16[2,240,128]{2,1,0:T(8,128)(2,1)S(1)}, u32[]{:S(2)}, u32[]{:S(2)}) collective-permute-start(bf16[2,240,128]{2,1,0:T(8,128)(2,1)S(1)} %across.1.refs_0_), channel_id=1, source_target_pairs={{0,8},{1,65},{4,12},{5,69},{8,0},{9,73},{12,4},{13,77},{2,10},{3,6... | collective-permute-start | bytes 368648 | tf_op jit(solution)/shard_map/ppermute | solution.py:57
  98.0 2.2 %collective-permute-start.26 = (bf16[2,240,128]{2,1,0:T(8,128)(2,1)S(1)}, bf16[2,240,128]{2,1,0:T(8,128)(2,1)S(1)}, u32[]{:S(2)}, u32[]{:S(2)}) collective-permute-start(bf16[2,240,128]{2,1,0:T(8,128)(2,1)S(1)} %across.1.refs_0_), channel_id=1, source_target_pairs={{0,12},{1,97},{4,8},{5,101},{8,4},{9,105},{12,0},{13,109},{2,14},{... | collective-permute-start | bytes 368648 | tf_op jit(solution)/shard_map/ppermute | solution.py:57
  100.2 2.7 %collective-permute-done.25.refs_1_ = bf16[2,240,128]{2,1,0:T(8,128)(2,1)S(1)} collective-permute-done((bf16[2,240,128]{2,1,0:T(8,128)(2,1)S(1)}, bf16[2,240,128]{2,1,0:T(8,128)(2,1)S(1)}, u32[]{:S(2)}, u32[]{:S(2)}) %collective-permute-start.25) | collective-permute-done | bytes 122912 | tf_op jit(solution)/shard_map/ppermute | solution.py:57
  102.9 1.3 %collective-permute-done.26.refs_2_ = bf16[2,240,128]{2,1,0:T(8,128)(2,1)S(1)} collective-permute-done((bf16[2,240,128]{2,1,0:T(8,128)(2,1)S(1)}, bf16[2,240,128]{2,1,0:T(8,128)(2,1)S(1)}, u32[]{:S(2)}, u32[]{:S(2)}) %collective-permute-start.26) | collective-permute-done | bytes 122912 | tf_op jit(solution)/shard_map/ppermute | solution.py:57
  104.2 2.2 %collective-permute-done.27.refs_3_ = bf16[2,240,128]{2,1,0:T(8,128)(2,1)S(1)} collective-permute-done((bf16[2,240,128]{2,1,0:T(8,128)(2,1)S(1)}, bf16[2,240,128]{2,1,0:T(8,128)(2,1)S(1)}, u32[]{:S(2)}, u32[]{:S(2)}) %collective-permute-start.27) | collective-permute-done | bytes 122912 | tf_op jit(solution)/shard_map/ppermute | solution.py:57
  106.4 0.9 collective-permute-start.31
  107.3 1.9 %collective-permute-start.32 = (bf16[4,240,128]{2,1,0:T(8,128)(2,1)S(1)}, bf16[4,240,128]{2,1,0:T(8,128)(2,1)S(1)}, u32[]{:S(2)}, u32[]{:S(2)}) collective-permute-start(bf16[4,240,128]{2,1,0:T(8,128)(2,1)S(1)} %get-tuple-element.137.refs_0_), channel_id=1, source_target_pairs={{0,96},{1,13},{4,100},{5,9},{8,104},{9,5},{12,108},{13,1},{2,98},{... | collective-permute-start | bytes 737288 | tf_op jit(solution)/shard_map/ppermute | solution.py:57
  109.2 0.8 collective-permute-start.33
  110.0 2.0 %collective-permute-start.28 = (bf16[4,240,128]{2,1,0:T(8,128)(2,1)S(1)}, bf16[4,240,128]{2,1,0:T(8,128)(2,1)S(1)}, u32[]{:S(2)}, u32[]{:S(2)}) collective-permute-start(bf16[4,240,128]{2,1,0:T(8,128)(2,1)S(1)} %get-tuple-element.136.refs_0_), channel_id=1, source_target_pairs={{0,64},{1,9},{4,68},{5,13},{8,72},{9,1},{12,76},{13,5},{2,66},{3,1... | collective-permute-start | bytes 737288 | tf_op jit(solution)/shard_map/ppermute | solution.py:57
  112.0 1.9 %collective-permute-start.29 = (bf16[4,240,128]{2,1,0:T(8,128)(2,1)S(1)}, bf16[4,240,128]{2,1,0:T(8,128)(2,1)S(1)}, u32[]{:S(2)}, u32[]{:S(2)}) collective-permute-start(bf16[4,240,128]{2,1,0:T(8,128)(2,1)S(1)} %get-tuple-element.136.refs_0_), channel_id=1, source_target_pairs={{0,96},{1,13},{4,100},{5,9},{8,104},{9,5},{12,108},{13,1},{2,98},{... | collective-permute-start | bytes 737288 | tf_op jit(solution)/shard_map/ppermute | solution.py:57
  113.9 0.4 collective-permute-done.31.refs_1_
  114.3 0.0 collective-permute-start.30
  114.3 2.5 %collective-permute-done.32.refs_2_ = bf16[4,240,128]{2,1,0:T(8,128)(2,1)S(1)} collective-permute-done((bf16[4,240,128]{2,1,0:T(8,128)(2,1)S(1)}, bf16[4,240,128]{2,1,0:T(8,128)(2,1)S(1)}, u32[]{:S(2)}, u32[]{:S(2)}) %collective-permute-start.32) | collective-permute-done | bytes 245792 | tf_op jit(solution)/shard_map/ppermute | solution.py:57
  116.8 1.5 %unpack.2 = (f32[2,560,128]{2,1,0:T(8,128)}, f32[2,128,512]{2,1,0:T(8,128)}, f32[2,512,128]{2,1,0:T(8,128)}, f32[2,128,512]{2,1,0:T(8,128)}, f32[2,512,128]{2,1,...) custom-call(bf16[4,240,128]{2,1,0:T(8,128)(2,1)S(1)} %get-tuple-element.137.refs_0_, ...), custom_call_target="tpu_custom_call" | custom-call | flops 1600000000 | bytes 2000000 | tf_op jit(solution)/shard_map/unpack/pallas_call | solution.py:621
  118.4 1.3 %collective-permute-done.28.refs_1_ = bf16[4,240,128]{2,1,0:T(8,128)(2,1)S(1)} collective-permute-done((bf16[4,240,128]{2,1,0:T(8,128)(2,1)S(1)}, bf16[4,240,128]{2,1,0:T(8,128)(2,1)S(1)}, u32[]{:S(2)}, u32[]{:S(2)}) %collective-permute-start.28) | collective-permute-done | bytes 245792 | tf_op jit(solution)/shard_map/ppermute | solution.py:57
  119.6 2.5 %collective-permute-done.29.refs_2_ = bf16[4,240,128]{2,1,0:T(8,128)(2,1)S(1)} collective-permute-done((bf16[4,240,128]{2,1,0:T(8,128)(2,1)S(1)}, bf16[4,240,128]{2,1,0:T(8,128)(2,1)S(1)}, u32[]{:S(2)}, u32[]{:S(2)}) %collective-permute-start.29) | collective-permute-done | bytes 245792 | tf_op jit(solution)/shard_map/ppermute | solution.py:57
  122.1 1.5 %unpack.3 = (f32[2,560,128]{2,1,0:T(8,128)}, f32[2,128,512]{2,1,0:T(8,128)}, f32[2,512,128]{2,1,0:T(8,128)}, f32[2,128,512]{2,1,0:T(8,128)}, f32[2,512,128]{2,1,...) custom-call(bf16[4,240,128]{2,1,0:T(8,128)(2,1)S(1)} %get-tuple-elem, ...), custom_call_target="tpu_custom_call", output_to_operand_aliasing={{0}: (4, {}), {1}: (5, {}), {2}: (6, {}), {3}: (7, {}), {4}... | custom-call | flops 1600000000 | bytes 2000000 | tf_op jit(solution)/shard_map/unpack/pallas_call | solution.py:621
  (31 shorter events, 0.1 us)
Async XLA Ops:
  2.3 6.5 %collective-permute-start.1 = (bf16[960,128]{1,0:T(8,128)(2,1)}, bf16[960,128]{1,0:T(8,128)(2,1)S(1)}, u32[]{:S(2)}, u32[]{:S(2)}) collective-permute-start(bf16[960,128]{1,0:T(8,128)(2,1)} %pack_quarter.1), channel_id=1, source_target_pairs={{0,2},{1,19},{4,6},{5,23},{8,10},{9,27},{12,14},{13,31},{2,0},{3,1... | collective-permute-start | bytes 737288 | tf_op jit(solution)/shard_map/ppermute | solution.py:57
  7.3 16.7 %copy-start.4 = (s32[768]{0:T(1024)S(1)}, s32[768]{0:T(1024)}, u32[]{:S(2)}) copy-start(s32[768]{0:T(1024)} %param.12) | copy-start | bytes 9220
  7.3 18.4 %copy-start = (bf16[2,3840,128]{2,1,0:T(8,128)(2,1)S(1)}, bf16[2,3840,128]{2,1,0:T(8,128)(2,1)}, u32[]{:S(2)}) copy-start(bf16[2,3840,128]{2,1,0:T(8,128)(2,1)} %get-tuple-element.88.s0) | copy-start | bytes 5898244
  7.3 18.4 %copy-start.1 = (bf16[768,336]{0,1:T(8,128)(2,1)S(1)}, bf16[768,336]{0,1:T(8,128)(2,1)}, u32[]{:S(2)}) copy-start(bf16[768,336]{0,1:T(8,128)(2,1)} %param.11) | copy-start | bytes 1548292
  8.8 14.3 %collective-permute-start.2 = (bf16[3840,128]{1,0:T(8,128)(2,1)}, bf16[3840,128]{1,0:T(8,128)(2,1)S(1)}, u32[]{:S(2)}, u32[]{:S(2)}) collective-permute-start(bf16[3840,128]{1,0:T(8,128)(2,1)} %get-tuple-element.91), channel_id=1, source_target_pairs={{0,2},{1,19},{4,6},{5,23},{8,10},{9,27},{12,14},{13,31},{2,0},{3,1... | collective-permute-start | bytes 2949128 | tf_op jit(solution)/shard_map/ppermute | solution.py:57
  10.4 13.6 %collective-permute-start = (bf16[2,3840,128]{2,1,0:T(8,128)(2,1)}, bf16[2,3840,128]{2,1,0:T(8,128)(2,1)S(1)}, u32[]{:S(2)}, u32[]{:S(2)}) collective-permute-start(bf16[2,3840,128]{2,1,0:T(8,128)(2,1)} %get-tuple-element.88.s0), channel_id=1, source_target_pairs={{0,1},{1,0},{4,5},{5,4},{8,9},{9,8},{12,13},{13,12},{2,3},{3,2},{6... | collective-permute-start | bytes 5898248 | tf_op jit(solution)/shard_map/ppermute | solution.py:57
  11.3 6.2 %collective-permute-start.3 = (bf16[960,128]{1,0:T(8,128)(2,1)S(1)}, bf16[960,128]{1,0:T(8,128)(2,1)S(1)}, u32[]{:S(2)}, u32[]{:S(2)}) collective-permute-start(bf16[960,128]{1,0:T(8,128)(2,1)S(1)} %collective-permute-done.1.q0), channel_id=1, source_target_pairs={{0,32},{1,5},{4,36},{5,1},{8,40},{9,13},{12,44},{13,9},{2,34},{3,7... | collective-permute-start | bytes 737288 | tf_op jit(solution)/shard_map/ppermute | solution.py:57
  12.9 10.0 %collective-permute-start.4 = (bf16[960,128]{1,0:T(8,128)(2,1)S(1)}, bf16[960,128]{1,0:T(8,128)(2,1)S(1)}, u32[]{:S(2)}, u32[]{:S(2)}) collective-permute-start(bf16[960,128]{1,0:T(8,128)(2,1)S(1)} %collective-permute-done.1.q0), channel_id=1, source_target_pairs={{0,96},{1,13},{4,100},{5,9},{8,104},{9,5},{12,108},{13,1},{2,98},{... | collective-permute-start | bytes 737288 | tf_op jit(solution)/shard_map/ppermute | solution.py:57
  15.0 7.9 %collective-permute-start.5 = (bf16[960,128]{1,0:T(8,128)(2,1)S(1)}, bf16[960,128]{1,0:T(8,128)(2,1)S(1)}, u32[]{:S(2)}, u32[]{:S(2)}) collective-permute-start(bf16[960,128]{1,0:T(8,128)(2,1)S(1)} %collective-permute-done.1.q0), channel_id=1, source_target_pairs={{0,64},{1,9},{4,68},{5,13},{8,72},{9,1},{12,76},{13,5},{2,66},{3,1... | collective-permute-start | bytes 737288 | tf_op jit(solution)/shard_map/ppermute | solution.py:57
  23.1 2.6 %collective-permute-start.6 = (bf16[3840,128]{1,0:T(8,128)(2,1)S(1)}, bf16[3840,128]{1,0:T(8,128)(2,1)S(1)}, u32[]{:S(2)}, u32[]{:S(2)}) collective-permute-start(bf16[3840,128]{1,0:T(8,128)(2,1)S(1)} %collective-permute-done.2.s2), channel_id=1, source_target_pairs={{0,1},{1,0},{4,5},{5,4},{8,9},{9,8},{12,13},{13,12},{2,3},{3,2},{6... | collective-permute-start | bytes 2949128 | tf_op jit(solution)/shard_map/ppermute | solution.py:57
  23.2 6.6 %collective-permute-start.7 = (bf16[3840,128]{1,0:T(8,128)(2,1)S(1)}, bf16[3840,128]{1,0:T(8,128)(2,1)S(1)}, u32[]{:S(2)}, u32[]{:S(2)}) collective-permute-start(bf16[3840,128]{1,0:T(8,128)(2,1)S(1)} %join.1.s2), channel_id=1, source_target_pairs={{0,1},{1,0},{4,5},{5,4},{8,9},{9,8},{12,13},{13,12},{2,3},{3,2},{6... | collective-permute-start | bytes 2949128 | tf_op jit(solution)/shard_map/ppermute | solution.py:57
  25.7 4.2 %copy-start.2 = (bf16[768,336]{0,1:T(8,128)(2,1)S(1)}, bf16[768,336]{0,1:T(8,128)(2,1)}, u32[]{:S(2)}) copy-start(bf16[768,336]{0,1:T(8,128)(2,1)} %param.21) | copy-start | bytes 1548292
  25.7 4.2 %copy-start.3 = (bf16[768,48]{0,1:T(8,128)(2,1)S(1)}, bf16[768,48]{0,1:T(8,128)(2,1)}, u32[]{:S(2)}) copy-start(bf16[768,48]{0,1:T(8,128)(2,1)} %param.20) | copy-start | bytes 221188
  40.4 4.4 %collective-permute-start.9 = (bf16[2,3840,128]{2,1,0:T(8,128)(2,1)S(1)}, bf16[2,3840,128]{2,1,0:T(8,128)(2,1)S(1)}, u32[]{:S(2)}, u32[]{:S(2)}) collective-permute-start(bf16[2,3840,128]{2,1,0:T(8,128)(2,1)S(1)} %get-tuple-element.109), channel_id=1, source_target_pairs={{0,1},{1,0},{4,5},{5,4},{8,9},{9,8},{12,13},{13,12},{2,3},{3,2},{6... | collective-permute-start | bytes 5898248 | tf_op jit(solution)/shard_map/ppermute | solution.py:57
  44.4 5.1 %collective-permute-start.8 = (bf16[2,2256,128]{2,1,0:T(8,128)(2,1)S(1)}, bf16[2,2256,128]{2,1,0:T(8,128)(2,1)S(1)}, u32[]{:S(2)}, u32[]{:S(2)}) collective-permute-start(bf16[2,2256,128]{2,1,0:T(8,128)(2,1)S(1)} %get-tuple-element.107), channel_id=1, source_target_pairs={{0,1},{1,0},{4,5},{5,4},{8,9},{9,8},{12,13},{13,12},{2,3},{3,2},{6... | collective-permute-start | bytes 3465224 | tf_op jit(solution)/shard_map/ppermute | solution.py:57
  46.0 11.9 %collective-permute-start.10 = (bf16[2,960,128]{2,1,0:T(8,128)(2,1)S(1)}, bf16[2,960,128]{2,1,0:T(8,128)(2,1)S(1)}, u32[]{:S(2)}, u32[]{:S(2)}) collective-permute-start(bf16[2,960,128]{2,1,0:T(8,128)(2,1)S(1)} %get-tuple-element.112), channel_id=1, source_target_pairs={{0,64},{1,9},{4,68},{5,13},{8,72},{9,1},{12,76},{13,5},{2,66},{3,1... | collective-permute-start | bytes 1474568 | tf_op jit(solution)/shard_map/ppermute | solution.py:57
  53.6 4.3 %collective-permute-start.11 = (bf16[1584,128]{1,0:T(8,128)(2,1)S(1)}, bf16[1584,128]{1,0:T(8,128)(2,1)S(1)}, u32[]{:S(2)}, u32[]{:S(2)}) collective-permute-start(bf16[1584,128]{1,0:T(8,128)(2,1)S(1)} %get-tuple-element.119), channel_id=1, source_target_pairs={{0,1},{1,0},{4,5},{5,4},{8,9},{9,8},{12,13},{13,12},{2,3},{3,2},{6... | collective-permute-start | bytes 1216520 | tf_op jit(solution)/shard_map/ppermute | solution.py:57
  54.1 3.9 %collective-permute-start.12 = (bf16[1584,128]{1,0:T(8,128)(2,1)S(1)}, bf16[1584,128]{1,0:T(8,128)(2,1)S(1)}, u32[]{:S(2)}, u32[]{:S(2)}) collective-permute-start(bf16[1584,128]{1,0:T(8,128)(2,1)S(1)} %get-tuple-element.120), channel_id=1, source_target_pairs={{0,1},{1,0},{4,5},{5,4},{8,9},{9,8},{12,13},{13,12},{2,3},{3,2},{6... | collective-permute-start | bytes 1216520 | tf_op jit(solution)/shard_map/ppermute | solution.py:57
  54.1 9.1 %collective-permute-start.16 = (bf16[2,960,128]{2,1,0:T(8,128)(2,1)S(1)}, bf16[2,960,128]{2,1,0:T(8,128)(2,1)S(1)}, u32[]{:S(2)}, u32[]{:S(2)}) collective-permute-start(bf16[2,960,128]{2,1,0:T(8,128)(2,1)S(1)} %get-tuple-element.110), channel_id=1, source_target_pairs={{0,32},{1,5},{4,36},{5,1},{8,40},{9,13},{12,44},{13,9},{2,34},{3,7... | collective-permute-start | bytes 1474568 | tf_op jit(solution)/shard_map/ppermute | solution.py:57
  55.7 10.0 %collective-permute-start.17 = (bf16[2,960,128]{2,1,0:T(8,128)(2,1)S(1)}, bf16[2,960,128]{2,1,0:T(8,128)(2,1)S(1)}, u32[]{:S(2)}, u32[]{:S(2)}) collective-permute-start(bf16[2,960,128]{2,1,0:T(8,128)(2,1)S(1)} %get-tuple-element.111), channel_id=1, source_target_pairs={{0,96},{1,13},{4,100},{5,9},{8,104},{9,5},{12,108},{13,1},{2,98},{... | collective-permute-start | bytes 1474568 | tf_op jit(solution)/shard_map/ppermute | solution.py:57
  59.0 13.2 %collective-permute-start.13 = (bf16[2,960,128]{2,1,0:T(8,128)(2,1)S(1)}, bf16[2,960,128]{2,1,0:T(8,128)(2,1)S(1)}, u32[]{:S(2)}, u32[]{:S(2)}) collective-permute-start(bf16[2,960,128]{2,1,0:T(8,128)(2,1)S(1)} %get-tuple-element.123), channel_id=1, source_target_pairs={{0,32},{1,5},{4,36},{5,1},{8,40},{9,13},{12,44},{13,9},{2,34},{3,7... | collective-permute-start | bytes 1474568 | tf_op jit(solution)/shard_map/ppermute | solution.py:57
  59.8 16.4 %collective-permute-start.14 = (bf16[2,960,128]{2,1,0:T(8,128)(2,1)S(1)}, bf16[2,960,128]{2,1,0:T(8,128)(2,1)S(1)}, u32[]{:S(2)}, u32[]{:S(2)}) collective-permute-start(bf16[2,960,128]{2,1,0:T(8,128)(2,1)S(1)} %get-tuple-element.124), channel_id=1, source_target_pairs={{0,96},{1,13},{4,100},{5,9},{8,104},{9,5},{12,108},{13,1},{2,98},{... | collective-permute-start | bytes 1474568 | tf_op jit(solution)/shard_map/ppermute | solution.py:57
  61.5 14.7 %collective-permute-start.15 = (bf16[2,960,128]{2,1,0:T(8,128)(2,1)S(1)}, bf16[2,960,128]{2,1,0:T(8,128)(2,1)S(1)}, u32[]{:S(2)}, u32[]{:S(2)}) collective-permute-start(bf16[2,960,128]{2,1,0:T(8,128)(2,1)S(1)} %get-tuple-element.125), channel_id=1, source_target_pairs={{0,64},{1,9},{4,68},{5,13},{8,72},{9,1},{12,76},{13,5},{2,66},{3,1... | collective-permute-start | bytes 1474568 | tf_op jit(solution)/shard_map/ppermute | solution.py:57
  65.9 6.3 %collective-permute-start.18 = (bf16[960,128]{1,0:T(8,128)(2,1)S(1)}, bf16[960,128]{1,0:T(8,128)(2,1)S(1)}, u32[]{:S(2)}, u32[]{:S(2)}) collective-permute-start(bf16[960,128]{1,0:T(8,128)(2,1)S(1)} %get-tuple-element.129), channel_id=1, source_target_pairs={{0,2},{1,19},{4,6},{5,23},{8,10},{9,27},{12,14},{13,31},{2,0},{3,1... | collective-permute-start | bytes 737288 | tf_op jit(solution)/shard_map/ppermute | solution.py:57
  76.9 5.6 %collective-permute-start.19 = (bf16[3,240,128]{2,1,0:T(8,128)(2,1)S(1)}, bf16[3,240,128]{2,1,0:T(8,128)(2,1)S(1)}, u32[]{:S(2)}, u32[]{:S(2)}) collective-permute-start(bf16[3,240,128]{2,1,0:T(8,128)(2,1)S(1)} %get-tuple-element.131), channel_id=1, source_target_pairs={{0,4},{1,33},{4,0},{5,37},{8,12},{9,41},{12,8},{13,45},{2,6},{3,35... | collective-permute-start | bytes 552968 | tf_op jit(solution)/shard_map/ppermute | solution.py:57
  78.1 7.6 %collective-permute-start.20 = (bf16[3,240,128]{2,1,0:T(8,128)(2,1)S(1)}, bf16[3,240,128]{2,1,0:T(8,128)(2,1)S(1)}, u32[]{:S(2)}, u32[]{:S(2)}) collective-permute-start(bf16[3,240,128]{2,1,0:T(8,128)(2,1)S(1)} %get-tuple-element.132), channel_id=1, source_target_pairs={{0,12},{1,97},{4,8},{5,101},{8,4},{9,105},{12,0},{13,109},{2,14},{... | collective-permute-start | bytes 552968 | tf_op jit(solution)/shard_map/ppermute | solution.py:57
  80.7 7.0 %collective-permute-start.21 = (bf16[3,240,128]{2,1,0:T(8,128)(2,1)S(1)}, bf16[3,240,128]{2,1,0:T(8,128)(2,1)S(1)}, u32[]{:S(2)}, u32[]{:S(2)}) collective-permute-start(bf16[3,240,128]{2,1,0:T(8,128)(2,1)S(1)} %get-tuple-element.133), channel_id=1, source_target_pairs={{0,8},{1,65},{4,12},{5,69},{8,0},{9,73},{12,4},{13,77},{2,10},{3,6... | collective-permute-start | bytes 552968 | tf_op jit(solution)/shard_map/ppermute | solution.py:57
  87.8 8.5 %collective-permute-start.22 = (bf16[2,240,128]{2,1,0:T(8,128)(2,1)S(1)}, bf16[2,240,128]{2,1,0:T(8,128)(2,1)S(1)}, u32[]{:S(2)}, u32[]{:S(2)}) collective-permute-start(bf16[2,240,128]{2,1,0:T(8,128)(2,1)S(1)} %get-tuple-element.134.near), channel_id=1, source_target_pairs={{0,16},{1,17},{4,20},{5,21},{8,24},{9,25},{12,28},{13,29},{2,18},{... | collective-permute-start | bytes 368648 | tf_op jit(solution)/shard_map/ppermute | solution.py:57
  90.9 5.4 %collective-permute-start.23 = (bf16[240,128]{1,0:T(8,128)(2,1)S(1)}, bf16[240,128]{1,0:T(8,128)(2,1)S(1)}, u32[]{:S(2)}, u32[]{:S(2)}) collective-permute-start(bf16[240,128]{1,0:T(8,128)(2,1)S(1)} %get-tuple-element.135), channel_id=1, source_target_pairs={{0,18},{1,19},{4,22},{5,23},{8,26},{9,27},{12,30},{13,31},{2,16},{... | collective-permute-start | bytes 184328 | tf_op jit(solution)/shard_map/ppermute | solution.py:57
  92.1 4.3 %collective-permute-start.24 = (bf16[240,128]{1,0:T(8,128)(2,1)S(1)}, bf16[240,128]{1,0:T(8,128)(2,1)S(1)}, u32[]{:S(2)}, u32[]{:S(2)}) collective-permute-start(bf16[240,128]{1,0:T(8,128)(2,1)S(1)} %get-tuple-element.135), channel_id=1, source_target_pairs={{0,2},{1,3},{4,6},{5,7},{8,10},{9,11},{12,14},{13,15},{2,0},{3,1},... | collective-permute-start | bytes 184328 | tf_op jit(solution)/shard_map/ppermute | solution.py:57
  96.4 6.5 %collective-permute-start.25 = (bf16[2,240,128]{2,1,0:T(8,128)(2,1)S(1)}, bf16[2,240,128]{2,1,0:T(8,128)(2,1)S(1)}, u32[]{:S(2)}, u32[]{:S(2)}) collective-permute-start(bf16[2,240,128]{2,1,0:T(8,128)(2,1)S(1)} %across.1.refs_0_), channel_id=1, source_target_pairs={{0,8},{1,65},{4,12},{5,69},{8,0},{9,73},{12,4},{13,77},{2,10},{3,6... | collective-permute-start | bytes 368648 | tf_op jit(solution)/shard_map/ppermute | solution.py:57
  98.0 6.2 %collective-permute-start.26 = (bf16[2,240,128]{2,1,0:T(8,128)(2,1)S(1)}, bf16[2,240,128]{2,1,0:T(8,128)(2,1)S(1)}, u32[]{:S(2)}, u32[]{:S(2)}) collective-permute-start(bf16[2,240,128]{2,1,0:T(8,128)(2,1)S(1)} %across.1.refs_0_), channel_id=1, source_target_pairs={{0,12},{1,97},{4,8},{5,101},{8,4},{9,105},{12,0},{13,109},{2,14},{... | collective-permute-start | bytes 368648 | tf_op jit(solution)/shard_map/ppermute | solution.py:57
  100.2 6.2 %collective-permute-start.27 = (bf16[2,240,128]{2,1,0:T(8,128)(2,1)S(1)}, bf16[2,240,128]{2,1,0:T(8,128)(2,1)S(1)}, u32[]{:S(2)}, u32[]{:S(2)}) collective-permute-start(bf16[2,240,128]{2,1,0:T(8,128)(2,1)S(1)} %across.1.refs_0_), channel_id=1, source_target_pairs={{0,4},{1,33},{4,0},{5,37},{8,12},{9,41},{12,8},{13,45},{2,6},{3,35... | collective-permute-start | bytes 368648 | tf_op jit(solution)/shard_map/ppermute | solution.py:57
  106.4 7.9 %collective-permute-start.31 = (bf16[4,240,128]{2,1,0:T(8,128)(2,1)S(1)}, bf16[4,240,128]{2,1,0:T(8,128)(2,1)S(1)}, u32[]{:S(2)}, u32[]{:S(2)}) collective-permute-start(bf16[4,240,128]{2,1,0:T(8,128)(2,1)S(1)} %get-tuple-element.137.refs_0_), channel_id=1, source_target_pairs={{0,64},{1,9},{4,68},{5,13},{8,72},{9,1},{12,76},{13,5},{2,66},{3,1... | collective-permute-start | bytes 737288 | tf_op jit(solution)/shard_map/ppermute | solution.py:57
  107.3 9.5 %collective-permute-start.32 = (bf16[4,240,128]{2,1,0:T(8,128)(2,1)S(1)}, bf16[4,240,128]{2,1,0:T(8,128)(2,1)S(1)}, u32[]{:S(2)}, u32[]{:S(2)}) collective-permute-start(bf16[4,240,128]{2,1,0:T(8,128)(2,1)S(1)} %get-tuple-element.137.refs_0_), channel_id=1, source_target_pairs={{0,96},{1,13},{4,100},{5,9},{8,104},{9,5},{12,108},{13,1},{2,98},{... | collective-permute-start | bytes 737288 | tf_op jit(solution)/shard_map/ppermute | solution.py:57
  109.2 7.6 %collective-permute-start.33 = (bf16[4,240,128]{2,1,0:T(8,128)(2,1)S(1)}, bf16[4,240,128]{2,1,0:T(8,128)(2,1)S(1)}, u32[]{:S(2)}, u32[]{:S(2)}) collective-permute-start(bf16[4,240,128]{2,1,0:T(8,128)(2,1)S(1)} %get-tuple-element.137.refs_0_), channel_id=1, source_target_pairs={{0,32},{1,5},{4,36},{5,1},{8,40},{9,13},{12,44},{13,9},{2,34},{3,7... | collective-permute-start | bytes 737288 | tf_op jit(solution)/shard_map/ppermute | solution.py:57
  110.0 9.6 %collective-permute-start.28 = (bf16[4,240,128]{2,1,0:T(8,128)(2,1)S(1)}, bf16[4,240,128]{2,1,0:T(8,128)(2,1)S(1)}, u32[]{:S(2)}, u32[]{:S(2)}) collective-permute-start(bf16[4,240,128]{2,1,0:T(8,128)(2,1)S(1)} %get-tuple-element.136.refs_0_), channel_id=1, source_target_pairs={{0,64},{1,9},{4,68},{5,13},{8,72},{9,1},{12,76},{13,5},{2,66},{3,1... | collective-permute-start | bytes 737288 | tf_op jit(solution)/shard_map/ppermute | solution.py:57
  112.0 10.1 %collective-permute-start.29 = (bf16[4,240,128]{2,1,0:T(8,128)(2,1)S(1)}, bf16[4,240,128]{2,1,0:T(8,128)(2,1)S(1)}, u32[]{:S(2)}, u32[]{:S(2)}) collective-permute-start(bf16[4,240,128]{2,1,0:T(8,128)(2,1)S(1)} %get-tuple-element.136.refs_0_), channel_id=1, source_target_pairs={{0,96},{1,13},{4,100},{5,9},{8,104},{9,5},{12,108},{13,1},{2,98},{... | collective-permute-start | bytes 737288 | tf_op jit(solution)/shard_map/ppermute | solution.py:57
  114.3 7.8 %collective-permute-start.30 = (bf16[4,240,128]{2,1,0:T(8,128)(2,1)S(1)}, bf16[4,240,128]{2,1,0:T(8,128)(2,1)S(1)}, u32[]{:S(2)}, u32[]{:S(2)}) collective-permute-start(bf16[4,240,128]{2,1,0:T(8,128)(2,1)S(1)} %get-tuple-element.136.refs_0_), channel_id=1, source_target_pairs={{0,32},{1,5},{4,36},{5,1},{8,40},{9,13},{12,44},{13,9},{2,34},{3,7... | collective-permute-start | bytes 737288 | tf_op jit(solution)/shard_map/ppermute | solution.py:57

commit v5 on v4

--- a/solution.py
+++ b/solution.py
@@ -14,7 +14,10 @@
 ENTRY, SECOND, THIRD, FOURTH, BACK, FORE, BASIS, USED = 0, 560, 1072, 1584, 2096, 2608, 3120, 3760
 PACK = 3840
 PEERS = (1, 3, 2)
-FAR_FIRST = (2, 3, 1)
+EARLY, EARLY_PACK, LATE = 1712, 1792, 2048
+EARLY_CHUNK, LATE_CHUNK = EARLY_PACK // 4, LATE // 4
+EARLY_PIECE, LATE_PIECE = EARLY_PACK // 16, LATE // 16
+FAR_FIRST = (1, 3, 2)
 CHUNK, PIECE = PACK // 4, PACK // 16
 
 
@@ -235,9 +238,9 @@
                     ].astype(BF)
             else:
                 out[at : at + count, :] = grad[:, 128 * slot : 128 * (slot + 1)].astype(BF)
-        if name == "basis":
+        if name == "basis" and not self.base:
             for out in self.outs:
-                out[:, USED - self.base : PACK - self.base, :] = jnp.zeros((2, PACK - USED, 128), BF)
+                out[:, USED:PACK, :] = jnp.zeros((2, PACK - USED, 128), BF)
 
 
 def backward_heads(g, fore_wide, label, weights, act_ref, slope_ref, theta_ref, grads):
@@ -373,25 +376,39 @@
     steep[...] = jnp.where(look_mask(labels), g, 0.0)
 
 
-def cut_kernel(rows, *refs):
-    refs = list(refs)
-    mine = [refs.pop(0) for _ in rows]
-    got = [(refs.pop(0), refs.pop(0)) if count < 0 else refs.pop(0) for count in rows]
+def cut_kernel(mine, got, *refs):
     outs, whole = refs[:4], refs[4]
     i1, _ = places()
-    at = 0
-    for count, kept, came in zip(rows, mine, got):
-        for half in range(2):
-            part = came[half] if count < 0 else came.at[half]
-            whole[half, at : at + abs(count), :] = (
-                kept[half].astype(F32) + part[...].astype(F32)
-            ).astype(BF)
-        at += abs(count)
+    whole[...] = (mine[...].astype(F32) + got[...].astype(F32)).astype(BF)
     for bits, out in zip((*PEERS, 0), outs):
         begin = pl.multiple_of((i1 ^ bits) * CHUNK, CHUNK)
         out[...] = whole[:, pl.ds(begin, CHUNK), :]
 
 
+def fold_heads_kernel(mine, got, near, rest, far):
+    sums = (mine[...].astype(F32) + got[...].astype(F32)).astype(BF)
+    near[...] = sums[0]
+    rest[...] = sums[1, : EARLY - FOURTH]
+    far[...] = sums[1, EARLY - FOURTH :]
+
+
+def cut_one_kernel(mine, got0, got1, near, rest, came, *refs):
+    outs, early, late = refs[:4], refs[4], refs[5]
+    i1, _ = places()
+    for half, got in enumerate((got0, got1)):
+        early[half, :LOW] = (mine[half].astype(F32) + got[...].astype(F32)).astype(BF)
+    early[0, LOW:EARLY] = near[: EARLY - LOW, :]
+    early[1, LOW:EARLY] = rest[...]
+    early[:, EARLY:] = jnp.zeros((2, EARLY_PACK - EARLY, 128), BF)
+    late[...] = (near[EARLY - LOW :, :].astype(F32) + came[...].astype(F32)).astype(BF)
+    for bits, out in zip((*PEERS, 0), outs):
+        begin = pl.multiple_of((i1 ^ bits) * EARLY_CHUNK, EARLY_CHUNK)
+        for half in range(2):
+            out[half * EARLY_CHUNK : (half + 1) * EARLY_CHUNK, :] = early[half, pl.ds(begin, EARLY_CHUNK), :]
+        begin = pl.multiple_of((i1 ^ bits) * LATE_CHUNK, LATE_CHUNK)
+        out[2 * EARLY_CHUNK :, :] = late[pl.ds(begin, LATE_CHUNK), :]
+
+
 def total(refs):
     a, b, c, d = (ref[...].astype(F32) for ref in refs)
     return ((a + b) + (c + d)).astype(BF)
@@ -402,24 +419,35 @@
 
 
 def piece_kernel(own, a, b, c, near, came, *refs):
-    outs, whole = refs[:4], refs[4]
+    outs, one, two = refs[:4], refs[4], refs[5]
     _, i2 = places()
-    whole[0], whole[2] = total((own, a, b, c))
-    whole[1] = (near[...].astype(F32) + came[...].astype(F32)).astype(BF)
+    one[...] = total((own, a, b, c))
+    two[...] = (near[...].astype(F32) + came[...].astype(F32)).astype(BF)
     for bits, out in zip((*PEERS, 0), outs):
-        begin = pl.multiple_of((i2 ^ bits) * PIECE, PIECE)
-        out[...] = whole[:, pl.ds(begin, PIECE), :]
+        at = 0
+        for ref, base, count in (
+            (one, 0, EARLY_PIECE),
+            (one, 2 * EARLY_CHUNK, LATE_PIECE),
+            (two, 0, PIECE),
+            (one, EARLY_CHUNK, EARLY_PIECE),
+        ):
+            begin = pl.multiple_of(base + (i2 ^ bits) * count, 16)
+            out[at : at + count, :] = ref[pl.ds(begin, count), :]
+            at += count
 
 
 def sum_kernel(own, a, b, c, near, far):
     sums = total((own, a, b, c))
-    near[...] = sums[:2]
-    far[...] = sums[2]
+    near[0] = sums[:PIECE]
+    near[1] = sums[PIECE : 2 * PIECE]
+    far[...] = sums[2 * PIECE :]
 
 
 def across_kernel(near, a, b, c, out):
     both = near[...].astype(F32) + a[...].astype(F32)
-    out[0] = (both[0] + (b[...].astype(F32) + c[...].astype(F32))).astype(BF)
+    add = b[...].astype(F32) + c[...].astype(F32)
+    out[0, :EARLY_PIECE] = (both[0, :EARLY_PIECE] + add).astype(BF)
+    out[0, EARLY_PIECE:] = both[0, EARLY_PIECE:].astype(BF)
     out[1] = both[1].astype(BF)
 
 
@@ -427,23 +455,34 @@
     for k in range(2):
         for n in range(4):
             refs[4 + k][n] = refs[n][k]
+    refs[6][...] = refs[3][0, :16]
 
 
 def unpack_kernel(k, *refs):
     stacks, outs, whole, bufs, sem = refs[:4], refs[-16:-9], refs[-9], refs[-8:-1], refs[-1]
     i1, i2 = places()
+    parts = ((0, EARLY_CHUNK, EARLY_PIECE), (EARLY_PACK, LATE_CHUNK, LATE_PIECE)) if k == 0 else ((0, CHUNK, PIECE),)
     for a, stack in zip((0, *FAR_FIRST), stacks):
         for slot, b in enumerate((0, *FAR_FIRST)):
-            at = pl.multiple_of((i1 ^ a) * CHUNK + (i2 ^ b) * PIECE, PIECE)
-            whole[pl.ds(at, PIECE), :] = stack[slot]
+            row = 0
+            for base, chunk, piece in parts:
+                at = pl.multiple_of(base + (i1 ^ a) * chunk + (i2 ^ b) * piece, 16)
+                whole[pl.ds(at, piece), :] = stack[slot, row : row + piece, :]
+                row += piece
+
+    def rows(begin, count):
+        if k == 0 and begin >= EARLY:
+            begin += EARLY_PACK - EARLY
+        return whole[begin : begin + count, :].astype(F32) * scale
+
     scale = 1.0 / math.sqrt(98304)
     copies = []
     for (name, (begin, count)), out, buf in zip(TABLES.items(), outs, bufs):
         if buf.shape[1] == 128:
-            buf[...] = whole[begin : begin + count, :].astype(F32) * scale
+            buf[...] = rows(begin, count)
         else:
             for i in range(count // 128):
-                part = whole[begin + 128 * i : begin + 128 * (i + 1), :].astype(F32) * scale
+                part = rows(begin + 128 * i, 128)
                 buf[:, 128 * i : 128 * (i + 1)] = part.T if name == "basis" else part
         copies.append(pltpu.make_async_copy(buf, out.at[k], sem.at[len(copies)]))
         copies[-1].start()
@@ -483,7 +522,7 @@
 
 ACTS = (4, 512, ROWS)
 KEPT = [(560, ROWS), ACTS, ACTS, (2, 512, ROWS)]
-TOP, LOW = PACK - FOURTH, FOURTH
+TOP, LOW = USED - FOURTH, FOURTH
 
 
 def plus(*parts):
@@ -555,20 +594,24 @@
     )(label, g1, adjoint, *slots1, act1, slope1, theta1)
     got1a = send(theirs1a, to_core())
 
-    def cut(rows, mine, got, name):
+    def small(kernel, name, outs, *args, scratch=()):
         return call(
-            functools.partial(cut_kernel, rows),
+            kernel,
             name,
-            [IN_VMEM] * (len(mine) + len(got)),
-            [(shape(2, CHUNK, 128, kind=BF), IN_VMEM)] * 4,
-            [vmem(2, PACK, 128)],
+            [IN_VMEM] * len(args),
+            [(shape(*dims, 128, kind=BF), IN_VMEM) for dims in outs],
+            scratch,
             M5,
-            2,
-        )(*mine, *got)
-
-    *out2, own2 = cut((PACK,), [mine2], [got2], "cut_two")
+            1,
+        )(*args)
+
+    *out2, own2 = small(cut_kernel, "cut_two", [(2, CHUNK)] * 4, mine2, got2, scratch=[vmem(2, PACK, 128)])
     got2 = [send(part, to_first(a)) for part, a in zip(out2, PEERS)]
-    d_pre, got1a, *out2 = lax.optimization_barrier((d_pre, got1a, *out2))
+    near1, rest1, far1 = small(
+        fold_heads_kernel, "fold_heads", [(TOP,), (EARLY - FOURTH,), (LATE,)], mine1a, got1a
+    )
+    d_pre, far1, *out2 = lax.optimization_barrier((d_pre, far1, *out2))
+    came1 = send(far1, to_x_by_core())
     steep, mine1b, *theirs1b = call(
         fourth_kernel,
         "backward_one_layers",
@@ -581,37 +624,38 @@
     )(label, g1, d_pre, *slots1, e1, act1, slope1)
     got1b = [send(part, to_core()) for part in theirs1b]
     mine1b, got2[2] = lax.optimization_barrier((mine1b, got2[2]))
-    *out1, own1 = cut((-LOW, TOP), [mine1b, mine1a], [*got1b, got1a], "cut_one")
+    *out1, own1 = small(
+        cut_one_kernel,
+        "cut_one",
+        [(2 * EARLY_CHUNK + LATE_CHUNK,)] * 4,
+        mine1b,
+        *got1b,
+        near1,
+        rest1,
+        came1,
+        scratch=[vmem(2, EARLY_PACK, 128), vmem(LATE, 128)],
+    )
     got1 = [send(part, to_first(a)) for part, a in zip(out1, PEERS)]
-
-    def small(kernel, name, outs, *args, scratch=()):
-        return call(
-            kernel,
-            name,
-            [IN_VMEM] * len(args),
-            [(shape(*dims, 128, kind=BF), IN_VMEM) for dims in outs],
-            scratch,
-            M5,
-            1,
-        )(*args)
 
     near2, far2 = small(fold_kernel, "fold", [(CHUNK,)] * 2, own2, *got2)
     *out, own = small(
         piece_kernel,
         "pieces",
-        [(3, PIECE)] * 4,
+        [(2 * PIECE + EARLY_PIECE,)] * 4,
         own1,
         *got1,
         near2,
         send(far2, to_x_by_core()),
-        scratch=[vmem(3, CHUNK, 128)],
+        scratch=[vmem(2 * EARLY_CHUNK + LATE_CHUNK, 128), vmem(CHUNK, 128)],
     )
     got = [send(part, to_second(b)) for part, b in zip(out, PEERS)]
-    near, far = small(sum_kernel, "sums", [(2, PIECE), (PIECE,)], own, *got)
-    got = [send(near, to_x(2)), send(far, to_x(3)), send(far, to_x(1))]
+    near, far = small(sum_kernel, "sums", [(2, PIECE), (EARLY_PIECE,)], own, *got)
+    x1, x3 = send(far, to_x(1)), send(far, to_x(3))
+    got = [send(near, to_x(2)), x3, x1]
     done = small(across_kernel, "across", [(2, PIECE)], near, *got)[0]
     got = [send(done, to_second(b)) for b in FAR_FIRST]
-    stack = small(stack_kernel, "stack", [(4, PIECE)] * 2, done, *got)
+    *stack, here = small(stack_kernel, "stack", [(4, PIECE)] * 2 + [(16,)], done, *got)
+    *stack, here = lax.optimization_barrier((*stack, send(here, to_core())))
     grads = ()
     for k in (1, 0):
         stacks = [stack[k]] + [send(stack[k], to_first(a)) for a in FAR_FIRST]
@@ -621,13 +665,13 @@
         grads = call(
             functools.partial(unpack_kernel, k),
             "unpack",
-            [IN_VMEM] * 4 + [ANYWHERE] * (len(grads)),
+            [IN_VMEM] * 4 + [ANYWHERE] * (len(grads) + 1),
             [(shape(2, *dims), ANYWHERE) for dims in outs],
             [vmem(PACK, 128)] + [vmem(*dims, kind=F32) for dims in outs] + [DMA((7,))],
             16,
             2,
             {4 + n: n for n in range(len(grads))},
-        )(*stacks, *grads)
+        )(*stacks, *grads, here)
     return (look.T, rest.T, steep.T, *grads)
 
 

time: 124 us -> 123 us (level)
  waiting for transfers between devices: 44.9 us -> 43 us
  starting transfers between devices: 43.8 us -> 45.1 us
    pallas_call x2 -> x0, Pallas kernels: 2.22 us -> none  [cut(): call(functools.partial(cut_kernel, rows), name, [IN_VMEM] * (len(mine) +...]
    ppermute x34 -> x36, waiting for transfers between devices: 44.9 us -> 43 us  [send(): return lax.ppermute(values, ('dp', 'mp'), where)]
    pallas_call x5 -> x8, Pallas kernels: 1.11 us -> 3.04 us  [small(): call(kernel, name, [IN_VMEM] * len(args), [(shape(*dims, 128, kind=BF), I...]
    ppermute x34 -> x36, starting transfers between devices: 43.8 us -> 45.1 us  [send(): return lax.ppermute(values, ('dp', 'mp'), where)]
  transfers between devices with their start and end apart: 34 -> 36, of which waited for: 19 -> 23; matrix products, arithmetic and copies ran while one was open for 0% -> 0% of each run, Pallas kernels for 16% -> 16%
where the time goes in v5:
time: 123 us
  starting transfers between devices  45.1 us (37%)
  waiting for transfers between devices  43 us (35%)
  Pallas kernels  33.7 us (27%)
    ppermute x36, starting transfers between devices, send(): return lax.ppermute(values, ('dp', 'mp'), where)  45.1 us
    ppermute x36, waiting for transfers between devices, send(): return lax.ppermute(values, ('dp', 'mp'), where)  43 us
    pallas_call x1, Pallas kernels, shards(): call(second_kernel, 'block_two', [IN_VMEM] * 9, [(shape(336, ROWS), IN_VM...  10.5 us
    pallas_call x1, Pallas kernels, shards(): call(fourth_kernel, 'backward_one_layers', [IN_VMEM] * 10, [(shape(336, R...  4.16 us
    pallas_call x1, Pallas kernels, shards(): call(first_kernel, 'forward_one', [IN_VMEM] * 6, [(shape(336, ROWS), IN_V...  4.13 us
    pallas_call x1, Pallas kernels, shards(): call(third_kernel, 'backward_one_heads', [IN_VMEM] * 10, [(shape(512, ROW...  3.76 us
    pallas_call x1, Pallas kernels, shards(): call(pack_kernel, 'pack', [IN_VMEM] * 7, [(shape(2, PACK, 128, kind=BF),...  3.33 us
    pallas_call x8, Pallas kernels, small(): call(kernel, name, [IN_VMEM] * len(args), [(shape(*dims, 128, kind=BF), I...  3.04 us
  transfers between devices with their start and end apart: 36, of which 23 were waited for; matrix products, arithmetic and copies ran while one was open for 0% of the time, Pallas kernels for 16%

profile of v5, /device:TPU:0, one launch (start us, length us, event | category | flops | bytes accessed | tf_op | source)
XLA Modules:
  0.0 122.8 jit_solution(16512162764441474241)
XLA Ops:
  0.6 1.7 %pack_quarter.1 = bf16[960,128]{1,0:T(8,128)(2,1)} custom-call(bf16[2,560,128]{2,1,0:T(8,128)(2,1)} %refs_0_.2, bf16[2,128,512]{2,1,0:T(8,128)(2,1)} %refs_1_.2, bf16[2,512,128]{2,1,0:T(8,128)(2,1)} %refs_2_.2, bf16[2,128,512]{2,1,0:T(8,128)(2,1)} %refs_3_.2, bf16[2,512,128]{2,1,0:T(8,128)(2,1)} %refs_4_.2, bf16[2,512,128]{2,1,0:T(8,128)(2,1)} %refs_5_.2, ...), custom_call_target="tpu_custom_call" | custom-call | flops 800000000 | bytes 1000000 | tf_op jit(solution)/shard_map/pack_quarter/pallas_call | solution.py:537
  2.3 1.7 %collective-permute-start.1 = (bf16[960,128]{1,0:T(8,128)(2,1)}, bf16[960,128]{1,0:T(8,128)(2,1)S(1)}, u32[]{:S(2)}, u32[]{:S(2)}) collective-permute-start(bf16[960,128]{1,0:T(8,128)(2,1)} %pack_quarter.1), channel_id=1, source_target_pairs={{0,2},{1,19},{4,6},{5,23},{8,10},{9,27},{12,14},{13,31},{2,0},{3,1... | collective-permute-start | bytes 737288 | tf_op jit(solution)/shard_map/ppermute | solution.py:60
  4.0 3.3 %pack.1 = (bf16[2,3840,128]{2,1,0:T(8,128)(2,1)}, bf16[3840,128]{1,0:T(8,128)(2,1)}) custom-call(bf16[2,560,128]{2,1,0:T(8,128)(2,1)} %refs_0_.2, bf16[2,128,512]{2,1,0:T(8,128)(2,1)} %refs_1_.2, bf16[2,512,128]{2,1,0:T(8,128)(2,1)} %refs_2_.2, bf16[2,128,512]{2,1,0:T(8,128)(2,1)} %refs_3_.2, bf16[2,512,128]{2,1,0:T(8,128)(2,1)} %refs_4_.2, ...), custom_call_target="tpu_custom_call" | custom-call | flops 2400000000 | bytes 3000000 | tf_op jit(solution)/shard_map/pack/pallas_call | solution.py:547
  7.3 1.5 %collective-permute-done.1.q0 = bf16[960,128]{1,0:T(8,128)(2,1)S(1)} collective-permute-done((bf16[960,128]{1,0:T(8,128)(2,1)}, bf16[960,128]{1,0:T(8,128)(2,1)S(1)}, u32[]{:S(2)}, u32[]{:S(2)}) %collective-permute-start.1) | collective-permute-done | bytes 245792 | tf_op jit(solution)/shard_map/ppermute | solution.py:60
  8.8 1.6 %collective-permute-start.2 = (bf16[3840,128]{1,0:T(8,128)(2,1)}, bf16[3840,128]{1,0:T(8,128)(2,1)S(1)}, u32[]{:S(2)}, u32[]{:S(2)}) collective-permute-start(bf16[3840,128]{1,0:T(8,128)(2,1)} %get-tuple-element.98), channel_id=1, source_target_pairs={{0,2},{1,19},{4,6},{5,23},{8,10},{9,27},{12,14},{13,31},{2,0},{3,1... | collective-permute-start | bytes 2949128 | tf_op jit(solution)/shard_map/ppermute | solution.py:60
  10.4 0.9 collective-permute-start
  11.3 3.2 %collective-permute-start.5 = (bf16[960,128]{1,0:T(8,128)(2,1)S(1)}, bf16[960,128]{1,0:T(8,128)(2,1)S(1)}, u32[]{:S(2)}, u32[]{:S(2)}) collective-permute-start(bf16[960,128]{1,0:T(8,128)(2,1)S(1)} %collective-permute-done.1.q0), channel_id=1, source_target_pairs={{0,64},{1,9},{4,68},{5,13},{8,72},{9,1},{12,76},{13,5},{2,66},{3,1... | collective-permute-start | bytes 737288 | tf_op jit(solution)/shard_map/ppermute | solution.py:60
  14.5 1.1 collective-permute-start.4
  15.5 3.4 %collective-permute-done.5.q3 = bf16[960,128]{1,0:T(8,128)(2,1)S(1)} collective-permute-done((bf16[960,128]{1,0:T(8,128)(2,1)S(1)}, bf16[960,128]{1,0:T(8,128)(2,1)S(1)}, u32[]{:S(2)}, u32[]{:S(2)}) %collective-permute-start.5) | collective-permute-done | bytes 245792 | tf_op jit(solution)/shard_map/ppermute | solution.py:60
  19.0 2.9 %collective-permute-done.4.q2 = bf16[960,128]{1,0:T(8,128)(2,1)S(1)} collective-permute-done((bf16[960,128]{1,0:T(8,128)(2,1)S(1)}, bf16[960,128]{1,0:T(8,128)(2,1)S(1)}, u32[]{:S(2)}, u32[]{:S(2)}) %collective-permute-start.4) | collective-permute-done | bytes 245792 | tf_op jit(solution)/shard_map/ppermute | solution.py:60
  22.0 1.2 collective-permute-done.2.s2
  23.2 0.8 collective-permute-start.7
  24.0 1.7 %collective-permute-done.6.s3 = bf16[3840,128]{1,0:T(8,128)(2,1)S(1)} collective-permute-done((bf16[3840,128]{1,0:T(8,128)(2,1)S(1)}, bf16[3840,128]{1,0:T(8,128)(2,1)S(1)}, u32[]{:S(2)}, u32[]{:S(2)}) %collective-permute-start.6) | collective-permute-done | bytes 983072 | tf_op jit(solution)/shard_map/ppermute | solution.py:60
  25.7 4.1 %forward_one.1 = (f32[336,768]{1,0:T(8,128)S(1)}, f32[48,768]{1,0:T(8,128)S(1)}, bf16[560,768]{1,0:T(8,128)(2,1)S(1)}, bf16[4,512,768]{2,1,0:T(8,128)(2,1)S(1)},...) custom-call(s32[1,768]{1,0:T(1,128)S(1)} %broadcast_in_dim.3.label, bf16[336,768]{1,0:T(8,128)(2,1)S(1)} %bitcast.6, ...), custom_call_target="tpu_custom_call" | custom-call | flops 4800000000 | bytes 6000000 | tf_op jit(solution)/shard_map/forward_one/pallas_call | solution.py:565
  29.9 10.5 %block_two.1 = (f32[336,768]{1,0:T(8,128)}, f32[48,768]{1,0:T(8,128)}, f32[336,768]{1,0:T(8,128)S(1)}, bf16[2,3840,128]{2,1,0:T(8,128)(2,1)S(1)}, bf16[2,3840,128]{2,1,0:T(8,128)(2,1)S(1)}) custom-call(s32[1,768]{1,0:T(1,128)S(1)} %broadcast_in_dim.3.label, f32[336,768]{1,0:T(8,128)S(1)} %get-tuple-element.101.state_in, ...), custom_call_target="tpu_custom_call" | custom-call | flops 11200000000 | bytes 14000000 | tf_op jit(solution)/shard_map/block_two/pallas_call | solution.py:575
  40.6 3.8 %backward_one_heads.1 = (bf16[512,768]{1,0:T(8,128)(2,1)S(1)}, bf16[2,2176,128]{2,1,0:T(8,128)(2,1)S(1)}, bf16[2,2176,128]{2,1,0:T(8,128)(2,1)S(1)}) custom-call(s32[1,768]{1,0:T(1,128)S(1)} %broadcast_in_dim.3.label, f32[336,768]{1,0:T(8,128)S(1)} %get-tuple-element.109.g_in, bf16[48,768]{1,0:T(8,128)(2,1)S(1)} %bitcast.9, ...), custom_call_target="tpu_custom_call" | custom-call | flops 4800000000 | bytes 6000000 | tf_op jit(solution)/shard_map/backward_one_heads/pallas_call | solution.py:586
  44.4 0.5 collective-permute-start.8
  44.8 1.2 cut_two.1
  46.0 3.5 %collective-permute-start.10 = (bf16[2,960,128]{2,1,0:T(8,128)(2,1)S(1)}, bf16[2,960,128]{2,1,0:T(8,128)(2,1)S(1)}, u32[]{:S(2)}, u32[]{:S(2)}) collective-permute-start(bf16[2,960,128]{2,1,0:T(8,128)(2,1)S(1)} %get-tuple-element.121), channel_id=1, source_target_pairs={{0,64},{1,9},{4,68},{5,13},{8,72},{9,1},{12,76},{13,5},{2,66},{3,1... | collective-permute-start | bytes 1474568 | tf_op jit(solution)/shard_map/ppermute | solution.py:60
  49.5 0.3 fold_heads.1
  49.7 1.6 %collective-permute-start.13 = (bf16[2048,128]{1,0:T(8,128)(2,1)S(1)}, bf16[2048,128]{1,0:T(8,128)(2,1)S(1)}, u32[]{:S(2)}, u32[]{:S(2)}) collective-permute-start(bf16[2048,128]{1,0:T(8,128)(2,1)S(1)} %get-tuple-element.131), channel_id=1, source_target_pairs={{0,2},{1,19},{4,6},{5,23},{8,10},{9,27},{12,14},{13,31},{2,0},{3,1... | collective-permute-start | bytes 1572872 | tf_op jit(solution)/shard_map/ppermute | solution.py:60
  51.3 4.2 %backward_one_layers.1 = (f32[336,768]{1,0:T(8,128)}, bf16[2,1584,128]{2,1,0:T(8,128)(2,1)S(1)}, bf16[1584,128]{1,0:T(8,128)(2,1)S(1)}, bf16[1584,128]{1,0:T(8,128)(2,1)S(1)}) custom-call(s32[1,768]{1,0:T(1,128)S(1)} %broadcast_in_dim.3.label, f32[336,768]{1,0:T(8,128)S(1)} %get-tuple-element.109.g_in, bf16[512,768]{1,0:T(8,128)(2,1)S(1)} %get-tuple-element.122.d_in, ...), custom_call_target="tpu_custom_call" | custom-call | flops 4800000000 | bytes 6000000 | tf_op jit(solution)/shard_map/backward_one_layers/pallas_call | solution.py:615
  55.5 1.4 %collective-permute-start.11 = (bf16[1584,128]{1,0:T(8,128)(2,1)S(1)}, bf16[1584,128]{1,0:T(8,128)(2,1)S(1)}, u32[]{:S(2)}, u32[]{:S(2)}) collective-permute-start(bf16[1584,128]{1,0:T(8,128)(2,1)S(1)} %get-tuple-element.127), channel_id=1, source_target_pairs={{0,1},{1,0},{4,5},{5,4},{8,9},{9,8},{12,13},{13,12},{2,3},{3,2},{6... | collective-permute-start | bytes 1216520 | tf_op jit(solution)/shard_map/ppermute | solution.py:60
  56.9 1.6 %collective-permute-start.17 = (bf16[2,960,128]{2,1,0:T(8,128)(2,1)S(1)}, bf16[2,960,128]{2,1,0:T(8,128)(2,1)S(1)}, u32[]{:S(2)}, u32[]{:S(2)}) collective-permute-start(bf16[2,960,128]{2,1,0:T(8,128)(2,1)S(1)} %get-tuple-element.119), channel_id=1, source_target_pairs={{0,32},{1,5},{4,36},{5,1},{8,40},{9,13},{12,44},{13,9},{2,34},{3,7... | collective-permute-start | bytes 1474568 | tf_op jit(solution)/shard_map/ppermute | solution.py:60
  58.5 2.2 %collective-permute-start.18 = (bf16[2,960,128]{2,1,0:T(8,128)(2,1)S(1)}, bf16[2,960,128]{2,1,0:T(8,128)(2,1)S(1)}, u32[]{:S(2)}, u32[]{:S(2)}) collective-permute-start(bf16[2,960,128]{2,1,0:T(8,128)(2,1)S(1)} %get-tuple-element.120), channel_id=1, source_target_pairs={{0,96},{1,13},{4,100},{5,9},{8,104},{9,5},{12,108},{13,1},{2,98},{... | collective-permute-start | bytes 1474568 | tf_op jit(solution)/shard_map/ppermute | solution.py:60
  60.8 0.7 cut_one.1
  61.5 0.8 collective-permute-start.14
  62.3 1.2 collective-permute-start.15
  63.5 2.2 %collective-permute-start.16 = (bf16[1408,128]{1,0:T(8,128)(2,1)S(1)}, bf16[1408,128]{1,0:T(8,128)(2,1)S(1)}, u32[]{:S(2)}, u32[]{:S(2)}) collective-permute-start(bf16[1408,128]{1,0:T(8,128)(2,1)S(1)} %get-tuple-element.135), channel_id=1, source_target_pairs={{0,64},{1,9},{4,68},{5,13},{8,72},{9,1},{12,76},{13,5},{2,66},{3,1... | collective-permute-start | bytes 1081352 | tf_op jit(solution)/shard_map/ppermute | solution.py:60
  65.7 2.8 %collective-permute-done.18.b = bf16[2,960,128]{2,1,0:T(8,128)(2,1)S(1)} collective-permute-done((bf16[2,960,128]{2,1,0:T(8,128)(2,1)S(1)}, bf16[2,960,128]{2,1,0:T(8,128)(2,1)S(1)}, u32[]{:S(2)}, u32[]{:S(2)}) %collective-permute-start.18) | collective-permute-done | bytes 491552 | tf_op jit(solution)/shard_map/ppermute | solution.py:60
  68.5 0.2 fold.1
  68.8 0.3 collective-permute-start.19
  69.1 6.0 %collective-permute-done.19.came = bf16[960,128]{1,0:T(8,128)(2,1)S(1)} collective-permute-done((bf16[960,128]{1,0:T(8,128)(2,1)S(1)}, bf16[960,128]{1,0:T(8,128)(2,1)S(1)}, u32[]{:S(2)}, u32[]{:S(2)}) %collective-permute-start.19) | collective-permute-done | bytes 245792 | tf_op jit(solution)/shard_map/ppermute | solution.py:60
  75.1 1.2 collective-permute-done.15.b
  76.3 0.5 pieces.1
  76.8 1.1 collective-permute-start.20
  77.9 1.7 %collective-permute-start.21 = (bf16[592,128]{1,0:T(8,128)(2,1)S(1)}, bf16[592,128]{1,0:T(8,128)(2,1)S(1)}, u32[]{:S(2)}, u32[]{:S(2)}) collective-permute-start(bf16[592,128]{1,0:T(8,128)(2,1)S(1)} %get-tuple-element.142), channel_id=1, source_target_pairs={{0,12},{1,97},{4,8},{5,101},{8,4},{9,105},{12,0},{13,109},{2,14},{... | collective-permute-start | bytes 454664 | tf_op jit(solution)/shard_map/ppermute | solution.py:60
  79.6 1.4 %collective-permute-start.22 = (bf16[592,128]{1,0:T(8,128)(2,1)S(1)}, bf16[592,128]{1,0:T(8,128)(2,1)S(1)}, u32[]{:S(2)}, u32[]{:S(2)}) collective-permute-start(bf16[592,128]{1,0:T(8,128)(2,1)S(1)} %get-tuple-element.143), channel_id=1, source_target_pairs={{0,8},{1,65},{4,12},{5,69},{8,0},{9,73},{12,4},{13,77},{2,10},{3,6... | collective-permute-start | bytes 454664 | tf_op jit(solution)/shard_map/ppermute | solution.py:60
  81.0 1.1 collective-permute-done.20.a
  82.1 2.2 %collective-permute-done.21.b = bf16[592,128]{1,0:T(8,128)(2,1)S(1)} collective-permute-done((bf16[592,128]{1,0:T(8,128)(2,1)S(1)}, bf16[592,128]{1,0:T(8,128)(2,1)S(1)}, u32[]{:S(2)}, u32[]{:S(2)}) %collective-permute-start.21) | collective-permute-done | bytes 151584 | tf_op jit(solution)/shard_map/ppermute | solution.py:60
  84.3 2.0 %collective-permute-done.22.c = bf16[592,128]{1,0:T(8,128)(2,1)S(1)} collective-permute-done((bf16[592,128]{1,0:T(8,128)(2,1)S(1)}, bf16[592,128]{1,0:T(8,128)(2,1)S(1)}, u32[]{:S(2)}, u32[]{:S(2)}) %collective-permute-start.22) | collective-permute-done | bytes 151584 | tf_op jit(solution)/shard_map/ppermute | solution.py:60
  86.3 2.9 %collective-permute-start.23 = (bf16[2,240,128]{2,1,0:T(8,128)(2,1)S(1)}, bf16[2,240,128]{2,1,0:T(8,128)(2,1)S(1)}, u32[]{:S(2)}, u32[]{:S(2)}) collective-permute-start(bf16[2,240,128]{2,1,0:T(8,128)(2,1)S(1)} %get-tuple-element.144.near), channel_id=1, source_target_pairs={{0,16},{1,17},{4,20},{5,21},{8,24},{9,25},{12,28},{13,29},{2,18},{... | collective-permute-start | bytes 368648 | tf_op jit(solution)/shard_map/ppermute | solution.py:60
  89.2 0.6 collective-permute-start.25
  89.8 0.7 collective-permute-start.24
  90.5 2.6 %collective-permute-done.25.c = bf16[112,128]{1,0:T(8,128)(2,1)S(1)} collective-permute-done((bf16[112,128]{1,0:T(8,128)(2,1)S(1)}, bf16[112,128]{1,0:T(8,128)(2,1)S(1)}, u32[]{:S(2)}, u32[]{:S(2)}) %collective-permute-start.25) | collective-permute-done | bytes 28704 | tf_op jit(solution)/shard_map/ppermute | solution.py:60
  93.1 1.8 %collective-permute-done.24.b = bf16[112,128]{1,0:T(8,128)(2,1)S(1)} collective-permute-done((bf16[112,128]{1,0:T(8,128)(2,1)S(1)}, bf16[112,128]{1,0:T(8,128)(2,1)S(1)}, u32[]{:S(2)}, u32[]{:S(2)}) %collective-permute-start.24) | collective-permute-done | bytes 28704 | tf_op jit(solution)/shard_map/ppermute | solution.py:60
  95.0 1.3 %collective-permute-start.28 = (bf16[2,240,128]{2,1,0:T(8,128)(2,1)S(1)}, bf16[2,240,128]{2,1,0:T(8,128)(2,1)S(1)}, u32[]{:S(2)}, u32[]{:S(2)}) collective-permute-start(bf16[2,240,128]{2,1,0:T(8,128)(2,1)S(1)} %across.1.refs_0_), channel_id=1, source_target_pairs={{0,8},{1,65},{4,12},{5,69},{8,0},{9,73},{12,4},{13,77},{2,10},{3,6... | collective-permute-start | bytes 368648 | tf_op jit(solution)/shard_map/ppermute | solution.py:60
  96.2 2.5 %collective-permute-start.27 = (bf16[2,240,128]{2,1,0:T(8,128)(2,1)S(1)}, bf16[2,240,128]{2,1,0:T(8,128)(2,1)S(1)}, u32[]{:S(2)}, u32[]{:S(2)}) collective-permute-start(bf16[2,240,128]{2,1,0:T(8,128)(2,1)S(1)} %across.1.refs_0_), channel_id=1, source_target_pairs={{0,12},{1,97},{4,8},{5,101},{8,4},{9,105},{12,0},{13,109},{2,14},{... | collective-permute-start | bytes 368648 | tf_op jit(solution)/shard_map/ppermute | solution.py:60
  98.7 2.7 %collective-permute-done.28.refs_3_ = bf16[2,240,128]{2,1,0:T(8,128)(2,1)S(1)} collective-permute-done((bf16[2,240,128]{2,1,0:T(8,128)(2,1)S(1)}, bf16[2,240,128]{2,1,0:T(8,128)(2,1)S(1)}, u32[]{:S(2)}, u32[]{:S(2)}) %collective-permute-start.28) | collective-permute-done | bytes 122912 | tf_op jit(solution)/shard_map/ppermute | solution.py:60
  101.5 1.3 %collective-permute-done.27.refs_2_ = bf16[2,240,128]{2,1,0:T(8,128)(2,1)S(1)} collective-permute-done((bf16[2,240,128]{2,1,0:T(8,128)(2,1)S(1)}, bf16[2,240,128]{2,1,0:T(8,128)(2,1)S(1)}, u32[]{:S(2)}, u32[]{:S(2)}) %collective-permute-start.27) | collective-permute-done | bytes 122912 | tf_op jit(solution)/shard_map/ppermute | solution.py:60
  102.7 0.9 collective-permute-done.26.refs_1_
  103.7 1.2 collective-permute-done.29.refs_4_.refs_11_
  104.9 2.1 %collective-permute-start.35 = (bf16[4,240,128]{2,1,0:T(8,128)(2,1)S(1)}, bf16[4,240,128]{2,1,0:T(8,128)(2,1)S(1)}, u32[]{:S(2)}, u32[]{:S(2)}) collective-permute-start(bf16[4,240,128]{2,1,0:T(8,128)(2,1)S(1)} %get-tuple-element.150.refs_0_), channel_id=1, source_target_pairs={{0,64},{1,9},{4,68},{5,13},{8,72},{9,1},{12,76},{13,5},{2,66},{3,1... | collective-permute-start | bytes 737288 | tf_op jit(solution)/shard_map/ppermute | solution.py:60
  107.0 1.1 collective-permute-start.34
  108.1 0.9 collective-permute-start.33
  108.9 2.7 %collective-permute-start.32 = (bf16[4,240,128]{2,1,0:T(8,128)(2,1)S(1)}, bf16[4,240,128]{2,1,0:T(8,128)(2,1)S(1)}, u32[]{:S(2)}, u32[]{:S(2)}) collective-permute-start(bf16[4,240,128]{2,1,0:T(8,128)(2,1)S(1)} %get-tuple-element.149.refs_0_), channel_id=1, source_target_pairs={{0,64},{1,9},{4,68},{5,13},{8,72},{9,1},{12,76},{13,5},{2,66},{3,1... | collective-permute-start | bytes 737288 | tf_op jit(solution)/shard_map/ppermute | solution.py:60
  111.7 1.1 collective-permute-start.31
  112.8 0.4 collective-permute-start.30
  113.2 2.0 %collective-permute-done.34.refs_2_ = bf16[4,240,128]{2,1,0:T(8,128)(2,1)S(1)} collective-permute-done((bf16[4,240,128]{2,1,0:T(8,128)(2,1)S(1)}, bf16[4,240,128]{2,1,0:T(8,128)(2,1)S(1)}, u32[]{:S(2)}, u32[]{:S(2)}) %collective-permute-start.34) | collective-permute-done | bytes 245792 | tf_op jit(solution)/shard_map/ppermute | solution.py:60
  115.2 0.6 collective-permute-done.33.refs_1_
  115.8 1.5 %unpack.2 = (f32[2,560,128]{2,1,0:T(8,128)}, f32[2,128,512]{2,1,0:T(8,128)}, f32[2,512,128]{2,1,0:T(8,128)}, f32[2,128,512]{2,1,0:T(8,128)}, f32[2,512,128]{2,1,...) custom-call(bf16[4,240,128]{2,1,0:T(8,128)(2,1)S(1)} %get-tuple-element.150.refs_0_, ...), custom_call_target="tpu_custom_call" | custom-call | flops 1600000000 | bytes 2000000 | tf_op jit(solution)/shard_map/unpack/pallas_call | solution.py:665
  117.3 1.3 %collective-permute-done.32.refs_3_ = bf16[4,240,128]{2,1,0:T(8,128)(2,1)S(1)} collective-permute-done((bf16[4,240,128]{2,1,0:T(8,128)(2,1)S(1)}, bf16[4,240,128]{2,1,0:T(8,128)(2,1)S(1)}, u32[]{:S(2)}, u32[]{:S(2)}) %collective-permute-start.32) | collective-permute-done | bytes 245792 | tf_op jit(solution)/shard_map/ppermute | solution.py:60
  118.6 2.5 %collective-permute-done.31.refs_2_ = bf16[4,240,128]{2,1,0:T(8,128)(2,1)S(1)} collective-permute-done((bf16[4,240,128]{2,1,0:T(8,128)(2,1)S(1)}, bf16[4,240,128]{2,1,0:T(8,128)(2,1)S(1)}, u32[]{:S(2)}, u32[]{:S(2)}) %collective-permute-start.31) | collective-permute-done | bytes 245792 | tf_op jit(solution)/shard_map/ppermute | solution.py:60
  121.1 1.5 %unpack.3 = (f32[2,560,128]{2,1,0:T(8,128)}, f32[2,128,512]{2,1,0:T(8,128)}, f32[2,512,128]{2,1,0:T(8,128)}, f32[2,128,512]{2,1,0:T(8,128)}, f32[2,512,128]{2,1,...) custom-call(bf16[4,240,128]{2,1,0:T(8,128)(2,1)S(1)} %get-tuple-elem, ...), custom_call_target="tpu_custom_call", output_to_operand_aliasing={{0}: (4, {}), {1}: (5, {}), {2}: (6, {}), {3}: (7, {}), {4}... | custom-call | flops 1600000000 | bytes 2000000 | tf_op jit(solution)/shard_map/unpack/pallas_call | solution.py:665
  (36 shorter events, 0.8 us)
Async XLA Ops:
  2.3 6.5 %collective-permute-start.1 = (bf16[960,128]{1,0:T(8,128)(2,1)}, bf16[960,128]{1,0:T(8,128)(2,1)S(1)}, u32[]{:S(2)}, u32[]{:S(2)}) collective-permute-start(bf16[960,128]{1,0:T(8,128)(2,1)} %pack_quarter.1), channel_id=1, source_target_pairs={{0,2},{1,19},{4,6},{5,23},{8,10},{9,27},{12,14},{13,31},{2,0},{3,1... | collective-permute-start | bytes 737288 | tf_op jit(solution)/shard_map/ppermute | solution.py:60
  7.3 16.7 %copy-start.4 = (s32[768]{0:T(1024)S(1)}, s32[768]{0:T(1024)}, u32[]{:S(2)}) copy-start(s32[768]{0:T(1024)} %param.12) | copy-start | bytes 9220
  7.3 18.4 %copy-start = (bf16[2,3840,128]{2,1,0:T(8,128)(2,1)S(1)}, bf16[2,3840,128]{2,1,0:T(8,128)(2,1)}, u32[]{:S(2)}) copy-start(bf16[2,3840,128]{2,1,0:T(8,128)(2,1)} %get-tuple-element.95.s0) | copy-start | bytes 5898244
  7.3 18.4 %copy-start.1 = (bf16[768,336]{0,1:T(8,128)(2,1)S(1)}, bf16[768,336]{0,1:T(8,128)(2,1)}, u32[]{:S(2)}) copy-start(bf16[768,336]{0,1:T(8,128)(2,1)} %param.11) | copy-start | bytes 1548292
  8.8 14.3 %collective-permute-start.2 = (bf16[3840,128]{1,0:T(8,128)(2,1)}, bf16[3840,128]{1,0:T(8,128)(2,1)S(1)}, u32[]{:S(2)}, u32[]{:S(2)}) collective-permute-start(bf16[3840,128]{1,0:T(8,128)(2,1)} %get-tuple-element.98), channel_id=1, source_target_pairs={{0,2},{1,19},{4,6},{5,23},{8,10},{9,27},{12,14},{13,31},{2,0},{3,1... | collective-permute-start | bytes 2949128 | tf_op jit(solution)/shard_map/ppermute | solution.py:60
  10.4 13.6 %collective-permute-start = (bf16[2,3840,128]{2,1,0:T(8,128)(2,1)}, bf16[2,3840,128]{2,1,0:T(8,128)(2,1)S(1)}, u32[]{:S(2)}, u32[]{:S(2)}) collective-permute-start(bf16[2,3840,128]{2,1,0:T(8,128)(2,1)} %get-tuple-element.95.s0), channel_id=1, source_target_pairs={{0,1},{1,0},{4,5},{5,4},{8,9},{9,8},{12,13},{13,12},{2,3},{3,2},{6... | collective-permute-start | bytes 5898248 | tf_op jit(solution)/shard_map/ppermute | solution.py:60
  11.3 7.7 %collective-permute-start.5 = (bf16[960,128]{1,0:T(8,128)(2,1)S(1)}, bf16[960,128]{1,0:T(8,128)(2,1)S(1)}, u32[]{:S(2)}, u32[]{:S(2)}) collective-permute-start(bf16[960,128]{1,0:T(8,128)(2,1)S(1)} %collective-permute-done.1.q0), channel_id=1, source_target_pairs={{0,64},{1,9},{4,68},{5,13},{8,72},{9,1},{12,76},{13,5},{2,66},{3,1... | collective-permute-start | bytes 737288 | tf_op jit(solution)/shard_map/ppermute | solution.py:60
  14.5 7.4 %collective-permute-start.4 = (bf16[960,128]{1,0:T(8,128)(2,1)S(1)}, bf16[960,128]{1,0:T(8,128)(2,1)S(1)}, u32[]{:S(2)}, u32[]{:S(2)}) collective-permute-start(bf16[960,128]{1,0:T(8,128)(2,1)S(1)} %collective-permute-done.1.q0), channel_id=1, source_target_pairs={{0,96},{1,13},{4,100},{5,9},{8,104},{9,5},{12,108},{13,1},{2,98},{... | collective-permute-start | bytes 737288 | tf_op jit(solution)/shard_map/ppermute | solution.py:60
  15.5 6.4 %collective-permute-start.3 = (bf16[960,128]{1,0:T(8,128)(2,1)S(1)}, bf16[960,128]{1,0:T(8,128)(2,1)S(1)}, u32[]{:S(2)}, u32[]{:S(2)}) collective-permute-start(bf16[960,128]{1,0:T(8,128)(2,1)S(1)} %collective-permute-done.1.q0), channel_id=1, source_target_pairs={{0,32},{1,5},{4,36},{5,1},{8,40},{9,13},{12,44},{13,9},{2,34},{3,7... | collective-permute-start | bytes 737288 | tf_op jit(solution)/shard_map/ppermute | solution.py:60
  23.1 2.6 %collective-permute-start.6 = (bf16[3840,128]{1,0:T(8,128)(2,1)S(1)}, bf16[3840,128]{1,0:T(8,128)(2,1)S(1)}, u32[]{:S(2)}, u32[]{:S(2)}) collective-permute-start(bf16[3840,128]{1,0:T(8,128)(2,1)S(1)} %collective-permute-done.2.s2), channel_id=1, source_target_pairs={{0,1},{1,0},{4,5},{5,4},{8,9},{9,8},{12,13},{13,12},{2,3},{3,2},{6... | collective-permute-start | bytes 2949128 | tf_op jit(solution)/shard_map/ppermute | solution.py:60
  23.2 6.6 %collective-permute-start.7 = (bf16[3840,128]{1,0:T(8,128)(2,1)S(1)}, bf16[3840,128]{1,0:T(8,128)(2,1)S(1)}, u32[]{:S(2)}, u32[]{:S(2)}) collective-permute-start(bf16[3840,128]{1,0:T(8,128)(2,1)S(1)} %join.1.s2), channel_id=1, source_target_pairs={{0,1},{1,0},{4,5},{5,4},{8,9},{9,8},{12,13},{13,12},{2,3},{3,2},{6... | collective-permute-start | bytes 2949128 | tf_op jit(solution)/shard_map/ppermute | solution.py:60
  25.7 4.2 %copy-start.2 = (bf16[768,336]{0,1:T(8,128)(2,1)S(1)}, bf16[768,336]{0,1:T(8,128)(2,1)}, u32[]{:S(2)}) copy-start(bf16[768,336]{0,1:T(8,128)(2,1)} %param.21) | copy-start | bytes 1548292
  25.7 4.2 %copy-start.3 = (bf16[768,48]{0,1:T(8,128)(2,1)S(1)}, bf16[768,48]{0,1:T(8,128)(2,1)}, u32[]{:S(2)}) copy-start(bf16[768,48]{0,1:T(8,128)(2,1)} %param.20) | copy-start | bytes 221188
  40.4 4.4 %collective-permute-start.9 = (bf16[2,3840,128]{2,1,0:T(8,128)(2,1)S(1)}, bf16[2,3840,128]{2,1,0:T(8,128)(2,1)S(1)}, u32[]{:S(2)}, u32[]{:S(2)}) collective-permute-start(bf16[2,3840,128]{2,1,0:T(8,128)(2,1)S(1)} %get-tuple-element.118), channel_id=1, source_target_pairs={{0,1},{1,0},{4,5},{5,4},{8,9},{9,8},{12,13},{13,12},{2,3},{3,2},{6... | collective-permute-start | bytes 5898248 | tf_op jit(solution)/shard_map/ppermute | solution.py:60
  44.4 5.1 %collective-permute-start.8 = (bf16[2,2176,128]{2,1,0:T(8,128)(2,1)S(1)}, bf16[2,2176,128]{2,1,0:T(8,128)(2,1)S(1)}, u32[]{:S(2)}, u32[]{:S(2)}) collective-permute-start(bf16[2,2176,128]{2,1,0:T(8,128)(2,1)S(1)} %get-tuple-element.115), channel_id=1, source_target_pairs={{0,1},{1,0},{4,5},{5,4},{8,9},{9,8},{12,13},{13,12},{2,3},{3,2},{6... | collective-permute-start | bytes 3342344 | tf_op jit(solution)/shard_map/ppermute | solution.py:60
  46.0 12.5 %collective-permute-start.10 = (bf16[2,960,128]{2,1,0:T(8,128)(2,1)S(1)}, bf16[2,960,128]{2,1,0:T(8,128)(2,1)S(1)}, u32[]{:S(2)}, u32[]{:S(2)}) collective-permute-start(bf16[2,960,128]{2,1,0:T(8,128)(2,1)S(1)} %get-tuple-element.121), channel_id=1, source_target_pairs={{0,64},{1,9},{4,68},{5,13},{8,72},{9,1},{12,76},{13,5},{2,66},{3,1... | collective-permute-start | bytes 1474568 | tf_op jit(solution)/shard_map/ppermute | solution.py:60
  49.7 11.0 %collective-permute-start.13 = (bf16[2048,128]{1,0:T(8,128)(2,1)S(1)}, bf16[2048,128]{1,0:T(8,128)(2,1)S(1)}, u32[]{:S(2)}, u32[]{:S(2)}) collective-permute-start(bf16[2048,128]{1,0:T(8,128)(2,1)S(1)} %get-tuple-element.131), channel_id=1, source_target_pairs={{0,2},{1,19},{4,6},{5,23},{8,10},{9,27},{12,14},{13,31},{2,0},{3,1... | collective-permute-start | bytes 1572872 | tf_op jit(solution)/shard_map/ppermute | solution.py:60
  55.5 5.3 %collective-permute-start.11 = (bf16[1584,128]{1,0:T(8,128)(2,1)S(1)}, bf16[1584,128]{1,0:T(8,128)(2,1)S(1)}, u32[]{:S(2)}, u32[]{:S(2)}) collective-permute-start(bf16[1584,128]{1,0:T(8,128)(2,1)S(1)} %get-tuple-element.127), channel_id=1, source_target_pairs={{0,1},{1,0},{4,5},{5,4},{8,9},{9,8},{12,13},{13,12},{2,3},{3,2},{6... | collective-permute-start | bytes 1216520 | tf_op jit(solution)/shard_map/ppermute | solution.py:60
  56.9 3.9 %collective-permute-start.12 = (bf16[1584,128]{1,0:T(8,128)(2,1)S(1)}, bf16[1584,128]{1,0:T(8,128)(2,1)S(1)}, u32[]{:S(2)}, u32[]{:S(2)}) collective-permute-start(bf16[1584,128]{1,0:T(8,128)(2,1)S(1)} %get-tuple-element.128), channel_id=1, source_target_pairs={{0,1},{1,0},{4,5},{5,4},{8,9},{9,8},{12,13},{13,12},{2,3},{3,2},{6... | collective-permute-start | bytes 1216520 | tf_op jit(solution)/shard_map/ppermute | solution.py:60
  56.9 8.8 %collective-permute-start.17 = (bf16[2,960,128]{2,1,0:T(8,128)(2,1)S(1)}, bf16[2,960,128]{2,1,0:T(8,128)(2,1)S(1)}, u32[]{:S(2)}, u32[]{:S(2)}) collective-permute-start(bf16[2,960,128]{2,1,0:T(8,128)(2,1)S(1)} %get-tuple-element.119), channel_id=1, source_target_pairs={{0,32},{1,5},{4,36},{5,1},{8,40},{9,13},{12,44},{13,9},{2,34},{3,7... | collective-permute-start | bytes 1474568 | tf_op jit(solution)/shard_map/ppermute | solution.py:60
  58.5 10.0 %collective-permute-start.18 = (bf16[2,960,128]{2,1,0:T(8,128)(2,1)S(1)}, bf16[2,960,128]{2,1,0:T(8,128)(2,1)S(1)}, u32[]{:S(2)}, u32[]{:S(2)}) collective-permute-start(bf16[2,960,128]{2,1,0:T(8,128)(2,1)S(1)} %get-tuple-element.120), channel_id=1, source_target_pairs={{0,96},{1,13},{4,100},{5,9},{8,104},{9,5},{12,108},{13,1},{2,98},{... | collective-permute-start | bytes 1474568 | tf_op jit(solution)/shard_map/ppermute | solution.py:60
  61.5 13.6 %collective-permute-start.14 = (bf16[1408,128]{1,0:T(8,128)(2,1)S(1)}, bf16[1408,128]{1,0:T(8,128)(2,1)S(1)}, u32[]{:S(2)}, u32[]{:S(2)}) collective-permute-start(bf16[1408,128]{1,0:T(8,128)(2,1)S(1)} %get-tuple-element.133), channel_id=1, source_target_pairs={{0,32},{1,5},{4,36},{5,1},{8,40},{9,13},{12,44},{13,9},{2,34},{3,7... | collective-permute-start | bytes 1081352 | tf_op jit(solution)/shard_map/ppermute | solution.py:60
  62.3 14.0 %collective-permute-start.15 = (bf16[1408,128]{1,0:T(8,128)(2,1)S(1)}, bf16[1408,128]{1,0:T(8,128)(2,1)S(1)}, u32[]{:S(2)}, u32[]{:S(2)}) collective-permute-start(bf16[1408,128]{1,0:T(8,128)(2,1)S(1)} %get-tuple-element.134), channel_id=1, source_target_pairs={{0,96},{1,13},{4,100},{5,9},{8,104},{9,5},{12,108},{13,1},{2,98},{... | collective-permute-start | bytes 1081352 | tf_op jit(solution)/shard_map/ppermute | solution.py:60
  63.5 12.8 %collective-permute-start.16 = (bf16[1408,128]{1,0:T(8,128)(2,1)S(1)}, bf16[1408,128]{1,0:T(8,128)(2,1)S(1)}, u32[]{:S(2)}, u32[]{:S(2)}) collective-permute-start(bf16[1408,128]{1,0:T(8,128)(2,1)S(1)} %get-tuple-element.135), channel_id=1, source_target_pairs={{0,64},{1,9},{4,68},{5,13},{8,72},{9,1},{12,76},{13,5},{2,66},{3,1... | collective-permute-start | bytes 1081352 | tf_op jit(solution)/shard_map/ppermute | solution.py:60
  68.8 6.3 %collective-permute-start.19 = (bf16[960,128]{1,0:T(8,128)(2,1)S(1)}, bf16[960,128]{1,0:T(8,128)(2,1)S(1)}, u32[]{:S(2)}, u32[]{:S(2)}) collective-permute-start(bf16[960,128]{1,0:T(8,128)(2,1)S(1)} %get-tuple-element.139), channel_id=1, source_target_pairs={{0,2},{1,19},{4,6},{5,23},{8,10},{9,27},{12,14},{13,31},{2,0},{3,1... | collective-permute-start | bytes 737288 | tf_op jit(solution)/shard_map/ppermute | solution.py:60
  76.8 5.3 %collective-permute-start.20 = (bf16[592,128]{1,0:T(8,128)(2,1)S(1)}, bf16[592,128]{1,0:T(8,128)(2,1)S(1)}, u32[]{:S(2)}, u32[]{:S(2)}) collective-permute-start(bf16[592,128]{1,0:T(8,128)(2,1)S(1)} %get-tuple-element.141), channel_id=1, source_target_pairs={{0,4},{1,33},{4,0},{5,37},{8,12},{9,41},{12,8},{13,45},{2,6},{3,35... | collective-permute-start | bytes 454664 | tf_op jit(solution)/shard_map/ppermute | solution.py:60
  77.9 6.4 %collective-permute-start.21 = (bf16[592,128]{1,0:T(8,128)(2,1)S(1)}, bf16[592,128]{1,0:T(8,128)(2,1)S(1)}, u32[]{:S(2)}, u32[]{:S(2)}) collective-permute-start(bf16[592,128]{1,0:T(8,128)(2,1)S(1)} %get-tuple-element.142), channel_id=1, source_target_pairs={{0,12},{1,97},{4,8},{5,101},{8,4},{9,105},{12,0},{13,109},{2,14},{... | collective-permute-start | bytes 454664 | tf_op jit(solution)/shard_map/ppermute | solution.py:60
  79.6 6.7 %collective-permute-start.22 = (bf16[592,128]{1,0:T(8,128)(2,1)S(1)}, bf16[592,128]{1,0:T(8,128)(2,1)S(1)}, u32[]{:S(2)}, u32[]{:S(2)}) collective-permute-start(bf16[592,128]{1,0:T(8,128)(2,1)S(1)} %get-tuple-element.143), channel_id=1, source_target_pairs={{0,8},{1,65},{4,12},{5,69},{8,0},{9,73},{12,4},{13,77},{2,10},{3,6... | collective-permute-start | bytes 454664 | tf_op jit(solution)/shard_map/ppermute | solution.py:60
  86.3 8.6 %collective-permute-start.23 = (bf16[2,240,128]{2,1,0:T(8,128)(2,1)S(1)}, bf16[2,240,128]{2,1,0:T(8,128)(2,1)S(1)}, u32[]{:S(2)}, u32[]{:S(2)}) collective-permute-start(bf16[2,240,128]{2,1,0:T(8,128)(2,1)S(1)} %get-tuple-element.144.near), channel_id=1, source_target_pairs={{0,16},{1,17},{4,20},{5,21},{8,24},{9,25},{12,28},{13,29},{2,18},{... | collective-permute-start | bytes 368648 | tf_op jit(solution)/shard_map/ppermute | solution.py:60
  89.2 3.9 %collective-permute-start.25 = (bf16[112,128]{1,0:T(8,128)(2,1)S(1)}, bf16[112,128]{1,0:T(8,128)(2,1)S(1)}, u32[]{:S(2)}, u32[]{:S(2)}) collective-permute-start(bf16[112,128]{1,0:T(8,128)(2,1)S(1)} %get-tuple-element.145), channel_id=1, source_target_pairs={{0,2},{1,3},{4,6},{5,7},{8,10},{9,11},{12,14},{13,15},{2,0},{3,1},... | collective-permute-start | bytes 86024 | tf_op jit(solution)/shard_map/ppermute | solution.py:60
  89.8 5.1 %collective-permute-start.24 = (bf16[112,128]{1,0:T(8,128)(2,1)S(1)}, bf16[112,128]{1,0:T(8,128)(2,1)S(1)}, u32[]{:S(2)}, u32[]{:S(2)}) collective-permute-start(bf16[112,128]{1,0:T(8,128)(2,1)S(1)} %get-tuple-element.145), channel_id=1, source_target_pairs={{0,18},{1,19},{4,22},{5,23},{8,26},{9,27},{12,30},{13,31},{2,16},{... | collective-permute-start | bytes 86024 | tf_op jit(solution)/shard_map/ppermute | solution.py:60
  95.0 6.5 %collective-permute-start.28 = (bf16[2,240,128]{2,1,0:T(8,128)(2,1)S(1)}, bf16[2,240,128]{2,1,0:T(8,128)(2,1)S(1)}, u32[]{:S(2)}, u32[]{:S(2)}) collective-permute-start(bf16[2,240,128]{2,1,0:T(8,128)(2,1)S(1)} %across.1.refs_0_), channel_id=1, source_target_pairs={{0,8},{1,65},{4,12},{5,69},{8,0},{9,73},{12,4},{13,77},{2,10},{3,6... | collective-permute-start | bytes 368648 | tf_op jit(solution)/shard_map/ppermute | solution.py:60
  96.2 6.5 %collective-permute-start.27 = (bf16[2,240,128]{2,1,0:T(8,128)(2,1)S(1)}, bf16[2,240,128]{2,1,0:T(8,128)(2,1)S(1)}, u32[]{:S(2)}, u32[]{:S(2)}) collective-permute-start(bf16[2,240,128]{2,1,0:T(8,128)(2,1)S(1)} %across.1.refs_0_), channel_id=1, source_target_pairs={{0,12},{1,97},{4,8},{5,101},{8,4},{9,105},{12,0},{13,109},{2,14},{... | collective-permute-start | bytes 368648 | tf_op jit(solution)/shard_map/ppermute | solution.py:60
  98.7 4.9 %collective-permute-start.26 = (bf16[2,240,128]{2,1,0:T(8,128)(2,1)S(1)}, bf16[2,240,128]{2,1,0:T(8,128)(2,1)S(1)}, u32[]{:S(2)}, u32[]{:S(2)}) collective-permute-start(bf16[2,240,128]{2,1,0:T(8,128)(2,1)S(1)} %across.1.refs_0_), channel_id=1, source_target_pairs={{0,4},{1,33},{4,0},{5,37},{8,12},{9,41},{12,8},{13,45},{2,6},{3,35... | collective-permute-start | bytes 368648 | tf_op jit(solution)/shard_map/ppermute | solution.py:60
  103.6 1.2 %collective-permute-start.29 = (bf16[16,128]{1,0:T(8,128)(2,1)S(1)}, bf16[16,128]{1,0:T(8,128)(2,1)S(1)}, u32[]{:S(2)}, u32[]{:S(2)}) collective-permute-start(bf16[16,128]{1,0:T(8,128)(2,1)S(1)} %get-tuple-element.148), channel_id=1, source_target_pairs={{0,1},{1,0},{4,5},{5,4},{8,9},{9,8},{12,13},{13,12},{2,3},{3,2},{6... | collective-permute-start | bytes 12296 | tf_op jit(solution)/shard_map/ppermute | solution.py:60
  104.9 7.9 %collective-permute-start.35 = (bf16[4,240,128]{2,1,0:T(8,128)(2,1)S(1)}, bf16[4,240,128]{2,1,0:T(8,128)(2,1)S(1)}, u32[]{:S(2)}, u32[]{:S(2)}) collective-permute-start(bf16[4,240,128]{2,1,0:T(8,128)(2,1)S(1)} %get-tuple-element.150.refs_0_), channel_id=1, source_target_pairs={{0,64},{1,9},{4,68},{5,13},{8,72},{9,1},{12,76},{13,5},{2,66},{3,1... | collective-permute-start | bytes 737288 | tf_op jit(solution)/shard_map/ppermute | solution.py:60
  107.0 8.3 %collective-permute-start.34 = (bf16[4,240,128]{2,1,0:T(8,128)(2,1)S(1)}, bf16[4,240,128]{2,1,0:T(8,128)(2,1)S(1)}, u32[]{:S(2)}, u32[]{:S(2)}) collective-permute-start(bf16[4,240,128]{2,1,0:T(8,128)(2,1)S(1)} %get-tuple-element.150.refs_0_), channel_id=1, source_target_pairs={{0,96},{1,13},{4,100},{5,9},{8,104},{9,5},{12,108},{13,1},{2,98},{... | collective-permute-start | bytes 737288 | tf_op jit(solution)/shard_map/ppermute | solution.py:60
  108.1 7.7 %collective-permute-start.33 = (bf16[4,240,128]{2,1,0:T(8,128)(2,1)S(1)}, bf16[4,240,128]{2,1,0:T(8,128)(2,1)S(1)}, u32[]{:S(2)}, u32[]{:S(2)}) collective-permute-start(bf16[4,240,128]{2,1,0:T(8,128)(2,1)S(1)} %get-tuple-element.150.refs_0_), channel_id=1, source_target_pairs={{0,32},{1,5},{4,36},{5,1},{8,40},{9,13},{12,44},{13,9},{2,34},{3,7... | collective-permute-start | bytes 737288 | tf_op jit(solution)/shard_map/ppermute | solution.py:60
  108.9 9.6 %collective-permute-start.32 = (bf16[4,240,128]{2,1,0:T(8,128)(2,1)S(1)}, bf16[4,240,128]{2,1,0:T(8,128)(2,1)S(1)}, u32[]{:S(2)}, u32[]{:S(2)}) collective-permute-start(bf16[4,240,128]{2,1,0:T(8,128)(2,1)S(1)} %get-tuple-element.149.refs_0_), channel_id=1, source_target_pairs={{0,64},{1,9},{4,68},{5,13},{8,72},{9,1},{12,76},{13,5},{2,66},{3,1... | collective-permute-start | bytes 737288 | tf_op jit(solution)/shard_map/ppermute | solution.py:60
  111.7 9.4 %collective-permute-start.31 = (bf16[4,240,128]{2,1,0:T(8,128)(2,1)S(1)}, bf16[4,240,128]{2,1,0:T(8,128)(2,1)S(1)}, u32[]{:S(2)}, u32[]{:S(2)}) collective-permute-start(bf16[4,240,128]{2,1,0:T(8,128)(2,1)S(1)} %get-tuple-element.149.refs_0_), channel_id=1, source_target_pairs={{0,96},{1,13},{4,100},{5,9},{8,104},{9,5},{12,108},{13,1},{2,98},{... | collective-permute-start | bytes 737288 | tf_op jit(solution)/shard_map/ppermute | solution.py:60
  112.8 8.3 %collective-permute-start.30 = (bf16[4,240,128]{2,1,0:T(8,128)(2,1)S(1)}, bf16[4,240,128]{2,1,0:T(8,128)(2,1)S(1)}, u32[]{:S(2)}, u32[]{:S(2)}) collective-permute-start(bf16[4,240,128]{2,1,0:T(8,128)(2,1)S(1)} %get-tuple-element.149.refs_0_), channel_id=1, source_target_pairs={{0,32},{1,5},{4,36},{5,1},{8,40},{9,13},{12,44},{13,9},{2,34},{3,7... | collective-permute-start | bytes 737288 | tf_op jit(solution)/shard_map/ppermute | solution.py:60

commit v6 on v5

--- a/solution.py
+++ b/solution.py
@@ -14,6 +14,7 @@
 ENTRY, SECOND, THIRD, FOURTH, BACK, FORE, BASIS, USED = 0, 560, 1072, 1584, 2096, 2608, 3120, 3760
 PACK = 3840
 PEERS = (1, 3, 2)
+SECOND_STEP = (2, 3, 1)
 EARLY, EARLY_PACK, LATE = 1712, 1792, 2048
 EARLY_CHUNK, LATE_CHUNK = EARLY_PACK // 4, LATE // 4
 EARLY_PIECE, LATE_PIECE = EARLY_PACK // 16, LATE // 16
@@ -376,13 +377,11 @@
     steep[...] = jnp.where(look_mask(labels), g, 0.0)
 
 
-def cut_kernel(mine, got, *refs):
-    outs, whole = refs[:4], refs[4]
+def cut_kernel(mine, got, *outs):
     i1, _ = places()
-    whole[...] = (mine[...].astype(F32) + got[...].astype(F32)).astype(BF)
     for bits, out in zip((*PEERS, 0), outs):
-        begin = pl.multiple_of((i1 ^ bits) * CHUNK, CHUNK)
-        out[...] = whole[:, pl.ds(begin, CHUNK), :]
+        rows = pl.ds(pl.multiple_of((i1 ^ bits) * CHUNK, CHUNK), CHUNK)
+        out[...] = (mine[:, rows, :].astype(F32) + got[:, rows, :].astype(F32)).astype(BF)
 
 
 def fold_heads_kernel(mine, got, near, rest, far):
@@ -423,7 +422,7 @@
     _, i2 = places()
     one[...] = total((own, a, b, c))
     two[...] = (near[...].astype(F32) + came[...].astype(F32)).astype(BF)
-    for bits, out in zip((*PEERS, 0), outs):
+    for bits, out in zip((*SECOND_STEP, 0), outs):
         at = 0
         for ref, base, count in (
             (one, 0, EARLY_PIECE),
@@ -605,7 +604,7 @@
             1,
         )(*args)
 
-    *out2, own2 = small(cut_kernel, "cut_two", [(2, CHUNK)] * 4, mine2, got2, scratch=[vmem(2, PACK, 128)])
+    *out2, own2 = small(cut_kernel, "cut_two", [(2, CHUNK)] * 4, mine2, got2)
     got2 = [send(part, to_first(a)) for part, a in zip(out2, PEERS)]
     near1, rest1, far1 = small(
         fold_heads_kernel, "fold_heads", [(TOP,), (EARLY - FOURTH,), (LATE,)], mine1a, got1a
@@ -648,7 +647,7 @@
         send(far2, to_x_by_core()),
         scratch=[vmem(2 * EARLY_CHUNK + LATE_CHUNK, 128), vmem(CHUNK, 128)],
     )
-    got = [send(part, to_second(b)) for part, b in zip(out, PEERS)]
+    got = [send(part, to_second(b)) for part, b in zip(out, SECOND_STEP)]
     near, far = small(sum_kernel, "sums", [(2, PIECE), (EARLY_PIECE,)], own, *got)
     x1, x3 = send(far, to_x(1)), send(far, to_x(3))
     got = [send(near, to_x(2)), x3, x1]

time: 123 us -> 121 us (0.984)
  transfers between devices with their start and end apart: 36 -> 36, of which waited for: 23 -> 23; matrix products, arithmetic and copies ran while one was open for 0% -> 0% of each run, Pallas kernels for 16% -> 15%
where the time goes in v6:
time: 121 us
  starting transfers between devices  44.7 us (37%)
  waiting for transfers between devices  41.9 us (35%)
  Pallas kernels  33 us (27%)
    ppermute x36, starting transfers between devices, send(): return lax.ppermute(values, ('dp', 'mp'), where)  44.7 us
    ppermute x36, waiting for transfers between devices, send(): return lax.ppermute(values, ('dp', 'mp'), where)  41.9 us
    pallas_call x1, Pallas kernels, shards(): call(second_kernel, 'block_two', [IN_VMEM] * 9, [(shape(336, ROWS), IN_VM...  10.5 us
    pallas_call x1, Pallas kernels, shards(): call(fourth_kernel, 'backward_one_layers', [IN_VMEM] * 10, [(shape(336, R...  4.16 us
    pallas_call x1, Pallas kernels, shards(): call(first_kernel, 'forward_one', [IN_VMEM] * 6, [(shape(336, ROWS), IN_V...  4.13 us
    pallas_call x1, Pallas kernels, shards(): call(third_kernel, 'backward_one_heads', [IN_VMEM] * 10, [(shape(512, ROW...  3.76 us
    pallas_call x1, Pallas kernels, shards(): call(pack_kernel, 'pack', [IN_VMEM] * 7, [(shape(2, PACK, 128, kind=BF),...  3.33 us
    pallas_call x2, Pallas kernels, shards(): call(functools.partial(unpack_kernel, k), 'unpack', [IN_VMEM] * 4 + [ANYW...  3.03 us
  transfers between devices with their start and end apart: 36, of which 23 were waited for; matrix products, arithmetic and copies ran while one was open for 0% of the time, Pallas kernels for 15%

profile of v6, /device:TPU:0, one launch (start us, length us, event | category | flops | bytes accessed | tf_op | source)
XLA Modules:
  0.0 120.7 jit_solution(12669038736293854082)
XLA Ops:
  0.6 1.7 %pack_quarter.1 = bf16[960,128]{1,0:T(8,128)(2,1)} custom-call(bf16[2,560,128]{2,1,0:T(8,128)(2,1)} %refs_0_.2, bf16[2,128,512]{2,1,0:T(8,128)(2,1)} %refs_1_.2, bf16[2,512,128]{2,1,0:T(8,128)(2,1)} %refs_2_.2, bf16[2,128,512]{2,1,0:T(8,128)(2,1)} %refs_3_.2, bf16[2,512,128]{2,1,0:T(8,128)(2,1)} %refs_4_.2, bf16[2,512,128]{2,1,0:T(8,128)(2,1)} %refs_5_.2, ...), custom_call_target="tpu_custom_call" | custom-call | flops 800000000 | bytes 1000000 | tf_op jit(solution)/shard_map/pack_quarter/pallas_call | solution.py:536
  2.3 1.7 %collective-permute-start.1 = (bf16[960,128]{1,0:T(8,128)(2,1)}, bf16[960,128]{1,0:T(8,128)(2,1)S(1)}, u32[]{:S(2)}, u32[]{:S(2)}) collective-permute-start(bf16[960,128]{1,0:T(8,128)(2,1)} %pack_quarter.1), channel_id=1, source_target_pairs={{0,2},{1,19},{4,6},{5,23},{8,10},{9,27},{12,14},{13,31},{2,0},{3,1... | collective-permute-start | bytes 737288 | tf_op jit(solution)/shard_map/ppermute | solution.py:61
  4.0 3.3 %pack.1 = (bf16[2,3840,128]{2,1,0:T(8,128)(2,1)}, bf16[3840,128]{1,0:T(8,128)(2,1)}) custom-call(bf16[2,560,128]{2,1,0:T(8,128)(2,1)} %refs_0_.2, bf16[2,128,512]{2,1,0:T(8,128)(2,1)} %refs_1_.2, bf16[2,512,128]{2,1,0:T(8,128)(2,1)} %refs_2_.2, bf16[2,128,512]{2,1,0:T(8,128)(2,1)} %refs_3_.2, bf16[2,512,128]{2,1,0:T(8,128)(2,1)} %refs_4_.2, ...), custom_call_target="tpu_custom_call" | custom-call | flops 2400000000 | bytes 3000000 | tf_op jit(solution)/shard_map/pack/pallas_call | solution.py:546
  7.3 1.5 %collective-permute-done.1.q0 = bf16[960,128]{1,0:T(8,128)(2,1)S(1)} collective-permute-done((bf16[960,128]{1,0:T(8,128)(2,1)}, bf16[960,128]{1,0:T(8,128)(2,1)S(1)}, u32[]{:S(2)}, u32[]{:S(2)}) %collective-permute-start.1) | collective-permute-done | bytes 245792 | tf_op jit(solution)/shard_map/ppermute | solution.py:61
  8.8 1.6 %collective-permute-start.2 = (bf16[3840,128]{1,0:T(8,128)(2,1)}, bf16[3840,128]{1,0:T(8,128)(2,1)S(1)}, u32[]{:S(2)}, u32[]{:S(2)}) collective-permute-start(bf16[3840,128]{1,0:T(8,128)(2,1)} %get-tuple-element.98), channel_id=1, source_target_pairs={{0,2},{1,19},{4,6},{5,23},{8,10},{9,27},{12,14},{13,31},{2,0},{3,1... | collective-permute-start | bytes 2949128 | tf_op jit(solution)/shard_map/ppermute | solution.py:61
  10.4 0.9 collective-permute-start
  11.3 3.2 %collective-permute-start.5 = (bf16[960,128]{1,0:T(8,128)(2,1)S(1)}, bf16[960,128]{1,0:T(8,128)(2,1)S(1)}, u32[]{:S(2)}, u32[]{:S(2)}) collective-permute-start(bf16[960,128]{1,0:T(8,128)(2,1)S(1)} %collective-permute-done.1.q0), channel_id=1, source_target_pairs={{0,64},{1,9},{4,68},{5,13},{8,72},{9,1},{12,76},{13,5},{2,66},{3,1... | collective-permute-start | bytes 737288 | tf_op jit(solution)/shard_map/ppermute | solution.py:61
  14.5 1.1 collective-permute-start.4
  15.5 3.4 %collective-permute-done.5.q3 = bf16[960,128]{1,0:T(8,128)(2,1)S(1)} collective-permute-done((bf16[960,128]{1,0:T(8,128)(2,1)S(1)}, bf16[960,128]{1,0:T(8,128)(2,1)S(1)}, u32[]{:S(2)}, u32[]{:S(2)}) %collective-permute-start.5) | collective-permute-done | bytes 245792 | tf_op jit(solution)/shard_map/ppermute | solution.py:61
  19.0 2.9 %collective-permute-done.4.q2 = bf16[960,128]{1,0:T(8,128)(2,1)S(1)} collective-permute-done((bf16[960,128]{1,0:T(8,128)(2,1)S(1)}, bf16[960,128]{1,0:T(8,128)(2,1)S(1)}, u32[]{:S(2)}, u32[]{:S(2)}) %collective-permute-start.4) | collective-permute-done | bytes 245792 | tf_op jit(solution)/shard_map/ppermute | solution.py:61
  22.0 1.2 collective-permute-done.2.s2
  23.2 0.8 collective-permute-start.7
  24.0 1.7 %collective-permute-done.6.s3 = bf16[3840,128]{1,0:T(8,128)(2,1)S(1)} collective-permute-done((bf16[3840,128]{1,0:T(8,128)(2,1)S(1)}, bf16[3840,128]{1,0:T(8,128)(2,1)S(1)}, u32[]{:S(2)}, u32[]{:S(2)}) %collective-permute-start.6) | collective-permute-done | bytes 983072 | tf_op jit(solution)/shard_map/ppermute | solution.py:61
  25.7 4.1 %forward_one.1 = (f32[336,768]{1,0:T(8,128)S(1)}, f32[48,768]{1,0:T(8,128)S(1)}, bf16[560,768]{1,0:T(8,128)(2,1)S(1)}, bf16[4,512,768]{2,1,0:T(8,128)(2,1)S(1)},...) custom-call(s32[1,768]{1,0:T(1,128)S(1)} %broadcast_in_dim.3.label, bf16[336,768]{1,0:T(8,128)(2,1)S(1)} %bitcast.6, ...), custom_call_target="tpu_custom_call" | custom-call | flops 4800000000 | bytes 6000000 | tf_op jit(solution)/shard_map/forward_one/pallas_call | solution.py:564
  29.9 10.5 %block_two.1 = (f32[336,768]{1,0:T(8,128)}, f32[48,768]{1,0:T(8,128)}, f32[336,768]{1,0:T(8,128)S(1)}, bf16[2,3840,128]{2,1,0:T(8,128)(2,1)S(1)}, bf16[2,3840,128]{2,1,0:T(8,128)(2,1)S(1)}) custom-call(s32[1,768]{1,0:T(1,128)S(1)} %broadcast_in_dim.3.label, f32[336,768]{1,0:T(8,128)S(1)} %get-tuple-element.101.state_in, ...), custom_call_target="tpu_custom_call" | custom-call | flops 11200000000 | bytes 14000000 | tf_op jit(solution)/shard_map/block_two/pallas_call | solution.py:574
  40.4 0.2 collective-permute-start.9
  40.6 3.8 %backward_one_heads.1 = (bf16[512,768]{1,0:T(8,128)(2,1)S(1)}, bf16[2,2176,128]{2,1,0:T(8,128)(2,1)S(1)}, bf16[2,2176,128]{2,1,0:T(8,128)(2,1)S(1)}) custom-call(s32[1,768]{1,0:T(1,128)S(1)} %broadcast_in_dim.3.label, f32[336,768]{1,0:T(8,128)S(1)} %get-tuple-element.109.g_in, bf16[48,768]{1,0:T(8,128)(2,1)S(1)} %bitcast.9, ...), custom_call_target="tpu_custom_call" | custom-call | flops 4800000000 | bytes 6000000 | tf_op jit(solution)/shard_map/backward_one_heads/pallas_call | solution.py:585
  44.4 0.5 collective-permute-start.8
  44.8 0.4 cut_two.1
  45.3 3.5 %collective-permute-start.10 = (bf16[2,960,128]{2,1,0:T(8,128)(2,1)S(1)}, bf16[2,960,128]{2,1,0:T(8,128)(2,1)S(1)}, u32[]{:S(2)}, u32[]{:S(2)}) collective-permute-start(bf16[2,960,128]{2,1,0:T(8,128)(2,1)S(1)} %get-tuple-element.121), channel_id=1, source_target_pairs={{0,64},{1,9},{4,68},{5,13},{8,72},{9,1},{12,76},{13,5},{2,66},{3,1... | collective-permute-start | bytes 1474568 | tf_op jit(solution)/shard_map/ppermute | solution.py:61
  48.8 0.3 fold_heads.1
  49.0 1.6 %collective-permute-start.13 = (bf16[2048,128]{1,0:T(8,128)(2,1)S(1)}, bf16[2048,128]{1,0:T(8,128)(2,1)S(1)}, u32[]{:S(2)}, u32[]{:S(2)}) collective-permute-start(bf16[2048,128]{1,0:T(8,128)(2,1)S(1)} %get-tuple-element.131), channel_id=1, source_target_pairs={{0,2},{1,19},{4,6},{5,23},{8,10},{9,27},{12,14},{13,31},{2,0},{3,1... | collective-permute-start | bytes 1572872 | tf_op jit(solution)/shard_map/ppermute | solution.py:61
  50.6 4.2 %backward_one_layers.1 = (f32[336,768]{1,0:T(8,128)}, bf16[2,1584,128]{2,1,0:T(8,128)(2,1)S(1)}, bf16[1584,128]{1,0:T(8,128)(2,1)S(1)}, bf16[1584,128]{1,0:T(8,128)(2,1)S(1)}) custom-call(s32[1,768]{1,0:T(1,128)S(1)} %broadcast_in_dim.3.label, f32[336,768]{1,0:T(8,128)S(1)} %get-tuple-element.109.g_in, bf16[512,768]{1,0:T(8,128)(2,1)S(1)} %get-tuple-element.122.d_in, ...), custom_call_target="tpu_custom_call" | custom-call | flops 4800000000 | bytes 6000000 | tf_op jit(solution)/shard_map/backward_one_layers/pallas_call | solution.py:614
  54.7 1.4 %collective-permute-start.11 = (bf16[1584,128]{1,0:T(8,128)(2,1)S(1)}, bf16[1584,128]{1,0:T(8,128)(2,1)S(1)}, u32[]{:S(2)}, u32[]{:S(2)}) collective-permute-start(bf16[1584,128]{1,0:T(8,128)(2,1)S(1)} %get-tuple-element.127), channel_id=1, source_target_pairs={{0,1},{1,0},{4,5},{5,4},{8,9},{9,8},{12,13},{13,12},{2,3},{3,2},{6... | collective-permute-start | bytes 1216520 | tf_op jit(solution)/shard_map/ppermute | solution.py:61
  56.2 1.6 %collective-permute-start.17 = (bf16[2,960,128]{2,1,0:T(8,128)(2,1)S(1)}, bf16[2,960,128]{2,1,0:T(8,128)(2,1)S(1)}, u32[]{:S(2)}, u32[]{:S(2)}) collective-permute-start(bf16[2,960,128]{2,1,0:T(8,128)(2,1)S(1)} %get-tuple-element.119), channel_id=1, source_target_pairs={{0,32},{1,5},{4,36},{5,1},{8,40},{9,13},{12,44},{13,9},{2,34},{3,7... | collective-permute-start | bytes 1474568 | tf_op jit(solution)/shard_map/ppermute | solution.py:61
  57.8 2.2 %collective-permute-start.18 = (bf16[2,960,128]{2,1,0:T(8,128)(2,1)S(1)}, bf16[2,960,128]{2,1,0:T(8,128)(2,1)S(1)}, u32[]{:S(2)}, u32[]{:S(2)}) collective-permute-start(bf16[2,960,128]{2,1,0:T(8,128)(2,1)S(1)} %get-tuple-element.120), channel_id=1, source_target_pairs={{0,96},{1,13},{4,100},{5,9},{8,104},{9,5},{12,108},{13,1},{2,98},{... | collective-permute-start | bytes 1474568 | tf_op jit(solution)/shard_map/ppermute | solution.py:61
  60.0 0.7 cut_one.1
  60.7 0.8 collective-permute-start.14
  61.6 1.2 collective-permute-start.15
  62.7 2.2 %collective-permute-start.16 = (bf16[1408,128]{1,0:T(8,128)(2,1)S(1)}, bf16[1408,128]{1,0:T(8,128)(2,1)S(1)}, u32[]{:S(2)}, u32[]{:S(2)}) collective-permute-start(bf16[1408,128]{1,0:T(8,128)(2,1)S(1)} %get-tuple-element.135), channel_id=1, source_target_pairs={{0,64},{1,9},{4,68},{5,13},{8,72},{9,1},{12,76},{13,5},{2,66},{3,1... | collective-permute-start | bytes 1081352 | tf_op jit(solution)/shard_map/ppermute | solution.py:61
  65.0 2.8 %collective-permute-done.18.b = bf16[2,960,128]{2,1,0:T(8,128)(2,1)S(1)} collective-permute-done((bf16[2,960,128]{2,1,0:T(8,128)(2,1)S(1)}, bf16[2,960,128]{2,1,0:T(8,128)(2,1)S(1)}, u32[]{:S(2)}, u32[]{:S(2)}) %collective-permute-start.18) | collective-permute-done | bytes 491552 | tf_op jit(solution)/shard_map/ppermute | solution.py:61
  67.8 0.2 fold.1
  68.1 0.6 collective-permute-start.19
  68.6 6.0 %collective-permute-done.19.came = bf16[960,128]{1,0:T(8,128)(2,1)S(1)} collective-permute-done((bf16[960,128]{1,0:T(8,128)(2,1)S(1)}, bf16[960,128]{1,0:T(8,128)(2,1)S(1)}, u32[]{:S(2)}, u32[]{:S(2)}) %collective-permute-start.19) | collective-permute-done | bytes 245792 | tf_op jit(solution)/shard_map/ppermute | solution.py:61
  74.6 0.9 collective-permute-done.15.b
  75.5 0.5 pieces.1
  76.1 2.4 %collective-permute-start.20 = (bf16[592,128]{1,0:T(8,128)(2,1)S(1)}, bf16[592,128]{1,0:T(8,128)(2,1)S(1)}, u32[]{:S(2)}, u32[]{:S(2)}) collective-permute-start(bf16[592,128]{1,0:T(8,128)(2,1)S(1)} %get-tuple-element.141), channel_id=1, source_target_pairs={{0,8},{1,65},{4,12},{5,69},{8,0},{9,73},{12,4},{13,77},{2,10},{3,6... | collective-permute-start | bytes 454664 | tf_op jit(solution)/shard_map/ppermute | solution.py:61
  78.5 1.3 %collective-permute-start.21 = (bf16[592,128]{1,0:T(8,128)(2,1)S(1)}, bf16[592,128]{1,0:T(8,128)(2,1)S(1)}, u32[]{:S(2)}, u32[]{:S(2)}) collective-permute-start(bf16[592,128]{1,0:T(8,128)(2,1)S(1)} %get-tuple-element.142), channel_id=1, source_target_pairs={{0,12},{1,97},{4,8},{5,101},{8,4},{9,105},{12,0},{13,109},{2,14},{... | collective-permute-start | bytes 454664 | tf_op jit(solution)/shard_map/ppermute | solution.py:61
  79.9 3.0 %collective-permute-done.20.a = bf16[592,128]{1,0:T(8,128)(2,1)S(1)} collective-permute-done((bf16[592,128]{1,0:T(8,128)(2,1)S(1)}, bf16[592,128]{1,0:T(8,128)(2,1)S(1)}, u32[]{:S(2)}, u32[]{:S(2)}) %collective-permute-start.20) | collective-permute-done | bytes 151584 | tf_op jit(solution)/shard_map/ppermute | solution.py:61
  82.9 2.1 %collective-permute-done.21.b = bf16[592,128]{1,0:T(8,128)(2,1)S(1)} collective-permute-done((bf16[592,128]{1,0:T(8,128)(2,1)S(1)}, bf16[592,128]{1,0:T(8,128)(2,1)S(1)}, u32[]{:S(2)}, u32[]{:S(2)}) %collective-permute-start.21) | collective-permute-done | bytes 151584 | tf_op jit(solution)/shard_map/ppermute | solution.py:61
  84.9 0.1 collective-permute-done.22.c
  85.1 2.5 %collective-permute-start.23 = (bf16[2,240,128]{2,1,0:T(8,128)(2,1)S(1)}, bf16[2,240,128]{2,1,0:T(8,128)(2,1)S(1)}, u32[]{:S(2)}, u32[]{:S(2)}) collective-permute-start(bf16[2,240,128]{2,1,0:T(8,128)(2,1)S(1)} %get-tuple-element.144.near), channel_id=1, source_target_pairs={{0,16},{1,17},{4,20},{5,21},{8,24},{9,25},{12,28},{13,29},{2,18},{... | collective-permute-start | bytes 368648 | tf_op jit(solution)/shard_map/ppermute | solution.py:61
  87.7 0.6 collective-permute-start.25
  88.2 1.1 collective-permute-start.24
  89.3 2.2 %collective-permute-done.25.c = bf16[112,128]{1,0:T(8,128)(2,1)S(1)} collective-permute-done((bf16[112,128]{1,0:T(8,128)(2,1)S(1)}, bf16[112,128]{1,0:T(8,128)(2,1)S(1)}, u32[]{:S(2)}, u32[]{:S(2)}) %collective-permute-start.25) | collective-permute-done | bytes 28704 | tf_op jit(solution)/shard_map/ppermute | solution.py:61
  91.5 1.8 %collective-permute-done.24.b = bf16[112,128]{1,0:T(8,128)(2,1)S(1)} collective-permute-done((bf16[112,128]{1,0:T(8,128)(2,1)S(1)}, bf16[112,128]{1,0:T(8,128)(2,1)S(1)}, u32[]{:S(2)}, u32[]{:S(2)}) %collective-permute-start.24) | collective-permute-done | bytes 28704 | tf_op jit(solution)/shard_map/ppermute | solution.py:61
  93.4 1.9 %collective-permute-start.28 = (bf16[2,240,128]{2,1,0:T(8,128)(2,1)S(1)}, bf16[2,240,128]{2,1,0:T(8,128)(2,1)S(1)}, u32[]{:S(2)}, u32[]{:S(2)}) collective-permute-start(bf16[2,240,128]{2,1,0:T(8,128)(2,1)S(1)} %across.1.refs_0_), channel_id=1, source_target_pairs={{0,8},{1,65},{4,12},{5,69},{8,0},{9,73},{12,4},{13,77},{2,10},{3,6... | collective-permute-start | bytes 368648 | tf_op jit(solution)/shard_map/ppermute | solution.py:61
  95.3 1.3 %collective-permute-start.27 = (bf16[2,240,128]{2,1,0:T(8,128)(2,1)S(1)}, bf16[2,240,128]{2,1,0:T(8,128)(2,1)S(1)}, u32[]{:S(2)}, u32[]{:S(2)}) collective-permute-start(bf16[2,240,128]{2,1,0:T(8,128)(2,1)S(1)} %across.1.refs_0_), channel_id=1, source_target_pairs={{0,12},{1,97},{4,8},{5,101},{8,4},{9,105},{12,0},{13,109},{2,14},{... | collective-permute-start | bytes 368648 | tf_op jit(solution)/shard_map/ppermute | solution.py:61
  96.6 0.4 collective-permute-start.26
  96.9 2.9 %collective-permute-done.28.refs_3_ = bf16[2,240,128]{2,1,0:T(8,128)(2,1)S(1)} collective-permute-done((bf16[2,240,128]{2,1,0:T(8,128)(2,1)S(1)}, bf16[2,240,128]{2,1,0:T(8,128)(2,1)S(1)}, u32[]{:S(2)}, u32[]{:S(2)}) %collective-permute-start.28) | collective-permute-done | bytes 122912 | tf_op jit(solution)/shard_map/ppermute | solution.py:61
  99.8 1.6 %collective-permute-done.27.refs_2_ = bf16[2,240,128]{2,1,0:T(8,128)(2,1)S(1)} collective-permute-done((bf16[2,240,128]{2,1,0:T(8,128)(2,1)S(1)}, bf16[2,240,128]{2,1,0:T(8,128)(2,1)S(1)}, u32[]{:S(2)}, u32[]{:S(2)}) %collective-permute-start.27) | collective-permute-done | bytes 122912 | tf_op jit(solution)/shard_map/ppermute | solution.py:61
  101.6 1.2 collective-permute-done.29.refs_4_.refs_11_
  102.7 2.1 %collective-permute-start.35 = (bf16[4,240,128]{2,1,0:T(8,128)(2,1)S(1)}, bf16[4,240,128]{2,1,0:T(8,128)(2,1)S(1)}, u32[]{:S(2)}, u32[]{:S(2)}) collective-permute-start(bf16[4,240,128]{2,1,0:T(8,128)(2,1)S(1)} %get-tuple-element.150.refs_0_), channel_id=1, source_target_pairs={{0,64},{1,9},{4,68},{5,13},{8,72},{9,1},{12,76},{13,5},{2,66},{3,1... | collective-permute-start | bytes 737288 | tf_op jit(solution)/shard_map/ppermute | solution.py:61
  104.8 1.1 collective-permute-start.34
  105.9 0.9 collective-permute-start.33
  106.8 2.7 %collective-permute-start.32 = (bf16[4,240,128]{2,1,0:T(8,128)(2,1)S(1)}, bf16[4,240,128]{2,1,0:T(8,128)(2,1)S(1)}, u32[]{:S(2)}, u32[]{:S(2)}) collective-permute-start(bf16[4,240,128]{2,1,0:T(8,128)(2,1)S(1)} %get-tuple-element.149.refs_0_), channel_id=1, source_target_pairs={{0,64},{1,9},{4,68},{5,13},{8,72},{9,1},{12,76},{13,5},{2,66},{3,1... | collective-permute-start | bytes 737288 | tf_op jit(solution)/shard_map/ppermute | solution.py:61
  109.5 1.1 collective-permute-start.31
  110.6 0.4 collective-permute-start.30
  111.0 2.1 %collective-permute-done.34.refs_2_ = bf16[4,240,128]{2,1,0:T(8,128)(2,1)S(1)} collective-permute-done((bf16[4,240,128]{2,1,0:T(8,128)(2,1)S(1)}, bf16[4,240,128]{2,1,0:T(8,128)(2,1)S(1)}, u32[]{:S(2)}, u32[]{:S(2)}) %collective-permute-start.34) | collective-permute-done | bytes 245792 | tf_op jit(solution)/shard_map/ppermute | solution.py:61
  113.1 0.6 collective-permute-done.33.refs_1_
  113.6 1.5 %unpack.2 = (f32[2,560,128]{2,1,0:T(8,128)}, f32[2,128,512]{2,1,0:T(8,128)}, f32[2,512,128]{2,1,0:T(8,128)}, f32[2,128,512]{2,1,0:T(8,128)}, f32[2,512,128]{2,1,...) custom-call(bf16[4,240,128]{2,1,0:T(8,128)(2,1)S(1)} %get-tuple-element.150.refs_0_, ...), custom_call_target="tpu_custom_call" | custom-call | flops 1600000000 | bytes 2000000 | tf_op jit(solution)/shard_map/unpack/pallas_call | solution.py:664
  115.2 1.3 %collective-permute-done.32.refs_3_ = bf16[4,240,128]{2,1,0:T(8,128)(2,1)S(1)} collective-permute-done((bf16[4,240,128]{2,1,0:T(8,128)(2,1)S(1)}, bf16[4,240,128]{2,1,0:T(8,128)(2,1)S(1)}, u32[]{:S(2)}, u32[]{:S(2)}) %collective-permute-start.32) | collective-permute-done | bytes 245792 | tf_op jit(solution)/shard_map/ppermute | solution.py:61
  116.4 2.5 %collective-permute-done.31.refs_2_ = bf16[4,240,128]{2,1,0:T(8,128)(2,1)S(1)} collective-permute-done((bf16[4,240,128]{2,1,0:T(8,128)(2,1)S(1)}, bf16[4,240,128]{2,1,0:T(8,128)(2,1)S(1)}, u32[]{:S(2)}, u32[]{:S(2)}) %collective-permute-start.31) | collective-permute-done | bytes 245792 | tf_op jit(solution)/shard_map/ppermute | solution.py:61
  118.9 1.5 %unpack.3 = (f32[2,560,128]{2,1,0:T(8,128)}, f32[2,128,512]{2,1,0:T(8,128)}, f32[2,512,128]{2,1,0:T(8,128)}, f32[2,128,512]{2,1,0:T(8,128)}, f32[2,512,128]{2,1,...) custom-call(bf16[4,240,128]{2,1,0:T(8,128)(2,1)S(1)} %get-tuple-elem, ...), custom_call_target="tpu_custom_call", output_to_operand_aliasing={{0}: (4, {}), {1}: (5, {}), {2}: (6, {}), {3}: (7, {}), {4}... | custom-call | flops 1600000000 | bytes 2000000 | tf_op jit(solution)/shard_map/unpack/pallas_call | solution.py:664
  (36 shorter events, 0.6 us)
Async XLA Ops:
  2.3 6.5 %collective-permute-start.1 = (bf16[960,128]{1,0:T(8,128)(2,1)}, bf16[960,128]{1,0:T(8,128)(2,1)S(1)}, u32[]{:S(2)}, u32[]{:S(2)}) collective-permute-start(bf16[960,128]{1,0:T(8,128)(2,1)} %pack_quarter.1), channel_id=1, source_target_pairs={{0,2},{1,19},{4,6},{5,23},{8,10},{9,27},{12,14},{13,31},{2,0},{3,1... | collective-permute-start | bytes 737288 | tf_op jit(solution)/shard_map/ppermute | solution.py:61
  7.3 16.7 %copy-start.4 = (s32[768]{0:T(1024)S(1)}, s32[768]{0:T(1024)}, u32[]{:S(2)}) copy-start(s32[768]{0:T(1024)} %param.12) | copy-start | bytes 9220
  7.3 18.4 %copy-start = (bf16[2,3840,128]{2,1,0:T(8,128)(2,1)S(1)}, bf16[2,3840,128]{2,1,0:T(8,128)(2,1)}, u32[]{:S(2)}) copy-start(bf16[2,3840,128]{2,1,0:T(8,128)(2,1)} %get-tuple-element.95.s0) | copy-start | bytes 5898244
  7.3 18.4 %copy-start.1 = (bf16[768,336]{0,1:T(8,128)(2,1)S(1)}, bf16[768,336]{0,1:T(8,128)(2,1)}, u32[]{:S(2)}) copy-start(bf16[768,336]{0,1:T(8,128)(2,1)} %param.11) | copy-start | bytes 1548292
  8.8 14.3 %collective-permute-start.2 = (bf16[3840,128]{1,0:T(8,128)(2,1)}, bf16[3840,128]{1,0:T(8,128)(2,1)S(1)}, u32[]{:S(2)}, u32[]{:S(2)}) collective-permute-start(bf16[3840,128]{1,0:T(8,128)(2,1)} %get-tuple-element.98), channel_id=1, source_target_pairs={{0,2},{1,19},{4,6},{5,23},{8,10},{9,27},{12,14},{13,31},{2,0},{3,1... | collective-permute-start | bytes 2949128 | tf_op jit(solution)/shard_map/ppermute | solution.py:61
  10.4 13.6 %collective-permute-start = (bf16[2,3840,128]{2,1,0:T(8,128)(2,1)}, bf16[2,3840,128]{2,1,0:T(8,128)(2,1)S(1)}, u32[]{:S(2)}, u32[]{:S(2)}) collective-permute-start(bf16[2,3840,128]{2,1,0:T(8,128)(2,1)} %get-tuple-element.95.s0), channel_id=1, source_target_pairs={{0,1},{1,0},{4,5},{5,4},{8,9},{9,8},{12,13},{13,12},{2,3},{3,2},{6... | collective-permute-start | bytes 5898248 | tf_op jit(solution)/shard_map/ppermute | solution.py:61
  11.3 7.7 %collective-permute-start.5 = (bf16[960,128]{1,0:T(8,128)(2,1)S(1)}, bf16[960,128]{1,0:T(8,128)(2,1)S(1)}, u32[]{:S(2)}, u32[]{:S(2)}) collective-permute-start(bf16[960,128]{1,0:T(8,128)(2,1)S(1)} %collective-permute-done.1.q0), channel_id=1, source_target_pairs={{0,64},{1,9},{4,68},{5,13},{8,72},{9,1},{12,76},{13,5},{2,66},{3,1... | collective-permute-start | bytes 737288 | tf_op jit(solution)/shard_map/ppermute | solution.py:61
  14.5 7.4 %collective-permute-start.4 = (bf16[960,128]{1,0:T(8,128)(2,1)S(1)}, bf16[960,128]{1,0:T(8,128)(2,1)S(1)}, u32[]{:S(2)}, u32[]{:S(2)}) collective-permute-start(bf16[960,128]{1,0:T(8,128)(2,1)S(1)} %collective-permute-done.1.q0), channel_id=1, source_target_pairs={{0,96},{1,13},{4,100},{5,9},{8,104},{9,5},{12,108},{13,1},{2,98},{... | collective-permute-start | bytes 737288 | tf_op jit(solution)/shard_map/ppermute | solution.py:61
  15.5 6.4 %collective-permute-start.3 = (bf16[960,128]{1,0:T(8,128)(2,1)S(1)}, bf16[960,128]{1,0:T(8,128)(2,1)S(1)}, u32[]{:S(2)}, u32[]{:S(2)}) collective-permute-start(bf16[960,128]{1,0:T(8,128)(2,1)S(1)} %collective-permute-done.1.q0), channel_id=1, source_target_pairs={{0,32},{1,5},{4,36},{5,1},{8,40},{9,13},{12,44},{13,9},{2,34},{3,7... | collective-permute-start | bytes 737288 | tf_op jit(solution)/shard_map/ppermute | solution.py:61
  23.1 2.6 %collective-permute-start.6 = (bf16[3840,128]{1,0:T(8,128)(2,1)S(1)}, bf16[3840,128]{1,0:T(8,128)(2,1)S(1)}, u32[]{:S(2)}, u32[]{:S(2)}) collective-permute-start(bf16[3840,128]{1,0:T(8,128)(2,1)S(1)} %collective-permute-done.2.s2), channel_id=1, source_target_pairs={{0,1},{1,0},{4,5},{5,4},{8,9},{9,8},{12,13},{13,12},{2,3},{3,2},{6... | collective-permute-start | bytes 2949128 | tf_op jit(solution)/shard_map/ppermute | solution.py:61
  23.2 6.6 %collective-permute-start.7 = (bf16[3840,128]{1,0:T(8,128)(2,1)S(1)}, bf16[3840,128]{1,0:T(8,128)(2,1)S(1)}, u32[]{:S(2)}, u32[]{:S(2)}) collective-permute-start(bf16[3840,128]{1,0:T(8,128)(2,1)S(1)} %join.1.s2), channel_id=1, source_target_pairs={{0,1},{1,0},{4,5},{5,4},{8,9},{9,8},{12,13},{13,12},{2,3},{3,2},{6... | collective-permute-start | bytes 2949128 | tf_op jit(solution)/shard_map/ppermute | solution.py:61
  25.7 4.2 %copy-start.2 = (bf16[768,336]{0,1:T(8,128)(2,1)S(1)}, bf16[768,336]{0,1:T(8,128)(2,1)}, u32[]{:S(2)}) copy-start(bf16[768,336]{0,1:T(8,128)(2,1)} %param.21) | copy-start | bytes 1548292
  25.7 4.2 %copy-start.3 = (bf16[768,48]{0,1:T(8,128)(2,1)S(1)}, bf16[768,48]{0,1:T(8,128)(2,1)}, u32[]{:S(2)}) copy-start(bf16[768,48]{0,1:T(8,128)(2,1)} %param.20) | copy-start | bytes 221188
  40.4 4.4 %collective-permute-start.9 = (bf16[2,3840,128]{2,1,0:T(8,128)(2,1)S(1)}, bf16[2,3840,128]{2,1,0:T(8,128)(2,1)S(1)}, u32[]{:S(2)}, u32[]{:S(2)}) collective-permute-start(bf16[2,3840,128]{2,1,0:T(8,128)(2,1)S(1)} %get-tuple-element.118), channel_id=1, source_target_pairs={{0,1},{1,0},{4,5},{5,4},{8,9},{9,8},{12,13},{13,12},{2,3},{3,2},{6... | collective-permute-start | bytes 5898248 | tf_op jit(solution)/shard_map/ppermute | solution.py:61
  44.4 4.4 %collective-permute-start.8 = (bf16[2,2176,128]{2,1,0:T(8,128)(2,1)S(1)}, bf16[2,2176,128]{2,1,0:T(8,128)(2,1)S(1)}, u32[]{:S(2)}, u32[]{:S(2)}) collective-permute-start(bf16[2,2176,128]{2,1,0:T(8,128)(2,1)S(1)} %get-tuple-element.115), channel_id=1, source_target_pairs={{0,1},{1,0},{4,5},{5,4},{8,9},{9,8},{12,13},{13,12},{2,3},{3,2},{6... | collective-permute-start | bytes 3342344 | tf_op jit(solution)/shard_map/ppermute | solution.py:61
  45.3 12.5 %collective-permute-start.10 = (bf16[2,960,128]{2,1,0:T(8,128)(2,1)S(1)}, bf16[2,960,128]{2,1,0:T(8,128)(2,1)S(1)}, u32[]{:S(2)}, u32[]{:S(2)}) collective-permute-start(bf16[2,960,128]{2,1,0:T(8,128)(2,1)S(1)} %get-tuple-element.121), channel_id=1, source_target_pairs={{0,64},{1,9},{4,68},{5,13},{8,72},{9,1},{12,76},{13,5},{2,66},{3,1... | collective-permute-start | bytes 1474568 | tf_op jit(solution)/shard_map/ppermute | solution.py:61
  49.0 11.0 %collective-permute-start.13 = (bf16[2048,128]{1,0:T(8,128)(2,1)S(1)}, bf16[2048,128]{1,0:T(8,128)(2,1)S(1)}, u32[]{:S(2)}, u32[]{:S(2)}) collective-permute-start(bf16[2048,128]{1,0:T(8,128)(2,1)S(1)} %get-tuple-element.131), channel_id=1, source_target_pairs={{0,2},{1,19},{4,6},{5,23},{8,10},{9,27},{12,14},{13,31},{2,0},{3,1... | collective-permute-start | bytes 1572872 | tf_op jit(solution)/shard_map/ppermute | solution.py:61
  54.7 5.3 %collective-permute-start.11 = (bf16[1584,128]{1,0:T(8,128)(2,1)S(1)}, bf16[1584,128]{1,0:T(8,128)(2,1)S(1)}, u32[]{:S(2)}, u32[]{:S(2)}) collective-permute-start(bf16[1584,128]{1,0:T(8,128)(2,1)S(1)} %get-tuple-element.127), channel_id=1, source_target_pairs={{0,1},{1,0},{4,5},{5,4},{8,9},{9,8},{12,13},{13,12},{2,3},{3,2},{6... | collective-permute-start | bytes 1216520 | tf_op jit(solution)/shard_map/ppermute | solution.py:61
  56.2 3.9 %collective-permute-start.12 = (bf16[1584,128]{1,0:T(8,128)(2,1)S(1)}, bf16[1584,128]{1,0:T(8,128)(2,1)S(1)}, u32[]{:S(2)}, u32[]{:S(2)}) collective-permute-start(bf16[1584,128]{1,0:T(8,128)(2,1)S(1)} %get-tuple-element.128), channel_id=1, source_target_pairs={{0,1},{1,0},{4,5},{5,4},{8,9},{9,8},{12,13},{13,12},{2,3},{3,2},{6... | collective-permute-start | bytes 1216520 | tf_op jit(solution)/shard_map/ppermute | solution.py:61
  56.2 8.8 %collective-permute-start.17 = (bf16[2,960,128]{2,1,0:T(8,128)(2,1)S(1)}, bf16[2,960,128]{2,1,0:T(8,128)(2,1)S(1)}, u32[]{:S(2)}, u32[]{:S(2)}) collective-permute-start(bf16[2,960,128]{2,1,0:T(8,128)(2,1)S(1)} %get-tuple-element.119), channel_id=1, source_target_pairs={{0,32},{1,5},{4,36},{5,1},{8,40},{9,13},{12,44},{13,9},{2,34},{3,7... | collective-permute-start | bytes 1474568 | tf_op jit(solution)/shard_map/ppermute | solution.py:61
  57.8 10.0 %collective-permute-start.18 = (bf16[2,960,128]{2,1,0:T(8,128)(2,1)S(1)}, bf16[2,960,128]{2,1,0:T(8,128)(2,1)S(1)}, u32[]{:S(2)}, u32[]{:S(2)}) collective-permute-start(bf16[2,960,128]{2,1,0:T(8,128)(2,1)S(1)} %get-tuple-element.120), channel_id=1, source_target_pairs={{0,96},{1,13},{4,100},{5,9},{8,104},{9,5},{12,108},{13,1},{2,98},{... | collective-permute-start | bytes 1474568 | tf_op jit(solution)/shard_map/ppermute | solution.py:61
  60.7 13.9 %collective-permute-start.14 = (bf16[1408,128]{1,0:T(8,128)(2,1)S(1)}, bf16[1408,128]{1,0:T(8,128)(2,1)S(1)}, u32[]{:S(2)}, u32[]{:S(2)}) collective-permute-start(bf16[1408,128]{1,0:T(8,128)(2,1)S(1)} %get-tuple-element.133), channel_id=1, source_target_pairs={{0,32},{1,5},{4,36},{5,1},{8,40},{9,13},{12,44},{13,9},{2,34},{3,7... | collective-permute-start | bytes 1081352 | tf_op jit(solution)/shard_map/ppermute | solution.py:61
  61.6 14.0 %collective-permute-start.15 = (bf16[1408,128]{1,0:T(8,128)(2,1)S(1)}, bf16[1408,128]{1,0:T(8,128)(2,1)S(1)}, u32[]{:S(2)}, u32[]{:S(2)}) collective-permute-start(bf16[1408,128]{1,0:T(8,128)(2,1)S(1)} %get-tuple-element.134), channel_id=1, source_target_pairs={{0,96},{1,13},{4,100},{5,9},{8,104},{9,5},{12,108},{13,1},{2,98},{... | collective-permute-start | bytes 1081352 | tf_op jit(solution)/shard_map/ppermute | solution.py:61
  62.7 12.8 %collective-permute-start.16 = (bf16[1408,128]{1,0:T(8,128)(2,1)S(1)}, bf16[1408,128]{1,0:T(8,128)(2,1)S(1)}, u32[]{:S(2)}, u32[]{:S(2)}) collective-permute-start(bf16[1408,128]{1,0:T(8,128)(2,1)S(1)} %get-tuple-element.135), channel_id=1, source_target_pairs={{0,64},{1,9},{4,68},{5,13},{8,72},{9,1},{12,76},{13,5},{2,66},{3,1... | collective-permute-start | bytes 1081352 | tf_op jit(solution)/shard_map/ppermute | solution.py:61
  68.1 6.5 %collective-permute-start.19 = (bf16[960,128]{1,0:T(8,128)(2,1)S(1)}, bf16[960,128]{1,0:T(8,128)(2,1)S(1)}, u32[]{:S(2)}, u32[]{:S(2)}) collective-permute-start(bf16[960,128]{1,0:T(8,128)(2,1)S(1)} %get-tuple-element.139), channel_id=1, source_target_pairs={{0,2},{1,19},{4,6},{5,23},{8,10},{9,27},{12,14},{13,31},{2,0},{3,1... | collective-permute-start | bytes 737288 | tf_op jit(solution)/shard_map/ppermute | solution.py:61
  76.1 6.8 %collective-permute-start.20 = (bf16[592,128]{1,0:T(8,128)(2,1)S(1)}, bf16[592,128]{1,0:T(8,128)(2,1)S(1)}, u32[]{:S(2)}, u32[]{:S(2)}) collective-permute-start(bf16[592,128]{1,0:T(8,128)(2,1)S(1)} %get-tuple-element.141), channel_id=1, source_target_pairs={{0,8},{1,65},{4,12},{5,69},{8,0},{9,73},{12,4},{13,77},{2,10},{3,6... | collective-permute-start | bytes 454664 | tf_op jit(solution)/shard_map/ppermute | solution.py:61
  78.5 6.4 %collective-permute-start.21 = (bf16[592,128]{1,0:T(8,128)(2,1)S(1)}, bf16[592,128]{1,0:T(8,128)(2,1)S(1)}, u32[]{:S(2)}, u32[]{:S(2)}) collective-permute-start(bf16[592,128]{1,0:T(8,128)(2,1)S(1)} %get-tuple-element.142), channel_id=1, source_target_pairs={{0,12},{1,97},{4,8},{5,101},{8,4},{9,105},{12,0},{13,109},{2,14},{... | collective-permute-start | bytes 454664 | tf_op jit(solution)/shard_map/ppermute | solution.py:61
  79.9 5.2 %collective-permute-start.22 = (bf16[592,128]{1,0:T(8,128)(2,1)S(1)}, bf16[592,128]{1,0:T(8,128)(2,1)S(1)}, u32[]{:S(2)}, u32[]{:S(2)}) collective-permute-start(bf16[592,128]{1,0:T(8,128)(2,1)S(1)} %get-tuple-element.143), channel_id=1, source_target_pairs={{0,4},{1,33},{4,0},{5,37},{8,12},{9,41},{12,8},{13,45},{2,6},{3,35... | collective-permute-start | bytes 454664 | tf_op jit(solution)/shard_map/ppermute | solution.py:61
  85.1 8.2 %collective-permute-start.23 = (bf16[2,240,128]{2,1,0:T(8,128)(2,1)S(1)}, bf16[2,240,128]{2,1,0:T(8,128)(2,1)S(1)}, u32[]{:S(2)}, u32[]{:S(2)}) collective-permute-start(bf16[2,240,128]{2,1,0:T(8,128)(2,1)S(1)} %get-tuple-element.144.near), channel_id=1, source_target_pairs={{0,16},{1,17},{4,20},{5,21},{8,24},{9,25},{12,28},{13,29},{2,18},{... | collective-permute-start | bytes 368648 | tf_op jit(solution)/shard_map/ppermute | solution.py:61
  87.7 3.9 %collective-permute-start.25 = (bf16[112,128]{1,0:T(8,128)(2,1)S(1)}, bf16[112,128]{1,0:T(8,128)(2,1)S(1)}, u32[]{:S(2)}, u32[]{:S(2)}) collective-permute-start(bf16[112,128]{1,0:T(8,128)(2,1)S(1)} %get-tuple-element.145), channel_id=1, source_target_pairs={{0,2},{1,3},{4,6},{5,7},{8,10},{9,11},{12,14},{13,15},{2,0},{3,1},... | collective-permute-start | bytes 86024 | tf_op jit(solution)/shard_map/ppermute | solution.py:61
  88.2 5.1 %collective-permute-start.24 = (bf16[112,128]{1,0:T(8,128)(2,1)S(1)}, bf16[112,128]{1,0:T(8,128)(2,1)S(1)}, u32[]{:S(2)}, u32[]{:S(2)}) collective-permute-start(bf16[112,128]{1,0:T(8,128)(2,1)S(1)} %get-tuple-element.145), channel_id=1, source_target_pairs={{0,18},{1,19},{4,22},{5,23},{8,26},{9,27},{12,30},{13,31},{2,16},{... | collective-permute-start | bytes 86024 | tf_op jit(solution)/shard_map/ppermute | solution.py:61
  93.4 6.5 %collective-permute-start.28 = (bf16[2,240,128]{2,1,0:T(8,128)(2,1)S(1)}, bf16[2,240,128]{2,1,0:T(8,128)(2,1)S(1)}, u32[]{:S(2)}, u32[]{:S(2)}) collective-permute-start(bf16[2,240,128]{2,1,0:T(8,128)(2,1)S(1)} %across.1.refs_0_), channel_id=1, source_target_pairs={{0,8},{1,65},{4,12},{5,69},{8,0},{9,73},{12,4},{13,77},{2,10},{3,6... | collective-permute-start | bytes 368648 | tf_op jit(solution)/shard_map/ppermute | solution.py:61
  95.3 6.1 %collective-permute-start.27 = (bf16[2,240,128]{2,1,0:T(8,128)(2,1)S(1)}, bf16[2,240,128]{2,1,0:T(8,128)(2,1)S(1)}, u32[]{:S(2)}, u32[]{:S(2)}) collective-permute-start(bf16[2,240,128]{2,1,0:T(8,128)(2,1)S(1)} %across.1.refs_0_), channel_id=1, source_target_pairs={{0,12},{1,97},{4,8},{5,101},{8,4},{9,105},{12,0},{13,109},{2,14},{... | collective-permute-start | bytes 368648 | tf_op jit(solution)/shard_map/ppermute | solution.py:61
  96.6 4.9 %collective-permute-start.26 = (bf16[2,240,128]{2,1,0:T(8,128)(2,1)S(1)}, bf16[2,240,128]{2,1,0:T(8,128)(2,1)S(1)}, u32[]{:S(2)}, u32[]{:S(2)}) collective-permute-start(bf16[2,240,128]{2,1,0:T(8,128)(2,1)S(1)} %across.1.refs_0_), channel_id=1, source_target_pairs={{0,4},{1,33},{4,0},{5,37},{8,12},{9,41},{12,8},{13,45},{2,6},{3,35... | collective-permute-start | bytes 368648 | tf_op jit(solution)/shard_map/ppermute | solution.py:61
  101.5 1.2 %collective-permute-start.29 = (bf16[16,128]{1,0:T(8,128)(2,1)S(1)}, bf16[16,128]{1,0:T(8,128)(2,1)S(1)}, u32[]{:S(2)}, u32[]{:S(2)}) collective-permute-start(bf16[16,128]{1,0:T(8,128)(2,1)S(1)} %get-tuple-element.148), channel_id=1, source_target_pairs={{0,1},{1,0},{4,5},{5,4},{8,9},{9,8},{12,13},{13,12},{2,3},{3,2},{6... | collective-permute-start | bytes 12296 | tf_op jit(solution)/shard_map/ppermute | solution.py:61
  102.7 7.9 %collective-permute-start.35 = (bf16[4,240,128]{2,1,0:T(8,128)(2,1)S(1)}, bf16[4,240,128]{2,1,0:T(8,128)(2,1)S(1)}, u32[]{:S(2)}, u32[]{:S(2)}) collective-permute-start(bf16[4,240,128]{2,1,0:T(8,128)(2,1)S(1)} %get-tuple-element.150.refs_0_), channel_id=1, source_target_pairs={{0,64},{1,9},{4,68},{5,13},{8,72},{9,1},{12,76},{13,5},{2,66},{3,1... | collective-permute-start | bytes 737288 | tf_op jit(solution)/shard_map/ppermute | solution.py:61
  104.8 8.3 %collective-permute-start.34 = (bf16[4,240,128]{2,1,0:T(8,128)(2,1)S(1)}, bf16[4,240,128]{2,1,0:T(8,128)(2,1)S(1)}, u32[]{:S(2)}, u32[]{:S(2)}) collective-permute-start(bf16[4,240,128]{2,1,0:T(8,128)(2,1)S(1)} %get-tuple-element.150.refs_0_), channel_id=1, source_target_pairs={{0,96},{1,13},{4,100},{5,9},{8,104},{9,5},{12,108},{13,1},{2,98},{... | collective-permute-start | bytes 737288 | tf_op jit(solution)/shard_map/ppermute | solution.py:61
  105.9 7.7 %collective-permute-start.33 = (bf16[4,240,128]{2,1,0:T(8,128)(2,1)S(1)}, bf16[4,240,128]{2,1,0:T(8,128)(2,1)S(1)}, u32[]{:S(2)}, u32[]{:S(2)}) collective-permute-start(bf16[4,240,128]{2,1,0:T(8,128)(2,1)S(1)} %get-tuple-element.150.refs_0_), channel_id=1, source_target_pairs={{0,32},{1,5},{4,36},{5,1},{8,40},{9,13},{12,44},{13,9},{2,34},{3,7... | collective-permute-start | bytes 737288 | tf_op jit(solution)/shard_map/ppermute | solution.py:61
  106.8 9.6 %collective-permute-start.32 = (bf16[4,240,128]{2,1,0:T(8,128)(2,1)S(1)}, bf16[4,240,128]{2,1,0:T(8,128)(2,1)S(1)}, u32[]{:S(2)}, u32[]{:S(2)}) collective-permute-start(bf16[4,240,128]{2,1,0:T(8,128)(2,1)S(1)} %get-tuple-element.149.refs_0_), channel_id=1, source_target_pairs={{0,64},{1,9},{4,68},{5,13},{8,72},{9,1},{12,76},{13,5},{2,66},{3,1... | collective-permute-start | bytes 737288 | tf_op jit(solution)/shard_map/ppermute | solution.py:61
  109.5 9.4 %collective-permute-start.31 = (bf16[4,240,128]{2,1,0:T(8,128)(2,1)S(1)}, bf16[4,240,128]{2,1,0:T(8,128)(2,1)S(1)}, u32[]{:S(2)}, u32[]{:S(2)}) collective-permute-start(bf16[4,240,128]{2,1,0:T(8,128)(2,1)S(1)} %get-tuple-element.149.refs_0_), channel_id=1, source_target_pairs={{0,96},{1,13},{4,100},{5,9},{8,104},{9,5},{12,108},{13,1},{2,98},{... | collective-permute-start | bytes 737288 | tf_op jit(solution)/shard_map/ppermute | solution.py:61
  110.6 8.3 %collective-permute-start.30 = (bf16[4,240,128]{2,1,0:T(8,128)(2,1)S(1)}, bf16[4,240,128]{2,1,0:T(8,128)(2,1)S(1)}, u32[]{:S(2)}, u32[]{:S(2)}) collective-permute-start(bf16[4,240,128]{2,1,0:T(8,128)(2,1)S(1)} %get-tuple-element.149.refs_0_), channel_id=1, source_target_pairs={{0,32},{1,5},{4,36},{5,1},{8,40},{9,13},{12,44},{13,9},{2,34},{3,7... | collective-permute-start | bytes 737288 | tf_op jit(solution)/shard_map/ppermute | solution.py:61

commit v7 on v6

--- a/solution.py
+++ b/solution.py
@@ -182,7 +182,7 @@
 
 
 def silu_both(pre):
-    s = 0.5 * jnp.tanh(0.5 * pre) + 0.5
+    s = jax.nn.sigmoid(pre)
     act = pre * s
     return act.astype(BF), (s + act * (1.0 - s)).astype(BF)
 

time: 121 us -> 120 us (level)
  no operation moved by 1% of the time
where the time goes in v7:
time: 120 us
  starting transfers between devices  44.7 us (37%)
  waiting for transfers between devices  41.9 us (35%)
  Pallas kernels  32.6 us (27%)
    ppermute x36, starting transfers between devices, send(): return lax.ppermute(values, ('dp', 'mp'), where)  44.7 us
    ppermute x36, waiting for transfers between devices, send(): return lax.ppermute(values, ('dp', 'mp'), where)  41.9 us
    pallas_call x1, Pallas kernels, shards(): call(second_kernel, 'block_two', [IN_VMEM] * 9, [(shape(336, ROWS), IN_VM...  10.5 us
    pallas_call x1, Pallas kernels, shards(): call(fourth_kernel, 'backward_one_layers', [IN_VMEM] * 10, [(shape(336, R...  4.16 us
    pallas_call x1, Pallas kernels, shards(): call(first_kernel, 'forward_one', [IN_VMEM] * 6, [(shape(336, ROWS), IN_V...  3.78 us
    pallas_call x1, Pallas kernels, shards(): call(third_kernel, 'backward_one_heads', [IN_VMEM] * 10, [(shape(512, ROW...  3.76 us
    pallas_call x1, Pallas kernels, shards(): call(pack_kernel, 'pack', [IN_VMEM] * 7, [(shape(2, PACK, 128, kind=BF),...  3.33 us
    pallas_call x2, Pallas kernels, shards(): call(functools.partial(unpack_kernel, k), 'unpack', [IN_VMEM] * 4 + [ANYW...  3.03 us
  transfers between devices with their start and end apart: 36, of which 23 were waited for; matrix products, arithmetic and copies ran while one was open for 0% of the time, Pallas kernels for 15%

profile of v7, /device:TPU:0, one launch (start us, length us, event | category | flops | bytes accessed | tf_op | source)
XLA Modules:
  0.0 120.3 jit_solution(4813939112755471146)
XLA Ops:
  0.6 1.7 %pack_quarter.1 = bf16[960,128]{1,0:T(8,128)(2,1)} custom-call(bf16[2,560,128]{2,1,0:T(8,128)(2,1)} %refs_0_.2, bf16[2,128,512]{2,1,0:T(8,128)(2,1)} %refs_1_.2, bf16[2,512,128]{2,1,0:T(8,128)(2,1)} %refs_2_.2, bf16[2,128,512]{2,1,0:T(8,128)(2,1)} %refs_3_.2, bf16[2,512,128]{2,1,0:T(8,128)(2,1)} %refs_4_.2, bf16[2,512,128]{2,1,0:T(8,128)(2,1)} %refs_5_.2, ...), custom_call_target="tpu_custom_call" | custom-call | flops 800000000 | bytes 1000000 | tf_op jit(solution)/shard_map/pack_quarter/pallas_call | solution.py:536
  2.3 1.7 %collective-permute-start.1 = (bf16[960,128]{1,0:T(8,128)(2,1)}, bf16[960,128]{1,0:T(8,128)(2,1)S(1)}, u32[]{:S(2)}, u32[]{:S(2)}) collective-permute-start(bf16[960,128]{1,0:T(8,128)(2,1)} %pack_quarter.1), channel_id=1, source_target_pairs={{0,2},{1,19},{4,6},{5,23},{8,10},{9,27},{12,14},{13,31},{2,0},{3,1... | collective-permute-start | bytes 737288 | tf_op jit(solution)/shard_map/ppermute | solution.py:61
  4.0 3.3 %pack.1 = (bf16[2,3840,128]{2,1,0:T(8,128)(2,1)}, bf16[3840,128]{1,0:T(8,128)(2,1)}) custom-call(bf16[2,560,128]{2,1,0:T(8,128)(2,1)} %refs_0_.2, bf16[2,128,512]{2,1,0:T(8,128)(2,1)} %refs_1_.2, bf16[2,512,128]{2,1,0:T(8,128)(2,1)} %refs_2_.2, bf16[2,128,512]{2,1,0:T(8,128)(2,1)} %refs_3_.2, bf16[2,512,128]{2,1,0:T(8,128)(2,1)} %refs_4_.2, ...), custom_call_target="tpu_custom_call" | custom-call | flops 2400000000 | bytes 3000000 | tf_op jit(solution)/shard_map/pack/pallas_call | solution.py:546
  7.3 1.5 %collective-permute-done.1.q0 = bf16[960,128]{1,0:T(8,128)(2,1)S(1)} collective-permute-done((bf16[960,128]{1,0:T(8,128)(2,1)}, bf16[960,128]{1,0:T(8,128)(2,1)S(1)}, u32[]{:S(2)}, u32[]{:S(2)}) %collective-permute-start.1) | collective-permute-done | bytes 245792 | tf_op jit(solution)/shard_map/ppermute | solution.py:61
  8.8 1.6 %collective-permute-start.2 = (bf16[3840,128]{1,0:T(8,128)(2,1)}, bf16[3840,128]{1,0:T(8,128)(2,1)S(1)}, u32[]{:S(2)}, u32[]{:S(2)}) collective-permute-start(bf16[3840,128]{1,0:T(8,128)(2,1)} %get-tuple-element.98), channel_id=1, source_target_pairs={{0,2},{1,19},{4,6},{5,23},{8,10},{9,27},{12,14},{13,31},{2,0},{3,1... | collective-permute-start | bytes 2949128 | tf_op jit(solution)/shard_map/ppermute | solution.py:61
  10.4 0.9 collective-permute-start
  11.3 3.2 %collective-permute-start.5 = (bf16[960,128]{1,0:T(8,128)(2,1)S(1)}, bf16[960,128]{1,0:T(8,128)(2,1)S(1)}, u32[]{:S(2)}, u32[]{:S(2)}) collective-permute-start(bf16[960,128]{1,0:T(8,128)(2,1)S(1)} %collective-permute-done.1.q0), channel_id=1, source_target_pairs={{0,64},{1,9},{4,68},{5,13},{8,72},{9,1},{12,76},{13,5},{2,66},{3,1... | collective-permute-start | bytes 737288 | tf_op jit(solution)/shard_map/ppermute | solution.py:61
  14.5 1.1 collective-permute-start.4
  15.5 3.4 %collective-permute-done.5.q3 = bf16[960,128]{1,0:T(8,128)(2,1)S(1)} collective-permute-done((bf16[960,128]{1,0:T(8,128)(2,1)S(1)}, bf16[960,128]{1,0:T(8,128)(2,1)S(1)}, u32[]{:S(2)}, u32[]{:S(2)}) %collective-permute-start.5) | collective-permute-done | bytes 245792 | tf_op jit(solution)/shard_map/ppermute | solution.py:61
  19.0 2.9 %collective-permute-done.4.q2 = bf16[960,128]{1,0:T(8,128)(2,1)S(1)} collective-permute-done((bf16[960,128]{1,0:T(8,128)(2,1)S(1)}, bf16[960,128]{1,0:T(8,128)(2,1)S(1)}, u32[]{:S(2)}, u32[]{:S(2)}) %collective-permute-start.4) | collective-permute-done | bytes 245792 | tf_op jit(solution)/shard_map/ppermute | solution.py:61
  22.0 1.2 collective-permute-done.2.s2
  23.2 0.8 collective-permute-start.7
  24.0 1.7 %collective-permute-done.6.s3 = bf16[3840,128]{1,0:T(8,128)(2,1)S(1)} collective-permute-done((bf16[3840,128]{1,0:T(8,128)(2,1)S(1)}, bf16[3840,128]{1,0:T(8,128)(2,1)S(1)}, u32[]{:S(2)}, u32[]{:S(2)}) %collective-permute-start.6) | collective-permute-done | bytes 983072 | tf_op jit(solution)/shard_map/ppermute | solution.py:61
  25.7 3.8 %forward_one.1 = (f32[336,768]{1,0:T(8,128)S(1)}, f32[48,768]{1,0:T(8,128)S(1)}, bf16[560,768]{1,0:T(8,128)(2,1)S(1)}, bf16[4,512,768]{2,1,0:T(8,128)(2,1)S(1)},...) custom-call(s32[1,768]{1,0:T(1,128)S(1)} %broadcast_in_dim.3.label, bf16[336,768]{1,0:T(8,128)(2,1)S(1)} %bitcast.6, ...), custom_call_target="tpu_custom_call" | custom-call | flops 4800000000 | bytes 6000000 | tf_op jit(solution)/shard_map/forward_one/pallas_call | solution.py:564
  29.5 10.5 %block_two.1 = (f32[336,768]{1,0:T(8,128)}, f32[48,768]{1,0:T(8,128)}, f32[336,768]{1,0:T(8,128)S(1)}, bf16[2,3840,128]{2,1,0:T(8,128)(2,1)S(1)}, bf16[2,3840,128]{2,1,0:T(8,128)(2,1)S(1)}) custom-call(s32[1,768]{1,0:T(1,128)S(1)} %broadcast_in_dim.3.label, f32[336,768]{1,0:T(8,128)S(1)} %get-tuple-element.101.state_in, ...), custom_call_target="tpu_custom_call" | custom-call | flops 11200000000 | bytes 14000000 | tf_op jit(solution)/shard_map/block_two/pallas_call | solution.py:574
  40.0 0.2 collective-permute-start.9
  40.2 3.8 %backward_one_heads.1 = (bf16[512,768]{1,0:T(8,128)(2,1)S(1)}, bf16[2,2176,128]{2,1,0:T(8,128)(2,1)S(1)}, bf16[2,2176,128]{2,1,0:T(8,128)(2,1)S(1)}) custom-call(s32[1,768]{1,0:T(1,128)S(1)} %broadcast_in_dim.3.label, f32[336,768]{1,0:T(8,128)S(1)} %get-tuple-element.109.g_in, bf16[48,768]{1,0:T(8,128)(2,1)S(1)} %bitcast.9, ...), custom_call_target="tpu_custom_call" | custom-call | flops 4800000000 | bytes 6000000 | tf_op jit(solution)/shard_map/backward_one_heads/pallas_call | solution.py:585
  44.0 0.5 collective-permute-start.8
  44.5 0.4 cut_two.1
  44.9 3.5 %collective-permute-start.10 = (bf16[2,960,128]{2,1,0:T(8,128)(2,1)S(1)}, bf16[2,960,128]{2,1,0:T(8,128)(2,1)S(1)}, u32[]{:S(2)}, u32[]{:S(2)}) collective-permute-start(bf16[2,960,128]{2,1,0:T(8,128)(2,1)S(1)} %get-tuple-element.121), channel_id=1, source_target_pairs={{0,64},{1,9},{4,68},{5,13},{8,72},{9,1},{12,76},{13,5},{2,66},{3,1... | collective-permute-start | bytes 1474568 | tf_op jit(solution)/shard_map/ppermute | solution.py:61
  48.4 0.3 fold_heads.1
  48.6 1.6 %collective-permute-start.13 = (bf16[2048,128]{1,0:T(8,128)(2,1)S(1)}, bf16[2048,128]{1,0:T(8,128)(2,1)S(1)}, u32[]{:S(2)}, u32[]{:S(2)}) collective-permute-start(bf16[2048,128]{1,0:T(8,128)(2,1)S(1)} %get-tuple-element.131), channel_id=1, source_target_pairs={{0,2},{1,19},{4,6},{5,23},{8,10},{9,27},{12,14},{13,31},{2,0},{3,1... | collective-permute-start | bytes 1572872 | tf_op jit(solution)/shard_map/ppermute | solution.py:61
  50.2 4.2 %backward_one_layers.1 = (f32[336,768]{1,0:T(8,128)}, bf16[2,1584,128]{2,1,0:T(8,128)(2,1)S(1)}, bf16[1584,128]{1,0:T(8,128)(2,1)S(1)}, bf16[1584,128]{1,0:T(8,128)(2,1)S(1)}) custom-call(s32[1,768]{1,0:T(1,128)S(1)} %broadcast_in_dim.3.label, f32[336,768]{1,0:T(8,128)S(1)} %get-tuple-element.109.g_in, bf16[512,768]{1,0:T(8,128)(2,1)S(1)} %get-tuple-element.122.d_in, ...), custom_call_target="tpu_custom_call" | custom-call | flops 4800000000 | bytes 6000000 | tf_op jit(solution)/shard_map/backward_one_layers/pallas_call | solution.py:614
  54.3 1.4 %collective-permute-start.11 = (bf16[1584,128]{1,0:T(8,128)(2,1)S(1)}, bf16[1584,128]{1,0:T(8,128)(2,1)S(1)}, u32[]{:S(2)}, u32[]{:S(2)}) collective-permute-start(bf16[1584,128]{1,0:T(8,128)(2,1)S(1)} %get-tuple-element.127), channel_id=1, source_target_pairs={{0,1},{1,0},{4,5},{5,4},{8,9},{9,8},{12,13},{13,12},{2,3},{3,2},{6... | collective-permute-start | bytes 1216520 | tf_op jit(solution)/shard_map/ppermute | solution.py:61
  55.8 1.6 %collective-permute-start.17 = (bf16[2,960,128]{2,1,0:T(8,128)(2,1)S(1)}, bf16[2,960,128]{2,1,0:T(8,128)(2,1)S(1)}, u32[]{:S(2)}, u32[]{:S(2)}) collective-permute-start(bf16[2,960,128]{2,1,0:T(8,128)(2,1)S(1)} %get-tuple-element.119), channel_id=1, source_target_pairs={{0,32},{1,5},{4,36},{5,1},{8,40},{9,13},{12,44},{13,9},{2,34},{3,7... | collective-permute-start | bytes 1474568 | tf_op jit(solution)/shard_map/ppermute | solution.py:61
  57.4 2.2 %collective-permute-start.18 = (bf16[2,960,128]{2,1,0:T(8,128)(2,1)S(1)}, bf16[2,960,128]{2,1,0:T(8,128)(2,1)S(1)}, u32[]{:S(2)}, u32[]{:S(2)}) collective-permute-start(bf16[2,960,128]{2,1,0:T(8,128)(2,1)S(1)} %get-tuple-element.120), channel_id=1, source_target_pairs={{0,96},{1,13},{4,100},{5,9},{8,104},{9,5},{12,108},{13,1},{2,98},{... | collective-permute-start | bytes 1474568 | tf_op jit(solution)/shard_map/ppermute | solution.py:61
  59.6 0.7 cut_one.1
  60.3 0.8 collective-permute-start.14
  61.2 1.2 collective-permute-start.15
  62.3 2.2 %collective-permute-start.16 = (bf16[1408,128]{1,0:T(8,128)(2,1)S(1)}, bf16[1408,128]{1,0:T(8,128)(2,1)S(1)}, u32[]{:S(2)}, u32[]{:S(2)}) collective-permute-start(bf16[1408,128]{1,0:T(8,128)(2,1)S(1)} %get-tuple-element.135), channel_id=1, source_target_pairs={{0,64},{1,9},{4,68},{5,13},{8,72},{9,1},{12,76},{13,5},{2,66},{3,1... | collective-permute-start | bytes 1081352 | tf_op jit(solution)/shard_map/ppermute | solution.py:61
  64.6 2.8 %collective-permute-done.18.b = bf16[2,960,128]{2,1,0:T(8,128)(2,1)S(1)} collective-permute-done((bf16[2,960,128]{2,1,0:T(8,128)(2,1)S(1)}, bf16[2,960,128]{2,1,0:T(8,128)(2,1)S(1)}, u32[]{:S(2)}, u32[]{:S(2)}) %collective-permute-start.18) | collective-permute-done | bytes 491552 | tf_op jit(solution)/shard_map/ppermute | solution.py:61
  67.4 0.2 fold.1
  67.7 0.6 collective-permute-start.19
  68.2 6.0 %collective-permute-done.19.came = bf16[960,128]{1,0:T(8,128)(2,1)S(1)} collective-permute-done((bf16[960,128]{1,0:T(8,128)(2,1)S(1)}, bf16[960,128]{1,0:T(8,128)(2,1)S(1)}, u32[]{:S(2)}, u32[]{:S(2)}) %collective-permute-start.19) | collective-permute-done | bytes 245792 | tf_op jit(solution)/shard_map/ppermute | solution.py:61
  74.2 0.9 collective-permute-done.15.b
  75.2 0.5 pieces.1
  75.7 2.4 %collective-permute-start.20 = (bf16[592,128]{1,0:T(8,128)(2,1)S(1)}, bf16[592,128]{1,0:T(8,128)(2,1)S(1)}, u32[]{:S(2)}, u32[]{:S(2)}) collective-permute-start(bf16[592,128]{1,0:T(8,128)(2,1)S(1)} %get-tuple-element.141), channel_id=1, source_target_pairs={{0,8},{1,65},{4,12},{5,69},{8,0},{9,73},{12,4},{13,77},{2,10},{3,6... | collective-permute-start | bytes 454664 | tf_op jit(solution)/shard_map/ppermute | solution.py:61
  78.1 1.3 %collective-permute-start.21 = (bf16[592,128]{1,0:T(8,128)(2,1)S(1)}, bf16[592,128]{1,0:T(8,128)(2,1)S(1)}, u32[]{:S(2)}, u32[]{:S(2)}) collective-permute-start(bf16[592,128]{1,0:T(8,128)(2,1)S(1)} %get-tuple-element.142), channel_id=1, source_target_pairs={{0,12},{1,97},{4,8},{5,101},{8,4},{9,105},{12,0},{13,109},{2,14},{... | collective-permute-start | bytes 454664 | tf_op jit(solution)/shard_map/ppermute | solution.py:61
  79.5 3.0 %collective-permute-done.20.a = bf16[592,128]{1,0:T(8,128)(2,1)S(1)} collective-permute-done((bf16[592,128]{1,0:T(8,128)(2,1)S(1)}, bf16[592,128]{1,0:T(8,128)(2,1)S(1)}, u32[]{:S(2)}, u32[]{:S(2)}) %collective-permute-start.20) | collective-permute-done | bytes 151584 | tf_op jit(solution)/shard_map/ppermute | solution.py:61
  82.5 2.1 %collective-permute-done.21.b = bf16[592,128]{1,0:T(8,128)(2,1)S(1)} collective-permute-done((bf16[592,128]{1,0:T(8,128)(2,1)S(1)}, bf16[592,128]{1,0:T(8,128)(2,1)S(1)}, u32[]{:S(2)}, u32[]{:S(2)}) %collective-permute-start.21) | collective-permute-done | bytes 151584 | tf_op jit(solution)/shard_map/ppermute | solution.py:61
  84.5 0.1 collective-permute-done.22.c
  84.7 2.5 %collective-permute-start.23 = (bf16[2,240,128]{2,1,0:T(8,128)(2,1)S(1)}, bf16[2,240,128]{2,1,0:T(8,128)(2,1)S(1)}, u32[]{:S(2)}, u32[]{:S(2)}) collective-permute-start(bf16[2,240,128]{2,1,0:T(8,128)(2,1)S(1)} %get-tuple-element.144.near), channel_id=1, source_target_pairs={{0,16},{1,17},{4,20},{5,21},{8,24},{9,25},{12,28},{13,29},{2,18},{... | collective-permute-start | bytes 368648 | tf_op jit(solution)/shard_map/ppermute | solution.py:61
  87.3 0.6 collective-permute-start.25
  87.8 1.1 collective-permute-start.24
  88.9 2.2 %collective-permute-done.25.c = bf16[112,128]{1,0:T(8,128)(2,1)S(1)} collective-permute-done((bf16[112,128]{1,0:T(8,128)(2,1)S(1)}, bf16[112,128]{1,0:T(8,128)(2,1)S(1)}, u32[]{:S(2)}, u32[]{:S(2)}) %collective-permute-start.25) | collective-permute-done | bytes 28704 | tf_op jit(solution)/shard_map/ppermute | solution.py:61
  91.1 1.8 %collective-permute-done.24.b = bf16[112,128]{1,0:T(8,128)(2,1)S(1)} collective-permute-done((bf16[112,128]{1,0:T(8,128)(2,1)S(1)}, bf16[112,128]{1,0:T(8,128)(2,1)S(1)}, u32[]{:S(2)}, u32[]{:S(2)}) %collective-permute-start.24) | collective-permute-done | bytes 28704 | tf_op jit(solution)/shard_map/ppermute | solution.py:61
  93.0 1.9 %collective-permute-start.28 = (bf16[2,240,128]{2,1,0:T(8,128)(2,1)S(1)}, bf16[2,240,128]{2,1,0:T(8,128)(2,1)S(1)}, u32[]{:S(2)}, u32[]{:S(2)}) collective-permute-start(bf16[2,240,128]{2,1,0:T(8,128)(2,1)S(1)} %across.1.refs_0_), channel_id=1, source_target_pairs={{0,8},{1,65},{4,12},{5,69},{8,0},{9,73},{12,4},{13,77},{2,10},{3,6... | collective-permute-start | bytes 368648 | tf_op jit(solution)/shard_map/ppermute | solution.py:61
  94.9 1.3 %collective-permute-start.27 = (bf16[2,240,128]{2,1,0:T(8,128)(2,1)S(1)}, bf16[2,240,128]{2,1,0:T(8,128)(2,1)S(1)}, u32[]{:S(2)}, u32[]{:S(2)}) collective-permute-start(bf16[2,240,128]{2,1,0:T(8,128)(2,1)S(1)} %across.1.refs_0_), channel_id=1, source_target_pairs={{0,12},{1,97},{4,8},{5,101},{8,4},{9,105},{12,0},{13,109},{2,14},{... | collective-permute-start | bytes 368648 | tf_op jit(solution)/shard_map/ppermute | solution.py:61
  96.2 0.4 collective-permute-start.26
  96.5 2.9 %collective-permute-done.28.refs_3_ = bf16[2,240,128]{2,1,0:T(8,128)(2,1)S(1)} collective-permute-done((bf16[2,240,128]{2,1,0:T(8,128)(2,1)S(1)}, bf16[2,240,128]{2,1,0:T(8,128)(2,1)S(1)}, u32[]{:S(2)}, u32[]{:S(2)}) %collective-permute-start.28) | collective-permute-done | bytes 122912 | tf_op jit(solution)/shard_map/ppermute | solution.py:61
  99.4 1.6 %collective-permute-done.27.refs_2_ = bf16[2,240,128]{2,1,0:T(8,128)(2,1)S(1)} collective-permute-done((bf16[2,240,128]{2,1,0:T(8,128)(2,1)S(1)}, bf16[2,240,128]{2,1,0:T(8,128)(2,1)S(1)}, u32[]{:S(2)}, u32[]{:S(2)}) %collective-permute-start.27) | collective-permute-done | bytes 122912 | tf_op jit(solution)/shard_map/ppermute | solution.py:61
  101.2 1.2 collective-permute-done.29.refs_4_.refs_11_
  102.3 2.1 %collective-permute-start.35 = (bf16[4,240,128]{2,1,0:T(8,128)(2,1)S(1)}, bf16[4,240,128]{2,1,0:T(8,128)(2,1)S(1)}, u32[]{:S(2)}, u32[]{:S(2)}) collective-permute-start(bf16[4,240,128]{2,1,0:T(8,128)(2,1)S(1)} %get-tuple-element.150.refs_0_), channel_id=1, source_target_pairs={{0,64},{1,9},{4,68},{5,13},{8,72},{9,1},{12,76},{13,5},{2,66},{3,1... | collective-permute-start | bytes 737288 | tf_op jit(solution)/shard_map/ppermute | solution.py:61
  104.4 1.1 collective-permute-start.34
  105.5 0.9 collective-permute-start.33
  106.4 2.7 %collective-permute-start.32 = (bf16[4,240,128]{2,1,0:T(8,128)(2,1)S(1)}, bf16[4,240,128]{2,1,0:T(8,128)(2,1)S(1)}, u32[]{:S(2)}, u32[]{:S(2)}) collective-permute-start(bf16[4,240,128]{2,1,0:T(8,128)(2,1)S(1)} %get-tuple-element.149.refs_0_), channel_id=1, source_target_pairs={{0,64},{1,9},{4,68},{5,13},{8,72},{9,1},{12,76},{13,5},{2,66},{3,1... | collective-permute-start | bytes 737288 | tf_op jit(solution)/shard_map/ppermute | solution.py:61
  109.1 1.1 collective-permute-start.31
  110.2 0.4 collective-permute-start.30
  110.6 2.1 %collective-permute-done.34.refs_2_ = bf16[4,240,128]{2,1,0:T(8,128)(2,1)S(1)} collective-permute-done((bf16[4,240,128]{2,1,0:T(8,128)(2,1)S(1)}, bf16[4,240,128]{2,1,0:T(8,128)(2,1)S(1)}, u32[]{:S(2)}, u32[]{:S(2)}) %collective-permute-start.34) | collective-permute-done | bytes 245792 | tf_op jit(solution)/shard_map/ppermute | solution.py:61
  112.7 0.6 collective-permute-done.33.refs_1_
  113.2 1.5 %unpack.2 = (f32[2,560,128]{2,1,0:T(8,128)}, f32[2,128,512]{2,1,0:T(8,128)}, f32[2,512,128]{2,1,0:T(8,128)}, f32[2,128,512]{2,1,0:T(8,128)}, f32[2,512,128]{2,1,...) custom-call(bf16[4,240,128]{2,1,0:T(8,128)(2,1)S(1)} %get-tuple-element.150.refs_0_, ...), custom_call_target="tpu_custom_call" | custom-call | flops 1600000000 | bytes 2000000 | tf_op jit(solution)/shard_map/unpack/pallas_call | solution.py:664
  114.8 1.3 %collective-permute-done.32.refs_3_ = bf16[4,240,128]{2,1,0:T(8,128)(2,1)S(1)} collective-permute-done((bf16[4,240,128]{2,1,0:T(8,128)(2,1)S(1)}, bf16[4,240,128]{2,1,0:T(8,128)(2,1)S(1)}, u32[]{:S(2)}, u32[]{:S(2)}) %collective-permute-start.32) | collective-permute-done | bytes 245792 | tf_op jit(solution)/shard_map/ppermute | solution.py:61
  116.0 2.5 %collective-permute-done.31.refs_2_ = bf16[4,240,128]{2,1,0:T(8,128)(2,1)S(1)} collective-permute-done((bf16[4,240,128]{2,1,0:T(8,128)(2,1)S(1)}, bf16[4,240,128]{2,1,0:T(8,128)(2,1)S(1)}, u32[]{:S(2)}, u32[]{:S(2)}) %collective-permute-start.31) | collective-permute-done | bytes 245792 | tf_op jit(solution)/shard_map/ppermute | solution.py:61
  118.6 1.5 %unpack.3 = (f32[2,560,128]{2,1,0:T(8,128)}, f32[2,128,512]{2,1,0:T(8,128)}, f32[2,512,128]{2,1,0:T(8,128)}, f32[2,128,512]{2,1,0:T(8,128)}, f32[2,512,128]{2,1,...) custom-call(bf16[4,240,128]{2,1,0:T(8,128)(2,1)S(1)} %get-tuple-elem, ...), custom_call_target="tpu_custom_call", output_to_operand_aliasing={{0}: (4, {}), {1}: (5, {}), {2}: (6, {}), {3}: (7, {}), {4}... | custom-call | flops 1600000000 | bytes 2000000 | tf_op jit(solution)/shard_map/unpack/pallas_call | solution.py:664
  (36 shorter events, 0.6 us)
Async XLA Ops:
  2.3 6.5 %collective-permute-start.1 = (bf16[960,128]{1,0:T(8,128)(2,1)}, bf16[960,128]{1,0:T(8,128)(2,1)S(1)}, u32[]{:S(2)}, u32[]{:S(2)}) collective-permute-start(bf16[960,128]{1,0:T(8,128)(2,1)} %pack_quarter.1), channel_id=1, source_target_pairs={{0,2},{1,19},{4,6},{5,23},{8,10},{9,27},{12,14},{13,31},{2,0},{3,1... | collective-permute-start | bytes 737288 | tf_op jit(solution)/shard_map/ppermute | solution.py:61
  7.3 16.7 %copy-start.4 = (s32[768]{0:T(1024)S(1)}, s32[768]{0:T(1024)}, u32[]{:S(2)}) copy-start(s32[768]{0:T(1024)} %param.12) | copy-start | bytes 9220
  7.3 18.4 %copy-start = (bf16[2,3840,128]{2,1,0:T(8,128)(2,1)S(1)}, bf16[2,3840,128]{2,1,0:T(8,128)(2,1)}, u32[]{:S(2)}) copy-start(bf16[2,3840,128]{2,1,0:T(8,128)(2,1)} %get-tuple-element.95.s0) | copy-start | bytes 5898244
  7.3 18.4 %copy-start.1 = (bf16[768,336]{0,1:T(8,128)(2,1)S(1)}, bf16[768,336]{0,1:T(8,128)(2,1)}, u32[]{:S(2)}) copy-start(bf16[768,336]{0,1:T(8,128)(2,1)} %param.11) | copy-start | bytes 1548292
  8.8 14.3 %collective-permute-start.2 = (bf16[3840,128]{1,0:T(8,128)(2,1)}, bf16[3840,128]{1,0:T(8,128)(2,1)S(1)}, u32[]{:S(2)}, u32[]{:S(2)}) collective-permute-start(bf16[3840,128]{1,0:T(8,128)(2,1)} %get-tuple-element.98), channel_id=1, source_target_pairs={{0,2},{1,19},{4,6},{5,23},{8,10},{9,27},{12,14},{13,31},{2,0},{3,1... | collective-permute-start | bytes 2949128 | tf_op jit(solution)/shard_map/ppermute | solution.py:61
  10.4 13.6 %collective-permute-start = (bf16[2,3840,128]{2,1,0:T(8,128)(2,1)}, bf16[2,3840,128]{2,1,0:T(8,128)(2,1)S(1)}, u32[]{:S(2)}, u32[]{:S(2)}) collective-permute-start(bf16[2,3840,128]{2,1,0:T(8,128)(2,1)} %get-tuple-element.95.s0), channel_id=1, source_target_pairs={{0,1},{1,0},{4,5},{5,4},{8,9},{9,8},{12,13},{13,12},{2,3},{3,2},{6... | collective-permute-start | bytes 5898248 | tf_op jit(solution)/shard_map/ppermute | solution.py:61
  11.3 7.7 %collective-permute-start.5 = (bf16[960,128]{1,0:T(8,128)(2,1)S(1)}, bf16[960,128]{1,0:T(8,128)(2,1)S(1)}, u32[]{:S(2)}, u32[]{:S(2)}) collective-permute-start(bf16[960,128]{1,0:T(8,128)(2,1)S(1)} %collective-permute-done.1.q0), channel_id=1, source_target_pairs={{0,64},{1,9},{4,68},{5,13},{8,72},{9,1},{12,76},{13,5},{2,66},{3,1... | collective-permute-start | bytes 737288 | tf_op jit(solution)/shard_map/ppermute | solution.py:61
  14.5 7.4 %collective-permute-start.4 = (bf16[960,128]{1,0:T(8,128)(2,1)S(1)}, bf16[960,128]{1,0:T(8,128)(2,1)S(1)}, u32[]{:S(2)}, u32[]{:S(2)}) collective-permute-start(bf16[960,128]{1,0:T(8,128)(2,1)S(1)} %collective-permute-done.1.q0), channel_id=1, source_target_pairs={{0,96},{1,13},{4,100},{5,9},{8,104},{9,5},{12,108},{13,1},{2,98},{... | collective-permute-start | bytes 737288 | tf_op jit(solution)/shard_map/ppermute | solution.py:61
  15.5 6.4 %collective-permute-start.3 = (bf16[960,128]{1,0:T(8,128)(2,1)S(1)}, bf16[960,128]{1,0:T(8,128)(2,1)S(1)}, u32[]{:S(2)}, u32[]{:S(2)}) collective-permute-start(bf16[960,128]{1,0:T(8,128)(2,1)S(1)} %collective-permute-done.1.q0), channel_id=1, source_target_pairs={{0,32},{1,5},{4,36},{5,1},{8,40},{9,13},{12,44},{13,9},{2,34},{3,7... | collective-permute-start | bytes 737288 | tf_op jit(solution)/shard_map/ppermute | solution.py:61
  23.1 2.6 %collective-permute-start.6 = (bf16[3840,128]{1,0:T(8,128)(2,1)S(1)}, bf16[3840,128]{1,0:T(8,128)(2,1)S(1)}, u32[]{:S(2)}, u32[]{:S(2)}) collective-permute-start(bf16[3840,128]{1,0:T(8,128)(2,1)S(1)} %collective-permute-done.2.s2), channel_id=1, source_target_pairs={{0,1},{1,0},{4,5},{5,4},{8,9},{9,8},{12,13},{13,12},{2,3},{3,2},{6... | collective-permute-start | bytes 2949128 | tf_op jit(solution)/shard_map/ppermute | solution.py:61
  23.2 6.3 %collective-permute-start.7 = (bf16[3840,128]{1,0:T(8,128)(2,1)S(1)}, bf16[3840,128]{1,0:T(8,128)(2,1)S(1)}, u32[]{:S(2)}, u32[]{:S(2)}) collective-permute-start(bf16[3840,128]{1,0:T(8,128)(2,1)S(1)} %join.1.s2), channel_id=1, source_target_pairs={{0,1},{1,0},{4,5},{5,4},{8,9},{9,8},{12,13},{13,12},{2,3},{3,2},{6... | collective-permute-start | bytes 2949128 | tf_op jit(solution)/shard_map/ppermute | solution.py:61
  25.7 3.8 %copy-start.2 = (bf16[768,336]{0,1:T(8,128)(2,1)S(1)}, bf16[768,336]{0,1:T(8,128)(2,1)}, u32[]{:S(2)}) copy-start(bf16[768,336]{0,1:T(8,128)(2,1)} %param.21) | copy-start | bytes 1548292
  25.7 3.8 %copy-start.3 = (bf16[768,48]{0,1:T(8,128)(2,1)S(1)}, bf16[768,48]{0,1:T(8,128)(2,1)}, u32[]{:S(2)}) copy-start(bf16[768,48]{0,1:T(8,128)(2,1)} %param.20) | copy-start | bytes 221188
  40.0 4.4 %collective-permute-start.9 = (bf16[2,3840,128]{2,1,0:T(8,128)(2,1)S(1)}, bf16[2,3840,128]{2,1,0:T(8,128)(2,1)S(1)}, u32[]{:S(2)}, u32[]{:S(2)}) collective-permute-start(bf16[2,3840,128]{2,1,0:T(8,128)(2,1)S(1)} %get-tuple-element.118), channel_id=1, source_target_pairs={{0,1},{1,0},{4,5},{5,4},{8,9},{9,8},{12,13},{13,12},{2,3},{3,2},{6... | collective-permute-start | bytes 5898248 | tf_op jit(solution)/shard_map/ppermute | solution.py:61
  44.0 4.4 %collective-permute-start.8 = (bf16[2,2176,128]{2,1,0:T(8,128)(2,1)S(1)}, bf16[2,2176,128]{2,1,0:T(8,128)(2,1)S(1)}, u32[]{:S(2)}, u32[]{:S(2)}) collective-permute-start(bf16[2,2176,128]{2,1,0:T(8,128)(2,1)S(1)} %get-tuple-element.115), channel_id=1, source_target_pairs={{0,1},{1,0},{4,5},{5,4},{8,9},{9,8},{12,13},{13,12},{2,3},{3,2},{6... | collective-permute-start | bytes 3342344 | tf_op jit(solution)/shard_map/ppermute | solution.py:61
  44.9 12.5 %collective-permute-start.10 = (bf16[2,960,128]{2,1,0:T(8,128)(2,1)S(1)}, bf16[2,960,128]{2,1,0:T(8,128)(2,1)S(1)}, u32[]{:S(2)}, u32[]{:S(2)}) collective-permute-start(bf16[2,960,128]{2,1,0:T(8,128)(2,1)S(1)} %get-tuple-element.121), channel_id=1, source_target_pairs={{0,64},{1,9},{4,68},{5,13},{8,72},{9,1},{12,76},{13,5},{2,66},{3,1... | collective-permute-start | bytes 1474568 | tf_op jit(solution)/shard_map/ppermute | solution.py:61
  48.6 11.0 %collective-permute-start.13 = (bf16[2048,128]{1,0:T(8,128)(2,1)S(1)}, bf16[2048,128]{1,0:T(8,128)(2,1)S(1)}, u32[]{:S(2)}, u32[]{:S(2)}) collective-permute-start(bf16[2048,128]{1,0:T(8,128)(2,1)S(1)} %get-tuple-element.131), channel_id=1, source_target_pairs={{0,2},{1,19},{4,6},{5,23},{8,10},{9,27},{12,14},{13,31},{2,0},{3,1... | collective-permute-start | bytes 1572872 | tf_op jit(solution)/shard_map/ppermute | solution.py:61
  54.3 5.3 %collective-permute-start.11 = (bf16[1584,128]{1,0:T(8,128)(2,1)S(1)}, bf16[1584,128]{1,0:T(8,128)(2,1)S(1)}, u32[]{:S(2)}, u32[]{:S(2)}) collective-permute-start(bf16[1584,128]{1,0:T(8,128)(2,1)S(1)} %get-tuple-element.127), channel_id=1, source_target_pairs={{0,1},{1,0},{4,5},{5,4},{8,9},{9,8},{12,13},{13,12},{2,3},{3,2},{6... | collective-permute-start | bytes 1216520 | tf_op jit(solution)/shard_map/ppermute | solution.py:61
  55.8 3.9 %collective-permute-start.12 = (bf16[1584,128]{1,0:T(8,128)(2,1)S(1)}, bf16[1584,128]{1,0:T(8,128)(2,1)S(1)}, u32[]{:S(2)}, u32[]{:S(2)}) collective-permute-start(bf16[1584,128]{1,0:T(8,128)(2,1)S(1)} %get-tuple-element.128), channel_id=1, source_target_pairs={{0,1},{1,0},{4,5},{5,4},{8,9},{9,8},{12,13},{13,12},{2,3},{3,2},{6... | collective-permute-start | bytes 1216520 | tf_op jit(solution)/shard_map/ppermute | solution.py:61
  55.8 8.8 %collective-permute-start.17 = (bf16[2,960,128]{2,1,0:T(8,128)(2,1)S(1)}, bf16[2,960,128]{2,1,0:T(8,128)(2,1)S(1)}, u32[]{:S(2)}, u32[]{:S(2)}) collective-permute-start(bf16[2,960,128]{2,1,0:T(8,128)(2,1)S(1)} %get-tuple-element.119), channel_id=1, source_target_pairs={{0,32},{1,5},{4,36},{5,1},{8,40},{9,13},{12,44},{13,9},{2,34},{3,7... | collective-permute-start | bytes 1474568 | tf_op jit(solution)/shard_map/ppermute | solution.py:61
  57.4 10.0 %collective-permute-start.18 = (bf16[2,960,128]{2,1,0:T(8,128)(2,1)S(1)}, bf16[2,960,128]{2,1,0:T(8,128)(2,1)S(1)}, u32[]{:S(2)}, u32[]{:S(2)}) collective-permute-start(bf16[2,960,128]{2,1,0:T(8,128)(2,1)S(1)} %get-tuple-element.120), channel_id=1, source_target_pairs={{0,96},{1,13},{4,100},{5,9},{8,104},{9,5},{12,108},{13,1},{2,98},{... | collective-permute-start | bytes 1474568 | tf_op jit(solution)/shard_map/ppermute | solution.py:61
  60.3 13.9 %collective-permute-start.14 = (bf16[1408,128]{1,0:T(8,128)(2,1)S(1)}, bf16[1408,128]{1,0:T(8,128)(2,1)S(1)}, u32[]{:S(2)}, u32[]{:S(2)}) collective-permute-start(bf16[1408,128]{1,0:T(8,128)(2,1)S(1)} %get-tuple-element.133), channel_id=1, source_target_pairs={{0,32},{1,5},{4,36},{5,1},{8,40},{9,13},{12,44},{13,9},{2,34},{3,7... | collective-permute-start | bytes 1081352 | tf_op jit(solution)/shard_map/ppermute | solution.py:61
  61.2 14.0 %collective-permute-start.15 = (bf16[1408,128]{1,0:T(8,128)(2,1)S(1)}, bf16[1408,128]{1,0:T(8,128)(2,1)S(1)}, u32[]{:S(2)}, u32[]{:S(2)}) collective-permute-start(bf16[1408,128]{1,0:T(8,128)(2,1)S(1)} %get-tuple-element.134), channel_id=1, source_target_pairs={{0,96},{1,13},{4,100},{5,9},{8,104},{9,5},{12,108},{13,1},{2,98},{... | collective-permute-start | bytes 1081352 | tf_op jit(solution)/shard_map/ppermute | solution.py:61
  62.3 12.8 %collective-permute-start.16 = (bf16[1408,128]{1,0:T(8,128)(2,1)S(1)}, bf16[1408,128]{1,0:T(8,128)(2,1)S(1)}, u32[]{:S(2)}, u32[]{:S(2)}) collective-permute-start(bf16[1408,128]{1,0:T(8,128)(2,1)S(1)} %get-tuple-element.135), channel_id=1, source_target_pairs={{0,64},{1,9},{4,68},{5,13},{8,72},{9,1},{12,76},{13,5},{2,66},{3,1... | collective-permute-start | bytes 1081352 | tf_op jit(solution)/shard_map/ppermute | solution.py:61
  67.7 6.5 %collective-permute-start.19 = (bf16[960,128]{1,0:T(8,128)(2,1)S(1)}, bf16[960,128]{1,0:T(8,128)(2,1)S(1)}, u32[]{:S(2)}, u32[]{:S(2)}) collective-permute-start(bf16[960,128]{1,0:T(8,128)(2,1)S(1)} %get-tuple-element.139), channel_id=1, source_target_pairs={{0,2},{1,19},{4,6},{5,23},{8,10},{9,27},{12,14},{13,31},{2,0},{3,1... | collective-permute-start | bytes 737288 | tf_op jit(solution)/shard_map/ppermute | solution.py:61
  75.7 6.8 %collective-permute-start.20 = (bf16[592,128]{1,0:T(8,128)(2,1)S(1)}, bf16[592,128]{1,0:T(8,128)(2,1)S(1)}, u32[]{:S(2)}, u32[]{:S(2)}) collective-permute-start(bf16[592,128]{1,0:T(8,128)(2,1)S(1)} %get-tuple-element.141), channel_id=1, source_target_pairs={{0,8},{1,65},{4,12},{5,69},{8,0},{9,73},{12,4},{13,77},{2,10},{3,6... | collective-permute-start | bytes 454664 | tf_op jit(solution)/shard_map/ppermute | solution.py:61
  78.1 6.4 %collective-permute-start.21 = (bf16[592,128]{1,0:T(8,128)(2,1)S(1)}, bf16[592,128]{1,0:T(8,128)(2,1)S(1)}, u32[]{:S(2)}, u32[]{:S(2)}) collective-permute-start(bf16[592,128]{1,0:T(8,128)(2,1)S(1)} %get-tuple-element.142), channel_id=1, source_target_pairs={{0,12},{1,97},{4,8},{5,101},{8,4},{9,105},{12,0},{13,109},{2,14},{... | collective-permute-start | bytes 454664 | tf_op jit(solution)/shard_map/ppermute | solution.py:61
  79.5 5.2 %collective-permute-start.22 = (bf16[592,128]{1,0:T(8,128)(2,1)S(1)}, bf16[592,128]{1,0:T(8,128)(2,1)S(1)}, u32[]{:S(2)}, u32[]{:S(2)}) collective-permute-start(bf16[592,128]{1,0:T(8,128)(2,1)S(1)} %get-tuple-element.143), channel_id=1, source_target_pairs={{0,4},{1,33},{4,0},{5,37},{8,12},{9,41},{12,8},{13,45},{2,6},{3,35... | collective-permute-start | bytes 454664 | tf_op jit(solution)/shard_map/ppermute | solution.py:61
  84.7 8.2 %collective-permute-start.23 = (bf16[2,240,128]{2,1,0:T(8,128)(2,1)S(1)}, bf16[2,240,128]{2,1,0:T(8,128)(2,1)S(1)}, u32[]{:S(2)}, u32[]{:S(2)}) collective-permute-start(bf16[2,240,128]{2,1,0:T(8,128)(2,1)S(1)} %get-tuple-element.144.near), channel_id=1, source_target_pairs={{0,16},{1,17},{4,20},{5,21},{8,24},{9,25},{12,28},{13,29},{2,18},{... | collective-permute-start | bytes 368648 | tf_op jit(solution)/shard_map/ppermute | solution.py:61
  87.3 3.9 %collective-permute-start.25 = (bf16[112,128]{1,0:T(8,128)(2,1)S(1)}, bf16[112,128]{1,0:T(8,128)(2,1)S(1)}, u32[]{:S(2)}, u32[]{:S(2)}) collective-permute-start(bf16[112,128]{1,0:T(8,128)(2,1)S(1)} %get-tuple-element.145), channel_id=1, source_target_pairs={{0,2},{1,3},{4,6},{5,7},{8,10},{9,11},{12,14},{13,15},{2,0},{3,1},... | collective-permute-start | bytes 86024 | tf_op jit(solution)/shard_map/ppermute | solution.py:61
  87.8 5.1 %collective-permute-start.24 = (bf16[112,128]{1,0:T(8,128)(2,1)S(1)}, bf16[112,128]{1,0:T(8,128)(2,1)S(1)}, u32[]{:S(2)}, u32[]{:S(2)}) collective-permute-start(bf16[112,128]{1,0:T(8,128)(2,1)S(1)} %get-tuple-element.145), channel_id=1, source_target_pairs={{0,18},{1,19},{4,22},{5,23},{8,26},{9,27},{12,30},{13,31},{2,16},{... | collective-permute-start | bytes 86024 | tf_op jit(solution)/shard_map/ppermute | solution.py:61
  93.0 6.5 %collective-permute-start.28 = (bf16[2,240,128]{2,1,0:T(8,128)(2,1)S(1)}, bf16[2,240,128]{2,1,0:T(8,128)(2,1)S(1)}, u32[]{:S(2)}, u32[]{:S(2)}) collective-permute-start(bf16[2,240,128]{2,1,0:T(8,128)(2,1)S(1)} %across.1.refs_0_), channel_id=1, source_target_pairs={{0,8},{1,65},{4,12},{5,69},{8,0},{9,73},{12,4},{13,77},{2,10},{3,6... | collective-permute-start | bytes 368648 | tf_op jit(solution)/shard_map/ppermute | solution.py:61
  94.9 6.1 %collective-permute-start.27 = (bf16[2,240,128]{2,1,0:T(8,128)(2,1)S(1)}, bf16[2,240,128]{2,1,0:T(8,128)(2,1)S(1)}, u32[]{:S(2)}, u32[]{:S(2)}) collective-permute-start(bf16[2,240,128]{2,1,0:T(8,128)(2,1)S(1)} %across.1.refs_0_), channel_id=1, source_target_pairs={{0,12},{1,97},{4,8},{5,101},{8,4},{9,105},{12,0},{13,109},{2,14},{... | collective-permute-start | bytes 368648 | tf_op jit(solution)/shard_map/ppermute | solution.py:61
  96.2 4.9 %collective-permute-start.26 = (bf16[2,240,128]{2,1,0:T(8,128)(2,1)S(1)}, bf16[2,240,128]{2,1,0:T(8,128)(2,1)S(1)}, u32[]{:S(2)}, u32[]{:S(2)}) collective-permute-start(bf16[2,240,128]{2,1,0:T(8,128)(2,1)S(1)} %across.1.refs_0_), channel_id=1, source_target_pairs={{0,4},{1,33},{4,0},{5,37},{8,12},{9,41},{12,8},{13,45},{2,6},{3,35... | collective-permute-start | bytes 368648 | tf_op jit(solution)/shard_map/ppermute | solution.py:61
  101.1 1.2 %collective-permute-start.29 = (bf16[16,128]{1,0:T(8,128)(2,1)S(1)}, bf16[16,128]{1,0:T(8,128)(2,1)S(1)}, u32[]{:S(2)}, u32[]{:S(2)}) collective-permute-start(bf16[16,128]{1,0:T(8,128)(2,1)S(1)} %get-tuple-element.148), channel_id=1, source_target_pairs={{0,1},{1,0},{4,5},{5,4},{8,9},{9,8},{12,13},{13,12},{2,3},{3,2},{6... | collective-permute-start | bytes 12296 | tf_op jit(solution)/shard_map/ppermute | solution.py:61
  102.3 7.9 %collective-permute-start.35 = (bf16[4,240,128]{2,1,0:T(8,128)(2,1)S(1)}, bf16[4,240,128]{2,1,0:T(8,128)(2,1)S(1)}, u32[]{:S(2)}, u32[]{:S(2)}) collective-permute-start(bf16[4,240,128]{2,1,0:T(8,128)(2,1)S(1)} %get-tuple-element.150.refs_0_), channel_id=1, source_target_pairs={{0,64},{1,9},{4,68},{5,13},{8,72},{9,1},{12,76},{13,5},{2,66},{3,1... | collective-permute-start | bytes 737288 | tf_op jit(solution)/shard_map/ppermute | solution.py:61
  104.4 8.3 %collective-permute-start.34 = (bf16[4,240,128]{2,1,0:T(8,128)(2,1)S(1)}, bf16[4,240,128]{2,1,0:T(8,128)(2,1)S(1)}, u32[]{:S(2)}, u32[]{:S(2)}) collective-permute-start(bf16[4,240,128]{2,1,0:T(8,128)(2,1)S(1)} %get-tuple-element.150.refs_0_), channel_id=1, source_target_pairs={{0,96},{1,13},{4,100},{5,9},{8,104},{9,5},{12,108},{13,1},{2,98},{... | collective-permute-start | bytes 737288 | tf_op jit(solution)/shard_map/ppermute | solution.py:61
  105.5 7.7 %collective-permute-start.33 = (bf16[4,240,128]{2,1,0:T(8,128)(2,1)S(1)}, bf16[4,240,128]{2,1,0:T(8,128)(2,1)S(1)}, u32[]{:S(2)}, u32[]{:S(2)}) collective-permute-start(bf16[4,240,128]{2,1,0:T(8,128)(2,1)S(1)} %get-tuple-element.150.refs_0_), channel_id=1, source_target_pairs={{0,32},{1,5},{4,36},{5,1},{8,40},{9,13},{12,44},{13,9},{2,34},{3,7... | collective-permute-start | bytes 737288 | tf_op jit(solution)/shard_map/ppermute | solution.py:61
  106.4 9.6 %collective-permute-start.32 = (bf16[4,240,128]{2,1,0:T(8,128)(2,1)S(1)}, bf16[4,240,128]{2,1,0:T(8,128)(2,1)S(1)}, u32[]{:S(2)}, u32[]{:S(2)}) collective-permute-start(bf16[4,240,128]{2,1,0:T(8,128)(2,1)S(1)} %get-tuple-element.149.refs_0_), channel_id=1, source_target_pairs={{0,64},{1,9},{4,68},{5,13},{8,72},{9,1},{12,76},{13,5},{2,66},{3,1... | collective-permute-start | bytes 737288 | tf_op jit(solution)/shard_map/ppermute | solution.py:61
  109.1 9.4 %collective-permute-start.31 = (bf16[4,240,128]{2,1,0:T(8,128)(2,1)S(1)}, bf16[4,240,128]{2,1,0:T(8,128)(2,1)S(1)}, u32[]{:S(2)}, u32[]{:S(2)}) collective-permute-start(bf16[4,240,128]{2,1,0:T(8,128)(2,1)S(1)} %get-tuple-element.149.refs_0_), channel_id=1, source_target_pairs={{0,96},{1,13},{4,100},{5,9},{8,104},{9,5},{12,108},{13,1},{2,98},{... | collective-permute-start | bytes 737288 | tf_op jit(solution)/shard_map/ppermute | solution.py:61
  110.2 8.3 %collective-permute-start.30 = (bf16[4,240,128]{2,1,0:T(8,128)(2,1)S(1)}, bf16[4,240,128]{2,1,0:T(8,128)(2,1)S(1)}, u32[]{:S(2)}, u32[]{:S(2)}) collective-permute-start(bf16[4,240,128]{2,1,0:T(8,128)(2,1)S(1)} %get-tuple-element.149.refs_0_), channel_id=1, source_target_pairs={{0,32},{1,5},{4,36},{5,1},{8,40},{9,13},{12,44},{13,9},{2,34},{3,7... | collective-permute-start | bytes 737288 | tf_op jit(solution)/shard_map/ppermute | solution.py:61

commit v8 on v7

--- a/solution.py
+++ b/solution.py
@@ -262,7 +262,7 @@
     return d_pre
 
 
-def backward_layers(g, d_pre, label, weights, e_ref, act_ref, slope_ref, grads):
+def backward_layers(g, d_pre, label, weights, e_ref, act_ref, slope_ref, grads, take=None):
     d_act = dot(weights.get("fourth"), d_pre)
     d_pre = (d_act * slope_ref[2].astype(F32)).astype(BF)
     grads.put("third", dot_t(act_ref[1], d_pre))
@@ -271,8 +271,11 @@
     grads.put("second", dot_t(act_ref[0], d_pre))
     d_act = dot(weights.get("second"), d_pre)
     d_pre = (d_act * slope_ref[0].astype(F32)).astype(BF)
+    if take:
+        take(g + pick_look(dot(weights.get("entry"), d_pre), label))
     grads.put("entry", dot_t(e_ref[...], d_pre))
-    return g + pick_look(dot(weights.get("entry"), d_pre), label)
+    if not take:
+        return g + pick_look(dot(weights.get("entry"), d_pre), label)
 
 
 def places():
@@ -370,11 +373,20 @@
     )
 
 
-def fourth_kernel(label, g_in, d_in, s0, s1, s2, s3, e, act, slope, steep, mine, near, far):
+def fourth_kernel(
+    label, g_in, d_in, s0, s1, s2, s3, e, act, slope, steep_out, mine, near, far, steep, sem
+):
     grads = Grads((mine, (near, far)))
     labels = label[...]
-    g = backward_layers(g_in[...], d_in[...], labels, Weights((s0.at[0], s1.at[0], s2, s3)), e, act, slope, grads)
-    steep[...] = jnp.where(look_mask(labels), g, 0.0)
+    weights = Weights((s0.at[0], s1.at[0], s2, s3))
+    copy = pltpu.make_async_copy(steep, steep_out, sem)
+
+    def take(new):
+        steep[...] = jnp.where(look_mask(labels), new, 0.0)
+        copy.start()
+
+    backward_layers(g_in[...], d_in[...], labels, weights, e, act, slope, grads, take)
+    copy.wait()
 
 
 def cut_kernel(mine, got, *outs):
@@ -615,9 +627,9 @@
         fourth_kernel,
         "backward_one_layers",
         [IN_VMEM] * 10,
-        [(shape(336, ROWS), IN_VMEM), (shape(2, LOW, 128, kind=BF), IN_VMEM)]
+        [(shape(336, ROWS), ANYWHERE), (shape(2, LOW, 128, kind=BF), IN_VMEM)]
         + [(shape(LOW, 128, kind=BF), IN_VMEM)] * 2,
-        [],
+        [vmem(336, ROWS, kind=F32), DMA],
         M4,
         6,
     )(label, g1, d_pre, *slots1, e1, act1, slope1)

time: 120 us -> 120 us (level)
  no operation moved by 1% of the time
where the time goes in v8:
time: 120 us
  starting transfers between devices  44.9 us (37%)
  waiting for transfers between devices  42.1 us (35%)
  Pallas kernels  32.2 us (27%)
    ppermute x36, starting transfers between devices, send(): return lax.ppermute(values, ('dp', 'mp'), where)  44.9 us
    ppermute x36, waiting for transfers between devices, send(): return lax.ppermute(values, ('dp', 'mp'), where)  42.1 us
    pallas_call x1, Pallas kernels, shards(): call(second_kernel, 'block_two', [IN_VMEM] * 9, [(shape(336, ROWS), IN_VM...  10.5 us
    pallas_call x1, Pallas kernels, shards(): call(first_kernel, 'forward_one', [IN_VMEM] * 6, [(shape(336, ROWS), IN_V...  3.78 us
    pallas_call x1, Pallas kernels, shards(): call(fourth_kernel, 'backward_one_layers', [IN_VMEM] * 10, [(shape(336, R...  3.76 us
    pallas_call x1, Pallas kernels, shards(): call(third_kernel, 'backward_one_heads', [IN_VMEM] * 10, [(shape(512, ROW...  3.76 us
    pallas_call x1, Pallas kernels, shards(): call(pack_kernel, 'pack', [IN_VMEM] * 7, [(shape(2, PACK, 128, kind=BF),...  3.33 us
    pallas_call x2, Pallas kernels, shards(): call(functools.partial(unpack_kernel, k), 'unpack', [IN_VMEM] * 4 + [ANYW...  3.03 us
  transfers between devices with their start and end apart: 36, of which 23 were waited for; matrix products, arithmetic and copies ran while one was open for 0% of the time, Pallas kernels for 15%

profile of v8, /device:TPU:0, one launch (start us, length us, event | category | flops | bytes accessed | tf_op | source)
XLA Modules:
  0.0 120.3 jit_solution(1711955248522172752)
XLA Ops:
  0.6 1.7 %pack_quarter.1 = bf16[960,128]{1,0:T(8,128)(2,1)} custom-call(bf16[2,560,128]{2,1,0:T(8,128)(2,1)} %refs_0_.2, bf16[2,128,512]{2,1,0:T(8,128)(2,1)} %refs_1_.2, bf16[2,512,128]{2,1,0:T(8,128)(2,1)} %refs_2_.2, bf16[2,128,512]{2,1,0:T(8,128)(2,1)} %refs_3_.2, bf16[2,512,128]{2,1,0:T(8,128)(2,1)} %refs_4_.2, bf16[2,512,128]{2,1,0:T(8,128)(2,1)} %refs_5_.2, ...), custom_call_target="tpu_custom_call" | custom-call | flops 800000000 | bytes 1000000 | tf_op jit(solution)/shard_map/pack_quarter/pallas_call | solution.py:548
  2.3 1.7 %collective-permute-start.1 = (bf16[960,128]{1,0:T(8,128)(2,1)}, bf16[960,128]{1,0:T(8,128)(2,1)S(1)}, u32[]{:S(2)}, u32[]{:S(2)}) collective-permute-start(bf16[960,128]{1,0:T(8,128)(2,1)} %pack_quarter.1), channel_id=1, source_target_pairs={{0,2},{1,19},{4,6},{5,23},{8,10},{9,27},{12,14},{13,31},{2,0},{3,1... | collective-permute-start | bytes 737288 | tf_op jit(solution)/shard_map/ppermute | solution.py:61
  4.0 3.3 %pack.1 = (bf16[2,3840,128]{2,1,0:T(8,128)(2,1)}, bf16[3840,128]{1,0:T(8,128)(2,1)}) custom-call(bf16[2,560,128]{2,1,0:T(8,128)(2,1)} %refs_0_.2, bf16[2,128,512]{2,1,0:T(8,128)(2,1)} %refs_1_.2, bf16[2,512,128]{2,1,0:T(8,128)(2,1)} %refs_2_.2, bf16[2,128,512]{2,1,0:T(8,128)(2,1)} %refs_3_.2, bf16[2,512,128]{2,1,0:T(8,128)(2,1)} %refs_4_.2, ...), custom_call_target="tpu_custom_call" | custom-call | flops 2400000000 | bytes 3000000 | tf_op jit(solution)/shard_map/pack/pallas_call | solution.py:558
  7.3 1.5 %collective-permute-done.1.q0 = bf16[960,128]{1,0:T(8,128)(2,1)S(1)} collective-permute-done((bf16[960,128]{1,0:T(8,128)(2,1)}, bf16[960,128]{1,0:T(8,128)(2,1)S(1)}, u32[]{:S(2)}, u32[]{:S(2)}) %collective-permute-start.1) | collective-permute-done | bytes 245792 | tf_op jit(solution)/shard_map/ppermute | solution.py:61
  8.8 1.6 %collective-permute-start.2 = (bf16[3840,128]{1,0:T(8,128)(2,1)}, bf16[3840,128]{1,0:T(8,128)(2,1)S(1)}, u32[]{:S(2)}, u32[]{:S(2)}) collective-permute-start(bf16[3840,128]{1,0:T(8,128)(2,1)} %get-tuple-element.98), channel_id=1, source_target_pairs={{0,2},{1,19},{4,6},{5,23},{8,10},{9,27},{12,14},{13,31},{2,0},{3,1... | collective-permute-start | bytes 2949128 | tf_op jit(solution)/shard_map/ppermute | solution.py:61
  10.4 0.9 collective-permute-start
  11.3 3.2 %collective-permute-start.5 = (bf16[960,128]{1,0:T(8,128)(2,1)S(1)}, bf16[960,128]{1,0:T(8,128)(2,1)S(1)}, u32[]{:S(2)}, u32[]{:S(2)}) collective-permute-start(bf16[960,128]{1,0:T(8,128)(2,1)S(1)} %collective-permute-done.1.q0), channel_id=1, source_target_pairs={{0,64},{1,9},{4,68},{5,13},{8,72},{9,1},{12,76},{13,5},{2,66},{3,1... | collective-permute-start | bytes 737288 | tf_op jit(solution)/shard_map/ppermute | solution.py:61
  14.5 1.1 collective-permute-start.4
  15.5 3.4 %collective-permute-done.5.q3 = bf16[960,128]{1,0:T(8,128)(2,1)S(1)} collective-permute-done((bf16[960,128]{1,0:T(8,128)(2,1)S(1)}, bf16[960,128]{1,0:T(8,128)(2,1)S(1)}, u32[]{:S(2)}, u32[]{:S(2)}) %collective-permute-start.5) | collective-permute-done | bytes 245792 | tf_op jit(solution)/shard_map/ppermute | solution.py:61
  19.0 2.9 %collective-permute-done.4.q2 = bf16[960,128]{1,0:T(8,128)(2,1)S(1)} collective-permute-done((bf16[960,128]{1,0:T(8,128)(2,1)S(1)}, bf16[960,128]{1,0:T(8,128)(2,1)S(1)}, u32[]{:S(2)}, u32[]{:S(2)}) %collective-permute-start.4) | collective-permute-done | bytes 245792 | tf_op jit(solution)/shard_map/ppermute | solution.py:61
  22.0 1.2 collective-permute-done.2.s2
  23.2 0.8 collective-permute-start.7
  24.0 1.7 %collective-permute-done.6.s3 = bf16[3840,128]{1,0:T(8,128)(2,1)S(1)} collective-permute-done((bf16[3840,128]{1,0:T(8,128)(2,1)S(1)}, bf16[3840,128]{1,0:T(8,128)(2,1)S(1)}, u32[]{:S(2)}, u32[]{:S(2)}) %collective-permute-start.6) | collective-permute-done | bytes 983072 | tf_op jit(solution)/shard_map/ppermute | solution.py:61
  25.7 3.8 %forward_one.1 = (f32[336,768]{1,0:T(8,128)S(1)}, f32[48,768]{1,0:T(8,128)S(1)}, bf16[560,768]{1,0:T(8,128)(2,1)S(1)}, bf16[4,512,768]{2,1,0:T(8,128)(2,1)S(1)},...) custom-call(s32[1,768]{1,0:T(1,128)S(1)} %broadcast_in_dim.3.label, bf16[336,768]{1,0:T(8,128)(2,1)S(1)} %bitcast.6, ...), custom_call_target="tpu_custom_call" | custom-call | flops 4800000000 | bytes 6000000 | tf_op jit(solution)/shard_map/forward_one/pallas_call | solution.py:576
  29.5 10.5 %block_two.1 = (f32[336,768]{1,0:T(8,128)}, f32[48,768]{1,0:T(8,128)}, f32[336,768]{1,0:T(8,128)S(1)}, bf16[2,3840,128]{2,1,0:T(8,128)(2,1)S(1)}, bf16[2,3840,128]{2,1,0:T(8,128)(2,1)S(1)}) custom-call(s32[1,768]{1,0:T(1,128)S(1)} %broadcast_in_dim.3.label, f32[336,768]{1,0:T(8,128)S(1)} %get-tuple-element.101.state_in, ...), custom_call_target="tpu_custom_call" | custom-call | flops 11200000000 | bytes 14000000 | tf_op jit(solution)/shard_map/block_two/pallas_call | solution.py:586
  40.0 0.2 collective-permute-start.9
  40.2 3.8 %backward_one_heads.1 = (bf16[512,768]{1,0:T(8,128)(2,1)S(1)}, bf16[2,2176,128]{2,1,0:T(8,128)(2,1)S(1)}, bf16[2,2176,128]{2,1,0:T(8,128)(2,1)S(1)}) custom-call(s32[1,768]{1,0:T(1,128)S(1)} %broadcast_in_dim.3.label, f32[336,768]{1,0:T(8,128)S(1)} %get-tuple-element.109.g_in, bf16[48,768]{1,0:T(8,128)(2,1)S(1)} %bitcast.9, ...), custom_call_target="tpu_custom_call" | custom-call | flops 4800000000 | bytes 6000000 | tf_op jit(solution)/shard_map/backward_one_heads/pallas_call | solution.py:597
  44.0 0.5 collective-permute-start.8
  44.5 0.4 cut_two.1
  44.9 3.5 %collective-permute-start.10 = (bf16[2,960,128]{2,1,0:T(8,128)(2,1)S(1)}, bf16[2,960,128]{2,1,0:T(8,128)(2,1)S(1)}, u32[]{:S(2)}, u32[]{:S(2)}) collective-permute-start(bf16[2,960,128]{2,1,0:T(8,128)(2,1)S(1)} %get-tuple-element.121), channel_id=1, source_target_pairs={{0,64},{1,9},{4,68},{5,13},{8,72},{9,1},{12,76},{13,5},{2,66},{3,1... | collective-permute-start | bytes 1474568 | tf_op jit(solution)/shard_map/ppermute | solution.py:61
  48.4 0.3 fold_heads.1
  48.6 1.6 %collective-permute-start.13 = (bf16[2048,128]{1,0:T(8,128)(2,1)S(1)}, bf16[2048,128]{1,0:T(8,128)(2,1)S(1)}, u32[]{:S(2)}, u32[]{:S(2)}) collective-permute-start(bf16[2048,128]{1,0:T(8,128)(2,1)S(1)} %get-tuple-element.131), channel_id=1, source_target_pairs={{0,2},{1,19},{4,6},{5,23},{8,10},{9,27},{12,14},{13,31},{2,0},{3,1... | collective-permute-start | bytes 1572872 | tf_op jit(solution)/shard_map/ppermute | solution.py:61
  50.2 3.8 %backward_one_layers.1 = (f32[336,768]{1,0:T(8,128)}, bf16[2,1584,128]{2,1,0:T(8,128)(2,1)S(1)}, bf16[1584,128]{1,0:T(8,128)(2,1)S(1)}, bf16[1584,128]{1,0:T(8,128)(2,1)S(1)}) custom-call(s32[1,768]{1,0:T(1,128)S(1)} %broadcast_in_dim.3.label, f32[336,768]{1,0:T(8,128)S(1)} %get-tuple-element.109.g_in, bf16[512,768]{1,0:T(8,128)(2,1)S(1)} %get-tuple-element.122.d_in, ...), custom_call_target="tpu_custom_call" | custom-call | flops 4800000000 | bytes 6000000 | tf_op jit(solution)/shard_map/backward_one_layers/pallas_call | solution.py:626
  54.0 1.5 %collective-permute-start.11 = (bf16[1584,128]{1,0:T(8,128)(2,1)S(1)}, bf16[1584,128]{1,0:T(8,128)(2,1)S(1)}, u32[]{:S(2)}, u32[]{:S(2)}) collective-permute-start(bf16[1584,128]{1,0:T(8,128)(2,1)S(1)} %get-tuple-element.127), channel_id=1, source_target_pairs={{0,1},{1,0},{4,5},{5,4},{8,9},{9,8},{12,13},{13,12},{2,3},{3,2},{6... | collective-permute-start | bytes 1216520 | tf_op jit(solution)/shard_map/ppermute | solution.py:61
  55.6 1.6 %collective-permute-start.17 = (bf16[2,960,128]{2,1,0:T(8,128)(2,1)S(1)}, bf16[2,960,128]{2,1,0:T(8,128)(2,1)S(1)}, u32[]{:S(2)}, u32[]{:S(2)}) collective-permute-start(bf16[2,960,128]{2,1,0:T(8,128)(2,1)S(1)} %get-tuple-element.119), channel_id=1, source_target_pairs={{0,32},{1,5},{4,36},{5,1},{8,40},{9,13},{12,44},{13,9},{2,34},{3,7... | collective-permute-start | bytes 1474568 | tf_op jit(solution)/shard_map/ppermute | solution.py:61
  57.2 2.2 %collective-permute-start.18 = (bf16[2,960,128]{2,1,0:T(8,128)(2,1)S(1)}, bf16[2,960,128]{2,1,0:T(8,128)(2,1)S(1)}, u32[]{:S(2)}, u32[]{:S(2)}) collective-permute-start(bf16[2,960,128]{2,1,0:T(8,128)(2,1)S(1)} %get-tuple-element.120), channel_id=1, source_target_pairs={{0,96},{1,13},{4,100},{5,9},{8,104},{9,5},{12,108},{13,1},{2,98},{... | collective-permute-start | bytes 1474568 | tf_op jit(solution)/shard_map/ppermute | solution.py:61
  59.4 0.7 cut_one.1
  60.1 0.8 collective-permute-start.14
  61.0 1.1 collective-permute-start.15
  62.0 2.3 %collective-permute-start.16 = (bf16[1408,128]{1,0:T(8,128)(2,1)S(1)}, bf16[1408,128]{1,0:T(8,128)(2,1)S(1)}, u32[]{:S(2)}, u32[]{:S(2)}) collective-permute-start(bf16[1408,128]{1,0:T(8,128)(2,1)S(1)} %get-tuple-element.135), channel_id=1, source_target_pairs={{0,64},{1,9},{4,68},{5,13},{8,72},{9,1},{12,76},{13,5},{2,66},{3,1... | collective-permute-start | bytes 1081352 | tf_op jit(solution)/shard_map/ppermute | solution.py:61
  64.4 2.8 %collective-permute-done.18.b = bf16[2,960,128]{2,1,0:T(8,128)(2,1)S(1)} collective-permute-done((bf16[2,960,128]{2,1,0:T(8,128)(2,1)S(1)}, bf16[2,960,128]{2,1,0:T(8,128)(2,1)S(1)}, u32[]{:S(2)}, u32[]{:S(2)}) %collective-permute-start.18) | collective-permute-done | bytes 491552 | tf_op jit(solution)/shard_map/ppermute | solution.py:61
  67.2 0.2 fold.1
  67.5 0.6 collective-permute-start.19
  68.0 6.0 %collective-permute-done.19.came = bf16[960,128]{1,0:T(8,128)(2,1)S(1)} collective-permute-done((bf16[960,128]{1,0:T(8,128)(2,1)S(1)}, bf16[960,128]{1,0:T(8,128)(2,1)S(1)}, u32[]{:S(2)}, u32[]{:S(2)}) %collective-permute-start.19) | collective-permute-done | bytes 245792 | tf_op jit(solution)/shard_map/ppermute | solution.py:61
  74.0 0.9 collective-permute-done.15.b
  74.9 0.5 pieces.1
  75.5 2.4 %collective-permute-start.20 = (bf16[592,128]{1,0:T(8,128)(2,1)S(1)}, bf16[592,128]{1,0:T(8,128)(2,1)S(1)}, u32[]{:S(2)}, u32[]{:S(2)}) collective-permute-start(bf16[592,128]{1,0:T(8,128)(2,1)S(1)} %get-tuple-element.141), channel_id=1, source_target_pairs={{0,8},{1,65},{4,12},{5,69},{8,0},{9,73},{12,4},{13,77},{2,10},{3,6... | collective-permute-start | bytes 454664 | tf_op jit(solution)/shard_map/ppermute | solution.py:61
  77.9 1.3 %collective-permute-start.21 = (bf16[592,128]{1,0:T(8,128)(2,1)S(1)}, bf16[592,128]{1,0:T(8,128)(2,1)S(1)}, u32[]{:S(2)}, u32[]{:S(2)}) collective-permute-start(bf16[592,128]{1,0:T(8,128)(2,1)S(1)} %get-tuple-element.142), channel_id=1, source_target_pairs={{0,12},{1,97},{4,8},{5,101},{8,4},{9,105},{12,0},{13,109},{2,14},{... | collective-permute-start | bytes 454664 | tf_op jit(solution)/shard_map/ppermute | solution.py:61
  79.2 3.0 %collective-permute-done.20.a = bf16[592,128]{1,0:T(8,128)(2,1)S(1)} collective-permute-done((bf16[592,128]{1,0:T(8,128)(2,1)S(1)}, bf16[592,128]{1,0:T(8,128)(2,1)S(1)}, u32[]{:S(2)}, u32[]{:S(2)}) %collective-permute-start.20) | collective-permute-done | bytes 151584 | tf_op jit(solution)/shard_map/ppermute | solution.py:61
  82.2 2.1 %collective-permute-done.21.b = bf16[592,128]{1,0:T(8,128)(2,1)S(1)} collective-permute-done((bf16[592,128]{1,0:T(8,128)(2,1)S(1)}, bf16[592,128]{1,0:T(8,128)(2,1)S(1)}, u32[]{:S(2)}, u32[]{:S(2)}) %collective-permute-start.21) | collective-permute-done | bytes 151584 | tf_op jit(solution)/shard_map/ppermute | solution.py:61
  84.3 0.1 collective-permute-done.22.c
  84.5 2.7 %collective-permute-start.23 = (bf16[2,240,128]{2,1,0:T(8,128)(2,1)S(1)}, bf16[2,240,128]{2,1,0:T(8,128)(2,1)S(1)}, u32[]{:S(2)}, u32[]{:S(2)}) collective-permute-start(bf16[2,240,128]{2,1,0:T(8,128)(2,1)S(1)} %get-tuple-element.144.near), channel_id=1, source_target_pairs={{0,16},{1,17},{4,20},{5,21},{8,24},{9,25},{12,28},{13,29},{2,18},{... | collective-permute-start | bytes 368648 | tf_op jit(solution)/shard_map/ppermute | solution.py:61
  87.3 0.6 collective-permute-start.25
  87.8 0.8 collective-permute-start.24
  88.7 2.4 %collective-permute-done.25.c = bf16[112,128]{1,0:T(8,128)(2,1)S(1)} collective-permute-done((bf16[112,128]{1,0:T(8,128)(2,1)S(1)}, bf16[112,128]{1,0:T(8,128)(2,1)S(1)}, u32[]{:S(2)}, u32[]{:S(2)}) %collective-permute-start.25) | collective-permute-done | bytes 28704 | tf_op jit(solution)/shard_map/ppermute | solution.py:61
  91.1 1.8 %collective-permute-done.24.b = bf16[112,128]{1,0:T(8,128)(2,1)S(1)} collective-permute-done((bf16[112,128]{1,0:T(8,128)(2,1)S(1)}, bf16[112,128]{1,0:T(8,128)(2,1)S(1)}, u32[]{:S(2)}, u32[]{:S(2)}) %collective-permute-start.24) | collective-permute-done | bytes 28704 | tf_op jit(solution)/shard_map/ppermute | solution.py:61
  93.0 1.9 %collective-permute-start.28 = (bf16[2,240,128]{2,1,0:T(8,128)(2,1)S(1)}, bf16[2,240,128]{2,1,0:T(8,128)(2,1)S(1)}, u32[]{:S(2)}, u32[]{:S(2)}) collective-permute-start(bf16[2,240,128]{2,1,0:T(8,128)(2,1)S(1)} %across.1.refs_0_), channel_id=1, source_target_pairs={{0,8},{1,65},{4,12},{5,69},{8,0},{9,73},{12,4},{13,77},{2,10},{3,6... | collective-permute-start | bytes 368648 | tf_op jit(solution)/shard_map/ppermute | solution.py:61
  94.9 1.3 %collective-permute-start.27 = (bf16[2,240,128]{2,1,0:T(8,128)(2,1)S(1)}, bf16[2,240,128]{2,1,0:T(8,128)(2,1)S(1)}, u32[]{:S(2)}, u32[]{:S(2)}) collective-permute-start(bf16[2,240,128]{2,1,0:T(8,128)(2,1)S(1)} %across.1.refs_0_), channel_id=1, source_target_pairs={{0,12},{1,97},{4,8},{5,101},{8,4},{9,105},{12,0},{13,109},{2,14},{... | collective-permute-start | bytes 368648 | tf_op jit(solution)/shard_map/ppermute | solution.py:61
  96.2 0.4 collective-permute-start.26
  96.5 2.9 %collective-permute-done.28.refs_3_ = bf16[2,240,128]{2,1,0:T(8,128)(2,1)S(1)} collective-permute-done((bf16[2,240,128]{2,1,0:T(8,128)(2,1)S(1)}, bf16[2,240,128]{2,1,0:T(8,128)(2,1)S(1)}, u32[]{:S(2)}, u32[]{:S(2)}) %collective-permute-start.28) | collective-permute-done | bytes 122912 | tf_op jit(solution)/shard_map/ppermute | solution.py:61
  99.4 1.6 %collective-permute-done.27.refs_2_ = bf16[2,240,128]{2,1,0:T(8,128)(2,1)S(1)} collective-permute-done((bf16[2,240,128]{2,1,0:T(8,128)(2,1)S(1)}, bf16[2,240,128]{2,1,0:T(8,128)(2,1)S(1)}, u32[]{:S(2)}, u32[]{:S(2)}) %collective-permute-start.27) | collective-permute-done | bytes 122912 | tf_op jit(solution)/shard_map/ppermute | solution.py:61
  101.2 1.2 collective-permute-done.29.refs_4_.refs_11_
  102.3 2.1 %collective-permute-start.35 = (bf16[4,240,128]{2,1,0:T(8,128)(2,1)S(1)}, bf16[4,240,128]{2,1,0:T(8,128)(2,1)S(1)}, u32[]{:S(2)}, u32[]{:S(2)}) collective-permute-start(bf16[4,240,128]{2,1,0:T(8,128)(2,1)S(1)} %get-tuple-element.150.refs_0_), channel_id=1, source_target_pairs={{0,64},{1,9},{4,68},{5,13},{8,72},{9,1},{12,76},{13,5},{2,66},{3,1... | collective-permute-start | bytes 737288 | tf_op jit(solution)/shard_map/ppermute | solution.py:61
  104.4 1.1 collective-permute-start.34
  105.5 0.9 collective-permute-start.33
  106.4 2.7 %collective-permute-start.32 = (bf16[4,240,128]{2,1,0:T(8,128)(2,1)S(1)}, bf16[4,240,128]{2,1,0:T(8,128)(2,1)S(1)}, u32[]{:S(2)}, u32[]{:S(2)}) collective-permute-start(bf16[4,240,128]{2,1,0:T(8,128)(2,1)S(1)} %get-tuple-element.149.refs_0_), channel_id=1, source_target_pairs={{0,64},{1,9},{4,68},{5,13},{8,72},{9,1},{12,76},{13,5},{2,66},{3,1... | collective-permute-start | bytes 737288 | tf_op jit(solution)/shard_map/ppermute | solution.py:61
  109.1 1.1 collective-permute-start.31
  110.2 0.4 collective-permute-start.30
  110.6 2.1 %collective-permute-done.34.refs_2_ = bf16[4,240,128]{2,1,0:T(8,128)(2,1)S(1)} collective-permute-done((bf16[4,240,128]{2,1,0:T(8,128)(2,1)S(1)}, bf16[4,240,128]{2,1,0:T(8,128)(2,1)S(1)}, u32[]{:S(2)}, u32[]{:S(2)}) %collective-permute-start.34) | collective-permute-done | bytes 245792 | tf_op jit(solution)/shard_map/ppermute | solution.py:61
  112.7 0.6 collective-permute-done.33.refs_1_
  113.2 1.5 %unpack.2 = (f32[2,560,128]{2,1,0:T(8,128)}, f32[2,128,512]{2,1,0:T(8,128)}, f32[2,512,128]{2,1,0:T(8,128)}, f32[2,128,512]{2,1,0:T(8,128)}, f32[2,512,128]{2,1,...) custom-call(bf16[4,240,128]{2,1,0:T(8,128)(2,1)S(1)} %get-tuple-element.150.refs_0_, ...), custom_call_target="tpu_custom_call" | custom-call | flops 1600000000 | bytes 2000000 | tf_op jit(solution)/shard_map/unpack/pallas_call | solution.py:676
  114.8 1.3 %collective-permute-done.32.refs_3_ = bf16[4,240,128]{2,1,0:T(8,128)(2,1)S(1)} collective-permute-done((bf16[4,240,128]{2,1,0:T(8,128)(2,1)S(1)}, bf16[4,240,128]{2,1,0:T(8,128)(2,1)S(1)}, u32[]{:S(2)}, u32[]{:S(2)}) %collective-permute-start.32) | collective-permute-done | bytes 245792 | tf_op jit(solution)/shard_map/ppermute | solution.py:61
  116.0 2.5 %collective-permute-done.31.refs_2_ = bf16[4,240,128]{2,1,0:T(8,128)(2,1)S(1)} collective-permute-done((bf16[4,240,128]{2,1,0:T(8,128)(2,1)S(1)}, bf16[4,240,128]{2,1,0:T(8,128)(2,1)S(1)}, u32[]{:S(2)}, u32[]{:S(2)}) %collective-permute-start.31) | collective-permute-done | bytes 245792 | tf_op jit(solution)/shard_map/ppermute | solution.py:61
  118.6 1.5 %unpack.3 = (f32[2,560,128]{2,1,0:T(8,128)}, f32[2,128,512]{2,1,0:T(8,128)}, f32[2,512,128]{2,1,0:T(8,128)}, f32[2,128,512]{2,1,0:T(8,128)}, f32[2,512,128]{2,1,...) custom-call(bf16[4,240,128]{2,1,0:T(8,128)(2,1)S(1)} %get-tuple-elem, ...), custom_call_target="tpu_custom_call", output_to_operand_aliasing={{0}: (4, {}), {1}: (5, {}), {2}: (6, {}), {3}: (7, {}), {4}... | custom-call | flops 1600000000 | bytes 2000000 | tf_op jit(solution)/shard_map/unpack/pallas_call | solution.py:676
  (36 shorter events, 0.7 us)
Async XLA Ops:
  2.3 6.5 %collective-permute-start.1 = (bf16[960,128]{1,0:T(8,128)(2,1)}, bf16[960,128]{1,0:T(8,128)(2,1)S(1)}, u32[]{:S(2)}, u32[]{:S(2)}) collective-permute-start(bf16[960,128]{1,0:T(8,128)(2,1)} %pack_quarter.1), channel_id=1, source_target_pairs={{0,2},{1,19},{4,6},{5,23},{8,10},{9,27},{12,14},{13,31},{2,0},{3,1... | collective-permute-start | bytes 737288 | tf_op jit(solution)/shard_map/ppermute | solution.py:61
  7.3 16.7 %copy-start.4 = (s32[768]{0:T(1024)S(1)}, s32[768]{0:T(1024)}, u32[]{:S(2)}) copy-start(s32[768]{0:T(1024)} %param.12) | copy-start | bytes 9220
  7.3 18.4 %copy-start = (bf16[2,3840,128]{2,1,0:T(8,128)(2,1)S(1)}, bf16[2,3840,128]{2,1,0:T(8,128)(2,1)}, u32[]{:S(2)}) copy-start(bf16[2,3840,128]{2,1,0:T(8,128)(2,1)} %get-tuple-element.95.s0) | copy-start | bytes 5898244
  7.3 18.4 %copy-start.1 = (bf16[768,336]{0,1:T(8,128)(2,1)S(1)}, bf16[768,336]{0,1:T(8,128)(2,1)}, u32[]{:S(2)}) copy-start(bf16[768,336]{0,1:T(8,128)(2,1)} %param.11) | copy-start | bytes 1548292
  8.8 14.3 %collective-permute-start.2 = (bf16[3840,128]{1,0:T(8,128)(2,1)}, bf16[3840,128]{1,0:T(8,128)(2,1)S(1)}, u32[]{:S(2)}, u32[]{:S(2)}) collective-permute-start(bf16[3840,128]{1,0:T(8,128)(2,1)} %get-tuple-element.98), channel_id=1, source_target_pairs={{0,2},{1,19},{4,6},{5,23},{8,10},{9,27},{12,14},{13,31},{2,0},{3,1... | collective-permute-start | bytes 2949128 | tf_op jit(solution)/shard_map/ppermute | solution.py:61
  10.4 13.6 %collective-permute-start = (bf16[2,3840,128]{2,1,0:T(8,128)(2,1)}, bf16[2,3840,128]{2,1,0:T(8,128)(2,1)S(1)}, u32[]{:S(2)}, u32[]{:S(2)}) collective-permute-start(bf16[2,3840,128]{2,1,0:T(8,128)(2,1)} %get-tuple-element.95.s0), channel_id=1, source_target_pairs={{0,1},{1,0},{4,5},{5,4},{8,9},{9,8},{12,13},{13,12},{2,3},{3,2},{6... | collective-permute-start | bytes 5898248 | tf_op jit(solution)/shard_map/ppermute | solution.py:61
  11.3 7.7 %collective-permute-start.5 = (bf16[960,128]{1,0:T(8,128)(2,1)S(1)}, bf16[960,128]{1,0:T(8,128)(2,1)S(1)}, u32[]{:S(2)}, u32[]{:S(2)}) collective-permute-start(bf16[960,128]{1,0:T(8,128)(2,1)S(1)} %collective-permute-done.1.q0), channel_id=1, source_target_pairs={{0,64},{1,9},{4,68},{5,13},{8,72},{9,1},{12,76},{13,5},{2,66},{3,1... | collective-permute-start | bytes 737288 | tf_op jit(solution)/shard_map/ppermute | solution.py:61
  14.5 7.4 %collective-permute-start.4 = (bf16[960,128]{1,0:T(8,128)(2,1)S(1)}, bf16[960,128]{1,0:T(8,128)(2,1)S(1)}, u32[]{:S(2)}, u32[]{:S(2)}) collective-permute-start(bf16[960,128]{1,0:T(8,128)(2,1)S(1)} %collective-permute-done.1.q0), channel_id=1, source_target_pairs={{0,96},{1,13},{4,100},{5,9},{8,104},{9,5},{12,108},{13,1},{2,98},{... | collective-permute-start | bytes 737288 | tf_op jit(solution)/shard_map/ppermute | solution.py:61
  15.5 6.4 %collective-permute-start.3 = (bf16[960,128]{1,0:T(8,128)(2,1)S(1)}, bf16[960,128]{1,0:T(8,128)(2,1)S(1)}, u32[]{:S(2)}, u32[]{:S(2)}) collective-permute-start(bf16[960,128]{1,0:T(8,128)(2,1)S(1)} %collective-permute-done.1.q0), channel_id=1, source_target_pairs={{0,32},{1,5},{4,36},{5,1},{8,40},{9,13},{12,44},{13,9},{2,34},{3,7... | collective-permute-start | bytes 737288 | tf_op jit(solution)/shard_map/ppermute | solution.py:61
  23.1 2.6 %collective-permute-start.6 = (bf16[3840,128]{1,0:T(8,128)(2,1)S(1)}, bf16[3840,128]{1,0:T(8,128)(2,1)S(1)}, u32[]{:S(2)}, u32[]{:S(2)}) collective-permute-start(bf16[3840,128]{1,0:T(8,128)(2,1)S(1)} %collective-permute-done.2.s2), channel_id=1, source_target_pairs={{0,1},{1,0},{4,5},{5,4},{8,9},{9,8},{12,13},{13,12},{2,3},{3,2},{6... | collective-permute-start | bytes 2949128 | tf_op jit(solution)/shard_map/ppermute | solution.py:61
  23.2 6.3 %collective-permute-start.7 = (bf16[3840,128]{1,0:T(8,128)(2,1)S(1)}, bf16[3840,128]{1,0:T(8,128)(2,1)S(1)}, u32[]{:S(2)}, u32[]{:S(2)}) collective-permute-start(bf16[3840,128]{1,0:T(8,128)(2,1)S(1)} %join.1.s2), channel_id=1, source_target_pairs={{0,1},{1,0},{4,5},{5,4},{8,9},{9,8},{12,13},{13,12},{2,3},{3,2},{6... | collective-permute-start | bytes 2949128 | tf_op jit(solution)/shard_map/ppermute | solution.py:61
  25.7 3.8 %copy-start.2 = (bf16[768,336]{0,1:T(8,128)(2,1)S(1)}, bf16[768,336]{0,1:T(8,128)(2,1)}, u32[]{:S(2)}) copy-start(bf16[768,336]{0,1:T(8,128)(2,1)} %param.21) | copy-start | bytes 1548292
  25.7 3.8 %copy-start.3 = (bf16[768,48]{0,1:T(8,128)(2,1)S(1)}, bf16[768,48]{0,1:T(8,128)(2,1)}, u32[]{:S(2)}) copy-start(bf16[768,48]{0,1:T(8,128)(2,1)} %param.20) | copy-start | bytes 221188
  40.0 4.4 %collective-permute-start.9 = (bf16[2,3840,128]{2,1,0:T(8,128)(2,1)S(1)}, bf16[2,3840,128]{2,1,0:T(8,128)(2,1)S(1)}, u32[]{:S(2)}, u32[]{:S(2)}) collective-permute-start(bf16[2,3840,128]{2,1,0:T(8,128)(2,1)S(1)} %get-tuple-element.118), channel_id=1, source_target_pairs={{0,1},{1,0},{4,5},{5,4},{8,9},{9,8},{12,13},{13,12},{2,3},{3,2},{6... | collective-permute-start | bytes 5898248 | tf_op jit(solution)/shard_map/ppermute | solution.py:61
  44.0 4.4 %collective-permute-start.8 = (bf16[2,2176,128]{2,1,0:T(8,128)(2,1)S(1)}, bf16[2,2176,128]{2,1,0:T(8,128)(2,1)S(1)}, u32[]{:S(2)}, u32[]{:S(2)}) collective-permute-start(bf16[2,2176,128]{2,1,0:T(8,128)(2,1)S(1)} %get-tuple-element.115), channel_id=1, source_target_pairs={{0,1},{1,0},{4,5},{5,4},{8,9},{9,8},{12,13},{13,12},{2,3},{3,2},{6... | collective-permute-start | bytes 3342344 | tf_op jit(solution)/shard_map/ppermute | solution.py:61
  44.9 12.3 %collective-permute-start.10 = (bf16[2,960,128]{2,1,0:T(8,128)(2,1)S(1)}, bf16[2,960,128]{2,1,0:T(8,128)(2,1)S(1)}, u32[]{:S(2)}, u32[]{:S(2)}) collective-permute-start(bf16[2,960,128]{2,1,0:T(8,128)(2,1)S(1)} %get-tuple-element.121), channel_id=1, source_target_pairs={{0,64},{1,9},{4,68},{5,13},{8,72},{9,1},{12,76},{13,5},{2,66},{3,1... | collective-permute-start | bytes 1474568 | tf_op jit(solution)/shard_map/ppermute | solution.py:61
  48.6 10.8 %collective-permute-start.13 = (bf16[2048,128]{1,0:T(8,128)(2,1)S(1)}, bf16[2048,128]{1,0:T(8,128)(2,1)S(1)}, u32[]{:S(2)}, u32[]{:S(2)}) collective-permute-start(bf16[2048,128]{1,0:T(8,128)(2,1)S(1)} %get-tuple-element.131), channel_id=1, source_target_pairs={{0,2},{1,19},{4,6},{5,23},{8,10},{9,27},{12,14},{13,31},{2,0},{3,1... | collective-permute-start | bytes 1572872 | tf_op jit(solution)/shard_map/ppermute | solution.py:61
  54.0 5.5 %collective-permute-start.11 = (bf16[1584,128]{1,0:T(8,128)(2,1)S(1)}, bf16[1584,128]{1,0:T(8,128)(2,1)S(1)}, u32[]{:S(2)}, u32[]{:S(2)}) collective-permute-start(bf16[1584,128]{1,0:T(8,128)(2,1)S(1)} %get-tuple-element.127), channel_id=1, source_target_pairs={{0,1},{1,0},{4,5},{5,4},{8,9},{9,8},{12,13},{13,12},{2,3},{3,2},{6... | collective-permute-start | bytes 1216520 | tf_op jit(solution)/shard_map/ppermute | solution.py:61
  55.5 3.9 %collective-permute-start.12 = (bf16[1584,128]{1,0:T(8,128)(2,1)S(1)}, bf16[1584,128]{1,0:T(8,128)(2,1)S(1)}, u32[]{:S(2)}, u32[]{:S(2)}) collective-permute-start(bf16[1584,128]{1,0:T(8,128)(2,1)S(1)} %get-tuple-element.128), channel_id=1, source_target_pairs={{0,1},{1,0},{4,5},{5,4},{8,9},{9,8},{12,13},{13,12},{2,3},{3,2},{6... | collective-permute-start | bytes 1216520 | tf_op jit(solution)/shard_map/ppermute | solution.py:61
  55.6 8.8 %collective-permute-start.17 = (bf16[2,960,128]{2,1,0:T(8,128)(2,1)S(1)}, bf16[2,960,128]{2,1,0:T(8,128)(2,1)S(1)}, u32[]{:S(2)}, u32[]{:S(2)}) collective-permute-start(bf16[2,960,128]{2,1,0:T(8,128)(2,1)S(1)} %get-tuple-element.119), channel_id=1, source_target_pairs={{0,32},{1,5},{4,36},{5,1},{8,40},{9,13},{12,44},{13,9},{2,34},{3,7... | collective-permute-start | bytes 1474568 | tf_op jit(solution)/shard_map/ppermute | solution.py:61
  57.2 10.0 %collective-permute-start.18 = (bf16[2,960,128]{2,1,0:T(8,128)(2,1)S(1)}, bf16[2,960,128]{2,1,0:T(8,128)(2,1)S(1)}, u32[]{:S(2)}, u32[]{:S(2)}) collective-permute-start(bf16[2,960,128]{2,1,0:T(8,128)(2,1)S(1)} %get-tuple-element.120), channel_id=1, source_target_pairs={{0,96},{1,13},{4,100},{5,9},{8,104},{9,5},{12,108},{13,1},{2,98},{... | collective-permute-start | bytes 1474568 | tf_op jit(solution)/shard_map/ppermute | solution.py:61
  60.1 13.9 %collective-permute-start.14 = (bf16[1408,128]{1,0:T(8,128)(2,1)S(1)}, bf16[1408,128]{1,0:T(8,128)(2,1)S(1)}, u32[]{:S(2)}, u32[]{:S(2)}) collective-permute-start(bf16[1408,128]{1,0:T(8,128)(2,1)S(1)} %get-tuple-element.133), channel_id=1, source_target_pairs={{0,32},{1,5},{4,36},{5,1},{8,40},{9,13},{12,44},{13,9},{2,34},{3,7... | collective-permute-start | bytes 1081352 | tf_op jit(solution)/shard_map/ppermute | solution.py:61
  61.0 14.0 %collective-permute-start.15 = (bf16[1408,128]{1,0:T(8,128)(2,1)S(1)}, bf16[1408,128]{1,0:T(8,128)(2,1)S(1)}, u32[]{:S(2)}, u32[]{:S(2)}) collective-permute-start(bf16[1408,128]{1,0:T(8,128)(2,1)S(1)} %get-tuple-element.134), channel_id=1, source_target_pairs={{0,96},{1,13},{4,100},{5,9},{8,104},{9,5},{12,108},{13,1},{2,98},{... | collective-permute-start | bytes 1081352 | tf_op jit(solution)/shard_map/ppermute | solution.py:61
  62.0 12.9 %collective-permute-start.16 = (bf16[1408,128]{1,0:T(8,128)(2,1)S(1)}, bf16[1408,128]{1,0:T(8,128)(2,1)S(1)}, u32[]{:S(2)}, u32[]{:S(2)}) collective-permute-start(bf16[1408,128]{1,0:T(8,128)(2,1)S(1)} %get-tuple-element.135), channel_id=1, source_target_pairs={{0,64},{1,9},{4,68},{5,13},{8,72},{9,1},{12,76},{13,5},{2,66},{3,1... | collective-permute-start | bytes 1081352 | tf_op jit(solution)/shard_map/ppermute | solution.py:61
  67.5 6.5 %collective-permute-start.19 = (bf16[960,128]{1,0:T(8,128)(2,1)S(1)}, bf16[960,128]{1,0:T(8,128)(2,1)S(1)}, u32[]{:S(2)}, u32[]{:S(2)}) collective-permute-start(bf16[960,128]{1,0:T(8,128)(2,1)S(1)} %get-tuple-element.139), channel_id=1, source_target_pairs={{0,2},{1,19},{4,6},{5,23},{8,10},{9,27},{12,14},{13,31},{2,0},{3,1... | collective-permute-start | bytes 737288 | tf_op jit(solution)/shard_map/ppermute | solution.py:61
  75.5 6.8 %collective-permute-start.20 = (bf16[592,128]{1,0:T(8,128)(2,1)S(1)}, bf16[592,128]{1,0:T(8,128)(2,1)S(1)}, u32[]{:S(2)}, u32[]{:S(2)}) collective-permute-start(bf16[592,128]{1,0:T(8,128)(2,1)S(1)} %get-tuple-element.141), channel_id=1, source_target_pairs={{0,8},{1,65},{4,12},{5,69},{8,0},{9,73},{12,4},{13,77},{2,10},{3,6... | collective-permute-start | bytes 454664 | tf_op jit(solution)/shard_map/ppermute | solution.py:61
  77.9 6.4 %collective-permute-start.21 = (bf16[592,128]{1,0:T(8,128)(2,1)S(1)}, bf16[592,128]{1,0:T(8,128)(2,1)S(1)}, u32[]{:S(2)}, u32[]{:S(2)}) collective-permute-start(bf16[592,128]{1,0:T(8,128)(2,1)S(1)} %get-tuple-element.142), channel_id=1, source_target_pairs={{0,12},{1,97},{4,8},{5,101},{8,4},{9,105},{12,0},{13,109},{2,14},{... | collective-permute-start | bytes 454664 | tf_op jit(solution)/shard_map/ppermute | solution.py:61
  79.2 5.2 %collective-permute-start.22 = (bf16[592,128]{1,0:T(8,128)(2,1)S(1)}, bf16[592,128]{1,0:T(8,128)(2,1)S(1)}, u32[]{:S(2)}, u32[]{:S(2)}) collective-permute-start(bf16[592,128]{1,0:T(8,128)(2,1)S(1)} %get-tuple-element.143), channel_id=1, source_target_pairs={{0,4},{1,33},{4,0},{5,37},{8,12},{9,41},{12,8},{13,45},{2,6},{3,35... | collective-permute-start | bytes 454664 | tf_op jit(solution)/shard_map/ppermute | solution.py:61
  84.5 8.4 %collective-permute-start.23 = (bf16[2,240,128]{2,1,0:T(8,128)(2,1)S(1)}, bf16[2,240,128]{2,1,0:T(8,128)(2,1)S(1)}, u32[]{:S(2)}, u32[]{:S(2)}) collective-permute-start(bf16[2,240,128]{2,1,0:T(8,128)(2,1)S(1)} %get-tuple-element.144.near), channel_id=1, source_target_pairs={{0,16},{1,17},{4,20},{5,21},{8,24},{9,25},{12,28},{13,29},{2,18},{... | collective-permute-start | bytes 368648 | tf_op jit(solution)/shard_map/ppermute | solution.py:61
  87.3 3.9 %collective-permute-start.25 = (bf16[112,128]{1,0:T(8,128)(2,1)S(1)}, bf16[112,128]{1,0:T(8,128)(2,1)S(1)}, u32[]{:S(2)}, u32[]{:S(2)}) collective-permute-start(bf16[112,128]{1,0:T(8,128)(2,1)S(1)} %get-tuple-element.145), channel_id=1, source_target_pairs={{0,2},{1,3},{4,6},{5,7},{8,10},{9,11},{12,14},{13,15},{2,0},{3,1},... | collective-permute-start | bytes 86024 | tf_op jit(solution)/shard_map/ppermute | solution.py:61
  87.8 5.1 %collective-permute-start.24 = (bf16[112,128]{1,0:T(8,128)(2,1)S(1)}, bf16[112,128]{1,0:T(8,128)(2,1)S(1)}, u32[]{:S(2)}, u32[]{:S(2)}) collective-permute-start(bf16[112,128]{1,0:T(8,128)(2,1)S(1)} %get-tuple-element.145), channel_id=1, source_target_pairs={{0,18},{1,19},{4,22},{5,23},{8,26},{9,27},{12,30},{13,31},{2,16},{... | collective-permute-start | bytes 86024 | tf_op jit(solution)/shard_map/ppermute | solution.py:61
  93.0 6.5 %collective-permute-start.28 = (bf16[2,240,128]{2,1,0:T(8,128)(2,1)S(1)}, bf16[2,240,128]{2,1,0:T(8,128)(2,1)S(1)}, u32[]{:S(2)}, u32[]{:S(2)}) collective-permute-start(bf16[2,240,128]{2,1,0:T(8,128)(2,1)S(1)} %across.1.refs_0_), channel_id=1, source_target_pairs={{0,8},{1,65},{4,12},{5,69},{8,0},{9,73},{12,4},{13,77},{2,10},{3,6... | collective-permute-start | bytes 368648 | tf_op jit(solution)/shard_map/ppermute | solution.py:61
  94.9 6.1 %collective-permute-start.27 = (bf16[2,240,128]{2,1,0:T(8,128)(2,1)S(1)}, bf16[2,240,128]{2,1,0:T(8,128)(2,1)S(1)}, u32[]{:S(2)}, u32[]{:S(2)}) collective-permute-start(bf16[2,240,128]{2,1,0:T(8,128)(2,1)S(1)} %across.1.refs_0_), channel_id=1, source_target_pairs={{0,12},{1,97},{4,8},{5,101},{8,4},{9,105},{12,0},{13,109},{2,14},{... | collective-permute-start | bytes 368648 | tf_op jit(solution)/shard_map/ppermute | solution.py:61
  96.2 4.9 %collective-permute-start.26 = (bf16[2,240,128]{2,1,0:T(8,128)(2,1)S(1)}, bf16[2,240,128]{2,1,0:T(8,128)(2,1)S(1)}, u32[]{:S(2)}, u32[]{:S(2)}) collective-permute-start(bf16[2,240,128]{2,1,0:T(8,128)(2,1)S(1)} %across.1.refs_0_), channel_id=1, source_target_pairs={{0,4},{1,33},{4,0},{5,37},{8,12},{9,41},{12,8},{13,45},{2,6},{3,35... | collective-permute-start | bytes 368648 | tf_op jit(solution)/shard_map/ppermute | solution.py:61
  101.1 1.2 %collective-permute-start.29 = (bf16[16,128]{1,0:T(8,128)(2,1)S(1)}, bf16[16,128]{1,0:T(8,128)(2,1)S(1)}, u32[]{:S(2)}, u32[]{:S(2)}) collective-permute-start(bf16[16,128]{1,0:T(8,128)(2,1)S(1)} %get-tuple-element.148), channel_id=1, source_target_pairs={{0,1},{1,0},{4,5},{5,4},{8,9},{9,8},{12,13},{13,12},{2,3},{3,2},{6... | collective-permute-start | bytes 12296 | tf_op jit(solution)/shard_map/ppermute | solution.py:61
  102.3 7.9 %collective-permute-start.35 = (bf16[4,240,128]{2,1,0:T(8,128)(2,1)S(1)}, bf16[4,240,128]{2,1,0:T(8,128)(2,1)S(1)}, u32[]{:S(2)}, u32[]{:S(2)}) collective-permute-start(bf16[4,240,128]{2,1,0:T(8,128)(2,1)S(1)} %get-tuple-element.150.refs_0_), channel_id=1, source_target_pairs={{0,64},{1,9},{4,68},{5,13},{8,72},{9,1},{12,76},{13,5},{2,66},{3,1... | collective-permute-start | bytes 737288 | tf_op jit(solution)/shard_map/ppermute | solution.py:61
  104.4 8.3 %collective-permute-start.34 = (bf16[4,240,128]{2,1,0:T(8,128)(2,1)S(1)}, bf16[4,240,128]{2,1,0:T(8,128)(2,1)S(1)}, u32[]{:S(2)}, u32[]{:S(2)}) collective-permute-start(bf16[4,240,128]{2,1,0:T(8,128)(2,1)S(1)} %get-tuple-element.150.refs_0_), channel_id=1, source_target_pairs={{0,96},{1,13},{4,100},{5,9},{8,104},{9,5},{12,108},{13,1},{2,98},{... | collective-permute-start | bytes 737288 | tf_op jit(solution)/shard_map/ppermute | solution.py:61
  105.5 7.7 %collective-permute-start.33 = (bf16[4,240,128]{2,1,0:T(8,128)(2,1)S(1)}, bf16[4,240,128]{2,1,0:T(8,128)(2,1)S(1)}, u32[]{:S(2)}, u32[]{:S(2)}) collective-permute-start(bf16[4,240,128]{2,1,0:T(8,128)(2,1)S(1)} %get-tuple-element.150.refs_0_), channel_id=1, source_target_pairs={{0,32},{1,5},{4,36},{5,1},{8,40},{9,13},{12,44},{13,9},{2,34},{3,7... | collective-permute-start | bytes 737288 | tf_op jit(solution)/shard_map/ppermute | solution.py:61
  106.4 9.6 %collective-permute-start.32 = (bf16[4,240,128]{2,1,0:T(8,128)(2,1)S(1)}, bf16[4,240,128]{2,1,0:T(8,128)(2,1)S(1)}, u32[]{:S(2)}, u32[]{:S(2)}) collective-permute-start(bf16[4,240,128]{2,1,0:T(8,128)(2,1)S(1)} %get-tuple-element.149.refs_0_), channel_id=1, source_target_pairs={{0,64},{1,9},{4,68},{5,13},{8,72},{9,1},{12,76},{13,5},{2,66},{3,1... | collective-permute-start | bytes 737288 | tf_op jit(solution)/shard_map/ppermute | solution.py:61
  109.1 9.4 %collective-permute-start.31 = (bf16[4,240,128]{2,1,0:T(8,128)(2,1)S(1)}, bf16[4,240,128]{2,1,0:T(8,128)(2,1)S(1)}, u32[]{:S(2)}, u32[]{:S(2)}) collective-permute-start(bf16[4,240,128]{2,1,0:T(8,128)(2,1)S(1)} %get-tuple-element.149.refs_0_), channel_id=1, source_target_pairs={{0,96},{1,13},{4,100},{5,9},{8,104},{9,5},{12,108},{13,1},{2,98},{... | collective-permute-start | bytes 737288 | tf_op jit(solution)/shard_map/ppermute | solution.py:61
  110.2 8.3 %collective-permute-start.30 = (bf16[4,240,128]{2,1,0:T(8,128)(2,1)S(1)}, bf16[4,240,128]{2,1,0:T(8,128)(2,1)S(1)}, u32[]{:S(2)}, u32[]{:S(2)}) collective-permute-start(bf16[4,240,128]{2,1,0:T(8,128)(2,1)S(1)} %get-tuple-element.149.refs_0_), channel_id=1, source_target_pairs={{0,32},{1,5},{4,36},{5,1},{8,40},{9,13},{12,44},{13,9},{2,34},{3,7... | collective-permute-start | bytes 737288 | tf_op jit(solution)/shard_map/ppermute | solution.py:61

commit v9 on v8

--- a/solution.py
+++ b/solution.py
@@ -634,7 +634,7 @@
         6,
     )(label, g1, d_pre, *slots1, e1, act1, slope1)
     got1b = [send(part, to_core()) for part in theirs1b]
-    mine1b, got2[2] = lax.optimization_barrier((mine1b, got2[2]))
+    mine1b, got2[0], got2[1] = lax.optimization_barrier((mine1b, got2[0], got2[1]))
     *out1, own1 = small(
         cut_one_kernel,
         "cut_one",

time: 120 us -> 121 us (level)
  transfers between devices with their start and end apart: 36 -> 36, of which waited for: 23 -> 21; matrix products, arithmetic and copies ran while one was open for 0% -> 0% of each run, Pallas kernels for 15% -> 15%
where the time goes in v9:
time: 121 us; the launch traced here: 120 us
  starting transfers between devices  45.4 us (38%)
  waiting for transfers between devices  41.6 us (34%)
  Pallas kernels  32.2 us (27%)
    ppermute x36, starting transfers between devices, send(): return lax.ppermute(values, ('dp', 'mp'), where)  45.4 us
    ppermute x36, waiting for transfers between devices, send(): return lax.ppermute(values, ('dp', 'mp'), where)  41.6 us
    pallas_call x1, Pallas kernels, shards(): call(second_kernel, 'block_two', [IN_VMEM] * 9, [(shape(336, ROWS), IN_VM...  10.5 us
    pallas_call x1, Pallas kernels, shards(): call(first_kernel, 'forward_one', [IN_VMEM] * 6, [(shape(336, ROWS), IN_V...  3.78 us
    pallas_call x1, Pallas kernels, shards(): call(fourth_kernel, 'backward_one_layers', [IN_VMEM] * 10, [(shape(336, R...  3.76 us
    pallas_call x1, Pallas kernels, shards(): call(third_kernel, 'backward_one_heads', [IN_VMEM] * 10, [(shape(512, ROW...  3.76 us
    pallas_call x1, Pallas kernels, shards(): call(pack_kernel, 'pack', [IN_VMEM] * 7, [(shape(2, PACK, 128, kind=BF),...  3.33 us
    pallas_call x2, Pallas kernels, shards(): call(functools.partial(unpack_kernel, k), 'unpack', [IN_VMEM] * 4 + [ANYW...  3.04 us
  transfers between devices with their start and end apart: 36, of which 21 were waited for; matrix products, arithmetic and copies ran while one was open for 0% of the time, Pallas kernels for 15%

profile of v9, /device:TPU:0, one launch (start us, length us, event | category | flops | bytes accessed | tf_op | source)
XLA Modules:
  0.0 120.3 jit_solution(13417193596172023234)
XLA Ops:
  0.6 1.7 %pack_quarter.1 = bf16[960,128]{1,0:T(8,128)(2,1)} custom-call(bf16[2,560,128]{2,1,0:T(8,128)(2,1)} %refs_0_.2, bf16[2,128,512]{2,1,0:T(8,128)(2,1)} %refs_1_.2, bf16[2,512,128]{2,1,0:T(8,128)(2,1)} %refs_2_.2, bf16[2,128,512]{2,1,0:T(8,128)(2,1)} %refs_3_.2, bf16[2,512,128]{2,1,0:T(8,128)(2,1)} %refs_4_.2, bf16[2,512,128]{2,1,0:T(8,128)(2,1)} %refs_5_.2, ...), custom_call_target="tpu_custom_call" | custom-call | flops 800000000 | bytes 1000000 | tf_op jit(solution)/shard_map/pack_quarter/pallas_call | solution.py:548
  2.3 1.7 %collective-permute-start.1 = (bf16[960,128]{1,0:T(8,128)(2,1)}, bf16[960,128]{1,0:T(8,128)(2,1)S(1)}, u32[]{:S(2)}, u32[]{:S(2)}) collective-permute-start(bf16[960,128]{1,0:T(8,128)(2,1)} %pack_quarter.1), channel_id=1, source_target_pairs={{0,2},{1,19},{4,6},{5,23},{8,10},{9,27},{12,14},{13,31},{2,0},{3,1... | collective-permute-start | bytes 737288 | tf_op jit(solution)/shard_map/ppermute | solution.py:61
  4.0 3.3 %pack.1 = (bf16[2,3840,128]{2,1,0:T(8,128)(2,1)}, bf16[3840,128]{1,0:T(8,128)(2,1)}) custom-call(bf16[2,560,128]{2,1,0:T(8,128)(2,1)} %refs_0_.2, bf16[2,128,512]{2,1,0:T(8,128)(2,1)} %refs_1_.2, bf16[2,512,128]{2,1,0:T(8,128)(2,1)} %refs_2_.2, bf16[2,128,512]{2,1,0:T(8,128)(2,1)} %refs_3_.2, bf16[2,512,128]{2,1,0:T(8,128)(2,1)} %refs_4_.2, ...), custom_call_target="tpu_custom_call" | custom-call | flops 2400000000 | bytes 3000000 | tf_op jit(solution)/shard_map/pack/pallas_call | solution.py:558
  7.3 1.5 %collective-permute-done.1.q0 = bf16[960,128]{1,0:T(8,128)(2,1)S(1)} collective-permute-done((bf16[960,128]{1,0:T(8,128)(2,1)}, bf16[960,128]{1,0:T(8,128)(2,1)S(1)}, u32[]{:S(2)}, u32[]{:S(2)}) %collective-permute-start.1) | collective-permute-done | bytes 245792 | tf_op jit(solution)/shard_map/ppermute | solution.py:61
  8.8 1.6 %collective-permute-start.2 = (bf16[3840,128]{1,0:T(8,128)(2,1)}, bf16[3840,128]{1,0:T(8,128)(2,1)S(1)}, u32[]{:S(2)}, u32[]{:S(2)}) collective-permute-start(bf16[3840,128]{1,0:T(8,128)(2,1)} %get-tuple-element.99), channel_id=1, source_target_pairs={{0,2},{1,19},{4,6},{5,23},{8,10},{9,27},{12,14},{13,31},{2,0},{3,1... | collective-permute-start | bytes 2949128 | tf_op jit(solution)/shard_map/ppermute | solution.py:61
  10.4 0.9 collective-permute-start
  11.3 3.2 %collective-permute-start.5 = (bf16[960,128]{1,0:T(8,128)(2,1)S(1)}, bf16[960,128]{1,0:T(8,128)(2,1)S(1)}, u32[]{:S(2)}, u32[]{:S(2)}) collective-permute-start(bf16[960,128]{1,0:T(8,128)(2,1)S(1)} %collective-permute-done.1.q0), channel_id=1, source_target_pairs={{0,64},{1,9},{4,68},{5,13},{8,72},{9,1},{12,76},{13,5},{2,66},{3,1... | collective-permute-start | bytes 737288 | tf_op jit(solution)/shard_map/ppermute | solution.py:61
  14.5 1.1 collective-permute-start.4
  15.5 3.4 %collective-permute-done.5.q3 = bf16[960,128]{1,0:T(8,128)(2,1)S(1)} collective-permute-done((bf16[960,128]{1,0:T(8,128)(2,1)S(1)}, bf16[960,128]{1,0:T(8,128)(2,1)S(1)}, u32[]{:S(2)}, u32[]{:S(2)}) %collective-permute-start.5) | collective-permute-done | bytes 245792 | tf_op jit(solution)/shard_map/ppermute | solution.py:61
  19.0 2.9 %collective-permute-done.4.q2 = bf16[960,128]{1,0:T(8,128)(2,1)S(1)} collective-permute-done((bf16[960,128]{1,0:T(8,128)(2,1)S(1)}, bf16[960,128]{1,0:T(8,128)(2,1)S(1)}, u32[]{:S(2)}, u32[]{:S(2)}) %collective-permute-start.4) | collective-permute-done | bytes 245792 | tf_op jit(solution)/shard_map/ppermute | solution.py:61
  22.0 1.2 collective-permute-done.2.s2
  23.2 0.8 collective-permute-start.7
  24.0 1.7 %collective-permute-done.6.s3 = bf16[3840,128]{1,0:T(8,128)(2,1)S(1)} collective-permute-done((bf16[3840,128]{1,0:T(8,128)(2,1)S(1)}, bf16[3840,128]{1,0:T(8,128)(2,1)S(1)}, u32[]{:S(2)}, u32[]{:S(2)}) %collective-permute-start.6) | collective-permute-done | bytes 983072 | tf_op jit(solution)/shard_map/ppermute | solution.py:61
  25.7 3.8 %forward_one.1 = (f32[336,768]{1,0:T(8,128)S(1)}, f32[48,768]{1,0:T(8,128)S(1)}, bf16[560,768]{1,0:T(8,128)(2,1)S(1)}, bf16[4,512,768]{2,1,0:T(8,128)(2,1)S(1)},...) custom-call(s32[1,768]{1,0:T(1,128)S(1)} %broadcast_in_dim.3.label, bf16[336,768]{1,0:T(8,128)(2,1)S(1)} %bitcast.6, ...), custom_call_target="tpu_custom_call" | custom-call | flops 4800000000 | bytes 6000000 | tf_op jit(solution)/shard_map/forward_one/pallas_call | solution.py:576
  29.5 10.5 %block_two.1 = (f32[336,768]{1,0:T(8,128)}, f32[48,768]{1,0:T(8,128)}, f32[336,768]{1,0:T(8,128)S(1)}, bf16[2,3840,128]{2,1,0:T(8,128)(2,1)S(1)}, bf16[2,3840,128]{2,1,0:T(8,128)(2,1)S(1)}) custom-call(s32[1,768]{1,0:T(1,128)S(1)} %broadcast_in_dim.3.label, f32[336,768]{1,0:T(8,128)S(1)} %get-tuple-element.102.state_in, ...), custom_call_target="tpu_custom_call" | custom-call | flops 11200000000 | bytes 14000000 | tf_op jit(solution)/shard_map/block_two/pallas_call | solution.py:586
  40.0 0.2 collective-permute-start.9
  40.2 3.8 %backward_one_heads.1 = (bf16[512,768]{1,0:T(8,128)(2,1)S(1)}, bf16[2,2176,128]{2,1,0:T(8,128)(2,1)S(1)}, bf16[2,2176,128]{2,1,0:T(8,128)(2,1)S(1)}) custom-call(s32[1,768]{1,0:T(1,128)S(1)} %broadcast_in_dim.3.label, f32[336,768]{1,0:T(8,128)S(1)} %get-tuple-element.110.g_in, bf16[48,768]{1,0:T(8,128)(2,1)S(1)} %bitcast.9, ...), custom_call_target="tpu_custom_call" | custom-call | flops 4800000000 | bytes 6000000 | tf_op jit(solution)/shard_map/backward_one_heads/pallas_call | solution.py:597
  44.0 0.5 collective-permute-start.8
  44.5 0.4 cut_two.1
  44.9 1.8 %collective-permute-start.10 = (bf16[2,960,128]{2,1,0:T(8,128)(2,1)S(1)}, bf16[2,960,128]{2,1,0:T(8,128)(2,1)S(1)}, u32[]{:S(2)}, u32[]{:S(2)}) collective-permute-start(bf16[2,960,128]{2,1,0:T(8,128)(2,1)S(1)} %get-tuple-element.120), channel_id=1, source_target_pairs={{0,32},{1,5},{4,36},{5,1},{8,40},{9,13},{12,44},{13,9},{2,34},{3,7... | collective-permute-start | bytes 1474568 | tf_op jit(solution)/shard_map/ppermute | solution.py:61
  46.7 0.2 collective-permute-done.8.got
  46.8 0.3 fold_heads.1
  47.1 3.3 %collective-permute-start.11 = (bf16[2,960,128]{2,1,0:T(8,128)(2,1)S(1)}, bf16[2,960,128]{2,1,0:T(8,128)(2,1)S(1)}, u32[]{:S(2)}, u32[]{:S(2)}) collective-permute-start(bf16[2,960,128]{2,1,0:T(8,128)(2,1)S(1)} %get-tuple-element.121), channel_id=1, source_target_pairs={{0,96},{1,13},{4,100},{5,9},{8,104},{9,5},{12,108},{13,1},{2,98},{... | collective-permute-start | bytes 1474568 | tf_op jit(solution)/shard_map/ppermute | solution.py:61
  50.4 1.5 %collective-permute-start.14 = (bf16[2048,128]{1,0:T(8,128)(2,1)S(1)}, bf16[2048,128]{1,0:T(8,128)(2,1)S(1)}, u32[]{:S(2)}, u32[]{:S(2)}) collective-permute-start(bf16[2048,128]{1,0:T(8,128)(2,1)S(1)} %get-tuple-element.132), channel_id=1, source_target_pairs={{0,2},{1,19},{4,6},{5,23},{8,10},{9,27},{12,14},{13,31},{2,0},{3,1... | collective-permute-start | bytes 1572872 | tf_op jit(solution)/shard_map/ppermute | solution.py:61
  51.9 3.8 %backward_one_layers.1 = (f32[336,768]{1,0:T(8,128)}, bf16[2,1584,128]{2,1,0:T(8,128)(2,1)S(1)}, bf16[1584,128]{1,0:T(8,128)(2,1)S(1)}, bf16[1584,128]{1,0:T(8,128)(2,1)S(1)}) custom-call(s32[1,768]{1,0:T(1,128)S(1)} %broadcast_in_dim.3.label, f32[336,768]{1,0:T(8,128)S(1)} %get-tuple-element.110.g_in, bf16[512,768]{1,0:T(8,128)(2,1)S(1)} %get-tuple-element.123.d_in, ...), custom_call_target="tpu_custom_call" | custom-call | flops 4800000000 | bytes 6000000 | tf_op jit(solution)/shard_map/backward_one_layers/pallas_call | solution.py:626
  55.7 2.0 %collective-permute-start.12 = (bf16[1584,128]{1,0:T(8,128)(2,1)S(1)}, bf16[1584,128]{1,0:T(8,128)(2,1)S(1)}, u32[]{:S(2)}, u32[]{:S(2)}) collective-permute-start(bf16[1584,128]{1,0:T(8,128)(2,1)S(1)} %get-tuple-element.128), channel_id=1, source_target_pairs={{0,1},{1,0},{4,5},{5,4},{8,9},{9,8},{12,13},{13,12},{2,3},{3,2},{6... | collective-permute-start | bytes 1216520 | tf_op jit(solution)/shard_map/ppermute | solution.py:61
  57.8 3.3 %collective-permute-start.18 = (bf16[2,960,128]{2,1,0:T(8,128)(2,1)S(1)}, bf16[2,960,128]{2,1,0:T(8,128)(2,1)S(1)}, u32[]{:S(2)}, u32[]{:S(2)}) collective-permute-start(bf16[2,960,128]{2,1,0:T(8,128)(2,1)S(1)} %get-tuple-element.122), channel_id=1, source_target_pairs={{0,64},{1,9},{4,68},{5,13},{8,72},{9,1},{12,76},{13,5},{2,66},{3,1... | collective-permute-start | bytes 1474568 | tf_op jit(solution)/shard_map/ppermute | solution.py:61
  61.1 0.7 cut_one.1
  61.8 0.8 collective-permute-start.15
  62.6 1.6 %collective-permute-start.16 = (bf16[1408,128]{1,0:T(8,128)(2,1)S(1)}, bf16[1408,128]{1,0:T(8,128)(2,1)S(1)}, u32[]{:S(2)}, u32[]{:S(2)}) collective-permute-start(bf16[1408,128]{1,0:T(8,128)(2,1)S(1)} %get-tuple-element.135), channel_id=1, source_target_pairs={{0,96},{1,13},{4,100},{5,9},{8,104},{9,5},{12,108},{13,1},{2,98},{... | collective-permute-start | bytes 1081352 | tf_op jit(solution)/shard_map/ppermute | solution.py:61
  64.3 1.7 %collective-permute-start.17 = (bf16[1408,128]{1,0:T(8,128)(2,1)S(1)}, bf16[1408,128]{1,0:T(8,128)(2,1)S(1)}, u32[]{:S(2)}, u32[]{:S(2)}) collective-permute-start(bf16[1408,128]{1,0:T(8,128)(2,1)S(1)} %get-tuple-element.136), channel_id=1, source_target_pairs={{0,64},{1,9},{4,68},{5,13},{8,72},{9,1},{12,76},{13,5},{2,66},{3,1... | collective-permute-start | bytes 1081352 | tf_op jit(solution)/shard_map/ppermute | solution.py:61
  66.0 2.2 %collective-permute-done.18.c = bf16[2,960,128]{2,1,0:T(8,128)(2,1)S(1)} collective-permute-done((bf16[2,960,128]{2,1,0:T(8,128)(2,1)S(1)}, bf16[2,960,128]{2,1,0:T(8,128)(2,1)S(1)}, u32[]{:S(2)}, u32[]{:S(2)}) %collective-permute-start.18) | collective-permute-done | bytes 491552 | tf_op jit(solution)/shard_map/ppermute | solution.py:61
  68.2 0.2 fold.1
  68.5 0.6 collective-permute-start.19
  69.0 6.0 %collective-permute-done.19.came = bf16[960,128]{1,0:T(8,128)(2,1)S(1)} collective-permute-done((bf16[960,128]{1,0:T(8,128)(2,1)S(1)}, bf16[960,128]{1,0:T(8,128)(2,1)S(1)}, u32[]{:S(2)}, u32[]{:S(2)}) %collective-permute-start.19) | collective-permute-done | bytes 245792 | tf_op jit(solution)/shard_map/ppermute | solution.py:61
  75.0 0.9 collective-permute-done.17.c
  75.9 0.5 pieces.1
  76.4 2.5 %collective-permute-start.20 = (bf16[592,128]{1,0:T(8,128)(2,1)S(1)}, bf16[592,128]{1,0:T(8,128)(2,1)S(1)}, u32[]{:S(2)}, u32[]{:S(2)}) collective-permute-start(bf16[592,128]{1,0:T(8,128)(2,1)S(1)} %get-tuple-element.143), channel_id=1, source_target_pairs={{0,8},{1,65},{4,12},{5,69},{8,0},{9,73},{12,4},{13,77},{2,10},{3,6... | collective-permute-start | bytes 454664 | tf_op jit(solution)/shard_map/ppermute | solution.py:61
  78.8 0.7 collective-permute-start.21
  79.6 0.4 collective-permute-start.22
  80.0 3.2 %collective-permute-done.20.a = bf16[592,128]{1,0:T(8,128)(2,1)S(1)} collective-permute-done((bf16[592,128]{1,0:T(8,128)(2,1)S(1)}, bf16[592,128]{1,0:T(8,128)(2,1)S(1)}, u32[]{:S(2)}, u32[]{:S(2)}) %collective-permute-start.20) | collective-permute-done | bytes 151584 | tf_op jit(solution)/shard_map/ppermute | solution.py:61
  83.2 2.1 %collective-permute-done.21.b = bf16[592,128]{1,0:T(8,128)(2,1)S(1)} collective-permute-done((bf16[592,128]{1,0:T(8,128)(2,1)S(1)}, bf16[592,128]{1,0:T(8,128)(2,1)S(1)}, u32[]{:S(2)}, u32[]{:S(2)}) %collective-permute-start.21) | collective-permute-done | bytes 151584 | tf_op jit(solution)/shard_map/ppermute | solution.py:61
  85.3 2.8 %collective-permute-start.23 = (bf16[2,240,128]{2,1,0:T(8,128)(2,1)S(1)}, bf16[2,240,128]{2,1,0:T(8,128)(2,1)S(1)}, u32[]{:S(2)}, u32[]{:S(2)}) collective-permute-start(bf16[2,240,128]{2,1,0:T(8,128)(2,1)S(1)} %get-tuple-element.146.near), channel_id=1, source_target_pairs={{0,16},{1,17},{4,20},{5,21},{8,24},{9,25},{12,28},{13,29},{2,18},{... | collective-permute-start | bytes 368648 | tf_op jit(solution)/shard_map/ppermute | solution.py:61
  88.1 0.2 collective-permute-start.25
  88.4 1.1 collective-permute-start.24
  89.5 2.5 %collective-permute-done.25.c = bf16[112,128]{1,0:T(8,128)(2,1)S(1)} collective-permute-done((bf16[112,128]{1,0:T(8,128)(2,1)S(1)}, bf16[112,128]{1,0:T(8,128)(2,1)S(1)}, u32[]{:S(2)}, u32[]{:S(2)}) %collective-permute-start.25) | collective-permute-done | bytes 28704 | tf_op jit(solution)/shard_map/ppermute | solution.py:61
  92.0 1.4 %collective-permute-done.24.b = bf16[112,128]{1,0:T(8,128)(2,1)S(1)} collective-permute-done((bf16[112,128]{1,0:T(8,128)(2,1)S(1)}, bf16[112,128]{1,0:T(8,128)(2,1)S(1)}, u32[]{:S(2)}, u32[]{:S(2)}) %collective-permute-start.24) | collective-permute-done | bytes 28704 | tf_op jit(solution)/shard_map/ppermute | solution.py:61
  93.5 2.0 %collective-permute-start.28 = (bf16[2,240,128]{2,1,0:T(8,128)(2,1)S(1)}, bf16[2,240,128]{2,1,0:T(8,128)(2,1)S(1)}, u32[]{:S(2)}, u32[]{:S(2)}) collective-permute-start(bf16[2,240,128]{2,1,0:T(8,128)(2,1)S(1)} %across.1.refs_0_), channel_id=1, source_target_pairs={{0,8},{1,65},{4,12},{5,69},{8,0},{9,73},{12,4},{13,77},{2,10},{3,6... | collective-permute-start | bytes 368648 | tf_op jit(solution)/shard_map/ppermute | solution.py:61
  95.4 1.2 %collective-permute-start.27 = (bf16[2,240,128]{2,1,0:T(8,128)(2,1)S(1)}, bf16[2,240,128]{2,1,0:T(8,128)(2,1)S(1)}, u32[]{:S(2)}, u32[]{:S(2)}) collective-permute-start(bf16[2,240,128]{2,1,0:T(8,128)(2,1)S(1)} %across.1.refs_0_), channel_id=1, source_target_pairs={{0,12},{1,97},{4,8},{5,101},{8,4},{9,105},{12,0},{13,109},{2,14},{... | collective-permute-start | bytes 368648 | tf_op jit(solution)/shard_map/ppermute | solution.py:61
  96.7 0.4 collective-permute-start.26
  97.1 2.9 %collective-permute-done.28.refs_3_ = bf16[2,240,128]{2,1,0:T(8,128)(2,1)S(1)} collective-permute-done((bf16[2,240,128]{2,1,0:T(8,128)(2,1)S(1)}, bf16[2,240,128]{2,1,0:T(8,128)(2,1)S(1)}, u32[]{:S(2)}, u32[]{:S(2)}) %collective-permute-start.28) | collective-permute-done | bytes 122912 | tf_op jit(solution)/shard_map/ppermute | solution.py:61
  100.0 1.6 %collective-permute-done.27.refs_2_ = bf16[2,240,128]{2,1,0:T(8,128)(2,1)S(1)} collective-permute-done((bf16[2,240,128]{2,1,0:T(8,128)(2,1)S(1)}, bf16[2,240,128]{2,1,0:T(8,128)(2,1)S(1)}, u32[]{:S(2)}, u32[]{:S(2)}) %collective-permute-start.27) | collective-permute-done | bytes 122912 | tf_op jit(solution)/shard_map/ppermute | solution.py:61
  101.7 1.2 collective-permute-done.29.refs_4_.refs_11_
  102.9 1.5 %collective-permute-start.35 = (bf16[4,240,128]{2,1,0:T(8,128)(2,1)S(1)}, bf16[4,240,128]{2,1,0:T(8,128)(2,1)S(1)}, u32[]{:S(2)}, u32[]{:S(2)}) collective-permute-start(bf16[4,240,128]{2,1,0:T(8,128)(2,1)S(1)} %get-tuple-element.152.refs_0_), channel_id=1, source_target_pairs={{0,64},{1,9},{4,68},{5,13},{8,72},{9,1},{12,76},{13,5},{2,66},{3,1... | collective-permute-start | bytes 737288 | tf_op jit(solution)/shard_map/ppermute | solution.py:61
  104.4 1.2 collective-permute-start.34
  105.6 0.8 collective-permute-start.33
  106.4 2.8 %collective-permute-start.32 = (bf16[4,240,128]{2,1,0:T(8,128)(2,1)S(1)}, bf16[4,240,128]{2,1,0:T(8,128)(2,1)S(1)}, u32[]{:S(2)}, u32[]{:S(2)}) collective-permute-start(bf16[4,240,128]{2,1,0:T(8,128)(2,1)S(1)} %get-tuple-element.151.refs_0_), channel_id=1, source_target_pairs={{0,64},{1,9},{4,68},{5,13},{8,72},{9,1},{12,76},{13,5},{2,66},{3,1... | collective-permute-start | bytes 737288 | tf_op jit(solution)/shard_map/ppermute | solution.py:61
  109.1 1.2 collective-permute-start.31
  110.3 0.4 collective-permute-done.35.refs_3_
  110.7 2.5 %collective-permute-done.34.refs_2_ = bf16[4,240,128]{2,1,0:T(8,128)(2,1)S(1)} collective-permute-done((bf16[4,240,128]{2,1,0:T(8,128)(2,1)S(1)}, bf16[4,240,128]{2,1,0:T(8,128)(2,1)S(1)}, u32[]{:S(2)}, u32[]{:S(2)}) %collective-permute-start.34) | collective-permute-done | bytes 245792 | tf_op jit(solution)/shard_map/ppermute | solution.py:61
  113.2 1.5 %unpack.2 = (f32[2,560,128]{2,1,0:T(8,128)}, f32[2,128,512]{2,1,0:T(8,128)}, f32[2,512,128]{2,1,0:T(8,128)}, f32[2,128,512]{2,1,0:T(8,128)}, f32[2,512,128]{2,1,...) custom-call(bf16[4,240,128]{2,1,0:T(8,128)(2,1)S(1)} %get-tuple-element.152.refs_0_, ...), custom_call_target="tpu_custom_call" | custom-call | flops 1600000000 | bytes 2000000 | tf_op jit(solution)/shard_map/unpack/pallas_call | solution.py:676
  114.7 1.3 %collective-permute-done.32.refs_3_ = bf16[4,240,128]{2,1,0:T(8,128)(2,1)S(1)} collective-permute-done((bf16[4,240,128]{2,1,0:T(8,128)(2,1)S(1)}, bf16[4,240,128]{2,1,0:T(8,128)(2,1)S(1)}, u32[]{:S(2)}, u32[]{:S(2)}) %collective-permute-start.32) | collective-permute-done | bytes 245792 | tf_op jit(solution)/shard_map/ppermute | solution.py:61
  116.0 2.5 %collective-permute-done.31.refs_2_ = bf16[4,240,128]{2,1,0:T(8,128)(2,1)S(1)} collective-permute-done((bf16[4,240,128]{2,1,0:T(8,128)(2,1)S(1)}, bf16[4,240,128]{2,1,0:T(8,128)(2,1)S(1)}, u32[]{:S(2)}, u32[]{:S(2)}) %collective-permute-start.31) | collective-permute-done | bytes 245792 | tf_op jit(solution)/shard_map/ppermute | solution.py:61
  118.5 1.5 %unpack.3 = (f32[2,560,128]{2,1,0:T(8,128)}, f32[2,128,512]{2,1,0:T(8,128)}, f32[2,512,128]{2,1,0:T(8,128)}, f32[2,128,512]{2,1,0:T(8,128)}, f32[2,512,128]{2,1,...) custom-call(bf16[4,240,128]{2,1,0:T(8,128)(2,1)S(1)} %get-tuple-elem, ...), custom_call_target="tpu_custom_call", output_to_operand_aliasing={{0}: (4, {}), {1}: (5, {}), {2}: (6, {}), {3}: (7, {}), {4}... | custom-call | flops 1600000000 | bytes 2000000 | tf_op jit(solution)/shard_map/unpack/pallas_call | solution.py:676
  (36 shorter events, 0.7 us)
Async XLA Ops:
  2.3 6.5 %collective-permute-start.1 = (bf16[960,128]{1,0:T(8,128)(2,1)}, bf16[960,128]{1,0:T(8,128)(2,1)S(1)}, u32[]{:S(2)}, u32[]{:S(2)}) collective-permute-start(bf16[960,128]{1,0:T(8,128)(2,1)} %pack_quarter.1), channel_id=1, source_target_pairs={{0,2},{1,19},{4,6},{5,23},{8,10},{9,27},{12,14},{13,31},{2,0},{3,1... | collective-permute-start | bytes 737288 | tf_op jit(solution)/shard_map/ppermute | solution.py:61
  7.3 16.7 %copy-start.4 = (s32[768]{0:T(1024)S(1)}, s32[768]{0:T(1024)}, u32[]{:S(2)}) copy-start(s32[768]{0:T(1024)} %param.12) | copy-start | bytes 9220
  7.3 18.4 %copy-start = (bf16[2,3840,128]{2,1,0:T(8,128)(2,1)S(1)}, bf16[2,3840,128]{2,1,0:T(8,128)(2,1)}, u32[]{:S(2)}) copy-start(bf16[2,3840,128]{2,1,0:T(8,128)(2,1)} %get-tuple-element.96.s0) | copy-start | bytes 5898244
  7.3 18.4 %copy-start.1 = (bf16[768,336]{0,1:T(8,128)(2,1)S(1)}, bf16[768,336]{0,1:T(8,128)(2,1)}, u32[]{:S(2)}) copy-start(bf16[768,336]{0,1:T(8,128)(2,1)} %param.11) | copy-start | bytes 1548292
  8.8 14.3 %collective-permute-start.2 = (bf16[3840,128]{1,0:T(8,128)(2,1)}, bf16[3840,128]{1,0:T(8,128)(2,1)S(1)}, u32[]{:S(2)}, u32[]{:S(2)}) collective-permute-start(bf16[3840,128]{1,0:T(8,128)(2,1)} %get-tuple-element.99), channel_id=1, source_target_pairs={{0,2},{1,19},{4,6},{5,23},{8,10},{9,27},{12,14},{13,31},{2,0},{3,1... | collective-permute-start | bytes 2949128 | tf_op jit(solution)/shard_map/ppermute | solution.py:61
  10.4 13.6 %collective-permute-start = (bf16[2,3840,128]{2,1,0:T(8,128)(2,1)}, bf16[2,3840,128]{2,1,0:T(8,128)(2,1)S(1)}, u32[]{:S(2)}, u32[]{:S(2)}) collective-permute-start(bf16[2,3840,128]{2,1,0:T(8,128)(2,1)} %get-tuple-element.96.s0), channel_id=1, source_target_pairs={{0,1},{1,0},{4,5},{5,4},{8,9},{9,8},{12,13},{13,12},{2,3},{3,2},{6... | collective-permute-start | bytes 5898248 | tf_op jit(solution)/shard_map/ppermute | solution.py:61
  11.3 7.7 %collective-permute-start.5 = (bf16[960,128]{1,0:T(8,128)(2,1)S(1)}, bf16[960,128]{1,0:T(8,128)(2,1)S(1)}, u32[]{:S(2)}, u32[]{:S(2)}) collective-permute-start(bf16[960,128]{1,0:T(8,128)(2,1)S(1)} %collective-permute-done.1.q0), channel_id=1, source_target_pairs={{0,64},{1,9},{4,68},{5,13},{8,72},{9,1},{12,76},{13,5},{2,66},{3,1... | collective-permute-start | bytes 737288 | tf_op jit(solution)/shard_map/ppermute | solution.py:61
  14.5 7.4 %collective-permute-start.4 = (bf16[960,128]{1,0:T(8,128)(2,1)S(1)}, bf16[960,128]{1,0:T(8,128)(2,1)S(1)}, u32[]{:S(2)}, u32[]{:S(2)}) collective-permute-start(bf16[960,128]{1,0:T(8,128)(2,1)S(1)} %collective-permute-done.1.q0), channel_id=1, source_target_pairs={{0,96},{1,13},{4,100},{5,9},{8,104},{9,5},{12,108},{13,1},{2,98},{... | collective-permute-start | bytes 737288 | tf_op jit(solution)/shard_map/ppermute | solution.py:61
  15.5 6.4 %collective-permute-start.3 = (bf16[960,128]{1,0:T(8,128)(2,1)S(1)}, bf16[960,128]{1,0:T(8,128)(2,1)S(1)}, u32[]{:S(2)}, u32[]{:S(2)}) collective-permute-start(bf16[960,128]{1,0:T(8,128)(2,1)S(1)} %collective-permute-done.1.q0), channel_id=1, source_target_pairs={{0,32},{1,5},{4,36},{5,1},{8,40},{9,13},{12,44},{13,9},{2,34},{3,7... | collective-permute-start | bytes 737288 | tf_op jit(solution)/shard_map/ppermute | solution.py:61
  23.1 2.6 %collective-permute-start.6 = (bf16[3840,128]{1,0:T(8,128)(2,1)S(1)}, bf16[3840,128]{1,0:T(8,128)(2,1)S(1)}, u32[]{:S(2)}, u32[]{:S(2)}) collective-permute-start(bf16[3840,128]{1,0:T(8,128)(2,1)S(1)} %collective-permute-done.2.s2), channel_id=1, source_target_pairs={{0,1},{1,0},{4,5},{5,4},{8,9},{9,8},{12,13},{13,12},{2,3},{3,2},{6... | collective-permute-start | bytes 2949128 | tf_op jit(solution)/shard_map/ppermute | solution.py:61
  23.2 6.3 %collective-permute-start.7 = (bf16[3840,128]{1,0:T(8,128)(2,1)S(1)}, bf16[3840,128]{1,0:T(8,128)(2,1)S(1)}, u32[]{:S(2)}, u32[]{:S(2)}) collective-permute-start(bf16[3840,128]{1,0:T(8,128)(2,1)S(1)} %join.1.s2), channel_id=1, source_target_pairs={{0,1},{1,0},{4,5},{5,4},{8,9},{9,8},{12,13},{13,12},{2,3},{3,2},{6... | collective-permute-start | bytes 2949128 | tf_op jit(solution)/shard_map/ppermute | solution.py:61
  25.7 3.8 %copy-start.2 = (bf16[768,336]{0,1:T(8,128)(2,1)S(1)}, bf16[768,336]{0,1:T(8,128)(2,1)}, u32[]{:S(2)}) copy-start(bf16[768,336]{0,1:T(8,128)(2,1)} %param.21) | copy-start | bytes 1548292
  25.7 3.8 %copy-start.3 = (bf16[768,48]{0,1:T(8,128)(2,1)S(1)}, bf16[768,48]{0,1:T(8,128)(2,1)}, u32[]{:S(2)}) copy-start(bf16[768,48]{0,1:T(8,128)(2,1)} %param.20) | copy-start | bytes 221188
  40.0 4.4 %collective-permute-start.9 = (bf16[2,3840,128]{2,1,0:T(8,128)(2,1)S(1)}, bf16[2,3840,128]{2,1,0:T(8,128)(2,1)S(1)}, u32[]{:S(2)}, u32[]{:S(2)}) collective-permute-start(bf16[2,3840,128]{2,1,0:T(8,128)(2,1)S(1)} %get-tuple-element.119), channel_id=1, source_target_pairs={{0,1},{1,0},{4,5},{5,4},{8,9},{9,8},{12,13},{13,12},{2,3},{3,2},{6... | collective-permute-start | bytes 5898248 | tf_op jit(solution)/shard_map/ppermute | solution.py:61
  44.0 2.8 %collective-permute-start.8 = (bf16[2,2176,128]{2,1,0:T(8,128)(2,1)S(1)}, bf16[2,2176,128]{2,1,0:T(8,128)(2,1)S(1)}, u32[]{:S(2)}, u32[]{:S(2)}) collective-permute-start(bf16[2,2176,128]{2,1,0:T(8,128)(2,1)S(1)} %get-tuple-element.116), channel_id=1, source_target_pairs={{0,1},{1,0},{4,5},{5,4},{8,9},{9,8},{12,13},{13,12},{2,3},{3,2},{6... | collective-permute-start | bytes 3342344 | tf_op jit(solution)/shard_map/ppermute | solution.py:61
  44.9 12.9 %collective-permute-start.10 = (bf16[2,960,128]{2,1,0:T(8,128)(2,1)S(1)}, bf16[2,960,128]{2,1,0:T(8,128)(2,1)S(1)}, u32[]{:S(2)}, u32[]{:S(2)}) collective-permute-start(bf16[2,960,128]{2,1,0:T(8,128)(2,1)S(1)} %get-tuple-element.120), channel_id=1, source_target_pairs={{0,32},{1,5},{4,36},{5,1},{8,40},{9,13},{12,44},{13,9},{2,34},{3,7... | collective-permute-start | bytes 1474568 | tf_op jit(solution)/shard_map/ppermute | solution.py:61
  47.1 14.0 %collective-permute-start.11 = (bf16[2,960,128]{2,1,0:T(8,128)(2,1)S(1)}, bf16[2,960,128]{2,1,0:T(8,128)(2,1)S(1)}, u32[]{:S(2)}, u32[]{:S(2)}) collective-permute-start(bf16[2,960,128]{2,1,0:T(8,128)(2,1)S(1)} %get-tuple-element.121), channel_id=1, source_target_pairs={{0,96},{1,13},{4,100},{5,9},{8,104},{9,5},{12,108},{13,1},{2,98},{... | collective-permute-start | bytes 1474568 | tf_op jit(solution)/shard_map/ppermute | solution.py:61
  50.4 10.7 %collective-permute-start.14 = (bf16[2048,128]{1,0:T(8,128)(2,1)S(1)}, bf16[2048,128]{1,0:T(8,128)(2,1)S(1)}, u32[]{:S(2)}, u32[]{:S(2)}) collective-permute-start(bf16[2048,128]{1,0:T(8,128)(2,1)S(1)} %get-tuple-element.132), channel_id=1, source_target_pairs={{0,2},{1,19},{4,6},{5,23},{8,10},{9,27},{12,14},{13,31},{2,0},{3,1... | collective-permute-start | bytes 1572872 | tf_op jit(solution)/shard_map/ppermute | solution.py:61
  55.7 5.4 %collective-permute-start.12 = (bf16[1584,128]{1,0:T(8,128)(2,1)S(1)}, bf16[1584,128]{1,0:T(8,128)(2,1)S(1)}, u32[]{:S(2)}, u32[]{:S(2)}) collective-permute-start(bf16[1584,128]{1,0:T(8,128)(2,1)S(1)} %get-tuple-element.128), channel_id=1, source_target_pairs={{0,1},{1,0},{4,5},{5,4},{8,9},{9,8},{12,13},{13,12},{2,3},{3,2},{6... | collective-permute-start | bytes 1216520 | tf_op jit(solution)/shard_map/ppermute | solution.py:61
  57.7 3.4 %collective-permute-start.13 = (bf16[1584,128]{1,0:T(8,128)(2,1)S(1)}, bf16[1584,128]{1,0:T(8,128)(2,1)S(1)}, u32[]{:S(2)}, u32[]{:S(2)}) collective-permute-start(bf16[1584,128]{1,0:T(8,128)(2,1)S(1)} %get-tuple-element.129), channel_id=1, source_target_pairs={{0,1},{1,0},{4,5},{5,4},{8,9},{9,8},{12,13},{13,12},{2,3},{3,2},{6... | collective-permute-start | bytes 1216520 | tf_op jit(solution)/shard_map/ppermute | solution.py:61
  57.8 10.4 %collective-permute-start.18 = (bf16[2,960,128]{2,1,0:T(8,128)(2,1)S(1)}, bf16[2,960,128]{2,1,0:T(8,128)(2,1)S(1)}, u32[]{:S(2)}, u32[]{:S(2)}) collective-permute-start(bf16[2,960,128]{2,1,0:T(8,128)(2,1)S(1)} %get-tuple-element.122), channel_id=1, source_target_pairs={{0,64},{1,9},{4,68},{5,13},{8,72},{9,1},{12,76},{13,5},{2,66},{3,1... | collective-permute-start | bytes 1474568 | tf_op jit(solution)/shard_map/ppermute | solution.py:61
  61.8 13.2 %collective-permute-start.15 = (bf16[1408,128]{1,0:T(8,128)(2,1)S(1)}, bf16[1408,128]{1,0:T(8,128)(2,1)S(1)}, u32[]{:S(2)}, u32[]{:S(2)}) collective-permute-start(bf16[1408,128]{1,0:T(8,128)(2,1)S(1)} %get-tuple-element.134), channel_id=1, source_target_pairs={{0,32},{1,5},{4,36},{5,1},{8,40},{9,13},{12,44},{13,9},{2,34},{3,7... | collective-permute-start | bytes 1081352 | tf_op jit(solution)/shard_map/ppermute | solution.py:61
  62.6 12.4 %collective-permute-start.16 = (bf16[1408,128]{1,0:T(8,128)(2,1)S(1)}, bf16[1408,128]{1,0:T(8,128)(2,1)S(1)}, u32[]{:S(2)}, u32[]{:S(2)}) collective-permute-start(bf16[1408,128]{1,0:T(8,128)(2,1)S(1)} %get-tuple-element.135), channel_id=1, source_target_pairs={{0,96},{1,13},{4,100},{5,9},{8,104},{9,5},{12,108},{13,1},{2,98},{... | collective-permute-start | bytes 1081352 | tf_op jit(solution)/shard_map/ppermute | solution.py:61
  64.3 11.6 %collective-permute-start.17 = (bf16[1408,128]{1,0:T(8,128)(2,1)S(1)}, bf16[1408,128]{1,0:T(8,128)(2,1)S(1)}, u32[]{:S(2)}, u32[]{:S(2)}) collective-permute-start(bf16[1408,128]{1,0:T(8,128)(2,1)S(1)} %get-tuple-element.136), channel_id=1, source_target_pairs={{0,64},{1,9},{4,68},{5,13},{8,72},{9,1},{12,76},{13,5},{2,66},{3,1... | collective-permute-start | bytes 1081352 | tf_op jit(solution)/shard_map/ppermute | solution.py:61
  68.5 6.5 %collective-permute-start.19 = (bf16[960,128]{1,0:T(8,128)(2,1)S(1)}, bf16[960,128]{1,0:T(8,128)(2,1)S(1)}, u32[]{:S(2)}, u32[]{:S(2)}) collective-permute-start(bf16[960,128]{1,0:T(8,128)(2,1)S(1)} %get-tuple-element.141), channel_id=1, source_target_pairs={{0,2},{1,19},{4,6},{5,23},{8,10},{9,27},{12,14},{13,31},{2,0},{3,1... | collective-permute-start | bytes 737288 | tf_op jit(solution)/shard_map/ppermute | solution.py:61
  76.4 6.8 %collective-permute-start.20 = (bf16[592,128]{1,0:T(8,128)(2,1)S(1)}, bf16[592,128]{1,0:T(8,128)(2,1)S(1)}, u32[]{:S(2)}, u32[]{:S(2)}) collective-permute-start(bf16[592,128]{1,0:T(8,128)(2,1)S(1)} %get-tuple-element.143), channel_id=1, source_target_pairs={{0,8},{1,65},{4,12},{5,69},{8,0},{9,73},{12,4},{13,77},{2,10},{3,6... | collective-permute-start | bytes 454664 | tf_op jit(solution)/shard_map/ppermute | solution.py:61
  78.8 6.4 %collective-permute-start.21 = (bf16[592,128]{1,0:T(8,128)(2,1)S(1)}, bf16[592,128]{1,0:T(8,128)(2,1)S(1)}, u32[]{:S(2)}, u32[]{:S(2)}) collective-permute-start(bf16[592,128]{1,0:T(8,128)(2,1)S(1)} %get-tuple-element.144), channel_id=1, source_target_pairs={{0,12},{1,97},{4,8},{5,101},{8,4},{9,105},{12,0},{13,109},{2,14},{... | collective-permute-start | bytes 454664 | tf_op jit(solution)/shard_map/ppermute | solution.py:61
  79.6 5.7 %collective-permute-start.22 = (bf16[592,128]{1,0:T(8,128)(2,1)S(1)}, bf16[592,128]{1,0:T(8,128)(2,1)S(1)}, u32[]{:S(2)}, u32[]{:S(2)}) collective-permute-start(bf16[592,128]{1,0:T(8,128)(2,1)S(1)} %get-tuple-element.145), channel_id=1, source_target_pairs={{0,4},{1,33},{4,0},{5,37},{8,12},{9,41},{12,8},{13,45},{2,6},{3,35... | collective-permute-start | bytes 454664 | tf_op jit(solution)/shard_map/ppermute | solution.py:61
  85.3 8.1 %collective-permute-start.23 = (bf16[2,240,128]{2,1,0:T(8,128)(2,1)S(1)}, bf16[2,240,128]{2,1,0:T(8,128)(2,1)S(1)}, u32[]{:S(2)}, u32[]{:S(2)}) collective-permute-start(bf16[2,240,128]{2,1,0:T(8,128)(2,1)S(1)} %get-tuple-element.146.near), channel_id=1, source_target_pairs={{0,16},{1,17},{4,20},{5,21},{8,24},{9,25},{12,28},{13,29},{2,18},{... | collective-permute-start | bytes 368648 | tf_op jit(solution)/shard_map/ppermute | solution.py:61
  88.1 3.9 %collective-permute-start.25 = (bf16[112,128]{1,0:T(8,128)(2,1)S(1)}, bf16[112,128]{1,0:T(8,128)(2,1)S(1)}, u32[]{:S(2)}, u32[]{:S(2)}) collective-permute-start(bf16[112,128]{1,0:T(8,128)(2,1)S(1)} %get-tuple-element.147), channel_id=1, source_target_pairs={{0,2},{1,3},{4,6},{5,7},{8,10},{9,11},{12,14},{13,15},{2,0},{3,1},... | collective-permute-start | bytes 86024 | tf_op jit(solution)/shard_map/ppermute | solution.py:61
  88.4 5.1 %collective-permute-start.24 = (bf16[112,128]{1,0:T(8,128)(2,1)S(1)}, bf16[112,128]{1,0:T(8,128)(2,1)S(1)}, u32[]{:S(2)}, u32[]{:S(2)}) collective-permute-start(bf16[112,128]{1,0:T(8,128)(2,1)S(1)} %get-tuple-element.147), channel_id=1, source_target_pairs={{0,18},{1,19},{4,22},{5,23},{8,26},{9,27},{12,30},{13,31},{2,16},{... | collective-permute-start | bytes 86024 | tf_op jit(solution)/shard_map/ppermute | solution.py:61
  93.5 6.5 %collective-permute-start.28 = (bf16[2,240,128]{2,1,0:T(8,128)(2,1)S(1)}, bf16[2,240,128]{2,1,0:T(8,128)(2,1)S(1)}, u32[]{:S(2)}, u32[]{:S(2)}) collective-permute-start(bf16[2,240,128]{2,1,0:T(8,128)(2,1)S(1)} %across.1.refs_0_), channel_id=1, source_target_pairs={{0,8},{1,65},{4,12},{5,69},{8,0},{9,73},{12,4},{13,77},{2,10},{3,6... | collective-permute-start | bytes 368648 | tf_op jit(solution)/shard_map/ppermute | solution.py:61
  95.4 6.1 %collective-permute-start.27 = (bf16[2,240,128]{2,1,0:T(8,128)(2,1)S(1)}, bf16[2,240,128]{2,1,0:T(8,128)(2,1)S(1)}, u32[]{:S(2)}, u32[]{:S(2)}) collective-permute-start(bf16[2,240,128]{2,1,0:T(8,128)(2,1)S(1)} %across.1.refs_0_), channel_id=1, source_target_pairs={{0,12},{1,97},{4,8},{5,101},{8,4},{9,105},{12,0},{13,109},{2,14},{... | collective-permute-start | bytes 368648 | tf_op jit(solution)/shard_map/ppermute | solution.py:61
  96.7 4.9 %collective-permute-start.26 = (bf16[2,240,128]{2,1,0:T(8,128)(2,1)S(1)}, bf16[2,240,128]{2,1,0:T(8,128)(2,1)S(1)}, u32[]{:S(2)}, u32[]{:S(2)}) collective-permute-start(bf16[2,240,128]{2,1,0:T(8,128)(2,1)S(1)} %across.1.refs_0_), channel_id=1, source_target_pairs={{0,4},{1,33},{4,0},{5,37},{8,12},{9,41},{12,8},{13,45},{2,6},{3,35... | collective-permute-start | bytes 368648 | tf_op jit(solution)/shard_map/ppermute | solution.py:61
  101.6 1.2 %collective-permute-start.29 = (bf16[16,128]{1,0:T(8,128)(2,1)S(1)}, bf16[16,128]{1,0:T(8,128)(2,1)S(1)}, u32[]{:S(2)}, u32[]{:S(2)}) collective-permute-start(bf16[16,128]{1,0:T(8,128)(2,1)S(1)} %get-tuple-element.150), channel_id=1, source_target_pairs={{0,1},{1,0},{4,5},{5,4},{8,9},{9,8},{12,13},{13,12},{2,3},{3,2},{6... | collective-permute-start | bytes 12296 | tf_op jit(solution)/shard_map/ppermute | solution.py:61
  102.9 7.8 %collective-permute-start.35 = (bf16[4,240,128]{2,1,0:T(8,128)(2,1)S(1)}, bf16[4,240,128]{2,1,0:T(8,128)(2,1)S(1)}, u32[]{:S(2)}, u32[]{:S(2)}) collective-permute-start(bf16[4,240,128]{2,1,0:T(8,128)(2,1)S(1)} %get-tuple-element.152.refs_0_), channel_id=1, source_target_pairs={{0,64},{1,9},{4,68},{5,13},{8,72},{9,1},{12,76},{13,5},{2,66},{3,1... | collective-permute-start | bytes 737288 | tf_op jit(solution)/shard_map/ppermute | solution.py:61
  104.4 8.8 %collective-permute-start.34 = (bf16[4,240,128]{2,1,0:T(8,128)(2,1)S(1)}, bf16[4,240,128]{2,1,0:T(8,128)(2,1)S(1)}, u32[]{:S(2)}, u32[]{:S(2)}) collective-permute-start(bf16[4,240,128]{2,1,0:T(8,128)(2,1)S(1)} %get-tuple-element.152.refs_0_), channel_id=1, source_target_pairs={{0,96},{1,13},{4,100},{5,9},{8,104},{9,5},{12,108},{13,1},{2,98},{... | collective-permute-start | bytes 737288 | tf_op jit(solution)/shard_map/ppermute | solution.py:61
  105.6 7.6 %collective-permute-start.33 = (bf16[4,240,128]{2,1,0:T(8,128)(2,1)S(1)}, bf16[4,240,128]{2,1,0:T(8,128)(2,1)S(1)}, u32[]{:S(2)}, u32[]{:S(2)}) collective-permute-start(bf16[4,240,128]{2,1,0:T(8,128)(2,1)S(1)} %get-tuple-element.152.refs_0_), channel_id=1, source_target_pairs={{0,32},{1,5},{4,36},{5,1},{8,40},{9,13},{12,44},{13,9},{2,34},{3,7... | collective-permute-start | bytes 737288 | tf_op jit(solution)/shard_map/ppermute | solution.py:61
  106.4 9.7 %collective-permute-start.32 = (bf16[4,240,128]{2,1,0:T(8,128)(2,1)S(1)}, bf16[4,240,128]{2,1,0:T(8,128)(2,1)S(1)}, u32[]{:S(2)}, u32[]{:S(2)}) collective-permute-start(bf16[4,240,128]{2,1,0:T(8,128)(2,1)S(1)} %get-tuple-element.151.refs_0_), channel_id=1, source_target_pairs={{0,64},{1,9},{4,68},{5,13},{8,72},{9,1},{12,76},{13,5},{2,66},{3,1... | collective-permute-start | bytes 737288 | tf_op jit(solution)/shard_map/ppermute | solution.py:61
  109.1 9.4 %collective-permute-start.31 = (bf16[4,240,128]{2,1,0:T(8,128)(2,1)S(1)}, bf16[4,240,128]{2,1,0:T(8,128)(2,1)S(1)}, u32[]{:S(2)}, u32[]{:S(2)}) collective-permute-start(bf16[4,240,128]{2,1,0:T(8,128)(2,1)S(1)} %get-tuple-element.151.refs_0_), channel_id=1, source_target_pairs={{0,96},{1,13},{4,100},{5,9},{8,104},{9,5},{12,108},{13,1},{2,98},{... | collective-permute-start | bytes 737288 | tf_op jit(solution)/shard_map/ppermute | solution.py:61
  110.7 7.9 %collective-permute-start.30 = (bf16[4,240,128]{2,1,0:T(8,128)(2,1)S(1)}, bf16[4,240,128]{2,1,0:T(8,128)(2,1)S(1)}, u32[]{:S(2)}, u32[]{:S(2)}) collective-permute-start(bf16[4,240,128]{2,1,0:T(8,128)(2,1)S(1)} %get-tuple-element.151.refs_0_), channel_id=1, source_target_pairs={{0,32},{1,5},{4,36},{5,1},{8,40},{9,13},{12,44},{13,9},{2,34},{3,7... | collective-permute-start | bytes 737288 | tf_op jit(solution)/shard_map/ppermute | solution.py:61
